TPU v7x, 256 devices: a whole 4x4x8 slice. The times are simulated.
256 devices in a mesh: dp: 4 (over x_hi, core), ctx: 64 (over x_lo, y, z).
Axes of the slice: x: 4 (x_hi: 2, x_lo: 2; x = x_hi * 2 + x_lo), y: 4, z: 8, core: 2. Of those that a mesh axis runs over, the one named last changes fastest.
Arguments:
- hidden: bfloat16 [49152, 1024], P(('dp', 'ctx')), parts along dimension 0, may hold values from -6 to 6
- flow_input: bfloat16 [64, 49152], P(None, ('dp', 'ctx')), parts along dimension 1, may hold values from -6 to 6
- w_query: bfloat16 [1024, 512], replicated, may hold values from -6 to 6
- w_key: bfloat16 [1024, 512], replicated, may hold values from -6 to 6
- w_value: bfloat16 [1024, 512], replicated, may hold values from -0.1875 to 0.1875
- w_output: bfloat16 [512, 1024], replicated, may hold values from -0.25 to 0.25
- w_up: bfloat16 [1024, 2048], replicated, may hold values from -0.1875 to 0.1875
- w_down: bfloat16 [2048, 1024], replicated, may hold values from -0.125 to 0.125
- w_shift: bfloat16 [64, 1024], replicated, may hold values from -0.1875 to 0.1875
- w_scale: bfloat16 [64, 1024], replicated, may hold values from -0.09375 to 0.09375
Outputs:
- latent: float32 [64, 49152], P(None, ('dp', 'ctx')), parts along dimension 1
- log_det: float32 [49152], P(('dp', 'ctx')), parts along dimension 0
There are 4 independent parts, one for each index of `dp`. A program takes and returns all parts, laid end to end along the dimension named above; an argument that names none is the same for every part. Nothing has to cross between parts.
All inputs are finite; a program needn't handle non-finite values.
Results may differ from a plain program's by a relative error of at most 0.015.
Values may be sent and summed in bfloat16 or wider, within the bound.
No kernel may reach another device: no remote copies, remote signals or barrier semaphores. Data moves between devices by JAX's collectives and lax.ppermute only.
A program may use at most 128 MiB of HBM per device.

v0:
```python
import math

import jax
import jax.numpy as jnp
from jax import lax
from jax.sharding import PartitionSpec as P

HEADS = 4
HEAD = 128


epsilon = 1e-05
masked_score = -1e30


def partner(block, axis, apart):
    count = lax.axis_size(axis)
    route = []
    for low in range(count):
        high = low | 1 << apart
        if high != low and high < count:
            route += [(low, high), (high, low)]
    return lax.ppermute(block, axis, route)


def layer_norm(values):
    mean = jnp.mean(values, axis=-1, keepdims=True)
    centred = values - mean
    spread = jnp.mean(centred * centred, axis=-1, keepdims=True)
    return centred * lax.rsqrt(spread + epsilon)


def attend_block(state, queries, query_place, keys, values, key_place, scale):
    top, total, numer = state
    scores = jnp.einsum("hqd,khd->hqk", queries, keys, preferred_element_type=jnp.float32) * scale
    allowed = key_place[None, None, :] <= query_place[None, :, None]
    scores = jnp.where(allowed, scores, masked_score)
    new_top = jnp.maximum(top, jnp.max(scores, axis=-1))
    weights = jnp.where(allowed, jnp.exp(scores - new_top[..., None]), 0.0)
    factor = jnp.exp(top - new_top)
    total = total * factor + jnp.sum(weights, axis=-1)
    numer = numer * factor[..., None] + jnp.einsum(
        "hqk,khd->hqd", weights.astype(jnp.bfloat16), values, preferred_element_type=jnp.float32
    )
    return (new_top, total, numer)


def on_device(
    hidden, flow_input, w_query, w_key, w_value, w_output, w_up, w_down, w_shift, w_scale
):
    rows = hidden.shape[0]
    half = rows // 2
    count = lax.axis_size("ctx")
    index = lax.axis_index("ctx")
    bits = count.bit_length() - 1
    residual = hidden.astype(jnp.float32)
    normed = layer_norm(residual).astype(jnp.bfloat16)
    queries = jnp.dot(normed, w_query, preferred_element_type=jnp.float32).astype(jnp.bfloat16)
    keys = jnp.dot(normed, w_key, preferred_element_type=jnp.float32).astype(jnp.bfloat16)
    values = jnp.dot(normed, w_value, preferred_element_type=jnp.float32).astype(jnp.bfloat16)
    local_place = index * rows + jnp.arange(rows, dtype=jnp.int32)
    query_heads = jnp.transpose(queries.reshape(rows, HEADS, HEAD), (1, 0, 2))
    scale = HEAD ** (-0.5)
    empty = (
        jnp.full((HEADS, half), masked_score, jnp.float32),
        jnp.zeros((HEADS, half), jnp.float32),
        jnp.zeros((HEADS, half, HEAD), jnp.float32),
    )
    state = (empty, empty)
    key_piece = lax.all_gather(keys, "ctx", axis=0, tiled=True)
    value_piece = lax.all_gather(values, "ctx", axis=0, tiled=True)
    length = key_piece.shape[0]
    block = math.gcd(length, 512)
    units = length // block
    key_blocks = key_piece.reshape(units, block, HEADS, HEAD)
    value_blocks = value_piece.reshape(units, block, HEADS, HEAD)

    def one_block(carry, item):
        key_block, value_block, unit = item
        flat = unit * block + jnp.arange(block, dtype=jnp.int32)
        first_key = jnp.min(flat)
        updated = []
        for side in range(2):
            query_place = local_place[side * half : (side + 1) * half]
            side_queries = query_heads[:, side * half : (side + 1) * half]
            updated.append(
                lax.cond(
                    first_key > jnp.max(query_place),
                    lambda kept: kept,
                    lambda kept: attend_block(
                        kept, side_queries, query_place, key_block, value_block, flat, scale
                    ),
                    carry[side],
                )
            )
        return (tuple(updated), None)

    state, unused = lax.scan(
        one_block, state, (key_blocks, value_blocks, jnp.arange(units, dtype=jnp.int32))
    )
    mixed = jnp.concatenate(
        [state[0][2] / state[0][1][..., None], state[1][2] / state[1][1][..., None]], axis=1
    )
    attended = jnp.transpose(mixed, (1, 0, 2)).reshape(rows, HEADS * HEAD).astype(jnp.bfloat16)
    first = residual + jnp.dot(attended, w_output, preferred_element_type=jnp.float32)
    inner = layer_norm(first).astype(jnp.bfloat16)
    expanded = jax.nn.gelu(jnp.dot(inner, w_up, preferred_element_type=jnp.float32)).astype(
        jnp.bfloat16
    )
    second = first + jnp.dot(expanded, w_down, preferred_element_type=jnp.float32)
    features = layer_norm(second).astype(jnp.bfloat16)
    shift = lax.dot_general(
        w_shift, features, (((1,), (1,)), ((), ())), preferred_element_type=jnp.float32
    )
    log_scale = lax.dot_general(
        w_scale, features, (((1,), (1,)), ((), ())), preferred_element_type=jnp.float32
    )
    moved = (flow_input.astype(jnp.float32) - shift) * jnp.exp(-log_scale)
    token_det = -jnp.sum(log_scale, axis=0)
    whole_moved, whole_det = (moved, token_det)
    for bit in range(bits):
        whole_moved, whole_det = (
            partner(whole_moved.astype(jnp.bfloat16), "ctx", bit).astype(whole_moved.dtype),
            partner(whole_det.astype(jnp.bfloat16), "ctx", bit).astype(whole_det.dtype),
        )
    latent = whole_moved[:, ::-1]
    log_det = whole_det[::-1]
    return (latent, log_det)


def solution(mesh):
    in_specs = (
        P(("dp", "ctx"), None),
        P(None, ("dp", "ctx")),
        P(),
        P(),
        P(),
        P(),
        P(),
        P(),
        P(),
        P(),
    )
    out_specs = (P(None, ("dp", "ctx")), P(("dp", "ctx")))
    return jax.shard_map(
        on_device, mesh=mesh, in_specs=in_specs, out_specs=out_specs, check_vma=False
    )
```

profile of v0, /device:TPU:24, one launch (start us, length us, event | category | flops | bytes accessed | tf_op | source)
XLA Modules:
  0.0 956.8 jit_solution(11750502018904992015)
XLA Ops:
  7.2 1.2 convert_reduce_fusion
  8.5 1.2 fusion.35
  9.7 2.5 convolution_convert_fusion.2
  12.3 2.5 convolution_convert_fusion.1
  14.8 1.7 fusion.29
  17.3 311.4 %all-gather.3.cloned.1.call-done = bf16[12288,512]{1,0:T(8,128)(2,1)} async-done(((bf16[192,512]{1,0:T(8,128)(2,1)}), bf16[12288,512]{1,0:T(8,128)(2,1)}) %all-gather.3.cloned.1.call-update) | async-done | bytes 12582928 | tf_op jit(solution)/shard_map/all_gather | solution.py:70
  328.6 18.2 %reshape.123 = bf16[24,512,4,128]{3,2,1,0:T(4,128)(2,1)} reshape(bf16[12288,512]{1,0:T(8,128)(2,1)} %all-gather.3.cloned.1.call-done) | data formatting | bytes 25165824 | tf_op jit(solution)/shard_map/reshape | solution.py:75
  346.8 305.8 %all-gather.5.cloned.1.call-done = bf16[12288,512]{1,0:T(8,128)(2,1)} async-done(((bf16[192,512]{1,0:T(8,128)(2,1)}), bf16[12288,512]{1,0:T(8,128)(2,1)}) %all-gather.5.cloned.1.call-update) | async-done | bytes 12582928 | tf_op jit(solution)/shard_map/all_gather | solution.py:71
  652.6 18.1 %reshape.124 = bf16[24,512,4,128]{3,2,1,0:T(4,128)(2,1)} reshape(bf16[12288,512]{1,0:T(8,128)(2,1)} %all-gather.5.cloned.1.call-done) | data formatting | bytes 25165824 | tf_op jit(solution)/shard_map/reshape | solution.py:76
  670.8 173.0 %while.22 = (s32[]{:T(128)}, f32[4,96]{1,0:T(4,128)S(1)}, f32[4,96]{1,0:T(4,128)S(1)}, f32[4,96,128]{2,1,0:T(8,128)S(1)}, f32[4,96]{1,0:T(4,128)S(1)}, /*index=5...) while((s32[]{:T(128)}, f32[4,96]{1,0:T(4,128)S(1)}, ...), condition=%wide.region_14.15_spmd.clone, body=%wide.region_4.14_spmd.clone.sunk | while | flops 205163200 | bytes 12445113 | solution.py:98
  670.8 1.6 constant_dynamic-slice_fusion.3
  675.6 1.3 conditional.7
  679.5 1.6 constant_dynamic-slice_fusion.3
  684.2 1.3 conditional.7
  686.9 1.2 conditional.6
  688.1 1.6 constant_dynamic-slice_fusion.3
  692.9 1.3 conditional.7
  695.5 1.2 conditional.6
  696.8 1.6 constant_dynamic-slice_fusion.3
  701.5 1.3 conditional.7
  704.2 1.2 conditional.6
  705.4 1.6 constant_dynamic-slice_fusion.3
  710.2 1.3 conditional.7
  714.1 1.6 constant_dynamic-slice_fusion.3
  718.8 1.3 conditional.7
  722.7 1.6 constant_dynamic-slice_fusion.3
  727.5 1.3 conditional.7
  731.4 1.6 constant_dynamic-slice_fusion.3
  736.1 1.3 conditional.7
  740.0 1.6 constant_dynamic-slice_fusion.3
  744.8 1.3 conditional.7
  748.7 1.6 constant_dynamic-slice_fusion.3
  753.4 1.3 conditional.7
  757.3 1.6 constant_dynamic-slice_fusion.3
  763.5 1.6 constant_dynamic-slice_fusion.3
  769.7 1.6 constant_dynamic-slice_fusion.3
  775.9 1.6 constant_dynamic-slice_fusion.3
  782.0 1.6 constant_dynamic-slice_fusion.3
  788.2 1.6 constant_dynamic-slice_fusion.3
  794.4 1.6 constant_dynamic-slice_fusion.3
  800.6 1.6 constant_dynamic-slice_fusion.3
  806.8 1.6 constant_dynamic-slice_fusion.3
  812.9 1.6 constant_dynamic-slice_fusion.3
  819.1 1.6 constant_dynamic-slice_fusion.3
  825.3 1.6 constant_dynamic-slice_fusion.3
  831.5 1.6 constant_dynamic-slice_fusion.3
  837.7 1.6 constant_dynamic-slice_fusion.3
  844.8 5.8 fusion.59
  852.8 2.8 collective-permute-done
  855.6 7.1 collective-permute-start.1
  862.7 1.9 collective-permute-done.1
  864.5 13.5 %collective-permute-start.2 = (bf16[64,192]{1,0:T(8,128)(2,1)S(1)}, bf16[64,192]{1,0:T(8,128)(2,1)S(1)}, u32[]{:S(2)}, u32[]{:S(2)}) collective-permute-start(bf16[64,192]{1,0:T(8,128)(2,1)S(1)} %collective-permute-done.1), channel_id=1, source_target_pairs={{0,4},{4,0},{1,5},{5,1},{2,6},{6,2},{3,7},{7,3},{8,12},{12,8},{9,1... | collective-permute-start | bytes 73736 | tf_op jit(solution)/shard_map/ppermute | solution.py:23
  878.1 1.9 collective-permute-done.2
  880.0 3.9 collective-permute-done.3
  883.9 5.4 collective-permute-done.4
  889.3 31.1 %collective-permute-start.5 = (bf16[64,192]{1,0:T(8,128)(2,1)S(1)}, bf16[64,192]{1,0:T(8,128)(2,1)S(1)}, u32[]{:S(2)}, u32[]{:S(2)}) collective-permute-start(bf16[64,192]{1,0:T(8,128)(2,1)S(1)} %collective-permute-done.4), channel_id=1, source_target_pairs={{0,32},{32,0},{1,33},{33,1},{2,34},{34,2},{3,35},{35,3},{4,36},{36... | collective-permute-start | bytes 73736 | tf_op jit(solution)/shard_map/ppermute | solution.py:23
  921.4 2.5 collective-permute-done.6
  923.9 3.0 collective-permute-start.7
  926.9 1.5 collective-permute-done.7
  928.4 6.3 collective-permute-start.8
  934.6 1.5 collective-permute-done.8
  936.2 3.5 collective-permute-done.9
  939.7 5.0 collective-permute-done.10
  944.8 3.5 collective-permute-done.11
  (423 shorter events, 73.9 us)
Async XLA Ops:
  7.2 836.9 %copy-start = (bf16[512,1024]{1,0:T(8,128)(2,1)S(1)}, bf16[512,1024]{1,0:T(8,128)(2,1)}, u32[]{:S(2)}) copy-start(bf16[512,1024]{1,0:T(8,128)(2,1)} %param.21) | copy-start | bytes 3145732
  7.2 7.6 copy-start.1
  7.2 321.5 %all-gather.3.cloned.1.call-start = ((), (), s32[]{:S(2)}) async-start(), calls=%async_computation | async-start | bytes 12779520 | tf_op jit(solution)/shard_map/all_gather | solution.py:70
  12.2 640.4 %all-gather.5.cloned.1.call-start = ((), (), s32[]{:S(2)}) async-start(), calls=%async_computation.1 | async-start | bytes 12779520 | tf_op jit(solution)/shard_map/all_gather | solution.py:71
  844.8 6.3 copy-start.3
  844.8 6.5 copy-start.2
  844.8 6.5 copy-start.4
  851.6 4.0 collective-permute-start
  855.6 9.0 collective-permute-start.1
  864.5 15.4 %collective-permute-start.2 = (bf16[64,192]{1,0:T(8,128)(2,1)S(1)}, bf16[64,192]{1,0:T(8,128)(2,1)S(1)}, u32[]{:S(2)}, u32[]{:S(2)}) collective-permute-start(bf16[64,192]{1,0:T(8,128)(2,1)S(1)} %collective-permute-done.1), channel_id=1, source_target_pairs={{0,4},{4,0},{1,5},{5,1},{2,6},{6,2},{3,7},{7,3},{8,12},{12,8},{9,1... | collective-permute-start | bytes 73736 | tf_op jit(solution)/shard_map/ppermute | solution.py:23
  880.0 3.9 collective-permute-start.3
  883.9 5.4 collective-permute-start.4
  889.3 59.7 %collective-permute-start.5 = (bf16[64,192]{1,0:T(8,128)(2,1)S(1)}, bf16[64,192]{1,0:T(8,128)(2,1)S(1)}, u32[]{:S(2)}, u32[]{:S(2)}) collective-permute-start(bf16[64,192]{1,0:T(8,128)(2,1)S(1)} %collective-permute-done.4), channel_id=1, source_target_pairs={{0,32},{32,0},{1,33},{33,1},{2,34},{34,2},{3,35},{35,3},{4,36},{36... | collective-permute-start | bytes 73736 | tf_op jit(solution)/shard_map/ppermute | solution.py:23
  920.4 3.5 collective-permute-start.6
  923.9 4.5 collective-permute-start.7
  928.4 7.8 collective-permute-start.8
  936.2 3.5 collective-permute-start.9
  939.7 5.0 collective-permute-start.10
  944.8 3.5 collective-permute-start.11
Sparse Core Ops, SparseCore 0:
  12.3 316.2 all-gather.2
  330.4 322.1 all-gather.4
where the time goes:
time: 959 us; the launch traced here: 957 us
  waiting for transfers between devices  651 us (68%)
  local copies, waits for them, and re-layouts  93.9 us (10%)
  loops' own time  77.8 us (8%)
  starting transfers between devices  63.3 us (7%)
  matrix products  28.6 us (3%)
  other arithmetic  28.2 us (3%)
  between operations  14.2 us (1%)
    all_gather x1, waiting for transfers between devices, on_device(): key_piece = lax.all_gather(keys, 'ctx', axis=0, tiled=True)  311 us
    all_gather x1, waiting for transfers between devices, on_device(): value_piece = lax.all_gather(values, 'ctx', axis=0, tiled=True)  306 us
    another operation x1, loops' own time, on_device(): lax.scan(one_block, state, (key_blocks, value_blocks, jnp.arange(units, d...  76.3 us
    ppermute x12, starting transfers between devices, partner(): return lax.ppermute(block, axis, route)  63.2 us
    dynamic_slice x96, local copies, waits for them, and re-layouts, on_device(): lax.scan(one_block, state, (key_blocks, value_blocks, jnp.arange(units, d...  54.9 us
    ppermute x12, waiting for transfers between devices, partner(): return lax.ppermute(block, axis, route)  33.5 us
  transfers between devices with their start and end apart: 14, of which 13 were waited for; matrix products, arithmetic and copies ran while one was open for 2% of the time, Pallas kernels for 0%

commit v1 on v0

v1 whole, which is shorter than its diff:
```python
import functools

import jax
import jax.numpy as jnp
from jax import lax
from jax.experimental import pallas as pl
from jax.experimental.pallas import tpu as pltpu
from jax.sharding import Mesh, PartitionSpec as P

HEADS = 4
HEAD = 128
epsilon = 1e-05
masked_score = -2e30
lowest = -1e30
POWER = HEAD**-0.5 * 1.4426950408889634
bf16 = jnp.bfloat16
f32 = jnp.float32
VMEM_LIMIT = 50 * 1024 * 1024

XL, Y, Z = 2, 4, 8
PLANES = XL * Y
TOKENS = 192
PIECE = TOKENS // 2
ROWS = PLANES * PIECE
TILE = 2 * TOKENS


def layer_norm(values):
    mean = jnp.mean(values, axis=-1, keepdims=True)
    centred = values - mean
    spread = jnp.mean(centred * centred, axis=-1, keepdims=True)
    return centred * lax.rsqrt(spread + epsilon)


def vmem():
    return pl.BlockSpec(memory_space=pltpu.VMEM)


def smem():
    return pl.BlockSpec(memory_space=pltpu.SMEM)


def params():
    return pltpu.CompilerParams(vmem_limit_bytes=VMEM_LIMIT)


def key_value_kernel(place, own, other, w_key, w_value, slots, normed):
    core = place[0]
    for part, rows in enumerate((own, other)):
        normed[part * PIECE : (part + 1) * PIECE, :] = layer_norm(rows[...].astype(f32)).astype(bf16)
    for column, weight in enumerate((w_key, w_value)):
        made = jnp.dot(normed[...], weight[...], preferred_element_type=f32).astype(bf16)
        for part in range(2):
            sequence = core if part == 0 else 1 - core
            for head in range(HEADS):
                slots[sequence * HEADS + head, :, column * HEAD : (column + 1) * HEAD] = made[
                    part * PIECE : (part + 1) * PIECE, head * HEAD : (head + 1) * HEAD
                ]


def query_kernel(place, normed, w_query, slots):
    core = place[0]
    made = jnp.dot(normed[...], w_query[...], preferred_element_type=f32).astype(bf16)
    for part in range(2):
        sequence = core if part == 0 else 1 - core
        for head in range(HEADS):
            slots[sequence * HEADS + head] = made[
                part * PIECE : (part + 1) * PIECE, head * HEAD : (head + 1) * HEAD
            ]


def attend_kernel(parts, sources, first, last, *refs):
    refs = list(refs)
    place = refs.pop(0)
    queries = refs.pop(0)
    segments = [refs.pop(0) for _ in parts]
    if first:
        top_in = total_in = numer_in = None
    else:
        top_in, total_in, numer_in = refs[:3]
        refs = refs[3:]
    core = place[0]
    ones = jnp.ones((2 * TOKENS, HEAD), bf16)
    row = lax.broadcasted_iota(jnp.int32, (TILE, 1), 0)
    row_side = (row % TOKENS) // PIECE
    row_half = jnp.where(row_side == 0, core, 1 - core)
    row_place = (row // TOKENS) * (Z * TOKENS) + row_half * PIECE + row % PIECE
    key = lax.broadcasted_iota(jnp.int32, (1, 2 * TOKENS), 1)
    key_place = (key // PIECE) * (Z * TOKENS) + key % PIECE + core * PIECE
    for tile in range(4):
        rows = slice(tile * TILE, (tile + 1) * TILE)
        tile_queries = queries[rows, :]
        scores = []
        for segment, part, source in zip(segments, parts, sources):
            groups = min(2, tile + 1 - 2 * part)
            if groups <= 0:
                continue
            count = groups * TOKENS
            product = lax.dot_general(
                tile_queries,
                segment[:count, :HEAD],
                (((1,), (1,)), ((), ())),
                preferred_element_type=f32,
            )
            if 2 * part + groups - 1 == tile:
                shift = place[1 + source] * TOKENS
                offset = (2 * (tile - 2 * part)) * (Z * TOKENS)
                allowed = key_place[:, :count] + shift <= row_place + offset
                product = jnp.where(allowed, product, masked_score)
            scores.append((segment, count, product))
        top = lowest if first else top_in[rows, :1]
        new_top = functools.reduce(
            jnp.maximum, [jnp.max(product, axis=-1, keepdims=True) for _, _, product in scores], top
        )
        sums = None
        for segment, count, product in scores:
            weights = jnp.exp2((product - new_top) * POWER).astype(bf16)
            with_ones = jnp.concatenate([segment[:count, HEAD:], ones[:count]], axis=1)
            term = jnp.dot(weights, with_ones, preferred_element_type=f32)
            sums = term if sums is None else sums + term
        numer, total = sums[:, :HEAD], sums[:, HEAD:]
        if not first:
            factor = jnp.exp2((top - new_top) * POWER)
            numer = numer + numer_in[rows, :] * factor
            total = total + total_in[rows, :] * factor
        new_top = jnp.broadcast_to(new_top, (TILE, HEAD))
        if not last:
            top_out, total_out, numer_out = refs
            top_out[rows, :] = new_top
            total_out[rows, :] = total
            numer_out[rows, :] = numer
        else:
            some = total > 0
            mixed = numer / jnp.where(some, total, 1.0)
            level = jnp.where(some, new_top * POWER + jnp.log2(jnp.where(some, total, 1.0)), lowest)
            high = level.astype(bf16)
            rest = level - high.astype(f32)
            middle = rest.astype(bf16)
            low = (rest - middle.astype(f32)).astype(bf16)
            lane = lax.broadcasted_iota(jnp.int32, (TILE, HEAD), 1)
            level = jnp.where(lane == 0, high, jnp.where(lane == 1, middle, low))
            for plane in range(2):
                for side in range(2):
                    start = plane * TOKENS + side * PIECE
                    out = refs[side]
                    out[2 * tile + plane, :, :HEAD] = mixed[start : start + PIECE].astype(bf16)
                    out[2 * tile + plane, :, HEAD:] = level[start : start + PIECE]


def attend(place, queries, segments, parts, sources, state, last):
    first = state is None
    keys = sum(segment.shape[0] for segment in segments)
    stat = jax.ShapeDtypeStruct((2 * ROWS, HEAD), f32)
    done = jax.ShapeDtypeStruct((PLANES, PIECE, 2 * HEAD), bf16)
    operands = [place, queries, *segments, *(state or ())]
    return pl.pallas_call(
        functools.partial(attend_kernel, parts, sources, first, last),
        out_shape=[done] * 2 if last else [stat] * 3,
        in_specs=[smem()] + [vmem()] * (len(operands) - 1),
        out_specs=[vmem()] * (2 if last else 3),
        compiler_params=params(),
        cost_estimate=pl.CostEstimate(
            flops=2 * ROWS * keys * HEAD * 6,
            bytes_accessed=4_000_000,
            transcendentals=ROWS * keys,
        ),
    )(*operands)


def shift_by(count, step):
    return [(index, (index + step) % count) for index in range(count)]


def merge(mine, theirs):
    def level(block):
        return sum(block[..., HEAD + index : HEAD + index + 1].astype(f32) for index in range(3))

    first, second = level(mine), level(theirs)
    top = jnp.maximum(first, second)
    first, second = jnp.exp2(first - top), jnp.exp2(second - top)
    both = first * mine[..., :HEAD].astype(f32) + second * theirs[..., :HEAD].astype(f32)
    return (both / (first + second)).astype(bf16)


def on_device(
    hidden, flow_input, w_query, w_key, w_value, w_output, w_up, w_down, w_shift, w_scale
):
    core = lax.axis_index("core")
    other_core = shift_by(2, 1)
    own = lax.dynamic_slice_in_dim(hidden, core * PIECE, PIECE, 0)
    other = lax.ppermute(
        lax.dynamic_slice_in_dim(hidden, (1 - core) * PIECE, PIECE, 0), "core", other_core
    )
    own_flow = lax.dynamic_slice_in_dim(flow_input, core * PIECE, PIECE, 1)
    other_flow = lax.ppermute(
        lax.dynamic_slice_in_dim(flow_input, (1 - core) * PIECE, PIECE, 1), "core", other_core
    )
    z = lax.axis_index("z")
    up_steps = [(z - step) % Z - z for step in range(5)]
    down_steps = [(z + step) % Z - z for step in range(4)]
    place = jnp.stack([core, *up_steps, *down_steps]).astype(jnp.int32)

    slots, normed = pl.pallas_call(
        key_value_kernel,
        out_shape=[
            jax.ShapeDtypeStruct((PLANES, PIECE, 2 * HEAD), bf16),
            jax.ShapeDtypeStruct((TOKENS, hidden.shape[1]), bf16),
        ],
        in_specs=[smem()] + [vmem()] * 4,
        out_specs=[vmem()] * 2,
        compiler_params=params(),
    )(place, own, other, w_key, w_value)
    keys_values = lax.all_to_all(slots, ("xl", "y"), 0, 0, tiled=True).reshape(ROWS, 2 * HEAD)
    slots = pl.pallas_call(
        query_kernel,
        out_shape=jax.ShapeDtypeStruct((PLANES, PIECE, HEAD), bf16),
        in_specs=[smem()] + [vmem()] * 2,
        out_specs=vmem(),
        compiler_params=params(),
    )(place, normed, w_query)
    own_queries = lax.all_to_all(slots, ("xl", "y"), 0, 0, tiled=True)
    other_queries = lax.ppermute(own_queries, "core", other_core)
    queries = jnp.stack([own_queries, other_queries], axis=1).reshape(2 * ROWS, HEAD)

    half = ROWS // 2
    up = [keys_values[:half], keys_values[half:]]
    down = list(up)
    state = attend(place, queries, up, (0, 1), (0, 0), None, False)
    for step in range(1, 4):
        for part in range(2):
            up[part] = lax.ppermute(up[part], "z", shift_by(Z, 1))
            down[part] = lax.ppermute(down[part], "z", shift_by(Z, -1))
        state = attend(
            place,
            queries,
            up + down,
            (0, 1, 0, 1),
            (step, step, 5 + step, 5 + step),
            state,
            False,
        )
    far = [
        lax.ppermute(up[0], "z", shift_by(Z, 1)),
        lax.ppermute(down[1], "z", shift_by(Z, -1)),
    ]
    mine, others = attend(place, queries, far, (0, 1), (4, 4), state, True)
    attended = merge(mine, lax.ppermute(others, "core", other_core))
    attended = lax.all_to_all(attended, ("xl", "y"), 0, 0, tiled=True)
    attended = attended.reshape(2, HEADS, PIECE, HEAD)
    attended = jnp.where(core == 0, attended, attended[::-1])
    attended = jnp.transpose(attended, (0, 2, 1, 3)).reshape(TOKENS, HEADS * HEAD)

    residual = jnp.concatenate([own, other], axis=0).astype(f32)
    first = residual + jnp.dot(attended, w_output, preferred_element_type=f32)
    inner = layer_norm(first).astype(bf16)
    expanded = jax.nn.gelu(jnp.dot(inner, w_up, preferred_element_type=f32)).astype(bf16)
    second = first + jnp.dot(expanded, w_down, preferred_element_type=f32)
    features = layer_norm(second).astype(bf16)
    shift = lax.dot_general(
        w_shift, features, (((1,), (1,)), ((), ())), preferred_element_type=f32
    )
    log_scale = lax.dot_general(
        w_scale, features, (((1,), (1,)), ((), ())), preferred_element_type=f32
    )
    flow = jnp.concatenate([own_flow, other_flow], axis=1).astype(f32)
    moved = (flow - shift) * jnp.exp(-log_scale)
    token_det = -jnp.sum(log_scale, axis=0, keepdims=True)
    det_high = token_det.astype(bf16)
    det_low = (token_det - det_high.astype(f32)).astype(bf16)
    sent = jnp.concatenate([moved.astype(bf16), det_high, det_low], axis=0)
    blocks = XL * Y * Z
    same = [
        (side * blocks + index, side * blocks + blocks - 1 - index)
        for side in range(2)
        for index in range(blocks)
    ]
    crossed = [
        (side * blocks + index, (1 - side) * blocks + blocks - 1 - index)
        for side in range(2)
        for index in range(blocks)
    ]
    axes = ("core", "xl", "y", "z")
    from_same = lax.ppermute(sent[:, :PIECE], axes, same)
    from_crossed = lax.ppermute(sent[:, PIECE:], axes, crossed)
    arrived = jnp.where(
        core == 0,
        jnp.concatenate([from_crossed, from_same], axis=1),
        jnp.concatenate([from_same, from_crossed], axis=1),
    )
    arrived = arrived.astype(f32).reshape(-1, 2, PIECE)[:, :, ::-1].reshape(-1, TOKENS)
    return (arrived[:64], arrived[64] + arrived[65])


def solution(mesh):
    parts = Mesh(mesh.devices.reshape(2, 2, XL, Y, Z), ("xh", "core", "xl", "y", "z"))
    everywhere = ("xh", "core", "xl", "y", "z")
    in_specs = (P(everywhere, None), P(None, everywhere)) + (P(),) * 8
    out_specs = (P(None, everywhere), P(everywhere))
    return jax.shard_map(
        on_device, mesh=parts, in_specs=in_specs, out_specs=out_specs, check_vma=False
    )
```

time: 959 us -> 124 us (0.13)
  the two profiles are of different devices: /device:TPU:24 before, /device:TPU:1 now
where the time goes in v1:
time: 124 us; the launch traced here: 123 us
  starting transfers between devices  53.9 us (43%)
  Pallas kernels  27 us (22%)
  waiting for transfers between devices  17 us (14%)
  local copies, waits for them, and re-layouts  14.4 us (12%)
  matrix products  6.78 us (5%)
  other arithmetic  2.7 us (2%)
    pallas_call x5, Pallas kernels, attend(): pl.pallas_call(functools.partial(attend_kernel, parts, sources, first, la...  23.3 us
    ppermute x6, starting transfers between devices, on_device(): down[part] = lax.ppermute(down[part], 'z', shift_by(Z, -1))  17.9 us
    unnamed x32, local copies, waits for them, and re-layouts  11.2 us
    ppermute x1, starting transfers between devices, on_device(): attended = merge(mine, lax.ppermute(others, 'core', other_core))  5.82 us
    dot_general x1, matrix products, on_device(): second = first + jnp.dot(expanded, w_down, preferred_element_type=f32)  5.78 us
    all_to_all x1, starting transfers between devices, on_device(): attended = lax.all_to_all(attended, ('xl', 'y'), 0, 0, tiled=True)  5.25 us
    all_to_all x1, waiting for transfers between devices, on_device(): lax.all_to_all(slots, ('xl', 'y'), 0, 0, tiled=True).reshape(ROWS, 2 * HEAD)  5.19 us
    all_to_all x1, waiting for transfers between devices, on_device(): attended = lax.all_to_all(attended, ('xl', 'y'), 0, 0, tiled=True)  4.81 us
  transfers between devices with their start and end apart: 23, of which 8 were waited for; matrix products, arithmetic and copies ran while one was open for 6% of the time, Pallas kernels for 18%

profile of v1, /device:TPU:1, one launch (start us, length us, event | category | flops | bytes accessed | tf_op | source)
XLA Modules:
  0.0 122.8 jit_solution(1350880172827800741)
XLA Ops:
  0.7 1.1 constant_dynamic-slice_fusion.1
  1.8 3.3 %collective-permute-start.1 = (bf16[96,1024]{1,0:T(8,128)(2,1)S(1)}, bf16[96,1024]{1,0:T(8,128)(2,1)S(1)}, u32[]{:S(2)}, u32[]{:S(2)}) collective-permute-start(bf16[96,1024]{1,0:T(8,128)(2,1)S(1)} %get-tuple-element.42), channel_id=1, source_target_pairs={{0,64},{64,0},{1,65},{65,1},{2,66},{66,2},{3,67},{67,3},{4,68},{68... | collective-permute-start | bytes 589832 | tf_op jit(solution)/shard_map/ppermute | solution.py:191
  5.1 0.1 stack.49.place.refs_0_
  5.2 1.0 collective-permute-done.1.other
  6.2 1.2 copy-done.2
  7.4 1.2 copy-done.3
  8.6 2.1 %shard_map.113 = (bf16[8,96,256]{2,1,0:T(8,128)(2,1)}, bf16[192,1024]{1,0:T(8,128)(2,1)S(1)}) custom-call(s32[10]{0:T(128)S(1)} %stack.49.place.refs_0_, bf16[96,1024]{1,0:T(8,128)(2,1)S(1)} %get-tuple-element.41.own, bf16[96,1024]{1,0:T(8,128)(2,1)S(1)} %collective-permute-done.1.other, bf16[1024,512]{1,0:T(8,128)(2,1)S(1)} %copy-done.2, ...), custom_call_target="tpu_custom_call" | custom-call | tf_op jit(solution)/shard_map/pallas_call | solution.py:203
  10.7 3.5 %all-to-all-start.1 = ((bf16[8,96,256]{2,1,0:T(8,128)(2,1)}), bf16[8,96,256]{2,1,0:T(8,128)(2,1)S(1)}, u32[]{:S(2)}, u32[]{:S(2)}) async-start(bf16[8,96,256]{2,1,0:T(8,128)(2,1)} %get-tuple-element.19), calls=%async_computation.1 | async-start | bytes 786432 | tf_op jit(solution)/shard_map/all_to_all | solution.py:213
  14.2 1.6 %shard_map.114 = bf16[8,96,128]{2,1,0:T(8,128)(2,1)} custom-call(s32[10]{0:T(128)S(1)} %stack.49.place.refs_0_, bf16[192,1024]{1,0:T(8,128)(2,1)S(1)} %get-tuple-element.18.normed, bf16[1024,512]{1,0:T(8,128)(2,1)S(1)} %copy-done.1), custom_call_target="tpu_custom_call" | custom-call | tf_op jit(solution)/shard_map/pallas_call | solution.py:214
  15.8 5.2 %all-to-all-done.1 = bf16[8,96,256]{2,1,0:T(8,128)(2,1)S(1)} async-done(((bf16[8,96,256]{2,1,0:T(8,128)(2,1)}), bf16[8,96,256]{2,1,0:T(8,128)(2,1)S(1)}, u32[]{:S(2)}, u32[]{:S(2)}) %all-to-all-start.1) | async-done | bytes 393248 | tf_op jit(solution)/shard_map/all_to_all | solution.py:213
  21.0 4.7 %all-to-all-start = ((bf16[8,96,128]{2,1,0:T(8,128)(2,1)}), bf16[8,96,128]{2,1,0:T(8,128)(2,1)S(1)}, u32[]{:S(2)}, u32[]{:S(2)}) async-start(bf16[8,96,128]{2,1,0:T(8,128)(2,1)} %shard_map.114), calls=%async_computation | async-start | bytes 393216 | tf_op jit(solution)/shard_map/all_to_all | solution.py:221
  25.7 1.7 %collective-permute-start.3 = (bf16[384,256]{1,0:T(8,128)(2,1)S(1)}, bf16[384,256]{1,0:T(8,128)(2,1)S(1)}, u32[]{:S(2)}, u32[]{:S(2)}) collective-permute-start(bf16[384,256]{1,0:T(8,128)(2,1)S(1)} %bitcast.51), channel_id=1, source_target_pairs={{0,1},{1,2},{2,3},{3,4},{4,5},{5,6},{6,7},{7,0},{8,9},{9,10},{10,1... | collective-permute-start | bytes 589832 | tf_op jit(solution)/shard_map/ppermute | solution.py:231
  27.5 4.0 %collective-permute-start.7 = (bf16[384,256]{1,0:T(8,128)(2,1)S(1)}, bf16[384,256]{1,0:T(8,128)(2,1)S(1)}, u32[]{:S(2)}, u32[]{:S(2)}) collective-permute-start(bf16[384,256]{1,0:T(8,128)(2,1)S(1)} %bitcast.48), channel_id=1, source_target_pairs={{0,7},{1,0},{2,1},{3,2},{4,3},{5,4},{6,5},{7,6},{8,15},{9,8},{10,9... | collective-permute-start | bytes 589832 | tf_op jit(solution)/shard_map/ppermute | solution.py:232
  31.5 2.7 %collective-permute-start.14 = (bf16[384,256]{1,0:T(8,128)(2,1)S(1)}, bf16[384,256]{1,0:T(8,128)(2,1)S(1)}, u32[]{:S(2)}, u32[]{:S(2)}) collective-permute-start(bf16[384,256]{1,0:T(8,128)(2,1)S(1)} %bitcast.52), channel_id=1, source_target_pairs={{0,7},{1,0},{2,1},{3,2},{4,3},{5,4},{6,5},{7,6},{8,15},{9,8},{10,9... | collective-permute-start | bytes 589832 | tf_op jit(solution)/shard_map/ppermute | solution.py:232
  34.2 2.0 %collective-permute-start.2 = (bf16[8,96,128]{2,1,0:T(8,128)(2,1)S(1)}, bf16[8,96,128]{2,1,0:T(8,128)(2,1)S(1)}, u32[]{:S(2)}, u32[]{:S(2)}) collective-permute-start(bf16[8,96,128]{2,1,0:T(8,128)(2,1)S(1)} %all-to-all-done), channel_id=1, source_target_pairs={{0,64},{64,0},{1,65},{65,1},{2,66},{66,2},{3,67},{67,3},{4,68},{68... | collective-permute-start | bytes 589832 | tf_op jit(solution)/shard_map/ppermute | solution.py:222
  36.1 3.2 %collective-permute-start.8 = (bf16[384,256]{1,0:T(8,128)(2,1)S(1)}, bf16[384,256]{1,0:T(8,128)(2,1)S(1)}, u32[]{:S(2)}, u32[]{:S(2)}) collective-permute-start(bf16[384,256]{1,0:T(8,128)(2,1)S(1)} %collective-permute-done.7.refs_5_), channel_id=1, source_target_pairs={{0,7},{1,0},{2,1},{3,2},{4,3},{5,4},{6,5},{7,6},{8,15},{9,8},{10,9... | collective-permute-start | bytes 589832 | tf_op jit(solution)/shard_map/ppermute | solution.py:232
  39.4 0.4 collective-permute-done.11.refs_3_
  39.7 2.7 %collective-permute-start.15 = (bf16[384,256]{1,0:T(8,128)(2,1)S(1)}, bf16[384,256]{1,0:T(8,128)(2,1)S(1)}, u32[]{:S(2)}, u32[]{:S(2)}) collective-permute-start(bf16[384,256]{1,0:T(8,128)(2,1)S(1)} %collective-permute-done.14.refs_4_), channel_id=1, source_target_pairs={{0,7},{1,0},{2,1},{3,2},{4,3},{5,4},{6,5},{7,6},{8,15},{9,8},{10,9... | collective-permute-start | bytes 589832 | tf_op jit(solution)/shard_map/ppermute | solution.py:232
  42.5 0.8 collective-permute-done.4.refs_2_
  43.3 2.7 %collective-permute-start.9 = (bf16[384,256]{1,0:T(8,128)(2,1)S(1)}, bf16[384,256]{1,0:T(8,128)(2,1)S(1)}, u32[]{:S(2)}, u32[]{:S(2)}) collective-permute-start(bf16[384,256]{1,0:T(8,128)(2,1)S(1)} %collective-permute-done.8.refs_5_), channel_id=1, source_target_pairs={{0,7},{1,0},{2,1},{3,2},{4,3},{5,4},{6,5},{7,6},{8,15},{9,8},{10,9... | collective-permute-start | bytes 589832 | tf_op jit(solution)/shard_map/ppermute | solution.py:232
  46.0 2.5 %shard_map.115 = (f32[1536,128]{1,0:T(8,128)S(1)}, f32[1536,128]{1,0:T(8,128)S(1)}, f32[1536,128]{1,0:T(8,128)S(1)}) custom-call(s32[10]{0:T(128)S(1)} %stack.49.place.refs_0_, bf16[1536,128]{1,0:T(8,128)(2,1)S(1)} %bitcast.43, bf16[384,256]{1,0:T(8,128)(2,1)S(1)} %bitcast.53, bf16[384,256]{1,0:T(8,128)(2,1)S(1)} %bitcast.50), custom_call_target="tpu_custom_call" | custom-call | flops 905969664 | bytes 4000000 | tf_op jit(solution)/shard_map/pallas_call | solution.py:156
  48.5 0.9 copy-done.4
  49.4 0.9 copy-done.5
  50.4 0.9 copy-done.6
  51.3 2.7 %collective-permute-start.16 = (bf16[384,256]{1,0:T(8,128)(2,1)S(1)}, bf16[384,256]{1,0:T(8,128)(2,1)S(1)}, u32[]{:S(2)}, u32[]{:S(2)}) collective-permute-start(bf16[384,256]{1,0:T(8,128)(2,1)S(1)} %collective-permute-done.15.refs_4_), channel_id=1, source_target_pairs={{0,7},{1,0},{2,1},{3,2},{4,3},{5,4},{6,5},{7,6},{8,15},{9,8},{10,9... | collective-permute-start | bytes 589832 | tf_op jit(solution)/shard_map/ppermute | solution.py:232
  54.0 5.9 %shard_map.116 = (f32[1536,128]{1,0:T(8,128)S(1)}, f32[1536,128]{1,0:T(8,128)S(1)}, f32[1536,128]{1,0:T(8,128)S(1)}) custom-call(s32[10]{0:T(128)S(1)} %stack.49.place.refs_0_, bf16[1536,128]{1,0:T(8,128)(2,1)S(1)} %bitcast.44, bf16[384,256]{1,0:T(8,128)(2,1)S(1)} %collective-permute-done.3.refs_2_, bf16[384,256]{1,0:T(8,128)(2,1)S(1)} %collective-permute-done.11.refs_3_, ...), custom_call_target="tpu_custom_call" | custom-call | flops 1811939328 | bytes 4000000 | tf_op jit(solution)/shard_map/pallas_call | solution.py:156
  59.8 0.9 copy-done.7
  60.7 0.9 copy-done.8
  61.7 0.9 copy-done.9
  62.6 1.5 %collective-permute-start.6 = (bf16[384,256]{1,0:T(8,128)(2,1)S(1)}, bf16[384,256]{1,0:T(8,128)(2,1)S(1)}, u32[]{:S(2)}, u32[]{:S(2)}) collective-permute-start(bf16[384,256]{1,0:T(8,128)(2,1)S(1)} %collective-permute-done.5.refs_2_), channel_id=1, source_target_pairs={{0,1},{1,2},{2,3},{3,4},{4,5},{5,6},{6,7},{7,0},{8,9},{9,10},{10,1... | collective-permute-start | bytes 589832 | tf_op jit(solution)/shard_map/ppermute | solution.py:243
  64.1 5.9 %shard_map.117 = (f32[1536,128]{1,0:T(8,128)S(1)}, f32[1536,128]{1,0:T(8,128)S(1)}, f32[1536,128]{1,0:T(8,128)S(1)}) custom-call(s32[10]{0:T(128)S(1)} %stack.49.place.refs_0_, bf16[1536,128]{1,0:T(8,128)(2,1)S(1)} %bitcast.45, bf16[384,256]{1,0:T(8,128)(2,1)S(1)} %collective-permute-done.4.refs_2_, bf16[384,256]{1,0:T(8,128)(2,1)S(1)} %collective-permute-done.12.refs_3_, ...), custom_call_target="tpu_custom_call" | custom-call | flops 1811939328 | bytes 4000000 | tf_op jit(solution)/shard_map/pallas_call | solution.py:156
  69.9 0.9 copy-done.10
  70.8 0.9 copy-done.11
  71.8 0.9 copy-done.12
  72.7 5.9 %shard_map.118 = (f32[1536,128]{1,0:T(8,128)S(1)}, f32[1536,128]{1,0:T(8,128)S(1)}, f32[1536,128]{1,0:T(8,128)S(1)}) custom-call(s32[10]{0:T(128)S(1)} %stack.49.place.refs_0_, bf16[1536,128]{1,0:T(8,128)(2,1)S(1)} %bitcast.46, bf16[384,256]{1,0:T(8,128)(2,1)S(1)} %collective-permute-done.5.refs_2_, bf16[384,256]{1,0:T(8,128)(2,1)S(1)} %collective-permute-done.13.refs_3_, ...), custom_call_target="tpu_custom_call" | custom-call | flops 1811939328 | bytes 4000000 | tf_op jit(solution)/shard_map/pallas_call | solution.py:156
  78.6 3.2 %shard_map.119 = (bf16[8,96,256]{2,1,0:T(8,128)(2,1)S(1)}, bf16[8,96,256]{2,1,0:T(8,128)(2,1)S(1)}) custom-call(s32[10]{0:T(128)S(1)} %stack.49.place.refs_0_, bf16[1536,128]{1,0:T(8,128)(2,1)S(1)} %bitcast.47, bf16[384,256]{1,0:T(8,128)(2,1)S(1)} %collective-permute-done.6.refs_2_, bf16[384,256]{1,0:T(8,128)(2,1)S(1)} %collective-permute-done.10.refs_3_, ...), custom_call_target="tpu_custom_call" | custom-call | flops 905969664 | bytes 4000000 | tf_op jit(solution)/shard_map/pallas_call | solution.py:156
  81.8 5.8 %collective-permute-start.17 = (bf16[8,96,256]{2,1,0:T(8,128)(2,1)S(1)}, bf16[8,96,256]{2,1,0:T(8,128)(2,1)S(1)}, u32[]{:S(2)}, u32[]{:S(2)}) collective-permute-start(bf16[8,96,256]{2,1,0:T(8,128)(2,1)S(1)} %get-tuple-element.33), channel_id=1, source_target_pairs={{0,64},{64,0},{1,65},{65,1},{2,66},{66,2},{3,67},{67,3},{4,68},{68... | collective-permute-start | bytes 1179656 | tf_op jit(solution)/shard_map/ppermute | solution.py:247
  87.6 1.3 %collective-permute-done.17 = bf16[8,96,256]{2,1,0:T(8,128)(2,1)S(1)} collective-permute-done((bf16[8,96,256]{2,1,0:T(8,128)(2,1)S(1)}, bf16[8,96,256]{2,1,0:T(8,128)(2,1)S(1)}, u32[]{:S(2)}, u32[]{:S(2)}) %collective-permute-start.17) | collective-permute-done | bytes 393248 | tf_op jit(solution)/shard_map/ppermute | solution.py:247
  89.0 0.3 fusion.16
  89.3 0.5 fusion.33
  89.8 1.1 divide_convert_fusion
  90.8 5.3 %all-to-all-start.2 = ((bf16[8,96,128]{2,1,0:T(8,128)(2,1)}), bf16[8,96,128]{2,1,0:T(8,128)(2,1)S(1)}, u32[]{:S(2)}, u32[]{:S(2)}) async-start(bf16[8,96,128]{2,1,0:T(8,128)(2,1)} %divide_convert_fusion), calls=%async_computation.2 | async-start | bytes 393216 | tf_op jit(solution)/shard_map/all_to_all | solution.py:248
  96.1 0.1 constant_dynamic-slice_fusion.3
  96.2 1.0 collective-permute-start
  97.2 4.8 %all-to-all-done.2 = bf16[8,96,128]{2,1,0:T(8,128)(2,1)S(1)} async-done(((bf16[8,96,128]{2,1,0:T(8,128)(2,1)}), bf16[8,96,128]{2,1,0:T(8,128)(2,1)S(1)}, u32[]{:S(2)}, u32[]{:S(2)}) %all-to-all-start.2) | async-done | bytes 196640 | tf_op jit(solution)/shard_map/all_to_all | solution.py:248
  102.0 0.1 copy.19
  102.1 0.1 reverse_select_fusion
  102.2 0.5 fusion.37
  102.7 0.2 multiply_reduce_fusion.1
  103.0 5.8 %fusion.38 = (f32[192]{0:T(256)S(1)}, f32[192,1024]{1,0:T(8,128)S(1)}) fusion(f32[192,1024]{1,0:T(8,128)S(1)} %get-tuple-element.50, bf16[2048,1024]{1,0:T(8,128)(2,1)} %param.17, bf16[1024,2048]{1,0:T(8,128)(2,1)} %param.16, f32[192]{0:T(256)S(1)} %add_rsqrt_fusion.1, f32[192]{0:T(256)S(1)} %broadcast_multiply_fusion.1), kind=kOutput, calls=%fused_computation.62 | convolution fusion | flops 1615134464 | bytes 9963776 | tf_op jit(solution)/shard_map/dot_general | solution.py:257
  108.8 0.2 multiply_reduce_fusion
  109.0 0.2 multiply_convert_fusion
  109.2 0.5 copy-done.14
  109.7 0.3 fusion.39
  110.0 0.3 fusion.27
  110.2 0.1 fusion.36
  110.3 3.7 %collective-permute-start.18 = (bf16[66,96]{1,0:T(8,128)(2,1)S(1)}, bf16[66,96]{1,0:T(8,128)(2,1)S(1)}, u32[]{:S(2)}, u32[]{:S(2)}) collective-permute-start(bf16[66,96]{1,0:T(8,128)(2,1)S(1)} %get-tuple-element.45), channel_id=1, source_target_pairs={{0,127},{1,126},{2,125},{3,124},{4,123},{5,122},{6,121},{7,120},{8... | collective-permute-start | bytes 38024 | tf_op jit(solution)/shard_map/ppermute | solution.py:284
  114.0 3.6 %collective-permute-start.19 = (bf16[66,96]{1,0:T(8,128)(2,1)S(1)}, bf16[66,96]{1,0:T(8,128)(2,1)S(1)}, u32[]{:S(2)}, u32[]{:S(2)}) collective-permute-start(bf16[66,96]{1,0:T(8,128)(2,1)S(1)} %get-tuple-element.46), channel_id=1, source_target_pairs={{0,63},{1,62},{2,61},{3,60},{4,59},{5,58},{6,57},{7,56},{8,55},{9,... | collective-permute-start | bytes 38024 | tf_op jit(solution)/shard_map/ppermute | solution.py:283
  117.6 0.2 collective-permute-done.18
  117.8 3.3 %collective-permute-done.19 = bf16[66,96]{1,0:T(8,128)(2,1)S(1)} collective-permute-done((bf16[66,96]{1,0:T(8,128)(2,1)S(1)}, bf16[66,96]{1,0:T(8,128)(2,1)S(1)}, u32[]{:S(2)}, u32[]{:S(2)}) %collective-permute-start.19) | collective-permute-done | bytes 12704 | tf_op jit(solution)/shard_map/ppermute | solution.py:283
  121.1 0.1 slice.83
  121.2 0.1 slice.85
  121.3 0.6 add.129
  122.1 0.7 slice.81
  (58 shorter events, 0.4 us)
Async XLA Ops:
  0.6 101.6 %copy-start = (bf16[512,1024]{1,0:T(8,128)(2,1)S(1)}, bf16[512,1024]{1,0:T(8,128)(2,1)}, u32[]{:S(2)}) copy-start(bf16[512,1024]{1,0:T(8,128)(2,1)} %param.15) | copy-start | bytes 3145732
  1.8 4.4 %collective-permute-start.1 = (bf16[96,1024]{1,0:T(8,128)(2,1)S(1)}, bf16[96,1024]{1,0:T(8,128)(2,1)S(1)}, u32[]{:S(2)}, u32[]{:S(2)}) collective-permute-start(bf16[96,1024]{1,0:T(8,128)(2,1)S(1)} %get-tuple-element.42), channel_id=1, source_target_pairs={{0,64},{64,0},{1,65},{65,1},{2,66},{66,2},{3,67},{67,3},{4,68},{68... | collective-permute-start | bytes 589832 | tf_op jit(solution)/shard_map/ppermute | solution.py:191
  6.2 1.2 copy-start.2
  7.4 1.2 copy-start.3
  8.6 5.6 %copy-start.1 = (bf16[1024,512]{1,0:T(8,128)(2,1)S(1)}, bf16[1024,512]{1,0:T(8,128)(2,1)}, u32[]{:S(2)}) copy-start(bf16[1024,512]{1,0:T(8,128)(2,1)} %w_query.1) | copy-start | bytes 3145732
  10.7 10.3 %all-to-all-start.1 = ((bf16[8,96,256]{2,1,0:T(8,128)(2,1)}), bf16[8,96,256]{2,1,0:T(8,128)(2,1)S(1)}, u32[]{:S(2)}, u32[]{:S(2)}) async-start(bf16[8,96,256]{2,1,0:T(8,128)(2,1)} %get-tuple-element.19), calls=%async_computation.1 | async-start | bytes 786432 | tf_op jit(solution)/shard_map/all_to_all | solution.py:213
  21.0 13.2 %all-to-all-start = ((bf16[8,96,128]{2,1,0:T(8,128)(2,1)}), bf16[8,96,128]{2,1,0:T(8,128)(2,1)S(1)}, u32[]{:S(2)}, u32[]{:S(2)}) async-start(bf16[8,96,128]{2,1,0:T(8,128)(2,1)} %shard_map.114), calls=%async_computation | async-start | bytes 393216 | tf_op jit(solution)/shard_map/all_to_all | solution.py:221
  25.7 10.4 %collective-permute-start.3 = (bf16[384,256]{1,0:T(8,128)(2,1)S(1)}, bf16[384,256]{1,0:T(8,128)(2,1)S(1)}, u32[]{:S(2)}, u32[]{:S(2)}) collective-permute-start(bf16[384,256]{1,0:T(8,128)(2,1)S(1)} %bitcast.51), channel_id=1, source_target_pairs={{0,1},{1,2},{2,3},{3,4},{4,5},{5,6},{6,7},{7,0},{8,9},{9,10},{10,1... | collective-permute-start | bytes 589832 | tf_op jit(solution)/shard_map/ppermute | solution.py:231
  27.5 8.7 %collective-permute-start.7 = (bf16[384,256]{1,0:T(8,128)(2,1)S(1)}, bf16[384,256]{1,0:T(8,128)(2,1)S(1)}, u32[]{:S(2)}, u32[]{:S(2)}) collective-permute-start(bf16[384,256]{1,0:T(8,128)(2,1)S(1)} %bitcast.48), channel_id=1, source_target_pairs={{0,7},{1,0},{2,1},{3,2},{4,3},{5,4},{6,5},{7,6},{8,15},{9,8},{10,9... | collective-permute-start | bytes 589832 | tf_op jit(solution)/shard_map/ppermute | solution.py:232
  31.5 8.2 %collective-permute-start.11 = (bf16[384,256]{1,0:T(8,128)(2,1)S(1)}, bf16[384,256]{1,0:T(8,128)(2,1)S(1)}, u32[]{:S(2)}, u32[]{:S(2)}) collective-permute-start(bf16[384,256]{1,0:T(8,128)(2,1)S(1)} %bitcast.49), channel_id=1, source_target_pairs={{0,1},{1,2},{2,3},{3,4},{4,5},{5,6},{6,7},{7,0},{8,9},{9,10},{10,1... | collective-permute-start | bytes 589832 | tf_op jit(solution)/shard_map/ppermute | solution.py:231
  31.5 8.2 %collective-permute-start.14 = (bf16[384,256]{1,0:T(8,128)(2,1)S(1)}, bf16[384,256]{1,0:T(8,128)(2,1)S(1)}, u32[]{:S(2)}, u32[]{:S(2)}) collective-permute-start(bf16[384,256]{1,0:T(8,128)(2,1)S(1)} %bitcast.52), channel_id=1, source_target_pairs={{0,7},{1,0},{2,1},{3,2},{4,3},{5,4},{6,5},{7,6},{8,15},{9,8},{10,9... | collective-permute-start | bytes 589832 | tf_op jit(solution)/shard_map/ppermute | solution.py:232
  34.2 8.2 %collective-permute-start.2 = (bf16[8,96,128]{2,1,0:T(8,128)(2,1)S(1)}, bf16[8,96,128]{2,1,0:T(8,128)(2,1)S(1)}, u32[]{:S(2)}, u32[]{:S(2)}) collective-permute-start(bf16[8,96,128]{2,1,0:T(8,128)(2,1)S(1)} %all-to-all-done), channel_id=1, source_target_pairs={{0,64},{64,0},{1,65},{65,1},{2,66},{66,2},{3,67},{67,3},{4,68},{68... | collective-permute-start | bytes 589832 | tf_op jit(solution)/shard_map/ppermute | solution.py:222
  36.1 7.2 %collective-permute-start.4 = (bf16[384,256]{1,0:T(8,128)(2,1)S(1)}, bf16[384,256]{1,0:T(8,128)(2,1)S(1)}, u32[]{:S(2)}, u32[]{:S(2)}) collective-permute-start(bf16[384,256]{1,0:T(8,128)(2,1)S(1)} %collective-permute-done.3.refs_2_), channel_id=1, source_target_pairs={{0,1},{1,2},{2,3},{3,4},{4,5},{5,6},{6,7},{7,0},{8,9},{9,10},{10,1... | collective-permute-start | bytes 589832 | tf_op jit(solution)/shard_map/ppermute | solution.py:231
  36.1 7.2 %collective-permute-start.8 = (bf16[384,256]{1,0:T(8,128)(2,1)S(1)}, bf16[384,256]{1,0:T(8,128)(2,1)S(1)}, u32[]{:S(2)}, u32[]{:S(2)}) collective-permute-start(bf16[384,256]{1,0:T(8,128)(2,1)S(1)} %collective-permute-done.7.refs_5_), channel_id=1, source_target_pairs={{0,7},{1,0},{2,1},{3,2},{4,3},{5,4},{6,5},{7,6},{8,15},{9,8},{10,9... | collective-permute-start | bytes 589832 | tf_op jit(solution)/shard_map/ppermute | solution.py:232
  39.7 11.5 %collective-permute-start.12 = (bf16[384,256]{1,0:T(8,128)(2,1)S(1)}, bf16[384,256]{1,0:T(8,128)(2,1)S(1)}, u32[]{:S(2)}, u32[]{:S(2)}) collective-permute-start(bf16[384,256]{1,0:T(8,128)(2,1)S(1)} %collective-permute-done.11.refs_3_), channel_id=1, source_target_pairs={{0,1},{1,2},{2,3},{3,4},{4,5},{5,6},{6,7},{7,0},{8,9},{9,10},{10,1... | collective-permute-start | bytes 589832 | tf_op jit(solution)/shard_map/ppermute | solution.py:231
  39.7 11.5 %collective-permute-start.15 = (bf16[384,256]{1,0:T(8,128)(2,1)S(1)}, bf16[384,256]{1,0:T(8,128)(2,1)S(1)}, u32[]{:S(2)}, u32[]{:S(2)}) collective-permute-start(bf16[384,256]{1,0:T(8,128)(2,1)S(1)} %collective-permute-done.14.refs_4_), channel_id=1, source_target_pairs={{0,7},{1,0},{2,1},{3,2},{4,3},{5,4},{6,5},{7,6},{8,15},{9,8},{10,9... | collective-permute-start | bytes 589832 | tf_op jit(solution)/shard_map/ppermute | solution.py:232
  43.3 19.3 %collective-permute-start.5 = (bf16[384,256]{1,0:T(8,128)(2,1)S(1)}, bf16[384,256]{1,0:T(8,128)(2,1)S(1)}, u32[]{:S(2)}, u32[]{:S(2)}) collective-permute-start(bf16[384,256]{1,0:T(8,128)(2,1)S(1)} %collective-permute-done.4.refs_2_), channel_id=1, source_target_pairs={{0,1},{1,2},{2,3},{3,4},{4,5},{5,6},{6,7},{7,0},{8,9},{9,10},{10,1... | collective-permute-start | bytes 589832 | tf_op jit(solution)/shard_map/ppermute | solution.py:231
  43.3 19.3 %collective-permute-start.9 = (bf16[384,256]{1,0:T(8,128)(2,1)S(1)}, bf16[384,256]{1,0:T(8,128)(2,1)S(1)}, u32[]{:S(2)}, u32[]{:S(2)}) collective-permute-start(bf16[384,256]{1,0:T(8,128)(2,1)S(1)} %collective-permute-done.8.refs_5_), channel_id=1, source_target_pairs={{0,7},{1,0},{2,1},{3,2},{4,3},{5,4},{6,5},{7,6},{8,15},{9,8},{10,9... | collective-permute-start | bytes 589832 | tf_op jit(solution)/shard_map/ppermute | solution.py:232
  48.5 0.9 copy-start.4
  49.4 0.9 copy-start.5
  50.4 0.9 copy-start.6
  51.3 21.4 %collective-permute-start.13 = (bf16[384,256]{1,0:T(8,128)(2,1)S(1)}, bf16[384,256]{1,0:T(8,128)(2,1)S(1)}, u32[]{:S(2)}, u32[]{:S(2)}) collective-permute-start(bf16[384,256]{1,0:T(8,128)(2,1)S(1)} %collective-permute-done.12.refs_3_), channel_id=1, source_target_pairs={{0,1},{1,2},{2,3},{3,4},{4,5},{5,6},{6,7},{7,0},{8,9},{9,10},{10,1... | collective-permute-start | bytes 589832 | tf_op jit(solution)/shard_map/ppermute | solution.py:231
  51.3 21.4 %collective-permute-start.16 = (bf16[384,256]{1,0:T(8,128)(2,1)S(1)}, bf16[384,256]{1,0:T(8,128)(2,1)S(1)}, u32[]{:S(2)}, u32[]{:S(2)}) collective-permute-start(bf16[384,256]{1,0:T(8,128)(2,1)S(1)} %collective-permute-done.15.refs_4_), channel_id=1, source_target_pairs={{0,7},{1,0},{2,1},{3,2},{4,3},{5,4},{6,5},{7,6},{8,15},{9,8},{10,9... | collective-permute-start | bytes 589832 | tf_op jit(solution)/shard_map/ppermute | solution.py:232
  59.8 0.9 copy-start.7
  60.7 0.9 copy-start.8
  61.7 0.9 copy-start.9
  62.6 16.0 %collective-permute-start.10 = (bf16[384,256]{1,0:T(8,128)(2,1)S(1)}, bf16[384,256]{1,0:T(8,128)(2,1)S(1)}, u32[]{:S(2)}, u32[]{:S(2)}) collective-permute-start(bf16[384,256]{1,0:T(8,128)(2,1)S(1)} %collective-permute-done.9.refs_5_), channel_id=1, source_target_pairs={{0,7},{1,0},{2,1},{3,2},{4,3},{5,4},{6,5},{7,6},{8,15},{9,8},{10,9... | collective-permute-start | bytes 589832 | tf_op jit(solution)/shard_map/ppermute | solution.py:244
  62.6 16.0 %collective-permute-start.6 = (bf16[384,256]{1,0:T(8,128)(2,1)S(1)}, bf16[384,256]{1,0:T(8,128)(2,1)S(1)}, u32[]{:S(2)}, u32[]{:S(2)}) collective-permute-start(bf16[384,256]{1,0:T(8,128)(2,1)S(1)} %collective-permute-done.5.refs_2_), channel_id=1, source_target_pairs={{0,1},{1,2},{2,3},{3,4},{4,5},{5,6},{6,7},{7,0},{8,9},{9,10},{10,1... | collective-permute-start | bytes 589832 | tf_op jit(solution)/shard_map/ppermute | solution.py:243
  69.9 0.9 copy-start.10
  70.8 0.9 copy-start.11
  71.8 0.9 copy-start.12
  81.8 7.2 %collective-permute-start.17 = (bf16[8,96,256]{2,1,0:T(8,128)(2,1)S(1)}, bf16[8,96,256]{2,1,0:T(8,128)(2,1)S(1)}, u32[]{:S(2)}, u32[]{:S(2)}) collective-permute-start(bf16[8,96,256]{2,1,0:T(8,128)(2,1)S(1)} %get-tuple-element.33), channel_id=1, source_target_pairs={{0,64},{64,0},{1,65},{65,1},{2,66},{66,2},{3,67},{67,3},{4,68},{68... | collective-permute-start | bytes 1179656 | tf_op jit(solution)/shard_map/ppermute | solution.py:247
  89.0 7.1 %copy-start.15 = (bf16[64,192]{1,0:T(8,128)(2,1)S(1)}, bf16[64,192]{1,0:T(8,128)(2,1)}, u32[]{:S(2)}) copy-start(bf16[64,192]{1,0:T(8,128)(2,1)} %param.11) | copy-start | bytes 73732
  90.8 11.2 %all-to-all-start.2 = ((bf16[8,96,128]{2,1,0:T(8,128)(2,1)}), bf16[8,96,128]{2,1,0:T(8,128)(2,1)S(1)}, u32[]{:S(2)}, u32[]{:S(2)}) async-start(bf16[8,96,128]{2,1,0:T(8,128)(2,1)} %divide_convert_fusion), calls=%async_computation.2 | async-start | bytes 393216 | tf_op jit(solution)/shard_map/all_to_all | solution.py:248
  96.2 13.7 %collective-permute-start = (bf16[64,96]{1,0:T(8,128)(2,1)S(1)}, bf16[64,96]{1,0:T(8,128)(2,1)S(1)}, u32[]{:S(2)}, u32[]{:S(2)}) collective-permute-start(bf16[64,96]{1,0:T(8,128)(2,1)S(1)} %get-tuple-element.48), channel_id=1, source_target_pairs={{0,64},{64,0},{1,65},{65,1},{2,66},{66,2},{3,67},{67,3},{4,68},{68... | collective-permute-start | bytes 36872 | tf_op jit(solution)/shard_map/ppermute | solution.py:195
  108.7 0.9 copy-start.14
  108.8 1.2 copy-start.13
  110.3 7.4 %collective-permute-start.18 = (bf16[66,96]{1,0:T(8,128)(2,1)S(1)}, bf16[66,96]{1,0:T(8,128)(2,1)S(1)}, u32[]{:S(2)}, u32[]{:S(2)}) collective-permute-start(bf16[66,96]{1,0:T(8,128)(2,1)S(1)} %get-tuple-element.45), channel_id=1, source_target_pairs={{0,127},{1,126},{2,125},{3,124},{4,123},{5,122},{6,121},{7,120},{8... | collective-permute-start | bytes 38024 | tf_op jit(solution)/shard_map/ppermute | solution.py:284
  114.0 7.0 %collective-permute-start.19 = (bf16[66,96]{1,0:T(8,128)(2,1)S(1)}, bf16[66,96]{1,0:T(8,128)(2,1)S(1)}, u32[]{:S(2)}, u32[]{:S(2)}) collective-permute-start(bf16[66,96]{1,0:T(8,128)(2,1)S(1)} %get-tuple-element.46), channel_id=1, source_target_pairs={{0,63},{1,62},{2,61},{3,60},{4,59},{5,58},{6,57},{7,56},{8,55},{9,... | collective-permute-start | bytes 38024 | tf_op jit(solution)/shard_map/ppermute | solution.py:283

commit v2 on v1

v2 whole, which is shorter than its diff:
```python
import functools

import jax
import jax.numpy as jnp
from jax import lax
from jax.experimental import pallas as pl
from jax.experimental.pallas import tpu as pltpu
from jax.sharding import Mesh, PartitionSpec as P

HEADS = 4
HEAD = 128
WIDTH = 1024
INNER = HEADS * HEAD
FF = 2048
CHANNELS = 64
epsilon = 1e-05
masked_score = -2e30
lowest = -1e30
POWER = HEAD**-0.5 * 1.4426950408889634
bf16 = jnp.bfloat16
f32 = jnp.float32

XL, Y, Z = 2, 4, 8
PLANES = XL * Y
TOKENS = 192
PIECE = TOKENS // 2
ROWS = PLANES * PIECE
TILE = 2 * TOKENS
TILES = 2 * ROWS // TILE
HALF = ROWS // 2
BLOCKS = HALF // HEAD
TALL = HEAD + 16
SENT = CHANNELS + 16


def layer_norm(values):
    mean = jnp.mean(values, axis=-1, keepdims=True)
    centred = values - mean
    spread = jnp.mean(centred * centred, axis=-1, keepdims=True)
    return centred * lax.rsqrt(spread + epsilon)


def vmem():
    return pl.BlockSpec(memory_space=pltpu.VMEM)


def smem():
    return pl.BlockSpec(memory_space=pltpu.SMEM)


def anywhere():
    return pl.BlockSpec(memory_space=pl.ANY)


def params(mebibytes):
    return pltpu.CompilerParams(vmem_limit_bytes=mebibytes << 20)


def qkv_kernel(place, hidden, other, w_query, w_key, w_value, slots, weights, normed, sems):
    core = place[0]
    sources = (w_key, w_value, w_query)
    copies = []
    for index, source in enumerate(sources):
        for part in range(2):
            rows = pl.ds(part * (WIDTH // 2), WIDTH // 2)
            copies.append(
                pltpu.make_async_copy(
                    source.at[rows], weights.at[index, rows], sems.at[2 * index + part]
                )
            )
    for copy in copies:
        copy.start()
    rows = pl.ds(pl.multiple_of(core * PIECE, PIECE), PIECE)
    normed[:PIECE, :] = layer_norm(hidden[rows, :].astype(f32)).astype(bf16)
    normed[PIECE:, :] = layer_norm(other[rows, :].astype(f32)).astype(bf16)
    for index, column in enumerate((1, 2, 0)):
        copies[2 * index].wait()
        copies[2 * index + 1].wait()
        made = jnp.dot(normed[...], weights[index], preferred_element_type=f32).astype(bf16)
        for part in range(2):
            sequence = core if part == 0 else 1 - core
            for head in range(HEADS):
                slots[sequence * HEADS + head, :, column * HEAD : (column + 1) * HEAD] = made[
                    part * PIECE : (part + 1) * PIECE, head * HEAD : (head + 1) * HEAD
                ]


def pack_kernel(slots, low, high, queries):
    for part, out in enumerate((low, high)):
        first = part * (PLANES // 2)
        values = []
        for plane in range(PLANES // 2):
            out[plane * PIECE : (plane + 1) * PIECE, :] = slots[first + plane, :, HEAD : 2 * HEAD]
            values.append(slots[first + plane, :, 2 * HEAD :])
        values = jnp.concatenate(values, axis=0)
        for block in range(BLOCKS):
            square = values[block * HEAD : (block + 1) * HEAD, :].astype(f32)
            out[HALF + block * HEAD : HALF + (block + 1) * HEAD, :] = square.T.astype(bf16)
    queries[...] = slots[:, :, :HEAD]


def attend_kernel(parts, sources, first, last, *refs):
    refs = list(refs)
    place = refs.pop(0)
    if first:
        own, other = refs.pop(0), refs.pop(0)
    else:
        queries = refs.pop(0)
    segments = [refs.pop(0) for _ in parts]
    if not first:
        top_in, numer_in = refs.pop(0), refs.pop(0)
    if first:
        queries = refs.pop(0)
        for tile in range(TILES):
            planes = (2 * tile, 2 * tile + 1)
            rows = [own[plane] for plane in planes] + [other[plane] for plane in planes]
            turned = jnp.concatenate(rows, axis=0).astype(f32).T
            queries[:, tile * TILE : (tile + 1) * TILE] = turned.astype(bf16)
    core = place[0]
    column = lax.broadcasted_iota(jnp.int32, (1, TILE), 1)
    column_half = jnp.where(column < TOKENS, core, 1 - core)
    column_plane = (column % TOKENS) // PIECE
    column_place = column_plane * (Z * TOKENS) + column_half * PIECE + column % PIECE
    key = lax.broadcasted_iota(jnp.int32, (HALF, 1), 0)
    key_place = (key // PIECE) * (Z * TOKENS) + key % PIECE + core * PIECE
    ones = jnp.ones((TALL - HEAD, HALF), bf16)
    values = []
    for segment in segments:
        blocks = [segment[HALF + index * HEAD : HALF + (index + 1) * HEAD, :] for index in range(BLOCKS)]
        values.append(jnp.concatenate([jnp.concatenate(blocks, axis=1), ones], axis=0))

    def score(tile):
        columns = slice(tile * TILE, (tile + 1) * TILE)
        found = []
        for segment, part, source, value in zip(segments, parts, sources, values):
            groups = min(2, tile + 1 - 2 * part)
            if groups <= 0:
                continue
            count = groups * TOKENS
            product = jnp.dot(segment[:count, :], queries[:, columns], preferred_element_type=f32)
            if 2 * part + groups - 1 == tile:
                shift = place[1 + source] * TOKENS
                offset = 2 * (tile - 2 * part) * (Z * TOKENS)
                allowed = key_place[:count] + shift <= column_place + offset
                product = jnp.where(allowed, product, masked_score)
            found.append((value[:, :count], product))
        return found

    def finish(tile, found):
        columns = slice(tile * TILE, (tile + 1) * TILE)
        top = jnp.full((1, TILE), lowest, f32) if first else top_in[:1, columns]
        new_top = top
        for _, product in found:
            new_top = jnp.maximum(new_top, jnp.max(product, axis=0, keepdims=True))
        if first:
            sums = jnp.zeros((TALL, TILE), f32)
        else:
            sums = numer_in[:, columns] * jnp.exp2((top - new_top) * POWER)
        for value, product in found:
            weights = jnp.exp2((product - new_top) * POWER).astype(bf16)
            sums = sums + jnp.dot(value, weights, preferred_element_type=f32)
        if not last:
            top_out, numer_out = refs
            top_out[:, columns] = jnp.broadcast_to(new_top, (8, TILE))
            numer_out[:, columns] = sums
            return
        total = sums[HEAD : HEAD + 1, :]
        some = total > 0
        total = jnp.where(some, total, 1.0)
        mixed = (sums[:HEAD, :] / total).T
        level = jnp.where(some, new_top * POWER + jnp.log2(total), lowest)
        level = jnp.broadcast_to(level, (HEAD, TILE)).T
        high = level.astype(bf16)
        rest = level - high.astype(f32)
        middle = rest.astype(bf16)
        low = (rest - middle.astype(f32)).astype(bf16)
        lane = lax.broadcasted_iota(jnp.int32, (TILE, HEAD), 1)
        level = jnp.where(lane == 0, high, jnp.where(lane == 1, middle, low))
        for side in range(2):
            for plane in range(2):
                start = side * TOKENS + plane * PIECE
                refs[side][2 * tile + plane, :, :HEAD] = mixed[start : start + PIECE].astype(bf16)
                refs[side][2 * tile + plane, :, HEAD:] = level[start : start + PIECE]

    found = score(0)
    for tile in range(TILES):
        following = score(tile + 1) if tile + 1 < TILES else None
        finish(tile, found)
        found = following


def attend(place, queries, segments, parts, sources, state, last):
    first = state is None
    stats = [jax.ShapeDtypeStruct((8, 2 * ROWS), f32), jax.ShapeDtypeStruct((TALL, 2 * ROWS), f32)]
    if last:
        shapes = [jax.ShapeDtypeStruct((PLANES, PIECE, 2 * HEAD), bf16)] * 2
    elif first:
        shapes = [jax.ShapeDtypeStruct((HEAD, 2 * ROWS), bf16), *stats]
    else:
        shapes = stats
    operands = [place, *queries, *segments, *(state or ())]
    return pl.pallas_call(
        functools.partial(attend_kernel, parts, sources, first, last),
        out_shape=shapes,
        in_specs=[smem()] + [vmem()] * (len(operands) - 1),
        out_specs=[vmem()] * len(shapes),
        compiler_params=params(24),
        cost_estimate=pl.CostEstimate(
            flops=2 * 2 * 2 * ROWS * HALF * HEAD * len(parts),
            bytes_accessed=3_000_000,
            transcendentals=ROWS * HALF * len(parts),
        ),
    )(*operands)


def merge_kernel(mine, theirs, out):
    def level(block):
        parts = [block[:, :, HEAD + index : HEAD + index + 1].astype(f32) for index in range(3)]
        return parts[0] + parts[1] + parts[2]

    first, second = level(mine), level(theirs)
    top = jnp.maximum(first, second)
    first, second = jnp.exp2(first - top), jnp.exp2(second - top)
    share = 1.0 / (first + second)
    out[...] = (
        (first * share) * mine[:, :, :HEAD].astype(f32)
        + (second * share) * theirs[:, :, :HEAD].astype(f32)
    ).astype(bf16)


FF_PARTS = 4
FF_PART = FF // FF_PARTS


def dense_kernel(
    place,
    attended,
    hidden,
    other,
    flow,
    other_flow,
    w_output,
    w_up,
    w_down,
    w_shift,
    w_scale,
    sent_own,
    sent_other,
    output,
    up,
    down,
    shift_scale,
    sems,
):
    core = place[0]
    copies = [pltpu.make_async_copy(w_output, output, sems.at[0])]
    for part in range(FF_PARTS):
        cut = pl.ds(part * FF_PART, FF_PART)
        copies.append(
            pltpu.make_async_copy(w_up.at[:, cut], up.at[:, cut], sems.at[1 + 2 * part])
        )
        copies.append(pltpu.make_async_copy(w_down.at[cut], down.at[cut], sems.at[2 + 2 * part]))
    for index, source in enumerate((w_shift, w_scale)):
        cut = pl.ds(index * CHANNELS, CHANNELS)
        copies.append(
            pltpu.make_async_copy(source, shift_scale.at[cut], sems.at[1 + 2 * FF_PARTS + index])
        )
    for copy in copies:
        copy.start()
    rows = pl.ds(pl.multiple_of(core * PIECE, PIECE), PIECE)
    residual = jnp.concatenate([hidden[rows, :], other[rows, :]], axis=0).astype(f32)
    sides = []
    for sequence in (core, 1 - core):
        heads = [attended[sequence * HEADS + head] for head in range(HEADS)]
        sides.append(jnp.concatenate(heads, axis=1))
    mixed = jnp.concatenate(sides, axis=0)
    copies[0].wait()
    first = residual + jnp.dot(mixed, output[...], preferred_element_type=f32)
    inner = layer_norm(first).astype(bf16)
    second = first
    for part in range(FF_PARTS):
        cut = slice(part * FF_PART, (part + 1) * FF_PART)
        copies[1 + 2 * part].wait()
        expanded = jnp.dot(inner, up[:, cut], preferred_element_type=f32)
        expanded = jax.nn.gelu(expanded).astype(bf16)
        copies[2 + 2 * part].wait()
        second = second + jnp.dot(expanded, down[cut, :], preferred_element_type=f32)
    features = layer_norm(second).astype(bf16)
    copies[-2].wait()
    copies[-1].wait()
    both = lax.dot_general(
        shift_scale[...], features, (((1,), (1,)), ((), ())), preferred_element_type=f32
    )
    shift, log_scale = both[:CHANNELS], both[CHANNELS:]
    determinant = -jnp.sum(log_scale, axis=0, keepdims=True)
    high = determinant.astype(bf16)
    low = (determinant - high.astype(f32)).astype(bf16)
    row = lax.broadcasted_iota(jnp.int32, (SENT - CHANNELS, TOKENS), 0)
    tail = jnp.where(row == 0, high.astype(f32), jnp.where(row == 1, low.astype(f32), 0.0))
    flows = []
    for source in (flow, other_flow):
        flows.append(jnp.where(core == 0, source[:, :PIECE].astype(f32), source[:, PIECE:].astype(f32)))
    moved = (jnp.concatenate(flows, axis=1) - shift) * jnp.exp(-log_scale)
    sent = jnp.concatenate([moved, tail], axis=0).astype(bf16)
    sent_own[...] = sent[:, :PIECE]
    sent_other[...] = sent[:, PIECE:]


def join_kernel(place, mine, theirs, out):
    core = place[0]
    row = lax.broadcasted_iota(jnp.int32, (PIECE, TOKENS), 0)
    column = lax.broadcasted_iota(jnp.int32, (PIECE, TOKENS), 1)
    total = None
    for source, half in ((mine, core), (theirs, 1 - core)):
        chosen = (column == TOKENS - 1 - half * PIECE - row).astype(f32).astype(bf16)
        term = jnp.dot(source[...], chosen, preferred_element_type=f32)
        total = term if total is None else total + term
    out[...] = total.astype(bf16)


def shift_by(count, step):
    return [(index, (index + step) % count) for index in range(count)]


def on_device(
    hidden, flow_input, w_query, w_key, w_value, w_output, w_up, w_down, w_shift, w_scale
):
    core = lax.axis_index("core")
    z = lax.axis_index("z")
    up_steps = [(z - step) % Z - z for step in range(5)]
    down_steps = [(z + step) % Z - z for step in range(4)]
    place = jnp.stack([core, *up_steps, *down_steps]).astype(jnp.int32)
    other_core = shift_by(2, 1)
    other = lax.ppermute(hidden, "core", other_core)
    other_flow = lax.ppermute(flow_input, "core", other_core)

    slots = pl.pallas_call(
        qkv_kernel,
        out_shape=jax.ShapeDtypeStruct((PLANES, PIECE, 3 * HEAD), bf16),
        in_specs=[smem()] + [vmem()] * 2 + [anywhere()] * 3,
        out_specs=vmem(),
        scratch_shapes=[
            pltpu.VMEM((3, WIDTH, INNER), bf16),
            pltpu.VMEM((TOKENS, WIDTH), bf16),
            pltpu.SemaphoreType.DMA((6,)),
        ],
        compiler_params=params(16),
    )(place, hidden, other, w_query, w_key, w_value)
    slots = lax.all_to_all(slots, ("xl", "y"), 0, 0, tiled=True)
    part = jax.ShapeDtypeStruct((ROWS, HEAD), bf16)
    *own_parts, own_queries = pl.pallas_call(
        pack_kernel,
        out_shape=[part, part, jax.ShapeDtypeStruct((PLANES, PIECE, HEAD), bf16)],
        in_specs=[vmem()],
        out_specs=[vmem()] * 3,
        compiler_params=params(8),
    )(slots)
    other_queries = lax.ppermute(own_queries, "core", other_core)

    up, down = list(own_parts), list(own_parts)
    queries, *state = attend(
        place, (own_queries, other_queries), own_parts, (0, 1), (0, 0), None, False
    )
    for step in range(1, 4):
        for part in range(2):
            up[part] = lax.ppermute(up[part], "z", shift_by(Z, 1))
            down[part] = lax.ppermute(down[part], "z", shift_by(Z, -1))
        state = attend(
            place,
            (queries,),
            up + down,
            (0, 1, 0, 1),
            (step, step, 5 + step, 5 + step),
            state,
            False,
        )
    far = [
        lax.ppermute(up[0], "z", shift_by(Z, 1)),
        lax.ppermute(down[1], "z", shift_by(Z, -1)),
    ]
    mine, others = attend(place, (queries,), far, (0, 1), (4, 4), state, True)
    theirs = lax.ppermute(others, "core", other_core)
    attended = pl.pallas_call(
        merge_kernel,
        out_shape=jax.ShapeDtypeStruct((PLANES, PIECE, HEAD), bf16),
        in_specs=[vmem()] * 2,
        out_specs=vmem(),
        compiler_params=params(8),
    )(mine, theirs)
    attended = lax.all_to_all(attended, ("xl", "y"), 0, 0, tiled=True)

    sent = jax.ShapeDtypeStruct((SENT, PIECE), bf16)
    sent_own, sent_other = pl.pallas_call(
        dense_kernel,
        out_shape=[sent, sent],
        in_specs=[smem()] + [vmem()] * 5 + [anywhere()] * 5,
        out_specs=[vmem()] * 2,
        scratch_shapes=[
            pltpu.VMEM((INNER, WIDTH), bf16),
            pltpu.VMEM((WIDTH, FF), bf16),
            pltpu.VMEM((FF, WIDTH), bf16),
            pltpu.VMEM((2 * CHANNELS, WIDTH), bf16),
            pltpu.SemaphoreType.DMA((3 + 2 * FF_PARTS,)),
        ],
        compiler_params=params(32),
    )(
        place,
        attended,
        hidden,
        other,
        flow_input,
        other_flow,
        w_output,
        w_up,
        w_down,
        w_shift,
        w_scale,
    )
    received = lax.ppermute(sent_other, "core", other_core)
    block = pl.pallas_call(
        join_kernel,
        out_shape=jax.ShapeDtypeStruct((SENT, TOKENS), bf16),
        in_specs=[smem()] + [vmem()] * 2,
        out_specs=vmem(),
        compiler_params=params(8),
    )(place, sent_own, received)
    count = XL * Y * Z
    mirrored = [(index, count - 1 - index) for index in range(count)]
    arrived = lax.ppermute(block, ("xl", "y", "z"), mirrored).astype(f32)
    return (arrived[:CHANNELS], arrived[CHANNELS] + arrived[CHANNELS + 1])


def solution(mesh):
    parts = Mesh(mesh.devices.reshape(2, 2, XL, Y, Z), ("xh", "core", "xl", "y", "z"))
    everywhere = ("xh", "core", "xl", "y", "z")
    in_specs = (P(everywhere, None), P(None, everywhere)) + (P(),) * 8
    out_specs = (P(None, everywhere), P(everywhere))
    return jax.shard_map(
        on_device, mesh=parts, in_specs=in_specs, out_specs=out_specs, check_vma=False
    )
```

time: 124 us -> 106 us (0.85)
  blocking collectives: 0 us -> 13.3 us
  starting transfers between devices: 53.9 us -> 40.6 us
  matrix products: 6.78 us -> 0 us
  local copies, waits for them, and re-layouts: 14.4 us -> 9.79 us
  Pallas kernels: 27 us -> 24 us
  other arithmetic: 2.7 us -> 0.57 us
    all_to_all x0 -> x1, blocking collectives: none -> 13.3 us  [on_device(): slots = lax.all_to_all(slots, ('xl', 'y'), 0, 0, tiled=True)]
    pallas_call x5, Pallas kernels: 23.3 us -> 13.4 us  [attend(): pl.pallas_call(functools.partial(attend_kernel, parts, sources, first, la...]
    all_to_all x2 -> x0, starting transfers between devices: 8.17 us -> none  [the longest x1 4.72 us: on_device(): own_queries = lax.all_to_all(slots, ('xl', 'y'), 0, 0, tiled=True)]
    pallas_call x2 -> x5, Pallas kernels: 3.7 us -> 10.5 us  [the longest x1 6.18 us: on_device(): pl.pallas_call(dense_kernel, out_shape=[sent, sent], in_specs=[smem()] +...]
    dot_general x4 -> x0, matrix products: 6.78 us -> none  [the longest x1 5.78 us: on_device(): second = first + jnp.dot(expanded, w_down, preferred_element_type=f32)]
    ppermute x5, starting transfers between devices: 17.4 us -> 10.7 us  [the longest x1 3.47 us: on_device(): theirs = lax.ppermute(others, 'core', other_core)]
    ppermute x5, waiting for transfers between devices: 5.78 us -> 11.2 us  [the longest x1 6.62 us: on_device(): arrived = lax.ppermute(block, ('xl', 'y', 'z'), mirrored).astype(f32)]
    all_to_all x2 -> x0, waiting for transfers between devices: 5.19 us -> none  [the longest x1 5.19 us: on_device(): lax.all_to_all(slots, ('xl', 'y'), 0, 0, tiled=True).reshape(ROWS, 2 * HEAD)]
  transfers between devices with their start and end apart: 23 -> 21, of which waited for: 8 -> 7; matrix products, arithmetic and copies ran while one was open for 6% -> 0% of each run, Pallas kernels for 18% -> 11%
where the time goes in v2:
time: 106 us; the launch traced here: 105 us
  starting transfers between devices  40.6 us (38%)
  Pallas kernels  24 us (23%)
  waiting for transfers between devices  16.1 us (15%)
  blocking collectives  13.3 us (13%)
  local copies, waits for them, and re-layouts  9.79 us (9%)
    ppermute x6, starting transfers between devices, on_device(): down[part] = lax.ppermute(down[part], 'z', shift_by(Z, -1))  17.4 us
    pallas_call x5, Pallas kernels, attend(): pl.pallas_call(functools.partial(attend_kernel, parts, sources, first, la...  13.4 us
    all_to_all x1, blocking collectives, on_device(): slots = lax.all_to_all(slots, ('xl', 'y'), 0, 0, tiled=True)  13.3 us
    unnamed x22, local copies, waits for them, and re-layouts  9.07 us
    ppermute x1, waiting for transfers between devices, on_device(): arrived = lax.ppermute(block, ('xl', 'y', 'z'), mirrored).astype(f32)  6.62 us
    pallas_call x1, Pallas kernels, on_device(): pl.pallas_call(dense_kernel, out_shape=[sent, sent], in_specs=[smem()] +...  6.18 us
    ppermute x1, starting transfers between devices, on_device(): other_queries = lax.ppermute(own_queries, 'core', other_core)  4.4 us
    all_to_all x1, waiting for transfers between devices, on_device(): attended = lax.all_to_all(attended, ('xl', 'y'), 0, 0, tiled=True)  4.17 us
  transfers between devices with their start and end apart: 21, of which 7 were waited for; matrix products, arithmetic and copies ran while one was open for 0% of the time, Pallas kernels for 11%

profile of v2, /device:TPU:1, one launch (start us, length us, event | category | flops | bytes accessed | tf_op | source)
XLA Modules:
  0.0 105.2 jit_solution(15152467990037321239)
XLA Ops:
  0.6 3.3 %collective-permute-start = (bf16[192,1024]{1,0:T(8,128)(2,1)}, bf16[192,1024]{1,0:T(8,128)(2,1)S(1)}, u32[]{:S(2)}, u32[]{:S(2)}) collective-permute-start(bf16[192,1024]{1,0:T(8,128)(2,1)} %hidden.3), channel_id=1, source_target_pairs={{0,64},{64,0},{1,65},{65,1},{2,66},{66,2},{3,67},{67,3},{4,68},{68... | collective-permute-start | bytes 1179656 | tf_op jit(solution)/shard_map/ppermute | solution.py:334
  4.0 0.1 stack.40.place.refs_0_
  4.0 1.5 %collective-permute-done.other = bf16[192,1024]{1,0:T(8,128)(2,1)S(1)} collective-permute-done((bf16[192,1024]{1,0:T(8,128)(2,1)}, bf16[192,1024]{1,0:T(8,128)(2,1)S(1)}, u32[]{:S(2)}, u32[]{:S(2)}) %collective-permute-start) | collective-permute-done | bytes 393248 | tf_op jit(solution)/shard_map/ppermute | solution.py:334
  5.5 1.0 copy-done.2
  6.5 1.2 %copy-done.4 = bf16[1024,512]{1,0:T(8,128)(2,1)S(1)} copy-done((bf16[1024,512]{1,0:T(8,128)(2,1)S(1)}, bf16[1024,512]{1,0:T(8,128)(2,1)}, u32[]{:S(2)}) %copy-start.4) | copy-done | bytes 1048600
  7.7 1.2 %copy-done.5 = bf16[1024,512]{1,0:T(8,128)(2,1)S(1)} copy-done((bf16[1024,512]{1,0:T(8,128)(2,1)S(1)}, bf16[1024,512]{1,0:T(8,128)(2,1)}, u32[]{:S(2)}) %copy-start.5) | copy-done | bytes 1048600
  9.0 1.2 %copy-done.6 = bf16[1024,512]{1,0:T(8,128)(2,1)S(1)} copy-done((bf16[1024,512]{1,0:T(8,128)(2,1)S(1)}, bf16[1024,512]{1,0:T(8,128)(2,1)}, u32[]{:S(2)}) %copy-start.6) | copy-done | bytes 1048600
  10.2 2.2 %shard_map.113 = bf16[8,96,384]{2,1,0:T(8,128)(2,1)S(1)} custom-call(s32[10]{0:T(128)S(1)} %stack.40.place.refs_0_, bf16[192,1024]{1,0:T(8,128)(2,1)S(1)} %copy-done.2, bf16[192,1024]{1,0:T(8,128)(2,1)S(1)} %collective-permute-done.other, bf16[1024,512]{1,0:T(8,128)(2,1)S(1)} %copy-done.4, bf16[1024,512]{1,0:T(8,128)(2,1)S(1)} %copy-done.5, ...), custom_call_target="tpu_custom_call" | custom-call | tf_op jit(solution)/shard_map/pallas_call | solution.py:337
  12.4 13.3 %all_to_all.10.slots = bf16[8,96,384]{2,1,0:T(8,128)(2,1)S(1)} all-to-all(bf16[8,96,384]{2,1,0:T(8,128)(2,1)S(1)} %shard_map.113), channel_id=1, replica_groups=mesh['xh'=2,'core'=2,'xl'=2,'y'=4,'z'=8] {'xl','y'}, dimensions={0} | all-to-all | bytes 1179648 | tf_op jit(solution)/shard_map/all_to_all | solution.py:349
  25.8 0.1 shard_map.114
  25.9 1.8 %collective-permute-start.2 = (bf16[768,128]{1,0:T(8,128)(2,1)S(1)}, bf16[768,128]{1,0:T(8,128)(2,1)S(1)}, u32[]{:S(2)}, u32[]{:S(2)}) collective-permute-start(bf16[768,128]{1,0:T(8,128)(2,1)S(1)} %get-tuple-element.19.refs_3_), channel_id=1, source_target_pairs={{0,1},{1,2},{2,3},{3,4},{4,5},{5,6},{6,7},{7,0},{8,9},{9,10},{10,1... | collective-permute-start | bytes 589832 | tf_op jit(solution)/shard_map/ppermute | solution.py:366
  27.6 4.0 %collective-permute-start.6 = (bf16[768,128]{1,0:T(8,128)(2,1)S(1)}, bf16[768,128]{1,0:T(8,128)(2,1)S(1)}, u32[]{:S(2)}, u32[]{:S(2)}) collective-permute-start(bf16[768,128]{1,0:T(8,128)(2,1)S(1)} %get-tuple-element.20.refs_4_), channel_id=1, source_target_pairs={{0,7},{1,0},{2,1},{3,2},{4,3},{5,4},{6,5},{7,6},{8,15},{9,8},{10,9... | collective-permute-start | bytes 589832 | tf_op jit(solution)/shard_map/ppermute | solution.py:367
  31.7 0.0 collective-permute-start.10
  31.7 2.7 %collective-permute-start.13 = (bf16[768,128]{1,0:T(8,128)(2,1)S(1)}, bf16[768,128]{1,0:T(8,128)(2,1)S(1)}, u32[]{:S(2)}, u32[]{:S(2)}) collective-permute-start(bf16[768,128]{1,0:T(8,128)(2,1)S(1)} %get-tuple-element.19.refs_3_), channel_id=1, source_target_pairs={{0,7},{1,0},{2,1},{3,2},{4,3},{5,4},{6,5},{7,6},{8,15},{9,8},{10,9... | collective-permute-start | bytes 589832 | tf_op jit(solution)/shard_map/ppermute | solution.py:367
  34.3 0.8 collective-permute-done.2.refs_2_
  35.1 0.0 collective-permute-start.3
  35.1 0.0 collective-permute-done.6.refs_5_
  35.1 2.7 %collective-permute-start.7 = (bf16[768,128]{1,0:T(8,128)(2,1)S(1)}, bf16[768,128]{1,0:T(8,128)(2,1)S(1)}, u32[]{:S(2)}, u32[]{:S(2)}) collective-permute-start(bf16[768,128]{1,0:T(8,128)(2,1)S(1)} %collective-permute-done.6.refs_5_), channel_id=1, source_target_pairs={{0,7},{1,0},{2,1},{3,2},{4,3},{5,4},{6,5},{7,6},{8,15},{9,8},{10,9... | collective-permute-start | bytes 589832 | tf_op jit(solution)/shard_map/ppermute | solution.py:367
  37.8 4.4 %collective-permute-start.1 = (bf16[8,96,128]{2,1,0:T(8,128)(2,1)S(1)}, bf16[8,96,128]{2,1,0:T(8,128)(2,1)S(1)}, u32[]{:S(2)}, u32[]{:S(2)}) collective-permute-start(bf16[8,96,128]{2,1,0:T(8,128)(2,1)S(1)} %get-tuple-element.18.refs_1_), channel_id=1, source_target_pairs={{0,64},{64,0},{1,65},{65,1},{2,66},{66,2},{3,67},{67,3},{4,68},{68... | collective-permute-start | bytes 589832 | tf_op jit(solution)/shard_map/ppermute | solution.py:358
  42.2 0.0 collective-permute-done.10.refs_3_
  42.2 0.0 collective-permute-start.11
  42.2 0.0 collective-permute-done.13.refs_4_
  42.2 2.7 %collective-permute-start.14 = (bf16[768,128]{1,0:T(8,128)(2,1)S(1)}, bf16[768,128]{1,0:T(8,128)(2,1)S(1)}, u32[]{:S(2)}, u32[]{:S(2)}) collective-permute-start(bf16[768,128]{1,0:T(8,128)(2,1)S(1)} %collective-permute-done.13.refs_4_), channel_id=1, source_target_pairs={{0,7},{1,0},{2,1},{3,2},{4,3},{5,4},{6,5},{7,6},{8,15},{9,8},{10,9... | collective-permute-start | bytes 589832 | tf_op jit(solution)/shard_map/ppermute | solution.py:367
  44.9 0.0 collective-permute-start.4
  44.9 0.0 collective-permute-done.7.refs_5_
  44.9 2.7 %collective-permute-start.8 = (bf16[768,128]{1,0:T(8,128)(2,1)S(1)}, bf16[768,128]{1,0:T(8,128)(2,1)S(1)}, u32[]{:S(2)}, u32[]{:S(2)}) collective-permute-start(bf16[768,128]{1,0:T(8,128)(2,1)S(1)} %collective-permute-done.7.refs_5_), channel_id=1, source_target_pairs={{0,7},{1,0},{2,1},{3,2},{4,3},{5,4},{6,5},{7,6},{8,15},{9,8},{10,9... | collective-permute-start | bytes 589832 | tf_op jit(solution)/shard_map/ppermute | solution.py:367
  47.5 0.0 collective-permute-done.1.refs_2_
  47.5 2.1 %shard_map.115 = (bf16[128,1536]{1,0:T(8,128)(2,1)S(1)}, f32[8,1536]{1,0:T(8,128)S(1)}, f32[144,1536]{1,0:T(8,128)S(1)}) custom-call(s32[10]{0:T(128)S(1)} %stack.40.place.refs_0_, bf16[8,96,128]{2,1,0:T(8,128)(2,1)S(1)} %get-tuple-element.18.refs_1_, bf16[8,96,128]{2,1,0:T(8,128)(2,1)S(1)} %collective-permute-done.1.refs_2_, ...), custom_call_target="tpu_custom_call" | custom-call | flops 603979776 | bytes 3000000 | tf_op jit(solution)/shard_map/pallas_call | solution.py:202
  49.6 0.3 collective-permute-start.12
  49.9 0.0 collective-permute-done.14.refs_4_
  49.9 2.7 %collective-permute-start.15 = (bf16[768,128]{1,0:T(8,128)(2,1)S(1)}, bf16[768,128]{1,0:T(8,128)(2,1)S(1)}, u32[]{:S(2)}, u32[]{:S(2)}) collective-permute-start(bf16[768,128]{1,0:T(8,128)(2,1)S(1)} %collective-permute-done.14.refs_4_), channel_id=1, source_target_pairs={{0,7},{1,0},{2,1},{3,2},{4,3},{5,4},{6,5},{7,6},{8,15},{9,8},{10,9... | collective-permute-start | bytes 589832 | tf_op jit(solution)/shard_map/ppermute | solution.py:367
  52.6 3.0 %shard_map.116 = (f32[8,1536]{1,0:T(8,128)S(1)}, f32[144,1536]{1,0:T(8,128)S(1)}) custom-call(s32[10]{0:T(128)S(1)} %stack.40.place.refs_0_, bf16[128,1536]{1,0:T(8,128)(2,1)S(1)} %get-tuple-element.21.refs_1_, bf16[768,128]{1,0:T(8,128)(2,1)S(1)} %collective-permute-done.2.refs_2_, bf16[768,128]{1,0:T(8,128)(2,1)S(1)} %collective-permute-done.10.refs_3_, ...), custom_call_target="tpu_custom_call" | custom-call | flops 1207959552 | bytes 3000000 | tf_op jit(solution)/shard_map/pallas_call | solution.py:202
  55.6 0.1 collective-permute-start.5
  55.7 0.0 collective-permute-done.8.refs_5_
  55.7 2.7 %collective-permute-start.9 = (bf16[768,128]{1,0:T(8,128)(2,1)S(1)}, bf16[768,128]{1,0:T(8,128)(2,1)S(1)}, u32[]{:S(2)}, u32[]{:S(2)}) collective-permute-start(bf16[768,128]{1,0:T(8,128)(2,1)S(1)} %collective-permute-done.8.refs_5_), channel_id=1, source_target_pairs={{0,7},{1,0},{2,1},{3,2},{4,3},{5,4},{6,5},{7,6},{8,15},{9,8},{10,9... | collective-permute-start | bytes 589832 | tf_op jit(solution)/shard_map/ppermute | solution.py:379
  58.3 3.0 %shard_map.117 = (f32[8,1536]{1,0:T(8,128)S(1)}, f32[144,1536]{1,0:T(8,128)S(1)}) custom-call(s32[10]{0:T(128)S(1)} %stack.40.place.refs_0_, bf16[128,1536]{1,0:T(8,128)(2,1)S(1)} %get-tuple-element.21.refs_1_, bf16[768,128]{1,0:T(8,128)(2,1)S(1)} %collective-permute-done.3.refs_2_, bf16[768,128]{1,0:T(8,128)(2,1)S(1)} %collective-permute-done.11.refs_3_, ...), custom_call_target="tpu_custom_call" | custom-call | flops 1207959552 | bytes 3000000 | tf_op jit(solution)/shard_map/pallas_call | solution.py:202
  61.4 0.0 copy-start.10
  61.4 0.0 copy-start.3
  61.4 0.0 copy-start.7
  61.4 0.0 copy-start.8
  61.4 0.0 copy-start.9
  61.4 0.0 collective-permute-done.12.refs_3_
  61.4 0.0 collective-permute-done.15.refs_4_
  61.4 3.0 %shard_map.118 = (f32[8,1536]{1,0:T(8,128)S(1)}, f32[144,1536]{1,0:T(8,128)S(1)}) custom-call(s32[10]{0:T(128)S(1)} %stack.40.place.refs_0_, bf16[128,1536]{1,0:T(8,128)(2,1)S(1)} %get-tuple-element.21.refs_1_, bf16[768,128]{1,0:T(8,128)(2,1)S(1)} %collective-permute-done.4.refs_2_, bf16[768,128]{1,0:T(8,128)(2,1)S(1)} %collective-permute-done.12.refs_3_, ...), custom_call_target="tpu_custom_call" | custom-call | flops 1207959552 | bytes 3000000 | tf_op jit(solution)/shard_map/pallas_call | solution.py:202
  64.5 0.0 collective-permute-done.9.refs_3_
  64.5 2.3 %shard_map.119 = (bf16[8,96,256]{2,1,0:T(8,128)(2,1)S(1)}, bf16[8,96,256]{2,1,0:T(8,128)(2,1)S(1)}) custom-call(s32[10]{0:T(128)S(1)} %stack.40.place.refs_0_, bf16[128,1536]{1,0:T(8,128)(2,1)S(1)} %get-tuple-element.21.refs_1_, bf16[768,128]{1,0:T(8,128)(2,1)S(1)} %collective-permute-done.5.refs_2_, bf16[768,128]{1,0:T(8,128)(2,1)S(1)} %collective-permute-done.9.refs_3_, ...), custom_call_target="tpu_custom_call" | custom-call | flops 603979776 | bytes 3000000 | tf_op jit(solution)/shard_map/pallas_call | solution.py:202
  66.8 3.5 %collective-permute-start.16 = (bf16[8,96,256]{2,1,0:T(8,128)(2,1)S(1)}, bf16[8,96,256]{2,1,0:T(8,128)(2,1)S(1)}, u32[]{:S(2)}, u32[]{:S(2)}) collective-permute-start(bf16[8,96,256]{2,1,0:T(8,128)(2,1)S(1)} %get-tuple-element.31), channel_id=1, source_target_pairs={{0,64},{64,0},{1,65},{65,1},{2,66},{66,2},{3,67},{67,3},{4,68},{68... | collective-permute-start | bytes 1179656 | tf_op jit(solution)/shard_map/ppermute | solution.py:382
  70.3 1.3 %collective-permute-done.16.theirs = bf16[8,96,256]{2,1,0:T(8,128)(2,1)S(1)} collective-permute-done((bf16[8,96,256]{2,1,0:T(8,128)(2,1)S(1)}, bf16[8,96,256]{2,1,0:T(8,128)(2,1)S(1)}, u32[]{:S(2)}, u32[]{:S(2)}) %collective-permute-start.16) | collective-permute-done | bytes 393248 | tf_op jit(solution)/shard_map/ppermute | solution.py:382
  71.7 1.3 %shard_map.120 = bf16[8,96,128]{2,1,0:T(8,128)(2,1)} custom-call(bf16[8,96,256]{2,1,0:T(8,128)(2,1)S(1)} %get-tuple-element.30.mine, bf16[8,96,256]{2,1,0:T(8,128)(2,1)S(1)} %collective-permute-done.16.theirs), custom_call_target="tpu_custom_call" | custom-call | tf_op jit(solution)/shard_map/pallas_call | solution.py:383
  72.9 3.4 %all-to-all-start.1 = ((bf16[8,96,128]{2,1,0:T(8,128)(2,1)}), bf16[8,96,128]{2,1,0:T(8,128)(2,1)S(1)}, u32[]{:S(2)}, u32[]{:S(2)}) async-start(bf16[8,96,128]{2,1,0:T(8,128)(2,1)} %shard_map.120), calls=%async_computation.1 | async-start | bytes 393216 | tf_op jit(solution)/shard_map/all_to_all | solution.py:390
  76.3 0.7 collective-permute-start.17
  77.0 0.9 collective-permute-done.17.other_flow
  77.9 4.2 %all-to-all-done.1.attended = bf16[8,96,128]{2,1,0:T(8,128)(2,1)S(1)} async-done(((bf16[8,96,128]{2,1,0:T(8,128)(2,1)}), bf16[8,96,128]{2,1,0:T(8,128)(2,1)S(1)}, u32[]{:S(2)}, u32[]{:S(2)}) %all-to-all-start.1) | async-done | bytes 196640 | tf_op jit(solution)/shard_map/all_to_all | solution.py:390
  82.1 0.0 copy-start
  82.1 2.2 %copy-done = bf16[1024,2048]{1,0:T(8,128)(2,1)S(1)} copy-done((bf16[1024,2048]{1,0:T(8,128)(2,1)S(1)}, bf16[1024,2048]{1,0:T(8,128)(2,1)}, u32[]{:S(2)}) %copy-start) | copy-done | bytes 4194328
  84.3 2.2 %copy-done.1 = bf16[2048,1024]{1,0:T(8,128)(2,1)S(1)} copy-done((bf16[2048,1024]{1,0:T(8,128)(2,1)S(1)}, bf16[2048,1024]{1,0:T(8,128)(2,1)}, u32[]{:S(2)}) %copy-start.1) | copy-done | bytes 4194328
  86.5 6.2 %shard_map.121 = (bf16[80,96]{1,0:T(8,128)(2,1)S(1)}, bf16[80,96]{1,0:T(8,128)(2,1)S(1)}) custom-call(s32[10]{0:T(128)S(1)} %stack.40.place.refs_0_, bf16[8,96,128]{2,1,0:T(8,128)(2,1)S(1)} %all-to-all-done.1.attended, bf16[192,1024]{1,0:T(8,128)(2,1)S(1)} %copy-done.3, bf16[192,1024]{1,0:T(8,128)(2,1)S(1)} %collective-permute-done.other, ...), custom_call_target="tpu_custom_call" | custom-call | tf_op jit(solution)/shard_map/pallas_call | solution.py:393
  92.6 1.8 %collective-permute-start.18 = (bf16[80,96]{1,0:T(8,128)(2,1)S(1)}, bf16[80,96]{1,0:T(8,128)(2,1)S(1)}, u32[]{:S(2)}, u32[]{:S(2)}) collective-permute-start(bf16[80,96]{1,0:T(8,128)(2,1)S(1)} %get-tuple-element.33), channel_id=1, source_target_pairs={{0,64},{64,0},{1,65},{65,1},{2,66},{66,2},{3,67},{67,3},{4,68},{68... | collective-permute-start | bytes 46088 | tf_op jit(solution)/shard_map/ppermute | solution.py:419
  94.5 0.8 collective-permute-done.18.theirs
  95.3 0.7 shard_map.122
  96.0 1.4 %collective-permute-start.19 = (bf16[80,192]{1,0:T(8,128)(2,1)S(1)}, bf16[80,192]{1,0:T(8,128)(2,1)S(1)}, u32[]{:S(2)}, u32[]{:S(2)}) collective-permute-start(bf16[80,192]{1,0:T(8,128)(2,1)S(1)} %shard_map.122), channel_id=1, source_target_pairs={{0,63},{1,62},{2,61},{3,60},{4,59},{5,58},{6,57},{7,56},{8,55},{9,... | collective-permute-start | bytes 92168 | tf_op jit(solution)/shard_map/ppermute | solution.py:429
  97.4 6.6 %collective-permute-done.19 = bf16[80,192]{1,0:T(8,128)(2,1)S(1)} collective-permute-done((bf16[80,192]{1,0:T(8,128)(2,1)S(1)}, bf16[80,192]{1,0:T(8,128)(2,1)S(1)}, u32[]{:S(2)}, u32[]{:S(2)}) %collective-permute-start.19) | collective-permute-done | bytes 30752 | tf_op jit(solution)/shard_map/ppermute | solution.py:429
  104.0 0.6 slice_add_fusion
  104.6 0.6 slice.12
  (15 shorter events, 0.0 us)
Async XLA Ops:
  0.6 4.9 %collective-permute-start = (bf16[192,1024]{1,0:T(8,128)(2,1)}, bf16[192,1024]{1,0:T(8,128)(2,1)S(1)}, u32[]{:S(2)}, u32[]{:S(2)}) collective-permute-start(bf16[192,1024]{1,0:T(8,128)(2,1)} %hidden.3), channel_id=1, source_target_pairs={{0,64},{64,0},{1,65},{65,1},{2,66},{66,2},{3,67},{67,3},{4,68},{68... | collective-permute-start | bytes 1179656 | tf_op jit(solution)/shard_map/ppermute | solution.py:334
  5.5 1.0 copy-start.2
  6.5 1.2 %copy-start.4 = (bf16[1024,512]{1,0:T(8,128)(2,1)S(1)}, bf16[1024,512]{1,0:T(8,128)(2,1)}, u32[]{:S(2)}) copy-start(bf16[1024,512]{1,0:T(8,128)(2,1)} %w_query.1) | copy-start | bytes 3145732
  7.7 1.2 %copy-start.5 = (bf16[1024,512]{1,0:T(8,128)(2,1)S(1)}, bf16[1024,512]{1,0:T(8,128)(2,1)}, u32[]{:S(2)}) copy-start(bf16[1024,512]{1,0:T(8,128)(2,1)} %w_key.1) | copy-start | bytes 3145732
  9.0 1.2 %copy-start.6 = (bf16[1024,512]{1,0:T(8,128)(2,1)S(1)}, bf16[1024,512]{1,0:T(8,128)(2,1)}, u32[]{:S(2)}) copy-start(bf16[1024,512]{1,0:T(8,128)(2,1)} %w_value.1) | copy-start | bytes 3145732
  25.9 9.2 %collective-permute-start.2 = (bf16[768,128]{1,0:T(8,128)(2,1)S(1)}, bf16[768,128]{1,0:T(8,128)(2,1)S(1)}, u32[]{:S(2)}, u32[]{:S(2)}) collective-permute-start(bf16[768,128]{1,0:T(8,128)(2,1)S(1)} %get-tuple-element.19.refs_3_), channel_id=1, source_target_pairs={{0,1},{1,2},{2,3},{3,4},{4,5},{5,6},{6,7},{7,0},{8,9},{9,10},{10,1... | collective-permute-start | bytes 589832 | tf_op jit(solution)/shard_map/ppermute | solution.py:366
  27.6 7.4 %collective-permute-start.6 = (bf16[768,128]{1,0:T(8,128)(2,1)S(1)}, bf16[768,128]{1,0:T(8,128)(2,1)S(1)}, u32[]{:S(2)}, u32[]{:S(2)}) collective-permute-start(bf16[768,128]{1,0:T(8,128)(2,1)S(1)} %get-tuple-element.20.refs_4_), channel_id=1, source_target_pairs={{0,7},{1,0},{2,1},{3,2},{4,3},{5,4},{6,5},{7,6},{8,15},{9,8},{10,9... | collective-permute-start | bytes 589832 | tf_op jit(solution)/shard_map/ppermute | solution.py:367
  31.7 10.5 %collective-permute-start.10 = (bf16[768,128]{1,0:T(8,128)(2,1)S(1)}, bf16[768,128]{1,0:T(8,128)(2,1)S(1)}, u32[]{:S(2)}, u32[]{:S(2)}) collective-permute-start(bf16[768,128]{1,0:T(8,128)(2,1)S(1)} %get-tuple-element.20.refs_4_), channel_id=1, source_target_pairs={{0,1},{1,2},{2,3},{3,4},{4,5},{5,6},{6,7},{7,0},{8,9},{9,10},{10,1... | collective-permute-start | bytes 589832 | tf_op jit(solution)/shard_map/ppermute | solution.py:366
  31.7 10.5 %collective-permute-start.13 = (bf16[768,128]{1,0:T(8,128)(2,1)S(1)}, bf16[768,128]{1,0:T(8,128)(2,1)S(1)}, u32[]{:S(2)}, u32[]{:S(2)}) collective-permute-start(bf16[768,128]{1,0:T(8,128)(2,1)S(1)} %get-tuple-element.19.refs_3_), channel_id=1, source_target_pairs={{0,7},{1,0},{2,1},{3,2},{4,3},{5,4},{6,5},{7,6},{8,15},{9,8},{10,9... | collective-permute-start | bytes 589832 | tf_op jit(solution)/shard_map/ppermute | solution.py:367
  35.1 9.8 %collective-permute-start.3 = (bf16[768,128]{1,0:T(8,128)(2,1)S(1)}, bf16[768,128]{1,0:T(8,128)(2,1)S(1)}, u32[]{:S(2)}, u32[]{:S(2)}) collective-permute-start(bf16[768,128]{1,0:T(8,128)(2,1)S(1)} %collective-permute-done.2.refs_2_), channel_id=1, source_target_pairs={{0,1},{1,2},{2,3},{3,4},{4,5},{5,6},{6,7},{7,0},{8,9},{9,10},{10,1... | collective-permute-start | bytes 589832 | tf_op jit(solution)/shard_map/ppermute | solution.py:366
  35.1 9.8 %collective-permute-start.7 = (bf16[768,128]{1,0:T(8,128)(2,1)S(1)}, bf16[768,128]{1,0:T(8,128)(2,1)S(1)}, u32[]{:S(2)}, u32[]{:S(2)}) collective-permute-start(bf16[768,128]{1,0:T(8,128)(2,1)S(1)} %collective-permute-done.6.refs_5_), channel_id=1, source_target_pairs={{0,7},{1,0},{2,1},{3,2},{4,3},{5,4},{6,5},{7,6},{8,15},{9,8},{10,9... | collective-permute-start | bytes 589832 | tf_op jit(solution)/shard_map/ppermute | solution.py:367
  37.8 9.8 %collective-permute-start.1 = (bf16[8,96,128]{2,1,0:T(8,128)(2,1)S(1)}, bf16[8,96,128]{2,1,0:T(8,128)(2,1)S(1)}, u32[]{:S(2)}, u32[]{:S(2)}) collective-permute-start(bf16[8,96,128]{2,1,0:T(8,128)(2,1)S(1)} %get-tuple-element.18.refs_1_), channel_id=1, source_target_pairs={{0,64},{64,0},{1,65},{65,1},{2,66},{66,2},{3,67},{67,3},{4,68},{68... | collective-permute-start | bytes 589832 | tf_op jit(solution)/shard_map/ppermute | solution.py:358
  42.2 7.4 %collective-permute-start.11 = (bf16[768,128]{1,0:T(8,128)(2,1)S(1)}, bf16[768,128]{1,0:T(8,128)(2,1)S(1)}, u32[]{:S(2)}, u32[]{:S(2)}) collective-permute-start(bf16[768,128]{1,0:T(8,128)(2,1)S(1)} %collective-permute-done.10.refs_3_), channel_id=1, source_target_pairs={{0,1},{1,2},{2,3},{3,4},{4,5},{5,6},{6,7},{7,0},{8,9},{9,10},{10,1... | collective-permute-start | bytes 589832 | tf_op jit(solution)/shard_map/ppermute | solution.py:366
  42.2 7.7 %collective-permute-start.14 = (bf16[768,128]{1,0:T(8,128)(2,1)S(1)}, bf16[768,128]{1,0:T(8,128)(2,1)S(1)}, u32[]{:S(2)}, u32[]{:S(2)}) collective-permute-start(bf16[768,128]{1,0:T(8,128)(2,1)S(1)} %collective-permute-done.13.refs_4_), channel_id=1, source_target_pairs={{0,7},{1,0},{2,1},{3,2},{4,3},{5,4},{6,5},{7,6},{8,15},{9,8},{10,9... | collective-permute-start | bytes 589832 | tf_op jit(solution)/shard_map/ppermute | solution.py:367
  44.9 10.7 %collective-permute-start.4 = (bf16[768,128]{1,0:T(8,128)(2,1)S(1)}, bf16[768,128]{1,0:T(8,128)(2,1)S(1)}, u32[]{:S(2)}, u32[]{:S(2)}) collective-permute-start(bf16[768,128]{1,0:T(8,128)(2,1)S(1)} %collective-permute-done.3.refs_2_), channel_id=1, source_target_pairs={{0,1},{1,2},{2,3},{3,4},{4,5},{5,6},{6,7},{7,0},{8,9},{9,10},{10,1... | collective-permute-start | bytes 589832 | tf_op jit(solution)/shard_map/ppermute | solution.py:366
  44.9 10.8 %collective-permute-start.8 = (bf16[768,128]{1,0:T(8,128)(2,1)S(1)}, bf16[768,128]{1,0:T(8,128)(2,1)S(1)}, u32[]{:S(2)}, u32[]{:S(2)}) collective-permute-start(bf16[768,128]{1,0:T(8,128)(2,1)S(1)} %collective-permute-done.7.refs_5_), channel_id=1, source_target_pairs={{0,7},{1,0},{2,1},{3,2},{4,3},{5,4},{6,5},{7,6},{8,15},{9,8},{10,9... | collective-permute-start | bytes 589832 | tf_op jit(solution)/shard_map/ppermute | solution.py:367
  49.6 11.8 %collective-permute-start.12 = (bf16[768,128]{1,0:T(8,128)(2,1)S(1)}, bf16[768,128]{1,0:T(8,128)(2,1)S(1)}, u32[]{:S(2)}, u32[]{:S(2)}) collective-permute-start(bf16[768,128]{1,0:T(8,128)(2,1)S(1)} %collective-permute-done.11.refs_3_), channel_id=1, source_target_pairs={{0,1},{1,2},{2,3},{3,4},{4,5},{5,6},{6,7},{7,0},{8,9},{9,10},{10,1... | collective-permute-start | bytes 589832 | tf_op jit(solution)/shard_map/ppermute | solution.py:366
  49.9 11.5 %collective-permute-start.15 = (bf16[768,128]{1,0:T(8,128)(2,1)S(1)}, bf16[768,128]{1,0:T(8,128)(2,1)S(1)}, u32[]{:S(2)}, u32[]{:S(2)}) collective-permute-start(bf16[768,128]{1,0:T(8,128)(2,1)S(1)} %collective-permute-done.14.refs_4_), channel_id=1, source_target_pairs={{0,7},{1,0},{2,1},{3,2},{4,3},{5,4},{6,5},{7,6},{8,15},{9,8},{10,9... | collective-permute-start | bytes 589832 | tf_op jit(solution)/shard_map/ppermute | solution.py:367
  55.6 8.9 %collective-permute-start.5 = (bf16[768,128]{1,0:T(8,128)(2,1)S(1)}, bf16[768,128]{1,0:T(8,128)(2,1)S(1)}, u32[]{:S(2)}, u32[]{:S(2)}) collective-permute-start(bf16[768,128]{1,0:T(8,128)(2,1)S(1)} %collective-permute-done.4.refs_2_), channel_id=1, source_target_pairs={{0,1},{1,2},{2,3},{3,4},{4,5},{5,6},{6,7},{7,0},{8,9},{9,10},{10,1... | collective-permute-start | bytes 589832 | tf_op jit(solution)/shard_map/ppermute | solution.py:378
  55.7 8.8 %collective-permute-start.9 = (bf16[768,128]{1,0:T(8,128)(2,1)S(1)}, bf16[768,128]{1,0:T(8,128)(2,1)S(1)}, u32[]{:S(2)}, u32[]{:S(2)}) collective-permute-start(bf16[768,128]{1,0:T(8,128)(2,1)S(1)} %collective-permute-done.8.refs_5_), channel_id=1, source_target_pairs={{0,7},{1,0},{2,1},{3,2},{4,3},{5,4},{6,5},{7,6},{8,15},{9,8},{10,9... | collective-permute-start | bytes 589832 | tf_op jit(solution)/shard_map/ppermute | solution.py:379
  61.4 15.0 %copy-start.10 = (bf16[64,192]{1,0:T(8,128)(2,1)S(1)}, bf16[64,192]{1,0:T(8,128)(2,1)}, u32[]{:S(2)}) copy-start(bf16[64,192]{1,0:T(8,128)(2,1)} %flow.1) | copy-start | bytes 73732
  61.4 20.7 %copy-start.3 = (bf16[192,1024]{1,0:T(8,128)(2,1)S(1)}, bf16[192,1024]{1,0:T(8,128)(2,1)}, u32[]{:S(2)}) copy-start(bf16[192,1024]{1,0:T(8,128)(2,1)} %hidden.3) | copy-start | bytes 1179652
  61.4 20.7 %copy-start.7 = (bf16[512,1024]{1,0:T(8,128)(2,1)S(1)}, bf16[512,1024]{1,0:T(8,128)(2,1)}, u32[]{:S(2)}) copy-start(bf16[512,1024]{1,0:T(8,128)(2,1)} %w_output.1) | copy-start | bytes 3145732
  61.4 20.7 %copy-start.8 = (bf16[64,1024]{1,0:T(8,128)(2,1)S(1)}, bf16[64,1024]{1,0:T(8,128)(2,1)}, u32[]{:S(2)}) copy-start(bf16[64,1024]{1,0:T(8,128)(2,1)} %w_shift.1) | copy-start | bytes 393220
  61.4 20.7 %copy-start.9 = (bf16[64,1024]{1,0:T(8,128)(2,1)S(1)}, bf16[64,1024]{1,0:T(8,128)(2,1)}, u32[]{:S(2)}) copy-start(bf16[64,1024]{1,0:T(8,128)(2,1)} %w_scale.1) | copy-start | bytes 393220
  66.8 4.8 %collective-permute-start.16 = (bf16[8,96,256]{2,1,0:T(8,128)(2,1)S(1)}, bf16[8,96,256]{2,1,0:T(8,128)(2,1)S(1)}, u32[]{:S(2)}, u32[]{:S(2)}) collective-permute-start(bf16[8,96,256]{2,1,0:T(8,128)(2,1)S(1)} %get-tuple-element.31), channel_id=1, source_target_pairs={{0,64},{64,0},{1,65},{65,1},{2,66},{66,2},{3,67},{67,3},{4,68},{68... | collective-permute-start | bytes 1179656 | tf_op jit(solution)/shard_map/ppermute | solution.py:382
  72.9 9.1 %all-to-all-start.1 = ((bf16[8,96,128]{2,1,0:T(8,128)(2,1)}), bf16[8,96,128]{2,1,0:T(8,128)(2,1)S(1)}, u32[]{:S(2)}, u32[]{:S(2)}) async-start(bf16[8,96,128]{2,1,0:T(8,128)(2,1)} %shard_map.120), calls=%async_computation.1 | async-start | bytes 393216 | tf_op jit(solution)/shard_map/all_to_all | solution.py:390
  76.3 1.5 %collective-permute-start.17 = (bf16[64,192]{1,0:T(8,128)(2,1)S(1)}, bf16[64,192]{1,0:T(8,128)(2,1)S(1)}, u32[]{:S(2)}, u32[]{:S(2)}) collective-permute-start(bf16[64,192]{1,0:T(8,128)(2,1)S(1)} %copy-done.10), channel_id=1, source_target_pairs={{0,64},{64,0},{1,65},{65,1},{2,66},{66,2},{3,67},{67,3},{4,68},{68... | collective-permute-start | bytes 73736 | tf_op jit(solution)/shard_map/ppermute | solution.py:335
  82.1 2.2 %copy-start = (bf16[1024,2048]{1,0:T(8,128)(2,1)S(1)}, bf16[1024,2048]{1,0:T(8,128)(2,1)}, u32[]{:S(2)}) copy-start(bf16[1024,2048]{1,0:T(8,128)(2,1)} %w_up.1) | copy-start | bytes 12582916
  84.3 2.2 %copy-start.1 = (bf16[2048,1024]{1,0:T(8,128)(2,1)S(1)}, bf16[2048,1024]{1,0:T(8,128)(2,1)}, u32[]{:S(2)}) copy-start(bf16[2048,1024]{1,0:T(8,128)(2,1)} %w_down.1) | copy-start | bytes 12582916
  92.6 2.7 %collective-permute-start.18 = (bf16[80,96]{1,0:T(8,128)(2,1)S(1)}, bf16[80,96]{1,0:T(8,128)(2,1)S(1)}, u32[]{:S(2)}, u32[]{:S(2)}) collective-permute-start(bf16[80,96]{1,0:T(8,128)(2,1)S(1)} %get-tuple-element.33), channel_id=1, source_target_pairs={{0,64},{64,0},{1,65},{65,1},{2,66},{66,2},{3,67},{67,3},{4,68},{68... | collective-permute-start | bytes 46088 | tf_op jit(solution)/shard_map/ppermute | solution.py:419
  96.0 8.0 %collective-permute-start.19 = (bf16[80,192]{1,0:T(8,128)(2,1)S(1)}, bf16[80,192]{1,0:T(8,128)(2,1)S(1)}, u32[]{:S(2)}, u32[]{:S(2)}) collective-permute-start(bf16[80,192]{1,0:T(8,128)(2,1)S(1)} %shard_map.122), channel_id=1, source_target_pairs={{0,63},{1,62},{2,61},{3,60},{4,59},{5,58},{6,57},{7,56},{8,55},{9,... | collective-permute-start | bytes 92168 | tf_op jit(solution)/shard_map/ppermute | solution.py:429

commit v3 on v2

--- a/solution.py
+++ b/solution.py
@@ -48,35 +48,50 @@
     return pl.BlockSpec(memory_space=pltpu.SMEM)
 
 
-def anywhere():
-    return pl.BlockSpec(memory_space=pl.ANY)
-
-
 def params(mebibytes):
     return pltpu.CompilerParams(vmem_limit_bytes=mebibytes << 20)
 
 
-def qkv_kernel(place, hidden, other, w_query, w_key, w_value, slots, weights, normed, sems):
-    core = place[0]
-    sources = (w_key, w_value, w_query)
+def in_hbm(array):
+    return pltpu.with_memory_space_constraint(array, pltpu.HBM)
+
+
+def hbm():
+    return pl.BlockSpec(memory_space=pltpu.HBM)
+
+
+def start_loads(sources, targets, sems):
     copies = []
-    for index, source in enumerate(sources):
-        for part in range(2):
-            rows = pl.ds(part * (WIDTH // 2), WIDTH // 2)
+    for source, target in zip(sources, targets):
+        pieces = 4 if source.shape[0] >= 512 else 1
+        size = source.shape[0] // pieces
+        for piece in range(pieces):
+            cut = pl.ds(piece * size, size)
             copies.append(
-                pltpu.make_async_copy(
-                    source.at[rows], weights.at[index, rows], sems.at[2 * index + part]
-                )
+                pltpu.make_async_copy(source.at[cut], target.at[cut], sems.at[len(copies)])
             )
     for copy in copies:
         copy.start()
+    return copies
+
+
+def load_kernel(place, hidden, w_query, w_key, w_value, own, query, key, value, sems, own_sem):
+    rows = pl.ds(pl.multiple_of(place[0] * PIECE, PIECE), PIECE)
+    copy = pltpu.make_async_copy(hidden.at[rows], own, own_sem)
+    copy.start()
+    copies = start_loads((w_key, w_value, w_query), (key, value, query), sems)
+    copy.wait()
+    for copy in copies:
+        copy.wait()
+
+
+def qkv_kernel(place, own, other, w_query, w_key, w_value, slots, normed):
+    core = place[0]
+    normed[:PIECE, :] = layer_norm(own[...].astype(f32)).astype(bf16)
     rows = pl.ds(pl.multiple_of(core * PIECE, PIECE), PIECE)
-    normed[:PIECE, :] = layer_norm(hidden[rows, :].astype(f32)).astype(bf16)
     normed[PIECE:, :] = layer_norm(other[rows, :].astype(f32)).astype(bf16)
-    for index, column in enumerate((1, 2, 0)):
-        copies[2 * index].wait()
-        copies[2 * index + 1].wait()
-        made = jnp.dot(normed[...], weights[index], preferred_element_type=f32).astype(bf16)
+    for column, weight in enumerate((w_query, w_key, w_value)):
+        made = jnp.dot(normed[...], weight[...], preferred_element_type=f32).astype(bf16)
         for part in range(2):
             sequence = core if part == 0 else 1 - core
             for head in range(HEADS):
@@ -99,7 +114,7 @@
     queries[...] = slots[:, :, :HEAD]
 
 
-def attend_kernel(parts, sources, first, last, *refs):
+def attend_kernel(parts, sources, first, last, load_count, *refs):
     refs = list(refs)
     place = refs.pop(0)
     if first:
@@ -109,6 +124,12 @@
     segments = [refs.pop(0) for _ in parts]
     if not first:
         top_in, numer_in = refs.pop(0), refs.pop(0)
+    loads = []
+    if load_count:
+        weights_in = [refs.pop(0) for _ in range(load_count)]
+        sems = refs.pop()
+        weights_out = [refs.pop() for _ in range(load_count)][::-1]
+        loads = start_loads(weights_in, weights_out, sems)
     if first:
         queries = refs.pop(0)
         for tile in range(TILES):
@@ -187,9 +208,11 @@
         following = score(tile + 1) if tile + 1 < TILES else None
         finish(tile, found)
         found = following
-
-
-def attend(place, queries, segments, parts, sources, state, last):
+    for load in loads:
+        load.wait()
+
+
+def attend(place, queries, segments, parts, sources, state, last, loads=()):
     first = state is None
     stats = [jax.ShapeDtypeStruct((8, 2 * ROWS), f32), jax.ShapeDtypeStruct((TALL, 2 * ROWS), f32)]
     if last:
@@ -199,11 +222,15 @@
     else:
         shapes = stats
     operands = [place, *queries, *segments, *(state or ())]
+    in_specs = [smem()] + [vmem()] * (len(operands) - 1) + [hbm()] * len(loads)
+    shapes = list(shapes) + [pltpu.VMEM(load.shape, load.dtype) for load in loads]
+    operands += [in_hbm(load) for load in loads]
     return pl.pallas_call(
-        functools.partial(attend_kernel, parts, sources, first, last),
+        functools.partial(attend_kernel, parts, sources, first, last, len(loads)),
         out_shape=shapes,
-        in_specs=[smem()] + [vmem()] * (len(operands) - 1),
+        in_specs=in_specs,
         out_specs=[vmem()] * len(shapes),
+        scratch_shapes=[pltpu.SemaphoreType.DMA((4 * len(loads),))] if loads else [],
         compiler_params=params(24),
         cost_estimate=pl.CostEstimate(
             flops=2 * 2 * 2 * ROWS * HALF * HEAD * len(parts),
@@ -214,28 +241,29 @@
 
 
 def merge_kernel(mine, theirs, out):
+    row = lax.broadcasted_iota(jnp.int32, (HEAD, HEAD), 0)
+    spread = (row < 3).astype(f32).astype(bf16)
+
     def level(block):
-        parts = [block[:, :, HEAD + index : HEAD + index + 1].astype(f32) for index in range(3)]
-        return parts[0] + parts[1] + parts[2]
+        stats = block[:, :, HEAD:].reshape(ROWS, HEAD)
+        return jnp.dot(stats, spread, preferred_element_type=f32)
 
     first, second = level(mine), level(theirs)
     top = jnp.maximum(first, second)
     first, second = jnp.exp2(first - top), jnp.exp2(second - top)
-    share = 1.0 / (first + second)
-    out[...] = (
-        (first * share) * mine[:, :, :HEAD].astype(f32)
-        + (second * share) * theirs[:, :, :HEAD].astype(f32)
-    ).astype(bf16)
-
-
-FF_PARTS = 4
+    both = first * mine[:, :, :HEAD].reshape(ROWS, HEAD).astype(f32)
+    both = both + second * theirs[:, :, :HEAD].reshape(ROWS, HEAD).astype(f32)
+    out[...] = (both / (first + second)).astype(bf16).reshape(PLANES, PIECE, HEAD)
+
+
+FF_PARTS = 2
 FF_PART = FF // FF_PARTS
 
 
 def dense_kernel(
     place,
     attended,
-    hidden,
+    own,
     other,
     flow,
     other_flow,
@@ -246,52 +274,30 @@
     w_scale,
     sent_own,
     sent_other,
-    output,
-    up,
-    down,
-    shift_scale,
-    sems,
 ):
     core = place[0]
-    copies = [pltpu.make_async_copy(w_output, output, sems.at[0])]
-    for part in range(FF_PARTS):
-        cut = pl.ds(part * FF_PART, FF_PART)
-        copies.append(
-            pltpu.make_async_copy(w_up.at[:, cut], up.at[:, cut], sems.at[1 + 2 * part])
-        )
-        copies.append(pltpu.make_async_copy(w_down.at[cut], down.at[cut], sems.at[2 + 2 * part]))
-    for index, source in enumerate((w_shift, w_scale)):
-        cut = pl.ds(index * CHANNELS, CHANNELS)
-        copies.append(
-            pltpu.make_async_copy(source, shift_scale.at[cut], sems.at[1 + 2 * FF_PARTS + index])
-        )
-    for copy in copies:
-        copy.start()
     rows = pl.ds(pl.multiple_of(core * PIECE, PIECE), PIECE)
-    residual = jnp.concatenate([hidden[rows, :], other[rows, :]], axis=0).astype(f32)
+    residual = jnp.concatenate([own[...], other[rows, :]], axis=0).astype(f32)
     sides = []
     for sequence in (core, 1 - core):
         heads = [attended[sequence * HEADS + head] for head in range(HEADS)]
         sides.append(jnp.concatenate(heads, axis=1))
     mixed = jnp.concatenate(sides, axis=0)
-    copies[0].wait()
-    first = residual + jnp.dot(mixed, output[...], preferred_element_type=f32)
+    first = residual + jnp.dot(mixed, w_output[...], preferred_element_type=f32)
     inner = layer_norm(first).astype(bf16)
     second = first
     for part in range(FF_PARTS):
         cut = slice(part * FF_PART, (part + 1) * FF_PART)
-        copies[1 + 2 * part].wait()
-        expanded = jnp.dot(inner, up[:, cut], preferred_element_type=f32)
+        expanded = jnp.dot(inner, w_up[:, cut], preferred_element_type=f32)
         expanded = jax.nn.gelu(expanded).astype(bf16)
-        copies[2 + 2 * part].wait()
-        second = second + jnp.dot(expanded, down[cut, :], preferred_element_type=f32)
+        second = second + jnp.dot(expanded, w_down[cut, :], preferred_element_type=f32)
     features = layer_norm(second).astype(bf16)
-    copies[-2].wait()
-    copies[-1].wait()
-    both = lax.dot_general(
-        shift_scale[...], features, (((1,), (1,)), ((), ())), preferred_element_type=f32
+    shift, log_scale = (
+        lax.dot_general(
+            weight[...], features, (((1,), (1,)), ((), ())), preferred_element_type=f32
+        )
+        for weight in (w_shift, w_scale)
     )
-    shift, log_scale = both[:CHANNELS], both[CHANNELS:]
     determinant = -jnp.sum(log_scale, axis=0, keepdims=True)
     high = determinant.astype(bf16)
     low = (determinant - high.astype(f32)).astype(bf16)
@@ -334,18 +340,24 @@
     other = lax.ppermute(hidden, "core", other_core)
     other_flow = lax.ppermute(flow_input, "core", other_core)
 
+    square = pltpu.VMEM((WIDTH, INNER), bf16)
+    own, *weights = pl.pallas_call(
+        load_kernel,
+        out_shape=[pltpu.VMEM((PIECE, WIDTH), bf16), square, square, square],
+        in_specs=[smem()] + [hbm()] * 4,
+        out_specs=[vmem()] * 4,
+        scratch_shapes=[pltpu.SemaphoreType.DMA((12,)), pltpu.SemaphoreType.DMA],
+        compiler_params=params(8),
+        cost_estimate=pl.CostEstimate(flops=0, bytes_accessed=6_600_000, transcendentals=0),
+    )(place, *(in_hbm(array) for array in (hidden, w_query, w_key, w_value)))
     slots = pl.pallas_call(
         qkv_kernel,
         out_shape=jax.ShapeDtypeStruct((PLANES, PIECE, 3 * HEAD), bf16),
-        in_specs=[smem()] + [vmem()] * 2 + [anywhere()] * 3,
+        in_specs=[smem()] + [vmem()] * 5,
         out_specs=vmem(),
-        scratch_shapes=[
-            pltpu.VMEM((3, WIDTH, INNER), bf16),
-            pltpu.VMEM((TOKENS, WIDTH), bf16),
-            pltpu.SemaphoreType.DMA((6,)),
-        ],
-        compiler_params=params(16),
-    )(place, hidden, other, w_query, w_key, w_value)
+        scratch_shapes=[pltpu.VMEM((TOKENS, WIDTH), bf16)],
+        compiler_params=params(8),
+    )(place, own, other, *weights)
     slots = lax.all_to_all(slots, ("xl", "y"), 0, 0, tiled=True)
     part = jax.ShapeDtypeStruct((ROWS, HEAD), bf16)
     *own_parts, own_queries = pl.pallas_call(
@@ -361,6 +373,8 @@
     queries, *state = attend(
         place, (own_queries, other_queries), own_parts, (0, 1), (0, 0), None, False
     )
+    loads = {1: (w_output, w_up), 2: (w_down, w_shift, w_scale), 3: ()}
+    dense_weights = []
     for step in range(1, 4):
         for part in range(2):
             up[part] = lax.ppermute(up[part], "z", shift_by(Z, 1))
@@ -373,7 +387,10 @@
             (step, step, 5 + step, 5 + step),
             state,
             False,
+            loads[step],
         )
+        dense_weights += state[2:]
+        state = state[:2]
     far = [
         lax.ppermute(up[0], "z", shift_by(Z, 1)),
         lax.ppermute(down[1], "z", shift_by(Z, -1)),
@@ -393,29 +410,10 @@
     sent_own, sent_other = pl.pallas_call(
         dense_kernel,
         out_shape=[sent, sent],
-        in_specs=[smem()] + [vmem()] * 5 + [anywhere()] * 5,
+        in_specs=[smem()] + [vmem()] * 10,
         out_specs=[vmem()] * 2,
-        scratch_shapes=[
-            pltpu.VMEM((INNER, WIDTH), bf16),
-            pltpu.VMEM((WIDTH, FF), bf16),
-            pltpu.VMEM((FF, WIDTH), bf16),
-            pltpu.VMEM((2 * CHANNELS, WIDTH), bf16),
-            pltpu.SemaphoreType.DMA((3 + 2 * FF_PARTS,)),
-        ],
-        compiler_params=params(32),
-    )(
-        place,
-        attended,
-        hidden,
-        other,
-        flow_input,
-        other_flow,
-        w_output,
-        w_up,
-        w_down,
-        w_shift,
-        w_scale,
-    )
+        compiler_params=params(16),
+    )(place, attended, own, other, flow_input, other_flow, *dense_weights)
     received = lax.ppermute(sent_other, "core", other_core)
     block = pl.pallas_call(
         join_kernel,

time: 106 us -> 106 us (level)
  Pallas kernels: 24 us -> 26.8 us
  starting transfers between devices: 40.6 us -> 39.5 us
    pallas_call x5, Pallas kernels: 13.4 us -> 17 us  [attend(): pl.pallas_call(functools.partial(attend_kernel, parts, sources, first, la...]
    pallas_call x0 -> x1, Pallas kernels: none -> 2.55 us  [on_device(): pl.pallas_call(load_kernel, out_shape=[pltpu.VMEM((PIECE, WIDTH), bf16),...]
    pallas_call x1, Pallas kernels: 6.18 us -> 3.81 us  [on_device(): pl.pallas_call(dense_kernel, out_shape=[sent, sent], in_specs=[smem()] +...]
    ppermute x1, waiting for transfers between devices: 1.47 us -> 0.01 us  [on_device(): other = lax.ppermute(hidden, 'core', other_core)]
    unnamed x22 -> x10, local copies, waits for them, and re-layouts: 9.07 us -> 8.34 us
  transfers between devices with their start and end apart: 21 -> 21, of which waited for: 7 -> 6; matrix products, arithmetic and copies ran while one was open for 0% -> 0% of each run, Pallas kernels for 11% -> 16%
where the time goes in v3:
time: 106 us
  starting transfers between devices  39.5 us (37%)
  Pallas kernels  26.8 us (25%)
  waiting for transfers between devices  15.6 us (15%)
  blocking collectives  13.6 us (13%)
  local copies, waits for them, and re-layouts  9.06 us (9%)
    ppermute x6, starting transfers between devices, on_device(): down[part] = lax.ppermute(down[part], 'z', shift_by(Z, -1))  17.4 us
    pallas_call x5, Pallas kernels, attend(): pl.pallas_call(functools.partial(attend_kernel, parts, sources, first, la...  17 us
    all_to_all x1, blocking collectives, on_device(): slots = lax.all_to_all(slots, ('xl', 'y'), 0, 0, tiled=True)  13.6 us
    unnamed x10, local copies, waits for them, and re-layouts  8.34 us
    ppermute x1, waiting for transfers between devices, on_device(): arrived = lax.ppermute(block, ('xl', 'y', 'z'), mirrored).astype(f32)  7.33 us
    all_to_all x1, waiting for transfers between devices, on_device(): attended = lax.all_to_all(attended, ('xl', 'y'), 0, 0, tiled=True)  4.16 us
    ppermute x1, starting transfers between devices, on_device(): other_queries = lax.ppermute(own_queries, 'core', other_core)  4.09 us
    pallas_call x1, Pallas kernels, on_device(): pl.pallas_call(dense_kernel, out_shape=[sent, sent], in_specs=[smem()] +...  3.81 us
  transfers between devices with their start and end apart: 21, of which 6 were waited for; matrix products, arithmetic and copies ran while one was open for 0% of the time, Pallas kernels for 16%

profile of v3, /device:TPU:1, one launch (start us, length us, event | category | flops | bytes accessed | tf_op | source)
XLA Modules:
  0.0 105.9 jit_solution(4946506148440272897)
XLA Ops:
  0.6 3.3 %collective-permute-start = (bf16[192,1024]{1,0:T(8,128)(2,1)}, bf16[192,1024]{1,0:T(8,128)(2,1)S(1)}, u32[]{:S(2)}, u32[]{:S(2)}) collective-permute-start(bf16[192,1024]{1,0:T(8,128)(2,1)} %hidden.1), channel_id=1, source_target_pairs={{0,64},{64,0},{1,65},{65,1},{2,66},{66,2},{3,67},{67,3},{4,68},{68... | collective-permute-start | bytes 1179656 | tf_op jit(solution)/shard_map/ppermute | solution.py:340
  4.0 0.1 stack.40.place.refs_0_
  4.0 2.5 %shard_map.113 = (bf16[96,1024]{1,0:T(8,128)(2,1)S(1)}, bf16[1024,512]{1,0:T(8,128)(2,1)S(1)}, bf16[1024,512]{1,0:T(8,128)(2,1)S(1)}, bf16[1024,512]{1,0:T(8,128)(2,1)S(1)}) custom-call(s32[10]{0:T(128)S(1)} %stack.40.place.refs_0_, bf16[192,1024]{1,0:T(8,128)(2,1)} %hidden.1, bf16[1024,512]{1,0:T(8,128)(2,1)} %w_query.1, bf16[1024,512]{1,0:T(8,128)(2,1)} %w_key.1, ...), custom_call_target="tpu_custom_call" | custom-call | bytes 6600000 | tf_op jit(solution)/shard_map/pallas_call | solution.py:344
  6.6 0.0 collective-permute-done.other
  6.6 1.6 %shard_map.114 = bf16[8,96,384]{2,1,0:T(8,128)(2,1)S(1)} custom-call(s32[10]{0:T(128)S(1)} %stack.40.place.refs_0_, bf16[96,1024]{1,0:T(8,128)(2,1)S(1)} %get-tuple-element.27.own, bf16[192,1024]{1,0:T(8,128)(2,1)S(1)} %collective-permute-done.other, bf16[1024,512]{1,0:T(8,128)(2,1)S(1)} %get-tuple-element.28.w_query, ...), custom_call_target="tpu_custom_call" | custom-call | tf_op jit(solution)/shard_map/pallas_call | solution.py:353
  8.2 13.6 %all_to_all.10.slots = bf16[8,96,384]{2,1,0:T(8,128)(2,1)S(1)} all-to-all(bf16[8,96,384]{2,1,0:T(8,128)(2,1)S(1)} %shard_map.114), channel_id=1, replica_groups=mesh['xh'=2,'core'=2,'xl'=2,'y'=4,'z'=8] {'xl','y'}, dimensions={0} | all-to-all | bytes 1179648 | tf_op jit(solution)/shard_map/all_to_all | solution.py:361
  21.7 0.1 shard_map.115
  21.9 1.7 %collective-permute-start.2 = (bf16[768,128]{1,0:T(8,128)(2,1)S(1)}, bf16[768,128]{1,0:T(8,128)(2,1)S(1)}, u32[]{:S(2)}, u32[]{:S(2)}) collective-permute-start(bf16[768,128]{1,0:T(8,128)(2,1)S(1)} %get-tuple-element.32.refs_3_), channel_id=1, source_target_pairs={{0,1},{1,2},{2,3},{3,4},{4,5},{5,6},{6,7},{7,0},{8,9},{9,10},{10,1... | collective-permute-start | bytes 589832 | tf_op jit(solution)/shard_map/ppermute | solution.py:380
  23.6 4.0 %collective-permute-start.6 = (bf16[768,128]{1,0:T(8,128)(2,1)S(1)}, bf16[768,128]{1,0:T(8,128)(2,1)S(1)}, u32[]{:S(2)}, u32[]{:S(2)}) collective-permute-start(bf16[768,128]{1,0:T(8,128)(2,1)S(1)} %get-tuple-element.33.refs_4_), channel_id=1, source_target_pairs={{0,7},{1,0},{2,1},{3,2},{4,3},{5,4},{6,5},{7,6},{8,15},{9,8},{10,9... | collective-permute-start | bytes 589832 | tf_op jit(solution)/shard_map/ppermute | solution.py:381
  27.6 0.0 collective-permute-start.10
  27.6 2.7 %collective-permute-start.13 = (bf16[768,128]{1,0:T(8,128)(2,1)S(1)}, bf16[768,128]{1,0:T(8,128)(2,1)S(1)}, u32[]{:S(2)}, u32[]{:S(2)}) collective-permute-start(bf16[768,128]{1,0:T(8,128)(2,1)S(1)} %get-tuple-element.32.refs_3_), channel_id=1, source_target_pairs={{0,7},{1,0},{2,1},{3,2},{4,3},{5,4},{6,5},{7,6},{8,15},{9,8},{10,9... | collective-permute-start | bytes 589832 | tf_op jit(solution)/shard_map/ppermute | solution.py:381
  30.3 1.0 collective-permute-done.2.refs_2_
  31.3 0.0 collective-permute-start.3
  31.3 0.0 collective-permute-done.6.refs_5_
  31.3 2.7 %collective-permute-start.7 = (bf16[768,128]{1,0:T(8,128)(2,1)S(1)}, bf16[768,128]{1,0:T(8,128)(2,1)S(1)}, u32[]{:S(2)}, u32[]{:S(2)}) collective-permute-start(bf16[768,128]{1,0:T(8,128)(2,1)S(1)} %collective-permute-done.6.refs_5_), channel_id=1, source_target_pairs={{0,7},{1,0},{2,1},{3,2},{4,3},{5,4},{6,5},{7,6},{8,15},{9,8},{10,9... | collective-permute-start | bytes 589832 | tf_op jit(solution)/shard_map/ppermute | solution.py:381
  34.0 4.1 %collective-permute-start.1 = (bf16[8,96,128]{2,1,0:T(8,128)(2,1)S(1)}, bf16[8,96,128]{2,1,0:T(8,128)(2,1)S(1)}, u32[]{:S(2)}, u32[]{:S(2)}) collective-permute-start(bf16[8,96,128]{2,1,0:T(8,128)(2,1)S(1)} %get-tuple-element.31.refs_1_), channel_id=1, source_target_pairs={{0,64},{64,0},{1,65},{65,1},{2,66},{66,2},{3,67},{67,3},{4,68},{68... | collective-permute-start | bytes 589832 | tf_op jit(solution)/shard_map/ppermute | solution.py:370
  38.1 0.0 collective-permute-done.10.refs_3_
  38.1 0.0 collective-permute-start.11
  38.1 0.0 collective-permute-done.13.refs_4_
  38.1 2.7 %collective-permute-start.14 = (bf16[768,128]{1,0:T(8,128)(2,1)S(1)}, bf16[768,128]{1,0:T(8,128)(2,1)S(1)}, u32[]{:S(2)}, u32[]{:S(2)}) collective-permute-start(bf16[768,128]{1,0:T(8,128)(2,1)S(1)} %collective-permute-done.13.refs_4_), channel_id=1, source_target_pairs={{0,7},{1,0},{2,1},{3,2},{4,3},{5,4},{6,5},{7,6},{8,15},{9,8},{10,9... | collective-permute-start | bytes 589832 | tf_op jit(solution)/shard_map/ppermute | solution.py:381
  40.8 0.0 collective-permute-done.3.refs_2_
  40.8 0.0 collective-permute-start.4
  40.8 0.0 collective-permute-done.7.refs_5_
  40.8 2.7 %collective-permute-start.8 = (bf16[768,128]{1,0:T(8,128)(2,1)S(1)}, bf16[768,128]{1,0:T(8,128)(2,1)S(1)}, u32[]{:S(2)}, u32[]{:S(2)}) collective-permute-start(bf16[768,128]{1,0:T(8,128)(2,1)S(1)} %collective-permute-done.7.refs_5_), channel_id=1, source_target_pairs={{0,7},{1,0},{2,1},{3,2},{4,3},{5,4},{6,5},{7,6},{8,15},{9,8},{10,9... | collective-permute-start | bytes 589832 | tf_op jit(solution)/shard_map/ppermute | solution.py:381
  43.4 0.0 collective-permute-done.1.refs_2_
  43.4 2.1 %shard_map.116 = (bf16[128,1536]{1,0:T(8,128)(2,1)S(1)}, f32[8,1536]{1,0:T(8,128)S(1)}, f32[144,1536]{1,0:T(8,128)S(1)}) custom-call(s32[10]{0:T(128)S(1)} %stack.40.place.refs_0_, bf16[8,96,128]{2,1,0:T(8,128)(2,1)S(1)} %get-tuple-element.31.refs_1_, bf16[8,96,128]{2,1,0:T(8,128)(2,1)S(1)} %collective-permute-done.1.refs_2_, ...), custom_call_target="tpu_custom_call" | custom-call | flops 603979776 | bytes 3000000 | tf_op jit(solution)/shard_map/pallas_call | solution.py:228
  45.5 0.0 collective-permute-done.11.refs_3_
  45.5 0.1 collective-permute-start.12
  45.6 0.0 collective-permute-done.14.refs_4_
  45.6 2.7 %collective-permute-start.15 = (bf16[768,128]{1,0:T(8,128)(2,1)S(1)}, bf16[768,128]{1,0:T(8,128)(2,1)S(1)}, u32[]{:S(2)}, u32[]{:S(2)}) collective-permute-start(bf16[768,128]{1,0:T(8,128)(2,1)S(1)} %collective-permute-done.14.refs_4_), channel_id=1, source_target_pairs={{0,7},{1,0},{2,1},{3,2},{4,3},{5,4},{6,5},{7,6},{8,15},{9,8},{10,9... | collective-permute-start | bytes 589832 | tf_op jit(solution)/shard_map/ppermute | solution.py:381
  48.3 5.2 %shard_map.117 = (f32[8,1536]{1,0:T(8,128)S(1)}, f32[144,1536]{1,0:T(8,128)S(1)}, bf16[512,1024]{1,0:T(8,128)(2,1)S(1)}, bf16[1024,2048]{1,0:T(8,128)(2,1)S(1)}) custom-call(s32[10]{0:T(128)S(1)} %stack.40.place.refs_0_, bf16[128,1536]{1,0:T(8,128)(2,1)S(1)} %get-tuple-element.34.refs_1_, bf16[768,128]{1,0:T(8,128)(2,1)S(1)} %collective-permute-done.2.refs_2_, ...), custom_call_target="tpu_custom_call" | custom-call | flops 1207959552 | bytes 3000000 | tf_op jit(solution)/shard_map/pallas_call | solution.py:228
  53.5 0.0 copy-start
  53.5 1.9 %copy-done = bf16[1024,2048]{1,0:T(8,128)(2,1)} copy-done((bf16[1024,2048]{1,0:T(8,128)(2,1)}, bf16[1024,2048]{1,0:T(8,128)(2,1)S(1)}, u32[]{:S(2)}) %copy-start) | copy-done | bytes 4194328
  55.4 0.0 collective-permute-done.4.refs_2_
  55.4 0.0 collective-permute-start.5
  55.4 0.0 collective-permute-done.8.refs_5_
  55.4 2.7 %collective-permute-start.9 = (bf16[768,128]{1,0:T(8,128)(2,1)S(1)}, bf16[768,128]{1,0:T(8,128)(2,1)S(1)}, u32[]{:S(2)}, u32[]{:S(2)}) collective-permute-start(bf16[768,128]{1,0:T(8,128)(2,1)S(1)} %collective-permute-done.8.refs_5_), channel_id=1, source_target_pairs={{0,7},{1,0},{2,1},{3,2},{4,3},{5,4},{6,5},{7,6},{8,15},{9,8},{10,9... | collective-permute-start | bytes 589832 | tf_op jit(solution)/shard_map/ppermute | solution.py:396
  58.1 4.4 %shard_map.118 = (f32[8,1536]{1,0:T(8,128)S(1)}, f32[144,1536]{1,0:T(8,128)S(1)}, bf16[2048,1024]{1,0:T(8,128)(2,1)S(1)}, bf16[64,1024]{1,0:T(8,128)(2,1)S(1)}, bf16[64,1024]{1,0:T(8,128)(2,1)S(1)}) custom-call(s32[10]{0:T(128)S(1)} %stack.40.place.refs_0_, bf16[128,1536]{1,0:T(8,128)(2,1)S(1)} %get-tuple-element.34.refs_1_, ...), custom_call_target="tpu_custom_call" | custom-call | flops 1207959552 | bytes 3000000 | tf_op jit(solution)/shard_map/pallas_call | solution.py:228
  62.6 0.0 copy-start.2
  62.6 2.0 %copy-done.2 = bf16[2048,1024]{1,0:T(8,128)(2,1)} copy-done((bf16[2048,1024]{1,0:T(8,128)(2,1)}, bf16[2048,1024]{1,0:T(8,128)(2,1)S(1)}, u32[]{:S(2)}) %copy-start.2) | copy-done | bytes 4194328
  64.6 0.0 collective-permute-done.12.refs_3_
  64.6 0.0 collective-permute-done.15.refs_4_
  64.6 3.0 %shard_map.119 = (f32[8,1536]{1,0:T(8,128)S(1)}, f32[144,1536]{1,0:T(8,128)S(1)}) custom-call(s32[10]{0:T(128)S(1)} %stack.40.place.refs_0_, bf16[128,1536]{1,0:T(8,128)(2,1)S(1)} %get-tuple-element.34.refs_1_, bf16[768,128]{1,0:T(8,128)(2,1)S(1)} %collective-permute-done.4.refs_2_, bf16[768,128]{1,0:T(8,128)(2,1)S(1)} %collective-permute-done.12.refs_3_, ...), custom_call_target="tpu_custom_call" | custom-call | flops 1207959552 | bytes 3000000 | tf_op jit(solution)/shard_map/pallas_call | solution.py:228
  67.6 0.0 collective-permute-done.5.refs_2_
  67.7 0.0 collective-permute-done.9.refs_3_
  67.7 2.3 %shard_map.120 = (bf16[8,96,256]{2,1,0:T(8,128)(2,1)S(1)}, bf16[8,96,256]{2,1,0:T(8,128)(2,1)S(1)}) custom-call(s32[10]{0:T(128)S(1)} %stack.40.place.refs_0_, bf16[128,1536]{1,0:T(8,128)(2,1)S(1)} %get-tuple-element.34.refs_1_, bf16[768,128]{1,0:T(8,128)(2,1)S(1)} %collective-permute-done.5.refs_2_, bf16[768,128]{1,0:T(8,128)(2,1)S(1)} %collective-permute-done.9.refs_3_, ...), custom_call_target="tpu_custom_call" | custom-call | flops 603979776 | bytes 3000000 | tf_op jit(solution)/shard_map/pallas_call | solution.py:228
  70.0 3.7 %collective-permute-start.16 = (bf16[8,96,256]{2,1,0:T(8,128)(2,1)S(1)}, bf16[8,96,256]{2,1,0:T(8,128)(2,1)S(1)}, u32[]{:S(2)}, u32[]{:S(2)}) collective-permute-start(bf16[8,96,256]{2,1,0:T(8,128)(2,1)S(1)} %get-tuple-element.44), channel_id=1, source_target_pairs={{0,64},{64,0},{1,65},{65,1},{2,66},{66,2},{3,67},{67,3},{4,68},{68... | collective-permute-start | bytes 1179656 | tf_op jit(solution)/shard_map/ppermute | solution.py:399
  73.7 1.3 %collective-permute-done.16.theirs = bf16[8,96,256]{2,1,0:T(8,128)(2,1)S(1)} collective-permute-done((bf16[8,96,256]{2,1,0:T(8,128)(2,1)S(1)}, bf16[8,96,256]{2,1,0:T(8,128)(2,1)S(1)}, u32[]{:S(2)}, u32[]{:S(2)}) %collective-permute-start.16) | collective-permute-done | bytes 393248 | tf_op jit(solution)/shard_map/ppermute | solution.py:399
  75.0 1.0 shard_map.121
  76.0 3.4 %all-to-all-start.1 = ((bf16[8,96,128]{2,1,0:T(8,128)(2,1)}), bf16[8,96,128]{2,1,0:T(8,128)(2,1)S(1)}, u32[]{:S(2)}, u32[]{:S(2)}) async-start(bf16[8,96,128]{2,1,0:T(8,128)(2,1)} %shard_map.121), calls=%async_computation.1 | async-start | bytes 393216 | tf_op jit(solution)/shard_map/all_to_all | solution.py:407
  79.4 0.0 copy-done.4
  79.4 0.7 collective-permute-start.17
  80.1 0.9 collective-permute-done.17.other_flow
  81.0 4.2 %all-to-all-done.1.attended = bf16[8,96,128]{2,1,0:T(8,128)(2,1)S(1)} async-done(((bf16[8,96,128]{2,1,0:T(8,128)(2,1)}), bf16[8,96,128]{2,1,0:T(8,128)(2,1)S(1)}, u32[]{:S(2)}, u32[]{:S(2)}) %all-to-all-start.1) | async-done | bytes 196640 | tf_op jit(solution)/shard_map/all_to_all | solution.py:407
  85.1 2.2 %copy-done.1 = bf16[1024,2048]{1,0:T(8,128)(2,1)S(1)} copy-done((bf16[1024,2048]{1,0:T(8,128)(2,1)S(1)}, bf16[1024,2048]{1,0:T(8,128)(2,1)}, u32[]{:S(2)}) %copy-start.1) | copy-done | bytes 4194328
  87.3 2.2 %copy-done.3 = bf16[2048,1024]{1,0:T(8,128)(2,1)S(1)} copy-done((bf16[2048,1024]{1,0:T(8,128)(2,1)S(1)}, bf16[2048,1024]{1,0:T(8,128)(2,1)}, u32[]{:S(2)}) %copy-start.3) | copy-done | bytes 4194328
  89.5 3.8 %shard_map.122 = (bf16[80,96]{1,0:T(8,128)(2,1)S(1)}, bf16[80,96]{1,0:T(8,128)(2,1)S(1)}) custom-call(s32[10]{0:T(128)S(1)} %stack.40.place.refs_0_, bf16[8,96,128]{2,1,0:T(8,128)(2,1)S(1)} %all-to-all-done.1.attended, bf16[96,1024]{1,0:T(8,128)(2,1)S(1)} %get-tuple-element.27.own, bf16[192,1024]{1,0:T(8,128)(2,1)S(1)} %collective-permute-done.other, ...), custom_call_target="tpu_custom_call" | custom-call | tf_op jit(solution)/shard_map/pallas_call | solution.py:410
  93.3 1.8 %collective-permute-start.18 = (bf16[80,96]{1,0:T(8,128)(2,1)S(1)}, bf16[80,96]{1,0:T(8,128)(2,1)S(1)}, u32[]{:S(2)}, u32[]{:S(2)}) collective-permute-start(bf16[80,96]{1,0:T(8,128)(2,1)S(1)} %get-tuple-element.51), channel_id=1, source_target_pairs={{0,64},{64,0},{1,65},{65,1},{2,66},{66,2},{3,67},{67,3},{4,68},{68... | collective-permute-start | bytes 46088 | tf_op jit(solution)/shard_map/ppermute | solution.py:417
  95.1 0.8 collective-permute-done.18.theirs
  96.0 0.7 shard_map.123
  96.7 0.7 collective-permute-start.19
  97.3 7.3 %collective-permute-done.19 = bf16[80,192]{1,0:T(8,128)(2,1)S(1)} collective-permute-done((bf16[80,192]{1,0:T(8,128)(2,1)S(1)}, bf16[80,192]{1,0:T(8,128)(2,1)S(1)}, u32[]{:S(2)}, u32[]{:S(2)}) %collective-permute-start.19) | collective-permute-done | bytes 30752 | tf_op jit(solution)/shard_map/ppermute | solution.py:427
  104.7 0.6 slice_add_fusion
  105.3 0.6 slice.12
  (4 shorter events, 0.0 us)
Async XLA Ops:
  0.6 6.0 %collective-permute-start = (bf16[192,1024]{1,0:T(8,128)(2,1)}, bf16[192,1024]{1,0:T(8,128)(2,1)S(1)}, u32[]{:S(2)}, u32[]{:S(2)}) collective-permute-start(bf16[192,1024]{1,0:T(8,128)(2,1)} %hidden.1), channel_id=1, source_target_pairs={{0,64},{64,0},{1,65},{65,1},{2,66},{66,2},{3,67},{67,3},{4,68},{68... | collective-permute-start | bytes 1179656 | tf_op jit(solution)/shard_map/ppermute | solution.py:340
  21.9 9.4 %collective-permute-start.2 = (bf16[768,128]{1,0:T(8,128)(2,1)S(1)}, bf16[768,128]{1,0:T(8,128)(2,1)S(1)}, u32[]{:S(2)}, u32[]{:S(2)}) collective-permute-start(bf16[768,128]{1,0:T(8,128)(2,1)S(1)} %get-tuple-element.32.refs_3_), channel_id=1, source_target_pairs={{0,1},{1,2},{2,3},{3,4},{4,5},{5,6},{6,7},{7,0},{8,9},{9,10},{10,1... | collective-permute-start | bytes 589832 | tf_op jit(solution)/shard_map/ppermute | solution.py:380
  23.6 7.7 %collective-permute-start.6 = (bf16[768,128]{1,0:T(8,128)(2,1)S(1)}, bf16[768,128]{1,0:T(8,128)(2,1)S(1)}, u32[]{:S(2)}, u32[]{:S(2)}) collective-permute-start(bf16[768,128]{1,0:T(8,128)(2,1)S(1)} %get-tuple-element.33.refs_4_), channel_id=1, source_target_pairs={{0,7},{1,0},{2,1},{3,2},{4,3},{5,4},{6,5},{7,6},{8,15},{9,8},{10,9... | collective-permute-start | bytes 589832 | tf_op jit(solution)/shard_map/ppermute | solution.py:381
  27.6 10.4 %collective-permute-start.10 = (bf16[768,128]{1,0:T(8,128)(2,1)S(1)}, bf16[768,128]{1,0:T(8,128)(2,1)S(1)}, u32[]{:S(2)}, u32[]{:S(2)}) collective-permute-start(bf16[768,128]{1,0:T(8,128)(2,1)S(1)} %get-tuple-element.33.refs_4_), channel_id=1, source_target_pairs={{0,1},{1,2},{2,3},{3,4},{4,5},{5,6},{6,7},{7,0},{8,9},{9,10},{10,1... | collective-permute-start | bytes 589832 | tf_op jit(solution)/shard_map/ppermute | solution.py:380
  27.6 10.4 %collective-permute-start.13 = (bf16[768,128]{1,0:T(8,128)(2,1)S(1)}, bf16[768,128]{1,0:T(8,128)(2,1)S(1)}, u32[]{:S(2)}, u32[]{:S(2)}) collective-permute-start(bf16[768,128]{1,0:T(8,128)(2,1)S(1)} %get-tuple-element.32.refs_3_), channel_id=1, source_target_pairs={{0,7},{1,0},{2,1},{3,2},{4,3},{5,4},{6,5},{7,6},{8,15},{9,8},{10,9... | collective-permute-start | bytes 589832 | tf_op jit(solution)/shard_map/ppermute | solution.py:381
  31.3 9.5 %collective-permute-start.3 = (bf16[768,128]{1,0:T(8,128)(2,1)S(1)}, bf16[768,128]{1,0:T(8,128)(2,1)S(1)}, u32[]{:S(2)}, u32[]{:S(2)}) collective-permute-start(bf16[768,128]{1,0:T(8,128)(2,1)S(1)} %collective-permute-done.2.refs_2_), channel_id=1, source_target_pairs={{0,1},{1,2},{2,3},{3,4},{4,5},{5,6},{6,7},{7,0},{8,9},{9,10},{10,1... | collective-permute-start | bytes 589832 | tf_op jit(solution)/shard_map/ppermute | solution.py:380
  31.3 9.5 %collective-permute-start.7 = (bf16[768,128]{1,0:T(8,128)(2,1)S(1)}, bf16[768,128]{1,0:T(8,128)(2,1)S(1)}, u32[]{:S(2)}, u32[]{:S(2)}) collective-permute-start(bf16[768,128]{1,0:T(8,128)(2,1)S(1)} %collective-permute-done.6.refs_5_), channel_id=1, source_target_pairs={{0,7},{1,0},{2,1},{3,2},{4,3},{5,4},{6,5},{7,6},{8,15},{9,8},{10,9... | collective-permute-start | bytes 589832 | tf_op jit(solution)/shard_map/ppermute | solution.py:381
  34.0 9.5 %collective-permute-start.1 = (bf16[8,96,128]{2,1,0:T(8,128)(2,1)S(1)}, bf16[8,96,128]{2,1,0:T(8,128)(2,1)S(1)}, u32[]{:S(2)}, u32[]{:S(2)}) collective-permute-start(bf16[8,96,128]{2,1,0:T(8,128)(2,1)S(1)} %get-tuple-element.31.refs_1_), channel_id=1, source_target_pairs={{0,64},{64,0},{1,65},{65,1},{2,66},{66,2},{3,67},{67,3},{4,68},{68... | collective-permute-start | bytes 589832 | tf_op jit(solution)/shard_map/ppermute | solution.py:370
  38.1 7.4 %collective-permute-start.11 = (bf16[768,128]{1,0:T(8,128)(2,1)S(1)}, bf16[768,128]{1,0:T(8,128)(2,1)S(1)}, u32[]{:S(2)}, u32[]{:S(2)}) collective-permute-start(bf16[768,128]{1,0:T(8,128)(2,1)S(1)} %collective-permute-done.10.refs_3_), channel_id=1, source_target_pairs={{0,1},{1,2},{2,3},{3,4},{4,5},{5,6},{6,7},{7,0},{8,9},{9,10},{10,1... | collective-permute-start | bytes 589832 | tf_op jit(solution)/shard_map/ppermute | solution.py:380
  38.1 7.5 %collective-permute-start.14 = (bf16[768,128]{1,0:T(8,128)(2,1)S(1)}, bf16[768,128]{1,0:T(8,128)(2,1)S(1)}, u32[]{:S(2)}, u32[]{:S(2)}) collective-permute-start(bf16[768,128]{1,0:T(8,128)(2,1)S(1)} %collective-permute-done.13.refs_4_), channel_id=1, source_target_pairs={{0,7},{1,0},{2,1},{3,2},{4,3},{5,4},{6,5},{7,6},{8,15},{9,8},{10,9... | collective-permute-start | bytes 589832 | tf_op jit(solution)/shard_map/ppermute | solution.py:381
  40.8 14.7 %collective-permute-start.4 = (bf16[768,128]{1,0:T(8,128)(2,1)S(1)}, bf16[768,128]{1,0:T(8,128)(2,1)S(1)}, u32[]{:S(2)}, u32[]{:S(2)}) collective-permute-start(bf16[768,128]{1,0:T(8,128)(2,1)S(1)} %collective-permute-done.3.refs_2_), channel_id=1, source_target_pairs={{0,1},{1,2},{2,3},{3,4},{4,5},{5,6},{6,7},{7,0},{8,9},{9,10},{10,1... | collective-permute-start | bytes 589832 | tf_op jit(solution)/shard_map/ppermute | solution.py:380
  40.8 14.7 %collective-permute-start.8 = (bf16[768,128]{1,0:T(8,128)(2,1)S(1)}, bf16[768,128]{1,0:T(8,128)(2,1)S(1)}, u32[]{:S(2)}, u32[]{:S(2)}) collective-permute-start(bf16[768,128]{1,0:T(8,128)(2,1)S(1)} %collective-permute-done.7.refs_5_), channel_id=1, source_target_pairs={{0,7},{1,0},{2,1},{3,2},{4,3},{5,4},{6,5},{7,6},{8,15},{9,8},{10,9... | collective-permute-start | bytes 589832 | tf_op jit(solution)/shard_map/ppermute | solution.py:381
  45.5 19.1 %collective-permute-start.12 = (bf16[768,128]{1,0:T(8,128)(2,1)S(1)}, bf16[768,128]{1,0:T(8,128)(2,1)S(1)}, u32[]{:S(2)}, u32[]{:S(2)}) collective-permute-start(bf16[768,128]{1,0:T(8,128)(2,1)S(1)} %collective-permute-done.11.refs_3_), channel_id=1, source_target_pairs={{0,1},{1,2},{2,3},{3,4},{4,5},{5,6},{6,7},{7,0},{8,9},{9,10},{10,1... | collective-permute-start | bytes 589832 | tf_op jit(solution)/shard_map/ppermute | solution.py:380
  45.6 19.0 %collective-permute-start.15 = (bf16[768,128]{1,0:T(8,128)(2,1)S(1)}, bf16[768,128]{1,0:T(8,128)(2,1)S(1)}, u32[]{:S(2)}, u32[]{:S(2)}) collective-permute-start(bf16[768,128]{1,0:T(8,128)(2,1)S(1)} %collective-permute-done.14.refs_4_), channel_id=1, source_target_pairs={{0,7},{1,0},{2,1},{3,2},{4,3},{5,4},{6,5},{7,6},{8,15},{9,8},{10,9... | collective-permute-start | bytes 589832 | tf_op jit(solution)/shard_map/ppermute | solution.py:381
  53.5 2.0 %copy-start = (bf16[1024,2048]{1,0:T(8,128)(2,1)}, bf16[1024,2048]{1,0:T(8,128)(2,1)S(1)}, u32[]{:S(2)}) copy-start(bf16[1024,2048]{1,0:T(8,128)(2,1)S(1)} %get-tuple-element.46.w_up) | copy-start | bytes 12582916
  55.4 12.2 %collective-permute-start.5 = (bf16[768,128]{1,0:T(8,128)(2,1)S(1)}, bf16[768,128]{1,0:T(8,128)(2,1)S(1)}, u32[]{:S(2)}, u32[]{:S(2)}) collective-permute-start(bf16[768,128]{1,0:T(8,128)(2,1)S(1)} %collective-permute-done.4.refs_2_), channel_id=1, source_target_pairs={{0,1},{1,2},{2,3},{3,4},{4,5},{5,6},{6,7},{7,0},{8,9},{9,10},{10,1... | collective-permute-start | bytes 589832 | tf_op jit(solution)/shard_map/ppermute | solution.py:395
  55.4 12.2 %collective-permute-start.9 = (bf16[768,128]{1,0:T(8,128)(2,1)S(1)}, bf16[768,128]{1,0:T(8,128)(2,1)S(1)}, u32[]{:S(2)}, u32[]{:S(2)}) collective-permute-start(bf16[768,128]{1,0:T(8,128)(2,1)S(1)} %collective-permute-done.8.refs_5_), channel_id=1, source_target_pairs={{0,7},{1,0},{2,1},{3,2},{4,3},{5,4},{6,5},{7,6},{8,15},{9,8},{10,9... | collective-permute-start | bytes 589832 | tf_op jit(solution)/shard_map/ppermute | solution.py:396
  62.6 2.0 %copy-start.2 = (bf16[2048,1024]{1,0:T(8,128)(2,1)}, bf16[2048,1024]{1,0:T(8,128)(2,1)S(1)}, u32[]{:S(2)}) copy-start(bf16[2048,1024]{1,0:T(8,128)(2,1)S(1)} %get-tuple-element.47.w_down) | copy-start | bytes 12582916
  64.6 14.8 %copy-start.4 = (bf16[64,192]{1,0:T(8,128)(2,1)S(1)}, bf16[64,192]{1,0:T(8,128)(2,1)}, u32[]{:S(2)}) copy-start(bf16[64,192]{1,0:T(8,128)(2,1)} %flow.1) | copy-start | bytes 73732
  70.0 5.0 %collective-permute-start.16 = (bf16[8,96,256]{2,1,0:T(8,128)(2,1)S(1)}, bf16[8,96,256]{2,1,0:T(8,128)(2,1)S(1)}, u32[]{:S(2)}, u32[]{:S(2)}) collective-permute-start(bf16[8,96,256]{2,1,0:T(8,128)(2,1)S(1)} %get-tuple-element.44), channel_id=1, source_target_pairs={{0,64},{64,0},{1,65},{65,1},{2,66},{66,2},{3,67},{67,3},{4,68},{68... | collective-permute-start | bytes 1179656 | tf_op jit(solution)/shard_map/ppermute | solution.py:399
  76.0 9.1 %all-to-all-start.1 = ((bf16[8,96,128]{2,1,0:T(8,128)(2,1)}), bf16[8,96,128]{2,1,0:T(8,128)(2,1)S(1)}, u32[]{:S(2)}, u32[]{:S(2)}) async-start(bf16[8,96,128]{2,1,0:T(8,128)(2,1)} %shard_map.121), calls=%async_computation.1 | async-start | bytes 393216 | tf_op jit(solution)/shard_map/all_to_all | solution.py:407
  79.4 1.5 %collective-permute-start.17 = (bf16[64,192]{1,0:T(8,128)(2,1)S(1)}, bf16[64,192]{1,0:T(8,128)(2,1)S(1)}, u32[]{:S(2)}, u32[]{:S(2)}) collective-permute-start(bf16[64,192]{1,0:T(8,128)(2,1)S(1)} %copy-done.4), channel_id=1, source_target_pairs={{0,64},{64,0},{1,65},{65,1},{2,66},{66,2},{3,67},{67,3},{4,68},{68... | collective-permute-start | bytes 73736 | tf_op jit(solution)/shard_map/ppermute | solution.py:341
  85.1 2.2 %copy-start.1 = (bf16[1024,2048]{1,0:T(8,128)(2,1)S(1)}, bf16[1024,2048]{1,0:T(8,128)(2,1)}, u32[]{:S(2)}) copy-start(bf16[1024,2048]{1,0:T(8,128)(2,1)} %copy-done) | copy-start | bytes 12582916
  87.3 2.2 %copy-start.3 = (bf16[2048,1024]{1,0:T(8,128)(2,1)S(1)}, bf16[2048,1024]{1,0:T(8,128)(2,1)}, u32[]{:S(2)}) copy-start(bf16[2048,1024]{1,0:T(8,128)(2,1)} %copy-done.2) | copy-start | bytes 12582916
  93.3 2.7 %collective-permute-start.18 = (bf16[80,96]{1,0:T(8,128)(2,1)S(1)}, bf16[80,96]{1,0:T(8,128)(2,1)S(1)}, u32[]{:S(2)}, u32[]{:S(2)}) collective-permute-start(bf16[80,96]{1,0:T(8,128)(2,1)S(1)} %get-tuple-element.51), channel_id=1, source_target_pairs={{0,64},{64,0},{1,65},{65,1},{2,66},{66,2},{3,67},{67,3},{4,68},{68... | collective-permute-start | bytes 46088 | tf_op jit(solution)/shard_map/ppermute | solution.py:417
  96.7 8.0 %collective-permute-start.19 = (bf16[80,192]{1,0:T(8,128)(2,1)S(1)}, bf16[80,192]{1,0:T(8,128)(2,1)S(1)}, u32[]{:S(2)}, u32[]{:S(2)}) collective-permute-start(bf16[80,192]{1,0:T(8,128)(2,1)S(1)} %shard_map.123), channel_id=1, source_target_pairs={{0,63},{1,62},{2,61},{3,60},{4,59},{5,58},{6,57},{7,56},{8,55},{9,... | collective-permute-start | bytes 92168 | tf_op jit(solution)/shard_map/ppermute | solution.py:427

commit v4 on v3

--- a/solution.py
+++ b/solution.py
@@ -114,7 +114,7 @@
     queries[...] = slots[:, :, :HEAD]
 
 
-def attend_kernel(parts, sources, first, last, load_count, *refs):
+def attend_kernel(parts, sources, first, last, after, *refs):
     refs = list(refs)
     place = refs.pop(0)
     if first:
@@ -124,12 +124,7 @@
     segments = [refs.pop(0) for _ in parts]
     if not first:
         top_in, numer_in = refs.pop(0), refs.pop(0)
-    loads = []
-    if load_count:
-        weights_in = [refs.pop(0) for _ in range(load_count)]
-        sems = refs.pop()
-        weights_out = [refs.pop() for _ in range(load_count)][::-1]
-        loads = start_loads(weights_in, weights_out, sems)
+    refs = refs[after:]
     if first:
         queries = refs.pop(0)
         for tile in range(TILES):
@@ -208,11 +203,9 @@
         following = score(tile + 1) if tile + 1 < TILES else None
         finish(tile, found)
         found = following
-    for load in loads:
-        load.wait()
-
-
-def attend(place, queries, segments, parts, sources, state, last, loads=()):
+
+
+def attend(place, queries, segments, parts, sources, state, last, after=()):
     first = state is None
     stats = [jax.ShapeDtypeStruct((8, 2 * ROWS), f32), jax.ShapeDtypeStruct((TALL, 2 * ROWS), f32)]
     if last:
@@ -221,19 +214,15 @@
         shapes = [jax.ShapeDtypeStruct((HEAD, 2 * ROWS), bf16), *stats]
     else:
         shapes = stats
-    operands = [place, *queries, *segments, *(state or ())]
-    in_specs = [smem()] + [vmem()] * (len(operands) - 1) + [hbm()] * len(loads)
-    shapes = list(shapes) + [pltpu.VMEM(load.shape, load.dtype) for load in loads]
-    operands += [in_hbm(load) for load in loads]
+    operands = [place, *queries, *segments, *(state or ()), *after]
     return pl.pallas_call(
-        functools.partial(attend_kernel, parts, sources, first, last, len(loads)),
+        functools.partial(attend_kernel, parts, sources, first, last, len(after)),
         out_shape=shapes,
-        in_specs=in_specs,
+        in_specs=[smem()] + [vmem()] * (len(operands) - 1),
         out_specs=[vmem()] * len(shapes),
-        scratch_shapes=[pltpu.SemaphoreType.DMA((4 * len(loads),))] if loads else [],
-        compiler_params=params(24),
+        compiler_params=params(16),
         cost_estimate=pl.CostEstimate(
-            flops=2 * 2 * 2 * ROWS * HALF * HEAD * len(parts),
+            flops=8 * 2 * 2 * ROWS * HALF * HEAD * len(parts),
             bytes_accessed=3_000_000,
             transcendentals=ROWS * HALF * len(parts),
         ),
@@ -373,8 +362,6 @@
     queries, *state = attend(
         place, (own_queries, other_queries), own_parts, (0, 1), (0, 0), None, False
     )
-    loads = {1: (w_output, w_up), 2: (w_down, w_shift, w_scale), 3: ()}
-    dense_weights = []
     for step in range(1, 4):
         for part in range(2):
             up[part] = lax.ppermute(up[part], "z", shift_by(Z, 1))
@@ -387,10 +374,8 @@
             (step, step, 5 + step, 5 + step),
             state,
             False,
-            loads[step],
+            (other_flow,) if step == 1 else (),
         )
-        dense_weights += state[2:]
-        state = state[:2]
     far = [
         lax.ppermute(up[0], "z", shift_by(Z, 1)),
         lax.ppermute(down[1], "z", shift_by(Z, -1)),
@@ -413,7 +398,19 @@
         in_specs=[smem()] + [vmem()] * 10,
         out_specs=[vmem()] * 2,
         compiler_params=params(16),
-    )(place, attended, own, other, flow_input, other_flow, *dense_weights)
+    )(
+        place,
+        attended,
+        own,
+        other,
+        flow_input,
+        other_flow,
+        w_output,
+        w_up,
+        w_down,
+        w_shift,
+        w_scale,
+    )
     received = lax.ppermute(sent_other, "core", other_core)
     block = pl.pallas_call(
         join_kernel,

time: 106 us -> 97.8 us (0.923)
  local copies, waits for them, and re-layouts: 9.06 us -> 0.75 us
  blocking collectives: 13.6 us -> 21.8 us
  Pallas kernels: 26.8 us -> 22.6 us
  starting transfers between devices: 39.5 us -> 36.5 us
    unnamed x10 -> x12, local copies, waits for them, and re-layouts: 8.34 us -> 0.04 us
    all_to_all x0 -> x1, blocking collectives: none -> 8.19 us  [on_device(): attended = lax.all_to_all(attended, ('xl', 'y'), 0, 0, tiled=True)]
    ppermute x6, waiting for transfers between devices: 1 us -> 8.41 us  [on_device(): up[part] = lax.ppermute(up[part], 'z', shift_by(Z, 1))]
    all_to_all x1 -> x0, waiting for transfers between devices: 4.16 us -> none  [on_device(): attended = lax.all_to_all(attended, ('xl', 'y'), 0, 0, tiled=True)]
    pallas_call x5, Pallas kernels: 17 us -> 13.5 us  [attend(): pl.pallas_call(functools.partial(attend_kernel, parts, sources, first, la...]
    all_to_all x1 -> x0, starting transfers between devices: 3.39 us -> none  [on_device(): attended = lax.all_to_all(attended, ('xl', 'y'), 0, 0, tiled=True)]
    ppermute x1, waiting for transfers between devices: 7.33 us -> 3.96 us  [on_device(): arrived = lax.ppermute(block, ('xl', 'y', 'z'), mirrored).astype(f32)]
    ppermute x1, starting transfers between devices: 0.66 us -> 3.9 us  [on_device(): arrived = lax.ppermute(block, ('xl', 'y', 'z'), mirrored).astype(f32)]
  transfers between devices with their start and end apart: 21 -> 20, of which waited for: 6 -> 5; matrix products, arithmetic and copies ran while one was open for 0% -> 0% of each run, Pallas kernels for 16% -> 14%
where the time goes in v4:
time: 97.8 us; the launch traced here: 97.6 us
  starting transfers between devices  36.5 us (37%)
  Pallas kernels  22.6 us (23%)
  blocking collectives  21.8 us (22%)
  waiting for transfers between devices  14.6 us (15%)
    ppermute x6, starting transfers between devices, on_device(): down[part] = lax.ppermute(down[part], 'z', shift_by(Z, -1))  19 us
    all_to_all x1, blocking collectives, on_device(): slots = lax.all_to_all(slots, ('xl', 'y'), 0, 0, tiled=True)  13.6 us
    pallas_call x5, Pallas kernels, attend(): pl.pallas_call(functools.partial(attend_kernel, parts, sources, first, la...  13.5 us
    ppermute x6, waiting for transfers between devices, on_device(): up[part] = lax.ppermute(up[part], 'z', shift_by(Z, 1))  8.41 us
    all_to_all x1, blocking collectives, on_device(): attended = lax.all_to_all(attended, ('xl', 'y'), 0, 0, tiled=True)  8.19 us
    ppermute x1, starting transfers between devices, on_device(): theirs = lax.ppermute(others, 'core', other_core)  4.05 us
    ppermute x1, waiting for transfers between devices, on_device(): arrived = lax.ppermute(block, ('xl', 'y', 'z'), mirrored).astype(f32)  3.96 us
    ppermute x1, starting transfers between devices, on_device(): arrived = lax.ppermute(block, ('xl', 'y', 'z'), mirrored).astype(f32)  3.9 us
  transfers between devices with their start and end apart: 20, of which 5 were waited for; matrix products, arithmetic and copies ran while one was open for 0% of the time, Pallas kernels for 14%

profile of v4, /device:TPU:1, one launch (start us, length us, event | category | flops | bytes accessed | tf_op | source)
XLA Modules:
  0.0 97.6 jit_solution(16851749517411768090)
XLA Ops:
  0.6 3.3 %collective-permute-start = (bf16[192,1024]{1,0:T(8,128)(2,1)}, bf16[192,1024]{1,0:T(8,128)(2,1)S(1)}, u32[]{:S(2)}, u32[]{:S(2)}) collective-permute-start(bf16[192,1024]{1,0:T(8,128)(2,1)} %hidden.1), channel_id=1, source_target_pairs={{0,64},{64,0},{1,65},{65,1},{2,66},{66,2},{3,67},{67,3},{4,68},{68... | collective-permute-start | bytes 1179656 | tf_op jit(solution)/shard_map/ppermute | solution.py:329
  4.0 0.1 stack.40.place.refs_0_
  4.0 2.5 %shard_map.113 = (bf16[96,1024]{1,0:T(8,128)(2,1)S(1)}, bf16[1024,512]{1,0:T(8,128)(2,1)S(1)}, bf16[1024,512]{1,0:T(8,128)(2,1)S(1)}, bf16[1024,512]{1,0:T(8,128)(2,1)S(1)}) custom-call(s32[10]{0:T(128)S(1)} %stack.40.place.refs_0_, bf16[192,1024]{1,0:T(8,128)(2,1)} %hidden.1, bf16[1024,512]{1,0:T(8,128)(2,1)} %w_query.1, bf16[1024,512]{1,0:T(8,128)(2,1)} %w_key.1, ...), custom_call_target="tpu_custom_call" | custom-call | bytes 6600000 | tf_op jit(solution)/shard_map/pallas_call | solution.py:333
  6.6 0.0 collective-permute-done.other
  6.6 1.6 %shard_map.114 = bf16[8,96,384]{2,1,0:T(8,128)(2,1)S(1)} custom-call(s32[10]{0:T(128)S(1)} %stack.40.place.refs_0_, bf16[96,1024]{1,0:T(8,128)(2,1)S(1)} %get-tuple-element.22.own, bf16[192,1024]{1,0:T(8,128)(2,1)S(1)} %collective-permute-done.other, bf16[1024,512]{1,0:T(8,128)(2,1)S(1)} %get-tuple-element.23.w_query, ...), custom_call_target="tpu_custom_call" | custom-call | tf_op jit(solution)/shard_map/pallas_call | solution.py:342
  8.2 13.6 %all_to_all.10.slots = bf16[8,96,384]{2,1,0:T(8,128)(2,1)S(1)} all-to-all(bf16[8,96,384]{2,1,0:T(8,128)(2,1)S(1)} %shard_map.114), channel_id=1, replica_groups=mesh['xh'=2,'core'=2,'xl'=2,'y'=4,'z'=8] {'xl','y'}, dimensions={0} | all-to-all | bytes 1179648 | tf_op jit(solution)/shard_map/all_to_all | solution.py:350
  21.7 0.1 shard_map.115
  21.9 1.5 %collective-permute-start.1 = (bf16[8,96,128]{2,1,0:T(8,128)(2,1)S(1)}, bf16[8,96,128]{2,1,0:T(8,128)(2,1)S(1)}, u32[]{:S(2)}, u32[]{:S(2)}) collective-permute-start(bf16[8,96,128]{2,1,0:T(8,128)(2,1)S(1)} %get-tuple-element.26.refs_1_), channel_id=1, source_target_pairs={{0,64},{64,0},{1,65},{65,1},{2,66},{66,2},{3,67},{67,3},{4,68},{68... | collective-permute-start | bytes 589832 | tf_op jit(solution)/shard_map/ppermute | solution.py:359
  23.4 0.0 copy-done.5
  23.4 0.1 collective-permute-start.16
  23.5 5.6 %collective-permute-start.13 = (bf16[768,128]{1,0:T(8,128)(2,1)S(1)}, bf16[768,128]{1,0:T(8,128)(2,1)S(1)}, u32[]{:S(2)}, u32[]{:S(2)}) collective-permute-start(bf16[768,128]{1,0:T(8,128)(2,1)S(1)} %get-tuple-element.27.refs_3_), channel_id=1, source_target_pairs={{0,7},{1,0},{2,1},{3,2},{4,3},{5,4},{6,5},{7,6},{8,15},{9,8},{10,9... | collective-permute-start | bytes 589832 | tf_op jit(solution)/shard_map/ppermute | solution.py:368
  29.1 0.0 collective-permute-start.2
  29.1 0.0 collective-permute-start.10
  29.1 0.0 collective-permute-done.1.refs_2_
  29.1 2.7 %collective-permute-start.6 = (bf16[768,128]{1,0:T(8,128)(2,1)S(1)}, bf16[768,128]{1,0:T(8,128)(2,1)S(1)}, u32[]{:S(2)}, u32[]{:S(2)}) collective-permute-start(bf16[768,128]{1,0:T(8,128)(2,1)S(1)} %get-tuple-element.28.refs_4_), channel_id=1, source_target_pairs={{0,7},{1,0},{2,1},{3,2},{4,3},{5,4},{6,5},{7,6},{8,15},{9,8},{10,9... | collective-permute-start | bytes 589832 | tf_op jit(solution)/shard_map/ppermute | solution.py:368
  31.8 2.1 %shard_map.116 = (bf16[128,1536]{1,0:T(8,128)(2,1)S(1)}, f32[8,1536]{1,0:T(8,128)S(1)}, f32[144,1536]{1,0:T(8,128)S(1)}) custom-call(s32[10]{0:T(128)S(1)} %stack.40.place.refs_0_, bf16[8,96,128]{2,1,0:T(8,128)(2,1)S(1)} %get-tuple-element.26.refs_1_, bf16[8,96,128]{2,1,0:T(8,128)(2,1)S(1)} %collective-permute-done.1.refs_2_, ...), custom_call_target="tpu_custom_call" | custom-call | flops 2415919104 | bytes 3000000 | tf_op jit(solution)/shard_map/pallas_call | solution.py:218
  33.9 6.4 %collective-permute-done.10.refs_3_ = bf16[768,128]{1,0:T(8,128)(2,1)S(1)} collective-permute-done((bf16[768,128]{1,0:T(8,128)(2,1)S(1)}, bf16[768,128]{1,0:T(8,128)(2,1)S(1)}, u32[]{:S(2)}, u32[]{:S(2)}) %collective-permute-start.10) | collective-permute-done | bytes 196640 | tf_op jit(solution)/shard_map/ppermute | solution.py:367
  40.3 0.0 collective-permute-start.11
  40.3 0.0 collective-permute-done.13.refs_4_
  40.3 2.7 %collective-permute-start.14 = (bf16[768,128]{1,0:T(8,128)(2,1)S(1)}, bf16[768,128]{1,0:T(8,128)(2,1)S(1)}, u32[]{:S(2)}, u32[]{:S(2)}) collective-permute-start(bf16[768,128]{1,0:T(8,128)(2,1)S(1)} %collective-permute-done.13.refs_4_), channel_id=1, source_target_pairs={{0,7},{1,0},{2,1},{3,2},{4,3},{5,4},{6,5},{7,6},{8,15},{9,8},{10,9... | collective-permute-start | bytes 589832 | tf_op jit(solution)/shard_map/ppermute | solution.py:368
  43.0 0.0 collective-permute-done.2.refs_2_
  43.0 0.0 collective-permute-start.3
  43.0 0.0 collective-permute-done.6.refs_5_
  43.0 2.7 %collective-permute-start.7 = (bf16[768,128]{1,0:T(8,128)(2,1)S(1)}, bf16[768,128]{1,0:T(8,128)(2,1)S(1)}, u32[]{:S(2)}, u32[]{:S(2)}) collective-permute-start(bf16[768,128]{1,0:T(8,128)(2,1)S(1)} %collective-permute-done.6.refs_5_), channel_id=1, source_target_pairs={{0,7},{1,0},{2,1},{3,2},{4,3},{5,4},{6,5},{7,6},{8,15},{9,8},{10,9... | collective-permute-start | bytes 589832 | tf_op jit(solution)/shard_map/ppermute | solution.py:368
  45.7 0.0 collective-permute-done.16.refs_8_.other_flow
  45.7 3.1 %shard_map.117 = (f32[8,1536]{1,0:T(8,128)S(1)}, f32[144,1536]{1,0:T(8,128)S(1)}) custom-call(s32[10]{0:T(128)S(1)} %stack.40.place.refs_0_, bf16[128,1536]{1,0:T(8,128)(2,1)S(1)} %get-tuple-element.29.refs_1_, bf16[768,128]{1,0:T(8,128)(2,1)S(1)} %collective-permute-done.2.refs_2_, bf16[768,128]{1,0:T(8,128)(2,1)S(1)} %collective-permute-done.10.refs_3_, ...), custom_call_target="tpu_custom_call" | custom-call | flops 4831838208 | bytes 3000000 | tf_op jit(solution)/shard_map/pallas_call | solution.py:218
  48.7 0.0 collective-permute-done.11.refs_3_
  48.7 0.1 collective-permute-start.12
  48.8 0.0 collective-permute-done.14.refs_4_
  48.8 2.7 %collective-permute-start.15 = (bf16[768,128]{1,0:T(8,128)(2,1)S(1)}, bf16[768,128]{1,0:T(8,128)(2,1)S(1)}, u32[]{:S(2)}, u32[]{:S(2)}) collective-permute-start(bf16[768,128]{1,0:T(8,128)(2,1)S(1)} %collective-permute-done.14.refs_4_), channel_id=1, source_target_pairs={{0,7},{1,0},{2,1},{3,2},{4,3},{5,4},{6,5},{7,6},{8,15},{9,8},{10,9... | collective-permute-start | bytes 589832 | tf_op jit(solution)/shard_map/ppermute | solution.py:368
  51.5 0.0 collective-permute-done.3.refs_2_
  51.5 0.0 collective-permute-start.4
  51.5 0.0 collective-permute-done.7.refs_5_
  51.5 2.7 %collective-permute-start.8 = (bf16[768,128]{1,0:T(8,128)(2,1)S(1)}, bf16[768,128]{1,0:T(8,128)(2,1)S(1)}, u32[]{:S(2)}, u32[]{:S(2)}) collective-permute-start(bf16[768,128]{1,0:T(8,128)(2,1)S(1)} %collective-permute-done.7.refs_5_), channel_id=1, source_target_pairs={{0,7},{1,0},{2,1},{3,2},{4,3},{5,4},{6,5},{7,6},{8,15},{9,8},{10,9... | collective-permute-start | bytes 589832 | tf_op jit(solution)/shard_map/ppermute | solution.py:368
  54.2 3.1 %shard_map.118 = (f32[8,1536]{1,0:T(8,128)S(1)}, f32[144,1536]{1,0:T(8,128)S(1)}) custom-call(s32[10]{0:T(128)S(1)} %stack.40.place.refs_0_, bf16[128,1536]{1,0:T(8,128)(2,1)S(1)} %get-tuple-element.29.refs_1_, bf16[768,128]{1,0:T(8,128)(2,1)S(1)} %collective-permute-done.3.refs_2_, bf16[768,128]{1,0:T(8,128)(2,1)S(1)} %collective-permute-done.11.refs_3_, ...), custom_call_target="tpu_custom_call" | custom-call | flops 4831838208 | bytes 3000000 | tf_op jit(solution)/shard_map/pallas_call | solution.py:218
  57.2 2.0 %collective-permute-done.4.refs_2_ = bf16[768,128]{1,0:T(8,128)(2,1)S(1)} collective-permute-done((bf16[768,128]{1,0:T(8,128)(2,1)S(1)}, bf16[768,128]{1,0:T(8,128)(2,1)S(1)}, u32[]{:S(2)}, u32[]{:S(2)}) %collective-permute-start.4) | collective-permute-done | bytes 196640 | tf_op jit(solution)/shard_map/ppermute | solution.py:367
  59.3 0.0 collective-permute-start.5
  59.3 0.0 collective-permute-done.8.refs_5_
  59.3 2.7 %collective-permute-start.9 = (bf16[768,128]{1,0:T(8,128)(2,1)S(1)}, bf16[768,128]{1,0:T(8,128)(2,1)S(1)}, u32[]{:S(2)}, u32[]{:S(2)}) collective-permute-start(bf16[768,128]{1,0:T(8,128)(2,1)S(1)} %collective-permute-done.8.refs_5_), channel_id=1, source_target_pairs={{0,7},{1,0},{2,1},{3,2},{4,3},{5,4},{6,5},{7,6},{8,15},{9,8},{10,9... | collective-permute-start | bytes 589832 | tf_op jit(solution)/shard_map/ppermute | solution.py:381
  61.9 0.0 collective-permute-done.12.refs_3_
  61.9 0.0 collective-permute-done.15.refs_4_
  61.9 3.0 %shard_map.119 = (f32[8,1536]{1,0:T(8,128)S(1)}, f32[144,1536]{1,0:T(8,128)S(1)}) custom-call(s32[10]{0:T(128)S(1)} %stack.40.place.refs_0_, bf16[128,1536]{1,0:T(8,128)(2,1)S(1)} %get-tuple-element.29.refs_1_, bf16[768,128]{1,0:T(8,128)(2,1)S(1)} %collective-permute-done.4.refs_2_, bf16[768,128]{1,0:T(8,128)(2,1)S(1)} %collective-permute-done.12.refs_3_, ...), custom_call_target="tpu_custom_call" | custom-call | flops 4831838208 | bytes 3000000 | tf_op jit(solution)/shard_map/pallas_call | solution.py:218
  65.0 0.0 collective-permute-done.5.refs_2_
  65.0 0.0 collective-permute-done.9.refs_3_
  65.0 0.0 copy-start
  65.0 0.0 copy-start.1
  65.0 0.0 copy-start.2
  65.1 0.0 copy-start.3
  65.1 0.0 copy-start.4
  65.1 2.3 %shard_map.120 = (bf16[8,96,256]{2,1,0:T(8,128)(2,1)S(1)}, bf16[8,96,256]{2,1,0:T(8,128)(2,1)S(1)}) custom-call(s32[10]{0:T(128)S(1)} %stack.40.place.refs_0_, bf16[128,1536]{1,0:T(8,128)(2,1)S(1)} %get-tuple-element.29.refs_1_, bf16[768,128]{1,0:T(8,128)(2,1)S(1)} %collective-permute-done.5.refs_2_, bf16[768,128]{1,0:T(8,128)(2,1)S(1)} %collective-permute-done.9.refs_3_, ...), custom_call_target="tpu_custom_call" | custom-call | flops 2415919104 | bytes 3000000 | tf_op jit(solution)/shard_map/pallas_call | solution.py:218
  67.4 4.1 %collective-permute-start.17 = (bf16[8,96,256]{2,1,0:T(8,128)(2,1)S(1)}, bf16[8,96,256]{2,1,0:T(8,128)(2,1)S(1)}, u32[]{:S(2)}, u32[]{:S(2)}) collective-permute-start(bf16[8,96,256]{2,1,0:T(8,128)(2,1)S(1)} %get-tuple-element.39), channel_id=1, source_target_pairs={{0,64},{64,0},{1,65},{65,1},{2,66},{66,2},{3,67},{67,3},{4,68},{68... | collective-permute-start | bytes 1179656 | tf_op jit(solution)/shard_map/ppermute | solution.py:384
  71.5 1.3 %collective-permute-done.17.theirs = bf16[8,96,256]{2,1,0:T(8,128)(2,1)S(1)} collective-permute-done((bf16[8,96,256]{2,1,0:T(8,128)(2,1)S(1)}, bf16[8,96,256]{2,1,0:T(8,128)(2,1)S(1)}, u32[]{:S(2)}, u32[]{:S(2)}) %collective-permute-start.17) | collective-permute-done | bytes 393248 | tf_op jit(solution)/shard_map/ppermute | solution.py:384
  72.8 0.3 shard_map.121
  73.1 8.2 %all_to_all.11.attended = bf16[8,96,128]{2,1,0:T(8,128)(2,1)S(1)} all-to-all(bf16[8,96,128]{2,1,0:T(8,128)(2,1)S(1)} %shard_map.121), channel_id=1, replica_groups=mesh['xh'=2,'core'=2,'xl'=2,'y'=4,'z'=8] {'xl','y'}, dimensions={0} | all-to-all | bytes 393216 | tf_op jit(solution)/shard_map/all_to_all | solution.py:392
  81.3 0.0 copy-done
  81.3 0.0 copy-done.1
  81.4 3.8 %shard_map.122 = (bf16[80,96]{1,0:T(8,128)(2,1)S(1)}, bf16[80,96]{1,0:T(8,128)(2,1)S(1)}) custom-call(s32[10]{0:T(128)S(1)} %stack.40.place.refs_0_, bf16[8,96,128]{2,1,0:T(8,128)(2,1)S(1)} %all_to_all.11.attended, bf16[96,1024]{1,0:T(8,128)(2,1)S(1)} %get-tuple-element.22.own, bf16[192,1024]{1,0:T(8,128)(2,1)S(1)} %collective-permute-done.other, ...), custom_call_target="tpu_custom_call" | custom-call | tf_op jit(solution)/shard_map/pallas_call | solution.py:395
  85.2 1.8 %collective-permute-start.18 = (bf16[80,96]{1,0:T(8,128)(2,1)S(1)}, bf16[80,96]{1,0:T(8,128)(2,1)S(1)}, u32[]{:S(2)}, u32[]{:S(2)}) collective-permute-start(bf16[80,96]{1,0:T(8,128)(2,1)S(1)} %get-tuple-element.41), channel_id=1, source_target_pairs={{0,64},{64,0},{1,65},{65,1},{2,66},{66,2},{3,67},{67,3},{4,68},{68... | collective-permute-start | bytes 46088 | tf_op jit(solution)/shard_map/ppermute | solution.py:414
  87.0 0.8 collective-permute-done.18.theirs
  87.8 0.7 shard_map.123
  88.5 3.9 %collective-permute-start.19 = (bf16[80,192]{1,0:T(8,128)(2,1)S(1)}, bf16[80,192]{1,0:T(8,128)(2,1)S(1)}, u32[]{:S(2)}, u32[]{:S(2)}) collective-permute-start(bf16[80,192]{1,0:T(8,128)(2,1)S(1)} %shard_map.123), channel_id=1, source_target_pairs={{0,63},{1,62},{2,61},{3,60},{4,59},{5,58},{6,57},{7,56},{8,55},{9,... | collective-permute-start | bytes 92168 | tf_op jit(solution)/shard_map/ppermute | solution.py:424
  92.4 4.0 %collective-permute-done.19 = bf16[80,192]{1,0:T(8,128)(2,1)S(1)} collective-permute-done((bf16[80,192]{1,0:T(8,128)(2,1)S(1)}, bf16[80,192]{1,0:T(8,128)(2,1)S(1)}, u32[]{:S(2)}, u32[]{:S(2)}) %collective-permute-start.19) | collective-permute-done | bytes 30752 | tf_op jit(solution)/shard_map/ppermute | solution.py:424
  96.4 0.6 slice_add_fusion
  97.0 0.6 slice.12
  (5 shorter events, 0.0 us)
Async XLA Ops:
  0.6 6.0 %collective-permute-start = (bf16[192,1024]{1,0:T(8,128)(2,1)}, bf16[192,1024]{1,0:T(8,128)(2,1)S(1)}, u32[]{:S(2)}, u32[]{:S(2)}) collective-permute-start(bf16[192,1024]{1,0:T(8,128)(2,1)} %hidden.1), channel_id=1, source_target_pairs={{0,64},{64,0},{1,65},{65,1},{2,66},{66,2},{3,67},{67,3},{4,68},{68... | collective-permute-start | bytes 1179656 | tf_op jit(solution)/shard_map/ppermute | solution.py:329
  4.0 19.4 %copy-start.5 = (bf16[64,192]{1,0:T(8,128)(2,1)S(1)}, bf16[64,192]{1,0:T(8,128)(2,1)}, u32[]{:S(2)}) copy-start(bf16[64,192]{1,0:T(8,128)(2,1)} %flow.1) | copy-start | bytes 73732
  21.9 7.2 %collective-permute-start.1 = (bf16[8,96,128]{2,1,0:T(8,128)(2,1)S(1)}, bf16[8,96,128]{2,1,0:T(8,128)(2,1)S(1)}, u32[]{:S(2)}, u32[]{:S(2)}) collective-permute-start(bf16[8,96,128]{2,1,0:T(8,128)(2,1)S(1)} %get-tuple-element.26.refs_1_), channel_id=1, source_target_pairs={{0,64},{64,0},{1,65},{65,1},{2,66},{66,2},{3,67},{67,3},{4,68},{68... | collective-permute-start | bytes 589832 | tf_op jit(solution)/shard_map/ppermute | solution.py:359
  23.4 22.2 %collective-permute-start.16 = (bf16[64,192]{1,0:T(8,128)(2,1)S(1)}, bf16[64,192]{1,0:T(8,128)(2,1)S(1)}, u32[]{:S(2)}, u32[]{:S(2)}) collective-permute-start(bf16[64,192]{1,0:T(8,128)(2,1)S(1)} %copy-done.5), channel_id=1, source_target_pairs={{0,64},{64,0},{1,65},{65,1},{2,66},{66,2},{3,67},{67,3},{4,68},{68... | collective-permute-start | bytes 73736 | tf_op jit(solution)/shard_map/ppermute | solution.py:330
  23.5 16.8 %collective-permute-start.13 = (bf16[768,128]{1,0:T(8,128)(2,1)S(1)}, bf16[768,128]{1,0:T(8,128)(2,1)S(1)}, u32[]{:S(2)}, u32[]{:S(2)}) collective-permute-start(bf16[768,128]{1,0:T(8,128)(2,1)S(1)} %get-tuple-element.27.refs_3_), channel_id=1, source_target_pairs={{0,7},{1,0},{2,1},{3,2},{4,3},{5,4},{6,5},{7,6},{8,15},{9,8},{10,9... | collective-permute-start | bytes 589832 | tf_op jit(solution)/shard_map/ppermute | solution.py:368
  29.1 13.9 %collective-permute-start.2 = (bf16[768,128]{1,0:T(8,128)(2,1)S(1)}, bf16[768,128]{1,0:T(8,128)(2,1)S(1)}, u32[]{:S(2)}, u32[]{:S(2)}) collective-permute-start(bf16[768,128]{1,0:T(8,128)(2,1)S(1)} %get-tuple-element.27.refs_3_), channel_id=1, source_target_pairs={{0,1},{1,2},{2,3},{3,4},{4,5},{5,6},{6,7},{7,0},{8,9},{9,10},{10,1... | collective-permute-start | bytes 589832 | tf_op jit(solution)/shard_map/ppermute | solution.py:367
  29.1 11.2 %collective-permute-start.10 = (bf16[768,128]{1,0:T(8,128)(2,1)S(1)}, bf16[768,128]{1,0:T(8,128)(2,1)S(1)}, u32[]{:S(2)}, u32[]{:S(2)}) collective-permute-start(bf16[768,128]{1,0:T(8,128)(2,1)S(1)} %get-tuple-element.28.refs_4_), channel_id=1, source_target_pairs={{0,1},{1,2},{2,3},{3,4},{4,5},{5,6},{6,7},{7,0},{8,9},{9,10},{10,1... | collective-permute-start | bytes 589832 | tf_op jit(solution)/shard_map/ppermute | solution.py:367
  29.1 13.9 %collective-permute-start.6 = (bf16[768,128]{1,0:T(8,128)(2,1)S(1)}, bf16[768,128]{1,0:T(8,128)(2,1)S(1)}, u32[]{:S(2)}, u32[]{:S(2)}) collective-permute-start(bf16[768,128]{1,0:T(8,128)(2,1)S(1)} %get-tuple-element.28.refs_4_), channel_id=1, source_target_pairs={{0,7},{1,0},{2,1},{3,2},{4,3},{5,4},{6,5},{7,6},{8,15},{9,8},{10,9... | collective-permute-start | bytes 589832 | tf_op jit(solution)/shard_map/ppermute | solution.py:368
  40.3 8.4 %collective-permute-start.11 = (bf16[768,128]{1,0:T(8,128)(2,1)S(1)}, bf16[768,128]{1,0:T(8,128)(2,1)S(1)}, u32[]{:S(2)}, u32[]{:S(2)}) collective-permute-start(bf16[768,128]{1,0:T(8,128)(2,1)S(1)} %collective-permute-done.10.refs_3_), channel_id=1, source_target_pairs={{0,1},{1,2},{2,3},{3,4},{4,5},{5,6},{6,7},{7,0},{8,9},{9,10},{10,1... | collective-permute-start | bytes 589832 | tf_op jit(solution)/shard_map/ppermute | solution.py:367
  40.3 8.5 %collective-permute-start.14 = (bf16[768,128]{1,0:T(8,128)(2,1)S(1)}, bf16[768,128]{1,0:T(8,128)(2,1)S(1)}, u32[]{:S(2)}, u32[]{:S(2)}) collective-permute-start(bf16[768,128]{1,0:T(8,128)(2,1)S(1)} %collective-permute-done.13.refs_4_), channel_id=1, source_target_pairs={{0,7},{1,0},{2,1},{3,2},{4,3},{5,4},{6,5},{7,6},{8,15},{9,8},{10,9... | collective-permute-start | bytes 589832 | tf_op jit(solution)/shard_map/ppermute | solution.py:368
  43.0 8.5 %collective-permute-start.3 = (bf16[768,128]{1,0:T(8,128)(2,1)S(1)}, bf16[768,128]{1,0:T(8,128)(2,1)S(1)}, u32[]{:S(2)}, u32[]{:S(2)}) collective-permute-start(bf16[768,128]{1,0:T(8,128)(2,1)S(1)} %collective-permute-done.2.refs_2_), channel_id=1, source_target_pairs={{0,1},{1,2},{2,3},{3,4},{4,5},{5,6},{6,7},{7,0},{8,9},{9,10},{10,1... | collective-permute-start | bytes 589832 | tf_op jit(solution)/shard_map/ppermute | solution.py:367
  43.0 8.5 %collective-permute-start.7 = (bf16[768,128]{1,0:T(8,128)(2,1)S(1)}, bf16[768,128]{1,0:T(8,128)(2,1)S(1)}, u32[]{:S(2)}, u32[]{:S(2)}) collective-permute-start(bf16[768,128]{1,0:T(8,128)(2,1)S(1)} %collective-permute-done.6.refs_5_), channel_id=1, source_target_pairs={{0,7},{1,0},{2,1},{3,2},{4,3},{5,4},{6,5},{7,6},{8,15},{9,8},{10,9... | collective-permute-start | bytes 589832 | tf_op jit(solution)/shard_map/ppermute | solution.py:368
  48.7 13.2 %collective-permute-start.12 = (bf16[768,128]{1,0:T(8,128)(2,1)S(1)}, bf16[768,128]{1,0:T(8,128)(2,1)S(1)}, u32[]{:S(2)}, u32[]{:S(2)}) collective-permute-start(bf16[768,128]{1,0:T(8,128)(2,1)S(1)} %collective-permute-done.11.refs_3_), channel_id=1, source_target_pairs={{0,1},{1,2},{2,3},{3,4},{4,5},{5,6},{6,7},{7,0},{8,9},{9,10},{10,1... | collective-permute-start | bytes 589832 | tf_op jit(solution)/shard_map/ppermute | solution.py:367
  48.8 13.1 %collective-permute-start.15 = (bf16[768,128]{1,0:T(8,128)(2,1)S(1)}, bf16[768,128]{1,0:T(8,128)(2,1)S(1)}, u32[]{:S(2)}, u32[]{:S(2)}) collective-permute-start(bf16[768,128]{1,0:T(8,128)(2,1)S(1)} %collective-permute-done.14.refs_4_), channel_id=1, source_target_pairs={{0,7},{1,0},{2,1},{3,2},{4,3},{5,4},{6,5},{7,6},{8,15},{9,8},{10,9... | collective-permute-start | bytes 589832 | tf_op jit(solution)/shard_map/ppermute | solution.py:368
  51.5 7.8 %collective-permute-start.4 = (bf16[768,128]{1,0:T(8,128)(2,1)S(1)}, bf16[768,128]{1,0:T(8,128)(2,1)S(1)}, u32[]{:S(2)}, u32[]{:S(2)}) collective-permute-start(bf16[768,128]{1,0:T(8,128)(2,1)S(1)} %collective-permute-done.3.refs_2_), channel_id=1, source_target_pairs={{0,1},{1,2},{2,3},{3,4},{4,5},{5,6},{6,7},{7,0},{8,9},{9,10},{10,1... | collective-permute-start | bytes 589832 | tf_op jit(solution)/shard_map/ppermute | solution.py:367
  51.5 7.8 %collective-permute-start.8 = (bf16[768,128]{1,0:T(8,128)(2,1)S(1)}, bf16[768,128]{1,0:T(8,128)(2,1)S(1)}, u32[]{:S(2)}, u32[]{:S(2)}) collective-permute-start(bf16[768,128]{1,0:T(8,128)(2,1)S(1)} %collective-permute-done.7.refs_5_), channel_id=1, source_target_pairs={{0,7},{1,0},{2,1},{3,2},{4,3},{5,4},{6,5},{7,6},{8,15},{9,8},{10,9... | collective-permute-start | bytes 589832 | tf_op jit(solution)/shard_map/ppermute | solution.py:368
  59.3 5.7 %collective-permute-start.5 = (bf16[768,128]{1,0:T(8,128)(2,1)S(1)}, bf16[768,128]{1,0:T(8,128)(2,1)S(1)}, u32[]{:S(2)}, u32[]{:S(2)}) collective-permute-start(bf16[768,128]{1,0:T(8,128)(2,1)S(1)} %collective-permute-done.4.refs_2_), channel_id=1, source_target_pairs={{0,1},{1,2},{2,3},{3,4},{4,5},{5,6},{6,7},{7,0},{8,9},{9,10},{10,1... | collective-permute-start | bytes 589832 | tf_op jit(solution)/shard_map/ppermute | solution.py:380
  59.3 5.8 %collective-permute-start.9 = (bf16[768,128]{1,0:T(8,128)(2,1)S(1)}, bf16[768,128]{1,0:T(8,128)(2,1)S(1)}, u32[]{:S(2)}, u32[]{:S(2)}) collective-permute-start(bf16[768,128]{1,0:T(8,128)(2,1)S(1)} %collective-permute-done.8.refs_5_), channel_id=1, source_target_pairs={{0,7},{1,0},{2,1},{3,2},{4,3},{5,4},{6,5},{7,6},{8,15},{9,8},{10,9... | collective-permute-start | bytes 589832 | tf_op jit(solution)/shard_map/ppermute | solution.py:381
  65.0 16.3 %copy-start = (bf16[1024,2048]{1,0:T(8,128)(2,1)S(1)}, bf16[1024,2048]{1,0:T(8,128)(2,1)}, u32[]{:S(2)}) copy-start(bf16[1024,2048]{1,0:T(8,128)(2,1)} %w_up.1) | copy-start | bytes 12582916
  65.0 16.3 %copy-start.1 = (bf16[2048,1024]{1,0:T(8,128)(2,1)S(1)}, bf16[2048,1024]{1,0:T(8,128)(2,1)}, u32[]{:S(2)}) copy-start(bf16[2048,1024]{1,0:T(8,128)(2,1)} %w_down.1) | copy-start | bytes 12582916
  65.0 16.3 %copy-start.2 = (bf16[512,1024]{1,0:T(8,128)(2,1)S(1)}, bf16[512,1024]{1,0:T(8,128)(2,1)}, u32[]{:S(2)}) copy-start(bf16[512,1024]{1,0:T(8,128)(2,1)} %w_output.1) | copy-start | bytes 3145732
  65.1 16.3 %copy-start.3 = (bf16[64,1024]{1,0:T(8,128)(2,1)S(1)}, bf16[64,1024]{1,0:T(8,128)(2,1)}, u32[]{:S(2)}) copy-start(bf16[64,1024]{1,0:T(8,128)(2,1)} %w_shift.1) | copy-start | bytes 393220
  65.1 16.3 %copy-start.4 = (bf16[64,1024]{1,0:T(8,128)(2,1)S(1)}, bf16[64,1024]{1,0:T(8,128)(2,1)}, u32[]{:S(2)}) copy-start(bf16[64,1024]{1,0:T(8,128)(2,1)} %w_scale.1) | copy-start | bytes 393220
  67.4 5.4 %collective-permute-start.17 = (bf16[8,96,256]{2,1,0:T(8,128)(2,1)S(1)}, bf16[8,96,256]{2,1,0:T(8,128)(2,1)S(1)}, u32[]{:S(2)}, u32[]{:S(2)}) collective-permute-start(bf16[8,96,256]{2,1,0:T(8,128)(2,1)S(1)} %get-tuple-element.39), channel_id=1, source_target_pairs={{0,64},{64,0},{1,65},{65,1},{2,66},{66,2},{3,67},{67,3},{4,68},{68... | collective-permute-start | bytes 1179656 | tf_op jit(solution)/shard_map/ppermute | solution.py:384
  85.2 2.7 %collective-permute-start.18 = (bf16[80,96]{1,0:T(8,128)(2,1)S(1)}, bf16[80,96]{1,0:T(8,128)(2,1)S(1)}, u32[]{:S(2)}, u32[]{:S(2)}) collective-permute-start(bf16[80,96]{1,0:T(8,128)(2,1)S(1)} %get-tuple-element.41), channel_id=1, source_target_pairs={{0,64},{64,0},{1,65},{65,1},{2,66},{66,2},{3,67},{67,3},{4,68},{68... | collective-permute-start | bytes 46088 | tf_op jit(solution)/shard_map/ppermute | solution.py:414
  88.5 7.9 %collective-permute-start.19 = (bf16[80,192]{1,0:T(8,128)(2,1)S(1)}, bf16[80,192]{1,0:T(8,128)(2,1)S(1)}, u32[]{:S(2)}, u32[]{:S(2)}) collective-permute-start(bf16[80,192]{1,0:T(8,128)(2,1)S(1)} %shard_map.123), channel_id=1, source_target_pairs={{0,63},{1,62},{2,61},{3,60},{4,59},{5,58},{6,57},{7,56},{8,55},{9,... | collective-permute-start | bytes 92168 | tf_op jit(solution)/shard_map/ppermute | solution.py:424

commit v5 on v4

--- a/solution.py
+++ b/solution.py
@@ -29,6 +29,7 @@
 TILES = 2 * ROWS // TILE
 HALF = ROWS // 2
 BLOCKS = HALF // HEAD
+FIRST_COST, COST = 4, 32
 TALL = HEAD + 16
 SENT = CHANNELS + 16
 
@@ -100,28 +101,35 @@
                 ]
 
 
-def pack_kernel(slots, low, high, queries):
-    for part, out in enumerate((low, high)):
+def pack_kernel(slots, chunk, queries):
+    for part in range(2):
         first = part * (PLANES // 2)
+        base = part * ROWS
         values = []
         for plane in range(PLANES // 2):
-            out[plane * PIECE : (plane + 1) * PIECE, :] = slots[first + plane, :, HEAD : 2 * HEAD]
+            start = base + plane * PIECE
+            chunk[start : start + PIECE, :] = slots[first + plane, :, HEAD : 2 * HEAD]
             values.append(slots[first + plane, :, 2 * HEAD :])
         values = jnp.concatenate(values, axis=0)
         for block in range(BLOCKS):
             square = values[block * HEAD : (block + 1) * HEAD, :].astype(f32)
-            out[HALF + block * HEAD : HALF + (block + 1) * HEAD, :] = square.T.astype(bf16)
+            start = base + HALF + block * HEAD
+            chunk[start : start + HEAD, :] = square.T.astype(bf16)
     queries[...] = slots[:, :, :HEAD]
 
 
-def attend_kernel(parts, sources, first, last, after, *refs):
+def attend_kernel(chunks, first, last, after, *refs):
     refs = list(refs)
     place = refs.pop(0)
     if first:
         own, other = refs.pop(0), refs.pop(0)
     else:
         queries = refs.pop(0)
-    segments = [refs.pop(0) for _ in parts]
+    segments = []
+    for halves, source in chunks:
+        chunk = refs.pop(0)
+        for index, part in enumerate(halves):
+            segments.append((chunk, index * ROWS, part, source))
     if not first:
         top_in, numer_in = refs.pop(0), refs.pop(0)
     refs = refs[after:]
@@ -141,19 +149,22 @@
     key_place = (key // PIECE) * (Z * TOKENS) + key % PIECE + core * PIECE
     ones = jnp.ones((TALL - HEAD, HALF), bf16)
     values = []
-    for segment in segments:
-        blocks = [segment[HALF + index * HEAD : HALF + (index + 1) * HEAD, :] for index in range(BLOCKS)]
+    for chunk, base, _, _ in segments:
+        starts = [base + HALF + index * HEAD for index in range(BLOCKS)]
+        blocks = [chunk[start : start + HEAD, :] for start in starts]
         values.append(jnp.concatenate([jnp.concatenate(blocks, axis=1), ones], axis=0))
 
     def score(tile):
         columns = slice(tile * TILE, (tile + 1) * TILE)
         found = []
-        for segment, part, source, value in zip(segments, parts, sources, values):
+        for (chunk, base, part, source), value in zip(segments, values):
             groups = min(2, tile + 1 - 2 * part)
             if groups <= 0:
                 continue
             count = groups * TOKENS
-            product = jnp.dot(segment[:count, :], queries[:, columns], preferred_element_type=f32)
+            product = jnp.dot(
+                chunk[base : base + count, :], queries[:, columns], preferred_element_type=f32
+            )
             if 2 * part + groups - 1 == tile:
                 shift = place[1 + source] * TOKENS
                 offset = 2 * (tile - 2 * part) * (Z * TOKENS)
@@ -205,8 +216,9 @@
         found = following
 
 
-def attend(place, queries, segments, parts, sources, state, last, after=()):
+def attend(place, queries, segments, chunks, state, last, after=()):
     first = state is None
+    count = sum(len(halves) for halves, _ in chunks)
     stats = [jax.ShapeDtypeStruct((8, 2 * ROWS), f32), jax.ShapeDtypeStruct((TALL, 2 * ROWS), f32)]
     if last:
         shapes = [jax.ShapeDtypeStruct((PLANES, PIECE, 2 * HEAD), bf16)] * 2
@@ -216,15 +228,15 @@
         shapes = stats
     operands = [place, *queries, *segments, *(state or ()), *after]
     return pl.pallas_call(
-        functools.partial(attend_kernel, parts, sources, first, last, len(after)),
+        functools.partial(attend_kernel, chunks, first, last, len(after)),
         out_shape=shapes,
         in_specs=[smem()] + [vmem()] * (len(operands) - 1),
         out_specs=[vmem()] * len(shapes),
         compiler_params=params(16),
         cost_estimate=pl.CostEstimate(
-            flops=8 * 2 * 2 * ROWS * HALF * HEAD * len(parts),
+            flops=(FIRST_COST if first else COST) * ROWS * HALF * HEAD * count,
             bytes_accessed=3_000_000,
-            transcendentals=ROWS * HALF * len(parts),
+            transcendentals=ROWS * HALF * count,
         ),
     )(*operands)
 
@@ -242,7 +254,9 @@
     first, second = jnp.exp2(first - top), jnp.exp2(second - top)
     both = first * mine[:, :, :HEAD].reshape(ROWS, HEAD).astype(f32)
     both = both + second * theirs[:, :, :HEAD].reshape(ROWS, HEAD).astype(f32)
-    out[...] = (both / (first + second)).astype(bf16).reshape(PLANES, PIECE, HEAD)
+    both = (both / (first + second)).astype(bf16).reshape(PLANES, PIECE, HEAD)
+    for plane in range(PLANES):
+        out[PLANES - 1 - plane] = both[plane]
 
 
 FF_PARTS = 2
@@ -252,7 +266,7 @@
 def dense_kernel(
     place,
     attended,
-    own,
+    hidden,
     other,
     flow,
     other_flow,
@@ -266,7 +280,7 @@
 ):
     core = place[0]
     rows = pl.ds(pl.multiple_of(core * PIECE, PIECE), PIECE)
-    residual = jnp.concatenate([own[...], other[rows, :]], axis=0).astype(f32)
+    residual = jnp.concatenate([hidden[rows, :], other[rows, :]], axis=0).astype(f32)
     sides = []
     for sequence in (core, 1 - core):
         heads = [attended[sequence * HEADS + head] for head in range(HEADS)]
@@ -301,7 +315,7 @@
     sent_other[...] = sent[:, PIECE:]
 
 
-def join_kernel(place, mine, theirs, out):
+def join_kernel(place, mine, theirs, latent, log_det):
     core = place[0]
     row = lax.broadcasted_iota(jnp.int32, (PIECE, TOKENS), 0)
     column = lax.broadcasted_iota(jnp.int32, (PIECE, TOKENS), 1)
@@ -310,7 +324,8 @@
         chosen = (column == TOKENS - 1 - half * PIECE - row).astype(f32).astype(bf16)
         term = jnp.dot(source[...], chosen, preferred_element_type=f32)
         total = term if total is None else total + term
-    out[...] = total.astype(bf16)
+    latent[...] = total[:CHANNELS]
+    log_det[...] = total[CHANNELS : CHANNELS + 1] + total[CHANNELS + 1 : CHANNELS + 2]
 
 
 def shift_by(count, step):
@@ -322,12 +337,18 @@
 ):
     core = lax.axis_index("core")
     z = lax.axis_index("z")
-    up_steps = [(z - step) % Z - z for step in range(5)]
-    down_steps = [(z + step) % Z - z for step in range(4)]
+    query_z = Z - 1 - z
+    up_steps = [(z - step) % Z - query_z for step in range(5)]
+    down_steps = [(z + step) % Z - query_z for step in range(4)]
     place = jnp.stack([core, *up_steps, *down_steps]).astype(jnp.int32)
     other_core = shift_by(2, 1)
     other = lax.ppermute(hidden, "core", other_core)
-    other_flow = lax.ppermute(flow_input, "core", other_core)
+    count = XL * Y * Z
+    mirrored = [(index, count - 1 - index) for index in range(count)]
+    far_hidden = lax.ppermute(hidden, ("xl", "y", "z"), mirrored)
+    far_flow = lax.ppermute(flow_input, ("xl", "y", "z"), mirrored)
+    other_far_hidden = lax.ppermute(far_hidden, "core", other_core)
+    other_far_flow = lax.ppermute(far_flow, "core", other_core)
 
     square = pltpu.VMEM((WIDTH, INNER), bf16)
     own, *weights = pl.pallas_call(
@@ -348,39 +369,40 @@
         compiler_params=params(8),
     )(place, own, other, *weights)
     slots = lax.all_to_all(slots, ("xl", "y"), 0, 0, tiled=True)
-    part = jax.ShapeDtypeStruct((ROWS, HEAD), bf16)
-    *own_parts, own_queries = pl.pallas_call(
+    chunk, queries = pl.pallas_call(
         pack_kernel,
-        out_shape=[part, part, jax.ShapeDtypeStruct((PLANES, PIECE, HEAD), bf16)],
+        out_shape=[
+            jax.ShapeDtypeStruct((2 * ROWS, HEAD), bf16),
+            jax.ShapeDtypeStruct((PLANES, PIECE, HEAD), bf16),
+        ],
         in_specs=[vmem()],
-        out_specs=[vmem()] * 3,
+        out_specs=[vmem()] * 2,
         compiler_params=params(8),
     )(slots)
-    other_queries = lax.ppermute(own_queries, "core", other_core)
-
-    up, down = list(own_parts), list(own_parts)
-    queries, *state = attend(
-        place, (own_queries, other_queries), own_parts, (0, 1), (0, 0), None, False
-    )
+    queries = lax.ppermute(queries, "z", [(index, Z - 1 - index) for index in range(Z)])
+    other_queries = lax.ppermute(queries, "core", other_core)
+
+    whole = (0, 1)
+    up = down = chunk
+    queries, *state = attend(place, (queries, other_queries), [chunk], [(whole, 0)], None, False)
+    early = {2: (other_far_hidden, other_far_flow)}
     for step in range(1, 4):
-        for part in range(2):
-            up[part] = lax.ppermute(up[part], "z", shift_by(Z, 1))
-            down[part] = lax.ppermute(down[part], "z", shift_by(Z, -1))
+        up = lax.ppermute(up, "z", shift_by(Z, 1))
+        down = lax.ppermute(down, "z", shift_by(Z, -1))
         state = attend(
             place,
             (queries,),
-            up + down,
-            (0, 1, 0, 1),
-            (step, step, 5 + step, 5 + step),
+            [up, down],
+            [(whole, step), (whole, 5 + step)],
             state,
             False,
-            (other_flow,) if step == 1 else (),
+            early.get(step, ()),
         )
     far = [
-        lax.ppermute(up[0], "z", shift_by(Z, 1)),
-        lax.ppermute(down[1], "z", shift_by(Z, -1)),
+        lax.ppermute(up[:ROWS], "z", shift_by(Z, 1)),
+        lax.ppermute(down[ROWS:], "z", shift_by(Z, -1)),
     ]
-    mine, others = attend(place, (queries,), far, (0, 1), (4, 4), state, True)
+    mine, others = attend(place, (queries,), far, [((0,), 4), ((1,), 4)], state, True)
     theirs = lax.ppermute(others, "core", other_core)
     attended = pl.pallas_call(
         merge_kernel,
@@ -401,10 +423,10 @@
     )(
         place,
         attended,
-        own,
-        other,
-        flow_input,
-        other_flow,
+        far_hidden,
+        other_far_hidden,
+        far_flow,
+        other_far_flow,
         w_output,
         w_up,
         w_down,
@@ -412,17 +434,17 @@
         w_scale,
     )
     received = lax.ppermute(sent_other, "core", other_core)
-    block = pl.pallas_call(
+    latent, log_det = pl.pallas_call(
         join_kernel,
-        out_shape=jax.ShapeDtypeStruct((SENT, TOKENS), bf16),
+        out_shape=[
+            jax.ShapeDtypeStruct((CHANNELS, TOKENS), f32),
+            jax.ShapeDtypeStruct((1, TOKENS), f32),
+        ],
         in_specs=[smem()] + [vmem()] * 2,
-        out_specs=vmem(),
+        out_specs=[vmem()] * 2,
         compiler_params=params(8),
     )(place, sent_own, received)
-    count = XL * Y * Z
-    mirrored = [(index, count - 1 - index) for index in range(count)]
-    arrived = lax.ppermute(block, ("xl", "y", "z"), mirrored).astype(f32)
-    return (arrived[:CHANNELS], arrived[CHANNELS] + arrived[CHANNELS + 1])
+    return (latent, log_det.reshape(TOKENS))
 
 
 def solution(mesh):

time: 97.8 us -> 120 us (1.23)
  waiting for transfers between devices: 14.6 us -> 42.9 us
  blocking collectives: 21.8 us -> 10.1 us
  starting transfers between devices: 36.5 us -> 42.1 us
  Pallas kernels: 22.6 us -> 24.1 us
    ppermute x17 -> x14, waiting for transfers between devices: 12.4 us -> 39.5 us  [the longest x1 23.5 us: on_device(): lax.ppermute(queries, 'z', [(index, Z - 1 - index) for index in range(Z)])]
    all_to_all x1 -> x0, blocking collectives: 13.6 us -> none  [on_device(): slots = lax.all_to_all(slots, ('xl', 'y'), 0, 0, tiled=True)]
    all_to_all x0 -> x1, starting transfers between devices: none -> 3.54 us  [on_device(): slots = lax.all_to_all(slots, ('xl', 'y'), 0, 0, tiled=True)]
    ppermute x17 -> x14, starting transfers between devices: 27.3 us -> 29.4 us  [the longest x1 8.7 us: on_device(): far_hidden = lax.ppermute(hidden, ('xl', 'y', 'z'), mirrored)]
    all_to_all x1, blocking collectives: 8.19 us -> 10.1 us  [on_device(): attended = lax.all_to_all(attended, ('xl', 'y'), 0, 0, tiled=True)]
    all_to_all x0 -> x1, waiting for transfers between devices: none -> 1.22 us  [on_device(): slots = lax.all_to_all(slots, ('xl', 'y'), 0, 0, tiled=True)]
  transfers between devices with their start and end apart: 20 -> 18, of which waited for: 5 -> 9; matrix products, arithmetic and copies ran while one was open for 0% -> 0% of each run, Pallas kernels for 14% -> 12%
where the time goes in v5:
time: 120 us
  waiting for transfers between devices  42.9 us (36%)
  starting transfers between devices  42.1 us (35%)
  Pallas kernels  24.1 us (20%)
  blocking collectives  10.1 us (8%)
    ppermute x1, waiting for transfers between devices, on_device(): lax.ppermute(queries, 'z', [(index, Z - 1 - index) for index in range(Z)])  23.5 us
    pallas_call x5, Pallas kernels, attend(): pl.pallas_call(functools.partial(attend_kernel, chunks, first, last, len(...  13.6 us
    all_to_all x1, blocking collectives, on_device(): attended = lax.all_to_all(attended, ('xl', 'y'), 0, 0, tiled=True)  10.1 us
    ppermute x1, starting transfers between devices, on_device(): far_hidden = lax.ppermute(hidden, ('xl', 'y', 'z'), mirrored)  8.7 us
    ppermute x3, starting transfers between devices, on_device(): down = lax.ppermute(down, 'z', shift_by(Z, -1))  6.23 us
    ppermute x3, waiting for transfers between devices, on_device(): down = lax.ppermute(down, 'z', shift_by(Z, -1))  6.13 us
    ppermute x1, starting transfers between devices, on_device(): lax.ppermute(queries, 'z', [(index, Z - 1 - index) for index in range(Z)])  5.17 us
    ppermute x1, waiting for transfers between devices, on_device(): far_flow = lax.ppermute(flow_input, ('xl', 'y', 'z'), mirrored)  4.92 us
  transfers between devices with their start and end apart: 18, of which 9 were waited for; matrix products, arithmetic and copies ran while one was open for 0% of the time, Pallas kernels for 12%

profile of v5, /device:TPU:1, one launch (start us, length us, event | category | flops | bytes accessed | tf_op | source)
XLA Modules:
  0.0 120.1 jit_solution(13927605545588823966)
XLA Ops:
  0.6 3.3 %collective-permute-start = (bf16[192,1024]{1,0:T(8,128)(2,1)}, bf16[192,1024]{1,0:T(8,128)(2,1)S(1)}, u32[]{:S(2)}, u32[]{:S(2)}) collective-permute-start(bf16[192,1024]{1,0:T(8,128)(2,1)} %hidden.1), channel_id=1, source_target_pairs={{0,64},{64,0},{1,65},{65,1},{2,66},{66,2},{3,67},{67,3},{4,68},{68... | collective-permute-start | bytes 1179656 | tf_op jit(solution)/shard_map/ppermute | solution.py:345
  4.0 0.1 stack.40.place.refs_0_
  4.0 0.0 copy-start.5
  4.0 0.0 copy-start.6
  4.1 2.5 %shard_map.113 = (bf16[96,1024]{1,0:T(8,128)(2,1)S(1)}, bf16[1024,512]{1,0:T(8,128)(2,1)S(1)}, bf16[1024,512]{1,0:T(8,128)(2,1)S(1)}, bf16[1024,512]{1,0:T(8,128)(2,1)S(1)}) custom-call(s32[10]{0:T(128)S(1)} %stack.40.place.refs_0_, bf16[192,1024]{1,0:T(8,128)(2,1)} %hidden.1, bf16[1024,512]{1,0:T(8,128)(2,1)} %w_query.1, bf16[1024,512]{1,0:T(8,128)(2,1)} %w_key.1, ...), custom_call_target="tpu_custom_call" | custom-call | bytes 6600000 | tf_op jit(solution)/shard_map/pallas_call | solution.py:354
  6.6 0.0 collective-permute-done.other
  6.6 2.4 %shard_map.114 = bf16[8,96,384]{2,1,0:T(8,128)(2,1)} custom-call(s32[10]{0:T(128)S(1)} %stack.40.place.refs_0_, bf16[96,1024]{1,0:T(8,128)(2,1)S(1)} %get-tuple-element.23.own, bf16[192,1024]{1,0:T(8,128)(2,1)S(1)} %collective-permute-done.other, bf16[1024,512]{1,0:T(8,128)(2,1)S(1)} %get-tuple-element.24.w_query, ...), custom_call_target="tpu_custom_call" | custom-call | tf_op jit(solution)/shard_map/pallas_call | solution.py:363
  9.0 3.5 %all-to-all-start = ((bf16[8,96,384]{2,1,0:T(8,128)(2,1)}), bf16[8,96,384]{2,1,0:T(8,128)(2,1)S(1)}, u32[]{:S(2)}, u32[]{:S(2)}) async-start(bf16[8,96,384]{2,1,0:T(8,128)(2,1)} %shard_map.114), calls=%async_computation | async-start | bytes 1179648 | tf_op jit(solution)/shard_map/all_to_all | solution.py:371
  12.5 0.0 copy-done.5
  12.6 8.7 %collective-permute-start.11 = (bf16[192,1024]{1,0:T(8,128)(2,1)S(1)}, bf16[192,1024]{1,0:T(8,128)(2,1)S(1)}, u32[]{:S(2)}, u32[]{:S(2)}) collective-permute-start(bf16[192,1024]{1,0:T(8,128)(2,1)S(1)} %copy-done.5), channel_id=1, source_target_pairs={{0,63},{1,62},{2,61},{3,60},{4,59},{5,58},{6,57},{7,56},{8,55},{9,... | collective-permute-start | bytes 1179656 | tf_op jit(solution)/shard_map/ppermute | solution.py:348
  21.2 1.2 %all-to-all-done.slots = bf16[8,96,384]{2,1,0:T(8,128)(2,1)S(1)} async-done(((bf16[8,96,384]{2,1,0:T(8,128)(2,1)}), bf16[8,96,384]{2,1,0:T(8,128)(2,1)S(1)}, u32[]{:S(2)}, u32[]{:S(2)}) %all-to-all-start) | async-done | bytes 589856 | tf_op jit(solution)/shard_map/all_to_all | solution.py:371
  22.5 0.1 shard_map.115
  22.6 0.9 collective-permute-start.3
  23.5 5.2 %collective-permute-start.1 = (bf16[8,96,128]{2,1,0:T(8,128)(2,1)S(1)}, bf16[8,96,128]{2,1,0:T(8,128)(2,1)S(1)}, u32[]{:S(2)}, u32[]{:S(2)}) collective-permute-start(bf16[8,96,128]{2,1,0:T(8,128)(2,1)S(1)} %get-tuple-element.27), channel_id=1, source_target_pairs={{0,7},{1,6},{2,5},{3,4},{4,3},{5,2},{6,1},{7,0},{8,15},{9,14},{10,... | collective-permute-start | bytes 589832 | tf_op jit(solution)/shard_map/ppermute | solution.py:382
  28.7 0.1 collective-permute-start.7
  28.8 23.5 %collective-permute-done.1.refs_1_ = bf16[8,96,128]{2,1,0:T(8,128)(2,1)S(1)} collective-permute-done((bf16[8,96,128]{2,1,0:T(8,128)(2,1)S(1)}, bf16[8,96,128]{2,1,0:T(8,128)(2,1)S(1)}, u32[]{:S(2)}, u32[]{:S(2)}) %collective-permute-start.1) | collective-permute-done | bytes 196640 | tf_op jit(solution)/shard_map/ppermute | solution.py:382
  52.3 1.5 %collective-permute-start.2 = (bf16[8,96,128]{2,1,0:T(8,128)(2,1)S(1)}, bf16[8,96,128]{2,1,0:T(8,128)(2,1)S(1)}, u32[]{:S(2)}, u32[]{:S(2)}) collective-permute-start(bf16[8,96,128]{2,1,0:T(8,128)(2,1)S(1)} %collective-permute-done.1.refs_1_), channel_id=1, source_target_pairs={{0,64},{64,0},{1,65},{65,1},{2,66},{66,2},{3,67},{67,3},{4,68},{68... | collective-permute-start | bytes 589832 | tf_op jit(solution)/shard_map/ppermute | solution.py:383
  53.8 0.0 copy-done.6
  53.8 2.1 %collective-permute-start.13 = (bf16[64,192]{1,0:T(8,128)(2,1)S(1)}, bf16[64,192]{1,0:T(8,128)(2,1)S(1)}, u32[]{:S(2)}, u32[]{:S(2)}) collective-permute-start(bf16[64,192]{1,0:T(8,128)(2,1)S(1)} %copy-done.6), channel_id=1, source_target_pairs={{0,63},{1,62},{2,61},{3,60},{4,59},{5,58},{6,57},{7,56},{8,55},{9,... | collective-permute-start | bytes 73736 | tf_op jit(solution)/shard_map/ppermute | solution.py:349
  55.9 4.9 %collective-permute-done.13.flow = bf16[64,192]{1,0:T(8,128)(2,1)S(1)} collective-permute-done((bf16[64,192]{1,0:T(8,128)(2,1)S(1)}, bf16[64,192]{1,0:T(8,128)(2,1)S(1)}, u32[]{:S(2)}, u32[]{:S(2)}) %collective-permute-start.13) | collective-permute-done | bytes 24608 | tf_op jit(solution)/shard_map/ppermute | solution.py:349
  60.8 1.2 collective-permute-start.14
  61.9 0.0 collective-permute-done.11.hidden
  61.9 0.0 collective-permute-start.12
  61.9 0.0 collective-permute-done.3.refs_2_
  61.9 0.1 collective-permute-start.4
  62.0 0.0 collective-permute-done.2.refs_2_
  62.0 2.1 %shard_map.116 = (bf16[128,1536]{1,0:T(8,128)(2,1)S(1)}, f32[8,1536]{1,0:T(8,128)S(1)}, f32[144,1536]{1,0:T(8,128)S(1)}) custom-call(s32[10]{0:T(128)S(1)} %stack.40.place.refs_0_, bf16[8,96,128]{2,1,0:T(8,128)(2,1)S(1)} %collective-permute-done.1.refs_1_, bf16[8,96,128]{2,1,0:T(8,128)(2,1)S(1)} %collective-permute-done.2.refs_2_, ...), custom_call_target="tpu_custom_call" | custom-call | flops 301989888 | bytes 3000000 | tf_op jit(solution)/shard_map/pallas_call | solution.py:230
  64.1 0.0 collective-permute-done.7.refs_3_
  64.1 2.7 %collective-permute-start.8 = (bf16[1536,128]{1,0:T(8,128)(2,1)S(1)}, bf16[1536,128]{1,0:T(8,128)(2,1)S(1)}, u32[]{:S(2)}, u32[]{:S(2)}) collective-permute-start(bf16[1536,128]{1,0:T(8,128)(2,1)S(1)} %collective-permute-done.7.refs_3_), channel_id=1, source_target_pairs={{0,7},{1,0},{2,1},{3,2},{4,3},{5,4},{6,5},{7,6},{8,15},{9,8},{10,9... | collective-permute-start | bytes 1179656 | tf_op jit(solution)/shard_map/ppermute | solution.py:391
  66.9 3.1 %shard_map.117 = (f32[8,1536]{1,0:T(8,128)S(1)}, f32[144,1536]{1,0:T(8,128)S(1)}) custom-call(s32[10]{0:T(128)S(1)} %stack.40.place.refs_0_, bf16[128,1536]{1,0:T(8,128)(2,1)S(1)} %get-tuple-element.29.refs_1_, bf16[1536,128]{1,0:T(8,128)(2,1)S(1)} %collective-permute-done.3.refs_2_, bf16[1536,128]{1,0:T(8,128)(2,1)S(1)} %collective-permute-done.7.refs_3_, ...), custom_call_target="tpu_custom_call" | custom-call | flops 4831838208 | bytes 3000000 | tf_op jit(solution)/shard_map/pallas_call | solution.py:230
  69.9 3.6 %collective-permute-done.4.refs_2_ = bf16[1536,128]{1,0:T(8,128)(2,1)S(1)} collective-permute-done((bf16[1536,128]{1,0:T(8,128)(2,1)S(1)}, bf16[1536,128]{1,0:T(8,128)(2,1)S(1)}, u32[]{:S(2)}, u32[]{:S(2)}) %collective-permute-start.4) | collective-permute-done | bytes 393248 | tf_op jit(solution)/shard_map/ppermute | solution.py:390
  73.5 0.0 collective-permute-start.5
  73.5 1.1 collective-permute-done.8.refs_3_
  74.6 3.4 %collective-permute-start.9 = (bf16[1536,128]{1,0:T(8,128)(2,1)S(1)}, bf16[1536,128]{1,0:T(8,128)(2,1)S(1)}, u32[]{:S(2)}, u32[]{:S(2)}) collective-permute-start(bf16[1536,128]{1,0:T(8,128)(2,1)S(1)} %collective-permute-done.8.refs_3_), channel_id=1, source_target_pairs={{0,7},{1,0},{2,1},{3,2},{4,3},{5,4},{6,5},{7,6},{8,15},{9,8},{10,9... | collective-permute-start | bytes 1179656 | tf_op jit(solution)/shard_map/ppermute | solution.py:391
  78.0 0.0 collective-permute-done.14.refs_7_.other_flow
  78.0 0.0 collective-permute-done.12.refs_6_.other
  78.0 3.1 %shard_map.118 = (f32[8,1536]{1,0:T(8,128)S(1)}, f32[144,1536]{1,0:T(8,128)S(1)}) custom-call(s32[10]{0:T(128)S(1)} %stack.40.place.refs_0_, bf16[128,1536]{1,0:T(8,128)(2,1)S(1)} %get-tuple-element.29.refs_1_, bf16[1536,128]{1,0:T(8,128)(2,1)S(1)} %collective-permute-done.4.refs_2_, bf16[1536,128]{1,0:T(8,128)(2,1)S(1)} %collective-permute-done.8.refs_3_, ...), custom_call_target="tpu_custom_call" | custom-call | flops 4831838208 | bytes 3000000 | tf_op jit(solution)/shard_map/pallas_call | solution.py:230
  81.1 5.0 %collective-permute-done.9.refs_3_ = bf16[1536,128]{1,0:T(8,128)(2,1)S(1)} collective-permute-done((bf16[1536,128]{1,0:T(8,128)(2,1)S(1)}, bf16[1536,128]{1,0:T(8,128)(2,1)S(1)}, u32[]{:S(2)}, u32[]{:S(2)}) %collective-permute-start.9) | collective-permute-done | bytes 393248 | tf_op jit(solution)/shard_map/ppermute | solution.py:391
  86.1 2.2 %collective-permute-start.10 = (bf16[768,128]{1,0:T(8,128)(2,1)S(1)}, bf16[768,128]{1,0:T(8,128)(2,1)S(1)}, u32[]{:S(2)}, u32[]{:S(2)}) collective-permute-start(bf16[768,128]{1,0:T(8,128)(2,1)S(1)} %slice.9), channel_id=1, source_target_pairs={{0,7},{1,0},{2,1},{3,2},{4,3},{5,4},{6,5},{7,6},{8,15},{9,8},{10,9... | collective-permute-start | bytes 589832 | tf_op jit(solution)/shard_map/ppermute | solution.py:403
  88.3 0.0 collective-permute-done.5.refs_2_
  88.4 1.4 %collective-permute-start.6 = (bf16[768,128]{1,0:T(8,128)(2,1)S(1)}, bf16[768,128]{1,0:T(8,128)(2,1)S(1)}, u32[]{:S(2)}, u32[]{:S(2)}) collective-permute-start(bf16[768,128]{1,0:T(8,128)(2,1)S(1)} %slice.8), channel_id=1, source_target_pairs={{0,1},{1,2},{2,3},{3,4},{4,5},{5,6},{6,7},{7,0},{8,9},{9,10},{10,1... | collective-permute-start | bytes 589832 | tf_op jit(solution)/shard_map/ppermute | solution.py:402
  89.8 3.1 %shard_map.119 = (f32[8,1536]{1,0:T(8,128)S(1)}, f32[144,1536]{1,0:T(8,128)S(1)}) custom-call(s32[10]{0:T(128)S(1)} %stack.40.place.refs_0_, bf16[128,1536]{1,0:T(8,128)(2,1)S(1)} %get-tuple-element.29.refs_1_, bf16[1536,128]{1,0:T(8,128)(2,1)S(1)} %collective-permute-done.5.refs_2_, bf16[1536,128]{1,0:T(8,128)(2,1)S(1)} %collective-permute-done.9.refs_3_, ...), custom_call_target="tpu_custom_call" | custom-call | flops 4831838208 | bytes 3000000 | tf_op jit(solution)/shard_map/pallas_call | solution.py:230
  92.8 0.0 collective-permute-done.10.refs_3_
  92.8 1.3 %collective-permute-done.6.refs_2_ = bf16[768,128]{1,0:T(8,128)(2,1)S(1)} collective-permute-done((bf16[768,128]{1,0:T(8,128)(2,1)S(1)}, bf16[768,128]{1,0:T(8,128)(2,1)S(1)}, u32[]{:S(2)}, u32[]{:S(2)}) %collective-permute-start.6) | collective-permute-done | bytes 196640 | tf_op jit(solution)/shard_map/ppermute | solution.py:402
  94.2 0.0 copy-start
  94.2 0.0 copy-start.1
  94.2 0.0 copy-start.2
  94.2 0.0 copy-start.3
  94.2 0.0 copy-start.4
  94.2 2.3 %shard_map.120 = (bf16[8,96,256]{2,1,0:T(8,128)(2,1)S(1)}, bf16[8,96,256]{2,1,0:T(8,128)(2,1)S(1)}) custom-call(s32[10]{0:T(128)S(1)} %stack.40.place.refs_0_, bf16[128,1536]{1,0:T(8,128)(2,1)S(1)} %get-tuple-element.29.refs_1_, bf16[768,128]{1,0:T(8,128)(2,1)S(1)} %collective-permute-done.6.refs_2_, bf16[768,128]{1,0:T(8,128)(2,1)S(1)} %collective-permute-done.10.refs_3_, ...), custom_call_target="tpu_custom_call" | custom-call | flops 2415919104 | bytes 3000000 | tf_op jit(solution)/shard_map/pallas_call | solution.py:230
  96.5 4.0 %collective-permute-start.15 = (bf16[8,96,256]{2,1,0:T(8,128)(2,1)S(1)}, bf16[8,96,256]{2,1,0:T(8,128)(2,1)S(1)}, u32[]{:S(2)}, u32[]{:S(2)}) collective-permute-start(bf16[8,96,256]{2,1,0:T(8,128)(2,1)S(1)} %get-tuple-element.39), channel_id=1, source_target_pairs={{0,64},{64,0},{1,65},{65,1},{2,66},{66,2},{3,67},{67,3},{4,68},{68... | collective-permute-start | bytes 1179656 | tf_op jit(solution)/shard_map/ppermute | solution.py:406
  100.5 1.3 %collective-permute-done.15.theirs = bf16[8,96,256]{2,1,0:T(8,128)(2,1)S(1)} collective-permute-done((bf16[8,96,256]{2,1,0:T(8,128)(2,1)S(1)}, bf16[8,96,256]{2,1,0:T(8,128)(2,1)S(1)}, u32[]{:S(2)}, u32[]{:S(2)}) %collective-permute-start.15) | collective-permute-done | bytes 393248 | tf_op jit(solution)/shard_map/ppermute | solution.py:406
  101.9 0.3 shard_map.121
  102.2 10.1 %all_to_all.10.attended = bf16[8,96,128]{2,1,0:T(8,128)(2,1)S(1)} all-to-all(bf16[8,96,128]{2,1,0:T(8,128)(2,1)S(1)} %shard_map.121), channel_id=1, replica_groups=mesh['xh'=2,'core'=2,'xl'=2,'y'=4,'z'=8] {'xl','y'}, dimensions={0} | all-to-all | bytes 393216 | tf_op jit(solution)/shard_map/all_to_all | solution.py:414
  112.3 0.0 copy-done
  112.3 0.0 copy-done.1
  112.3 0.0 copy-done.2
  112.3 0.0 copy-done.3
  112.3 0.0 copy-done.4
  112.3 3.8 %shard_map.122 = (bf16[80,96]{1,0:T(8,128)(2,1)S(1)}, bf16[80,96]{1,0:T(8,128)(2,1)S(1)}) custom-call(s32[10]{0:T(128)S(1)} %stack.40.place.refs_0_, bf16[8,96,128]{2,1,0:T(8,128)(2,1)S(1)} %all_to_all.10.attended, bf16[192,1024]{1,0:T(8,128)(2,1)S(1)} %collective-permute-done.11.hidden, bf16[192,1024]{1,0:T(8,128)(2,1)S(1)} %collective-permute-done.12.refs_6_.other, ...), custom_call_target="tpu_custom_call" | custom-call | tf_op jit(solution)/shard_map/pallas_call | solution.py:417
  116.1 1.7 %collective-permute-start.16 = (bf16[80,96]{1,0:T(8,128)(2,1)S(1)}, bf16[80,96]{1,0:T(8,128)(2,1)S(1)}, u32[]{:S(2)}, u32[]{:S(2)}) collective-permute-start(bf16[80,96]{1,0:T(8,128)(2,1)S(1)} %get-tuple-element.41), channel_id=1, source_target_pairs={{0,64},{64,0},{1,65},{65,1},{2,66},{66,2},{3,67},{67,3},{4,68},{68... | collective-permute-start | bytes 46088 | tf_op jit(solution)/shard_map/ppermute | solution.py:436
  117.9 0.8 collective-permute-done.16.theirs
  118.7 1.3 %shard_map.123 = (f32[64,192]{1,0:T(8,128)}, f32[1,192]{1,0:T(1,128)}) custom-call(s32[10]{0:T(128)S(1)} %stack.40.place.refs_0_, bf16[80,96]{1,0:T(8,128)(2,1)S(1)} %get-tuple-element.40.mine, bf16[80,96]{1,0:T(8,128)(2,1)S(1)} %collective-permute-done.16.theirs), custom_call_target="tpu_custom_call" | custom-call | tf_op jit(solution)/shard_map/pallas_call | solution.py:437
  (2 shorter events, 0.0 us)
Async XLA Ops:
  0.6 6.0 %collective-permute-start = (bf16[192,1024]{1,0:T(8,128)(2,1)}, bf16[192,1024]{1,0:T(8,128)(2,1)S(1)}, u32[]{:S(2)}, u32[]{:S(2)}) collective-permute-start(bf16[192,1024]{1,0:T(8,128)(2,1)} %hidden.1), channel_id=1, source_target_pairs={{0,64},{64,0},{1,65},{65,1},{2,66},{66,2},{3,67},{67,3},{4,68},{68... | collective-permute-start | bytes 1179656 | tf_op jit(solution)/shard_map/ppermute | solution.py:345
  4.0 8.5 %copy-start.5 = (bf16[192,1024]{1,0:T(8,128)(2,1)S(1)}, bf16[192,1024]{1,0:T(8,128)(2,1)}, u32[]{:S(2)}) copy-start(bf16[192,1024]{1,0:T(8,128)(2,1)} %hidden.1) | copy-start | bytes 1179652
  4.0 49.8 %copy-start.6 = (bf16[64,192]{1,0:T(8,128)(2,1)S(1)}, bf16[64,192]{1,0:T(8,128)(2,1)}, u32[]{:S(2)}) copy-start(bf16[64,192]{1,0:T(8,128)(2,1)} %param.11) | copy-start | bytes 73732
  9.0 13.5 %all-to-all-start = ((bf16[8,96,384]{2,1,0:T(8,128)(2,1)}), bf16[8,96,384]{2,1,0:T(8,128)(2,1)S(1)}, u32[]{:S(2)}, u32[]{:S(2)}) async-start(bf16[8,96,384]{2,1,0:T(8,128)(2,1)} %shard_map.114), calls=%async_computation | async-start | bytes 1179648 | tf_op jit(solution)/shard_map/all_to_all | solution.py:371
  12.6 49.4 %collective-permute-start.11 = (bf16[192,1024]{1,0:T(8,128)(2,1)S(1)}, bf16[192,1024]{1,0:T(8,128)(2,1)S(1)}, u32[]{:S(2)}, u32[]{:S(2)}) collective-permute-start(bf16[192,1024]{1,0:T(8,128)(2,1)S(1)} %copy-done.5), channel_id=1, source_target_pairs={{0,63},{1,62},{2,61},{3,60},{4,59},{5,58},{6,57},{7,56},{8,55},{9,... | collective-permute-start | bytes 1179656 | tf_op jit(solution)/shard_map/ppermute | solution.py:348
  22.6 39.3 %collective-permute-start.3 = (bf16[1536,128]{1,0:T(8,128)(2,1)S(1)}, bf16[1536,128]{1,0:T(8,128)(2,1)S(1)}, u32[]{:S(2)}, u32[]{:S(2)}) collective-permute-start(bf16[1536,128]{1,0:T(8,128)(2,1)S(1)} %get-tuple-element.28.refs_3_), channel_id=1, source_target_pairs={{0,1},{1,2},{2,3},{3,4},{4,5},{5,6},{6,7},{7,0},{8,9},{9,10},{10,1... | collective-permute-start | bytes 1179656 | tf_op jit(solution)/shard_map/ppermute | solution.py:390
  23.5 28.8 %collective-permute-start.1 = (bf16[8,96,128]{2,1,0:T(8,128)(2,1)S(1)}, bf16[8,96,128]{2,1,0:T(8,128)(2,1)S(1)}, u32[]{:S(2)}, u32[]{:S(2)}) collective-permute-start(bf16[8,96,128]{2,1,0:T(8,128)(2,1)S(1)} %get-tuple-element.27), channel_id=1, source_target_pairs={{0,7},{1,6},{2,5},{3,4},{4,3},{5,2},{6,1},{7,0},{8,15},{9,14},{10,... | collective-permute-start | bytes 589832 | tf_op jit(solution)/shard_map/ppermute | solution.py:382
  28.7 35.4 %collective-permute-start.7 = (bf16[1536,128]{1,0:T(8,128)(2,1)S(1)}, bf16[1536,128]{1,0:T(8,128)(2,1)S(1)}, u32[]{:S(2)}, u32[]{:S(2)}) collective-permute-start(bf16[1536,128]{1,0:T(8,128)(2,1)S(1)} %get-tuple-element.28.refs_3_), channel_id=1, source_target_pairs={{0,7},{1,0},{2,1},{3,2},{4,3},{5,4},{6,5},{7,6},{8,15},{9,8},{10,9... | collective-permute-start | bytes 1179656 | tf_op jit(solution)/shard_map/ppermute | solution.py:391
  52.3 9.7 %collective-permute-start.2 = (bf16[8,96,128]{2,1,0:T(8,128)(2,1)S(1)}, bf16[8,96,128]{2,1,0:T(8,128)(2,1)S(1)}, u32[]{:S(2)}, u32[]{:S(2)}) collective-permute-start(bf16[8,96,128]{2,1,0:T(8,128)(2,1)S(1)} %collective-permute-done.1.refs_1_), channel_id=1, source_target_pairs={{0,64},{64,0},{1,65},{65,1},{2,66},{66,2},{3,67},{67,3},{4,68},{68... | collective-permute-start | bytes 589832 | tf_op jit(solution)/shard_map/ppermute | solution.py:383
  53.8 7.0 %collective-permute-start.13 = (bf16[64,192]{1,0:T(8,128)(2,1)S(1)}, bf16[64,192]{1,0:T(8,128)(2,1)S(1)}, u32[]{:S(2)}, u32[]{:S(2)}) collective-permute-start(bf16[64,192]{1,0:T(8,128)(2,1)S(1)} %copy-done.6), channel_id=1, source_target_pairs={{0,63},{1,62},{2,61},{3,60},{4,59},{5,58},{6,57},{7,56},{8,55},{9,... | collective-permute-start | bytes 73736 | tf_op jit(solution)/shard_map/ppermute | solution.py:349
  60.8 17.2 %collective-permute-start.14 = (bf16[64,192]{1,0:T(8,128)(2,1)S(1)}, bf16[64,192]{1,0:T(8,128)(2,1)S(1)}, u32[]{:S(2)}, u32[]{:S(2)}) collective-permute-start(bf16[64,192]{1,0:T(8,128)(2,1)S(1)} %collective-permute-done.13.flow), channel_id=1, source_target_pairs={{0,64},{64,0},{1,65},{65,1},{2,66},{66,2},{3,67},{67,3},{4,68},{68... | collective-permute-start | bytes 73736 | tf_op jit(solution)/shard_map/ppermute | solution.py:351
  61.9 16.1 %collective-permute-start.12 = (bf16[192,1024]{1,0:T(8,128)(2,1)S(1)}, bf16[192,1024]{1,0:T(8,128)(2,1)S(1)}, u32[]{:S(2)}, u32[]{:S(2)}) collective-permute-start(bf16[192,1024]{1,0:T(8,128)(2,1)S(1)} %collective-permute-done.11.hidden), channel_id=1, source_target_pairs={{0,64},{64,0},{1,65},{65,1},{2,66},{66,2},{3,67},{67,3},{4,68},{68... | collective-permute-start | bytes 1179656 | tf_op jit(solution)/shard_map/ppermute | solution.py:350
  61.9 11.6 %collective-permute-start.4 = (bf16[1536,128]{1,0:T(8,128)(2,1)S(1)}, bf16[1536,128]{1,0:T(8,128)(2,1)S(1)}, u32[]{:S(2)}, u32[]{:S(2)}) collective-permute-start(bf16[1536,128]{1,0:T(8,128)(2,1)S(1)} %collective-permute-done.3.refs_2_), channel_id=1, source_target_pairs={{0,1},{1,2},{2,3},{3,4},{4,5},{5,6},{6,7},{7,0},{8,9},{9,10},{10,1... | collective-permute-start | bytes 1179656 | tf_op jit(solution)/shard_map/ppermute | solution.py:390
  64.1 10.5 %collective-permute-start.8 = (bf16[1536,128]{1,0:T(8,128)(2,1)S(1)}, bf16[1536,128]{1,0:T(8,128)(2,1)S(1)}, u32[]{:S(2)}, u32[]{:S(2)}) collective-permute-start(bf16[1536,128]{1,0:T(8,128)(2,1)S(1)} %collective-permute-done.7.refs_3_), channel_id=1, source_target_pairs={{0,7},{1,0},{2,1},{3,2},{4,3},{5,4},{6,5},{7,6},{8,15},{9,8},{10,9... | collective-permute-start | bytes 1179656 | tf_op jit(solution)/shard_map/ppermute | solution.py:391
  73.5 14.8 %collective-permute-start.5 = (bf16[1536,128]{1,0:T(8,128)(2,1)S(1)}, bf16[1536,128]{1,0:T(8,128)(2,1)S(1)}, u32[]{:S(2)}, u32[]{:S(2)}) collective-permute-start(bf16[1536,128]{1,0:T(8,128)(2,1)S(1)} %collective-permute-done.4.refs_2_), channel_id=1, source_target_pairs={{0,1},{1,2},{2,3},{3,4},{4,5},{5,6},{6,7},{7,0},{8,9},{9,10},{10,1... | collective-permute-start | bytes 1179656 | tf_op jit(solution)/shard_map/ppermute | solution.py:390
  74.6 11.5 %collective-permute-start.9 = (bf16[1536,128]{1,0:T(8,128)(2,1)S(1)}, bf16[1536,128]{1,0:T(8,128)(2,1)S(1)}, u32[]{:S(2)}, u32[]{:S(2)}) collective-permute-start(bf16[1536,128]{1,0:T(8,128)(2,1)S(1)} %collective-permute-done.8.refs_3_), channel_id=1, source_target_pairs={{0,7},{1,0},{2,1},{3,2},{4,3},{5,4},{6,5},{7,6},{8,15},{9,8},{10,9... | collective-permute-start | bytes 1179656 | tf_op jit(solution)/shard_map/ppermute | solution.py:391
  86.1 6.7 %collective-permute-start.10 = (bf16[768,128]{1,0:T(8,128)(2,1)S(1)}, bf16[768,128]{1,0:T(8,128)(2,1)S(1)}, u32[]{:S(2)}, u32[]{:S(2)}) collective-permute-start(bf16[768,128]{1,0:T(8,128)(2,1)S(1)} %slice.9), channel_id=1, source_target_pairs={{0,7},{1,0},{2,1},{3,2},{4,3},{5,4},{6,5},{7,6},{8,15},{9,8},{10,9... | collective-permute-start | bytes 589832 | tf_op jit(solution)/shard_map/ppermute | solution.py:403
  88.4 5.8 %collective-permute-start.6 = (bf16[768,128]{1,0:T(8,128)(2,1)S(1)}, bf16[768,128]{1,0:T(8,128)(2,1)S(1)}, u32[]{:S(2)}, u32[]{:S(2)}) collective-permute-start(bf16[768,128]{1,0:T(8,128)(2,1)S(1)} %slice.8), channel_id=1, source_target_pairs={{0,1},{1,2},{2,3},{3,4},{4,5},{5,6},{6,7},{7,0},{8,9},{9,10},{10,1... | collective-permute-start | bytes 589832 | tf_op jit(solution)/shard_map/ppermute | solution.py:402
  94.2 18.1 %copy-start = (bf16[1024,2048]{1,0:T(8,128)(2,1)S(1)}, bf16[1024,2048]{1,0:T(8,128)(2,1)}, u32[]{:S(2)}) copy-start(bf16[1024,2048]{1,0:T(8,128)(2,1)} %w_up.1) | copy-start | bytes 12582916
  94.2 18.1 %copy-start.1 = (bf16[2048,1024]{1,0:T(8,128)(2,1)S(1)}, bf16[2048,1024]{1,0:T(8,128)(2,1)}, u32[]{:S(2)}) copy-start(bf16[2048,1024]{1,0:T(8,128)(2,1)} %w_down.1) | copy-start | bytes 12582916
  94.2 18.1 %copy-start.2 = (bf16[512,1024]{1,0:T(8,128)(2,1)S(1)}, bf16[512,1024]{1,0:T(8,128)(2,1)}, u32[]{:S(2)}) copy-start(bf16[512,1024]{1,0:T(8,128)(2,1)} %w_output.1) | copy-start | bytes 3145732
  94.2 18.1 %copy-start.3 = (bf16[64,1024]{1,0:T(8,128)(2,1)S(1)}, bf16[64,1024]{1,0:T(8,128)(2,1)}, u32[]{:S(2)}) copy-start(bf16[64,1024]{1,0:T(8,128)(2,1)} %w_shift.1) | copy-start | bytes 393220
  94.2 18.1 %copy-start.4 = (bf16[64,1024]{1,0:T(8,128)(2,1)S(1)}, bf16[64,1024]{1,0:T(8,128)(2,1)}, u32[]{:S(2)}) copy-start(bf16[64,1024]{1,0:T(8,128)(2,1)} %w_scale.1) | copy-start | bytes 393220
  96.5 5.4 %collective-permute-start.15 = (bf16[8,96,256]{2,1,0:T(8,128)(2,1)S(1)}, bf16[8,96,256]{2,1,0:T(8,128)(2,1)S(1)}, u32[]{:S(2)}, u32[]{:S(2)}) collective-permute-start(bf16[8,96,256]{2,1,0:T(8,128)(2,1)S(1)} %get-tuple-element.39), channel_id=1, source_target_pairs={{0,64},{64,0},{1,65},{65,1},{2,66},{66,2},{3,67},{67,3},{4,68},{68... | collective-permute-start | bytes 1179656 | tf_op jit(solution)/shard_map/ppermute | solution.py:406
  116.1 2.6 %collective-permute-start.16 = (bf16[80,96]{1,0:T(8,128)(2,1)S(1)}, bf16[80,96]{1,0:T(8,128)(2,1)S(1)}, u32[]{:S(2)}, u32[]{:S(2)}) collective-permute-start(bf16[80,96]{1,0:T(8,128)(2,1)S(1)} %get-tuple-element.41), channel_id=1, source_target_pairs={{0,64},{64,0},{1,65},{65,1},{2,66},{66,2},{3,67},{67,3},{4,68},{68... | collective-permute-start | bytes 46088 | tf_op jit(solution)/shard_map/ppermute | solution.py:436

commit v6 on v5

--- a/solution.py
+++ b/solution.py
@@ -255,8 +255,7 @@
     both = first * mine[:, :, :HEAD].reshape(ROWS, HEAD).astype(f32)
     both = both + second * theirs[:, :, :HEAD].reshape(ROWS, HEAD).astype(f32)
     both = (both / (first + second)).astype(bf16).reshape(PLANES, PIECE, HEAD)
-    for plane in range(PLANES):
-        out[PLANES - 1 - plane] = both[plane]
+    out[...] = both
 
 
 FF_PARTS = 2
@@ -266,7 +265,7 @@
 def dense_kernel(
     place,
     attended,
-    hidden,
+    own,
     other,
     flow,
     other_flow,
@@ -280,7 +279,7 @@
 ):
     core = place[0]
     rows = pl.ds(pl.multiple_of(core * PIECE, PIECE), PIECE)
-    residual = jnp.concatenate([hidden[rows, :], other[rows, :]], axis=0).astype(f32)
+    residual = jnp.concatenate([own[...], other[rows, :]], axis=0).astype(f32)
     sides = []
     for sequence in (core, 1 - core):
         heads = [attended[sequence * HEADS + head] for head in range(HEADS)]
@@ -315,7 +314,7 @@
     sent_other[...] = sent[:, PIECE:]
 
 
-def join_kernel(place, mine, theirs, latent, log_det):
+def join_kernel(place, mine, theirs, out):
     core = place[0]
     row = lax.broadcasted_iota(jnp.int32, (PIECE, TOKENS), 0)
     column = lax.broadcasted_iota(jnp.int32, (PIECE, TOKENS), 1)
@@ -324,8 +323,7 @@
         chosen = (column == TOKENS - 1 - half * PIECE - row).astype(f32).astype(bf16)
         term = jnp.dot(source[...], chosen, preferred_element_type=f32)
         total = term if total is None else total + term
-    latent[...] = total[:CHANNELS]
-    log_det[...] = total[CHANNELS : CHANNELS + 1] + total[CHANNELS + 1 : CHANNELS + 2]
+    out[...] = total.astype(bf16)
 
 
 def shift_by(count, step):
@@ -337,18 +335,12 @@
 ):
     core = lax.axis_index("core")
     z = lax.axis_index("z")
-    query_z = Z - 1 - z
-    up_steps = [(z - step) % Z - query_z for step in range(5)]
-    down_steps = [(z + step) % Z - query_z for step in range(4)]
+    up_steps = [(z - step) % Z - z for step in range(5)]
+    down_steps = [(z + step) % Z - z for step in range(4)]
     place = jnp.stack([core, *up_steps, *down_steps]).astype(jnp.int32)
     other_core = shift_by(2, 1)
     other = lax.ppermute(hidden, "core", other_core)
-    count = XL * Y * Z
-    mirrored = [(index, count - 1 - index) for index in range(count)]
-    far_hidden = lax.ppermute(hidden, ("xl", "y", "z"), mirrored)
-    far_flow = lax.ppermute(flow_input, ("xl", "y", "z"), mirrored)
-    other_far_hidden = lax.ppermute(far_hidden, "core", other_core)
-    other_far_flow = lax.ppermute(far_flow, "core", other_core)
+    other_flow = lax.ppermute(flow_input, "core", other_core)
 
     square = pltpu.VMEM((WIDTH, INNER), bf16)
     own, *weights = pl.pallas_call(
@@ -379,13 +371,12 @@
         out_specs=[vmem()] * 2,
         compiler_params=params(8),
     )(slots)
-    queries = lax.ppermute(queries, "z", [(index, Z - 1 - index) for index in range(Z)])
     other_queries = lax.ppermute(queries, "core", other_core)
 
     whole = (0, 1)
     up = down = chunk
     queries, *state = attend(place, (queries, other_queries), [chunk], [(whole, 0)], None, False)
-    early = {2: (other_far_hidden, other_far_flow)}
+    early = {1: (other_flow,)}
     for step in range(1, 4):
         up = lax.ppermute(up, "z", shift_by(Z, 1))
         down = lax.ppermute(down, "z", shift_by(Z, -1))
@@ -423,10 +414,10 @@
     )(
         place,
         attended,
-        far_hidden,
-        other_far_hidden,
-        far_flow,
-        other_far_flow,
+        own,
+        other,
+        flow_input,
+        other_flow,
         w_output,
         w_up,
         w_down,
@@ -434,17 +425,17 @@
         w_scale,
     )
     received = lax.ppermute(sent_other, "core", other_core)
-    latent, log_det = pl.pallas_call(
+    block = pl.pallas_call(
         join_kernel,
-        out_shape=[
-            jax.ShapeDtypeStruct((CHANNELS, TOKENS), f32),
-            jax.ShapeDtypeStruct((1, TOKENS), f32),
-        ],
+        out_shape=jax.ShapeDtypeStruct((SENT, TOKENS), bf16),
         in_specs=[smem()] + [vmem()] * 2,
-        out_specs=[vmem()] * 2,
+        out_specs=vmem(),
         compiler_params=params(8),
     )(place, sent_own, received)
-    return (latent, log_det.reshape(TOKENS))
+    count = XL * Y * Z
+    mirrored = [(index, count - 1 - index) for index in range(count)]
+    arrived = lax.ppermute(block, ("xl", "y", "z"), mirrored).astype(f32)
+    return (arrived[:CHANNELS], arrived[CHANNELS] + arrived[CHANNELS + 1])
 
 
 def solution(mesh):

time: 120 us -> 95.9 us (0.80)
  waiting for transfers between devices: 42.9 us -> 17.2 us
  blocking collectives: 10.1 us -> 23.9 us
  starting transfers between devices: 42.1 us -> 29.8 us
  Pallas kernels: 24.1 us -> 22.6 us
    ppermute x5 -> x2, waiting for transfers between devices: 28.4 us -> 3.96 us  [the longest x1 3.96 us: on_device(): arrived = lax.ppermute(block, ('xl', 'y', 'z'), mirrored).astype(f32)]
    all_to_all x0 -> x1, blocking collectives: none -> 13.6 us  [on_device(): slots = lax.all_to_all(slots, ('xl', 'y'), 0, 0, tiled=True)]
    ppermute x5 -> x2, starting transfers between devices: 17.1 us -> 4.04 us  [the longest x1 4.03 us: on_device(): arrived = lax.ppermute(block, ('xl', 'y', 'z'), mirrored).astype(f32)]
    ppermute x3, waiting for transfers between devices: 3.57 us -> 10 us  [on_device(): up = lax.ppermute(up, 'z', shift_by(Z, 1))]
    ppermute x3, waiting for transfers between devices: 6.13 us -> 0.01 us  [on_device(): down = lax.ppermute(down, 'z', shift_by(Z, -1))]
    all_to_all x1 -> x0, starting transfers between devices: 3.54 us -> none  [on_device(): slots = lax.all_to_all(slots, ('xl', 'y'), 0, 0, tiled=True)]
    ppermute x3, starting transfers between devices: 6.23 us -> 9.37 us  [on_device(): down = lax.ppermute(down, 'z', shift_by(Z, -1))]
    ppermute x1, waiting for transfers between devices: 1.34 us -> 0.01 us  [on_device(): lax.ppermute(up[:ROWS], 'z', shift_by(Z, 1))]
  transfers between devices with their start and end apart: 18 -> 14, of which waited for: 9 -> 7; matrix products, arithmetic and copies ran while one was open for 0% -> 0% of each run, Pallas kernels for 12% -> 14%
where the time goes in v6:
time: 95.9 us; the launch traced here: 95.7 us
  starting transfers between devices  29.8 us (31%)
  blocking collectives  23.9 us (25%)
  Pallas kernels  22.6 us (24%)
  waiting for transfers between devices  17.2 us (18%)
    all_to_all x1, blocking collectives, on_device(): slots = lax.all_to_all(slots, ('xl', 'y'), 0, 0, tiled=True)  13.6 us
    pallas_call x5, Pallas kernels, attend(): pl.pallas_call(functools.partial(attend_kernel, chunks, first, last, len(...  13.5 us
    all_to_all x1, blocking collectives, on_device(): attended = lax.all_to_all(attended, ('xl', 'y'), 0, 0, tiled=True)  10.3 us
    ppermute x3, waiting for transfers between devices, on_device(): up = lax.ppermute(up, 'z', shift_by(Z, 1))  10 us
    ppermute x3, starting transfers between devices, on_device(): down = lax.ppermute(down, 'z', shift_by(Z, -1))  9.37 us
    ppermute x1, starting transfers between devices, on_device(): theirs = lax.ppermute(others, 'core', other_core)  5.03 us
    ppermute x1, starting transfers between devices, on_device(): arrived = lax.ppermute(block, ('xl', 'y', 'z'), mirrored).astype(f32)  4.03 us
    ppermute x1, waiting for transfers between devices, on_device(): arrived = lax.ppermute(block, ('xl', 'y', 'z'), mirrored).astype(f32)  3.96 us
  transfers between devices with their start and end apart: 14, of which 7 were waited for; matrix products, arithmetic and copies ran while one was open for 0% of the time, Pallas kernels for 14%

profile of v6, /device:TPU:1, one launch (start us, length us, event | category | flops | bytes accessed | tf_op | source)
XLA Modules:
  0.0 95.7 jit_solution(12072413438703809528)
XLA Ops:
  0.6 3.3 %collective-permute-start = (bf16[192,1024]{1,0:T(8,128)(2,1)}, bf16[192,1024]{1,0:T(8,128)(2,1)S(1)}, u32[]{:S(2)}, u32[]{:S(2)}) collective-permute-start(bf16[192,1024]{1,0:T(8,128)(2,1)} %hidden.1), channel_id=1, source_target_pairs={{0,64},{64,0},{1,65},{65,1},{2,66},{66,2},{3,67},{67,3},{4,68},{68... | collective-permute-start | bytes 1179656 | tf_op jit(solution)/shard_map/ppermute | solution.py:342
  4.0 0.1 stack.40.place.refs_0_
  4.0 0.0 copy-start.5
  4.0 2.5 %shard_map.113 = (bf16[96,1024]{1,0:T(8,128)(2,1)S(1)}, bf16[1024,512]{1,0:T(8,128)(2,1)S(1)}, bf16[1024,512]{1,0:T(8,128)(2,1)S(1)}, bf16[1024,512]{1,0:T(8,128)(2,1)S(1)}) custom-call(s32[10]{0:T(128)S(1)} %stack.40.place.refs_0_, bf16[192,1024]{1,0:T(8,128)(2,1)} %hidden.1, bf16[1024,512]{1,0:T(8,128)(2,1)} %w_query.1, bf16[1024,512]{1,0:T(8,128)(2,1)} %w_key.1, ...), custom_call_target="tpu_custom_call" | custom-call | bytes 6600000 | tf_op jit(solution)/shard_map/pallas_call | solution.py:346
  6.6 0.0 collective-permute-done.other
  6.6 1.6 %shard_map.114 = bf16[8,96,384]{2,1,0:T(8,128)(2,1)S(1)} custom-call(s32[10]{0:T(128)S(1)} %stack.40.place.refs_0_, bf16[96,1024]{1,0:T(8,128)(2,1)S(1)} %get-tuple-element.21.own, bf16[192,1024]{1,0:T(8,128)(2,1)S(1)} %collective-permute-done.other, bf16[1024,512]{1,0:T(8,128)(2,1)S(1)} %get-tuple-element.22.w_query, ...), custom_call_target="tpu_custom_call" | custom-call | tf_op jit(solution)/shard_map/pallas_call | solution.py:355
  8.2 13.6 %all_to_all.10.slots = bf16[8,96,384]{2,1,0:T(8,128)(2,1)S(1)} all-to-all(bf16[8,96,384]{2,1,0:T(8,128)(2,1)S(1)} %shard_map.114), channel_id=1, replica_groups=mesh['xh'=2,'core'=2,'xl'=2,'y'=4,'z'=8] {'xl','y'}, dimensions={0} | all-to-all | bytes 1179648 | tf_op jit(solution)/shard_map/all_to_all | solution.py:363
  21.7 0.1 shard_map.115
  21.9 1.7 %collective-permute-start.2 = (bf16[1536,128]{1,0:T(8,128)(2,1)S(1)}, bf16[1536,128]{1,0:T(8,128)(2,1)S(1)}, u32[]{:S(2)}, u32[]{:S(2)}) collective-permute-start(bf16[1536,128]{1,0:T(8,128)(2,1)S(1)} %get-tuple-element.26.refs_3_), channel_id=1, source_target_pairs={{0,1},{1,2},{2,3},{3,4},{4,5},{5,6},{6,7},{7,0},{8,9},{9,10},{10,1... | collective-permute-start | bytes 1179656 | tf_op jit(solution)/shard_map/ppermute | solution.py:381
  23.6 4.0 %collective-permute-start.6 = (bf16[1536,128]{1,0:T(8,128)(2,1)S(1)}, bf16[1536,128]{1,0:T(8,128)(2,1)S(1)}, u32[]{:S(2)}, u32[]{:S(2)}) collective-permute-start(bf16[1536,128]{1,0:T(8,128)(2,1)S(1)} %get-tuple-element.26.refs_3_), channel_id=1, source_target_pairs={{0,7},{1,0},{2,1},{3,2},{4,3},{5,4},{6,5},{7,6},{8,15},{9,8},{10,9... | collective-permute-start | bytes 1179656 | tf_op jit(solution)/shard_map/ppermute | solution.py:382
  27.6 1.7 %collective-permute-start.1 = (bf16[8,96,128]{2,1,0:T(8,128)(2,1)S(1)}, bf16[8,96,128]{2,1,0:T(8,128)(2,1)S(1)}, u32[]{:S(2)}, u32[]{:S(2)}) collective-permute-start(bf16[8,96,128]{2,1,0:T(8,128)(2,1)S(1)} %get-tuple-element.25.refs_1_), channel_id=1, source_target_pairs={{0,64},{64,0},{1,65},{65,1},{2,66},{66,2},{3,67},{67,3},{4,68},{68... | collective-permute-start | bytes 589832 | tf_op jit(solution)/shard_map/ppermute | solution.py:374
  29.4 0.0 copy-done.5
  29.4 0.0 collective-permute-start.10
  29.4 1.1 %collective-permute-done.1.refs_2_ = bf16[8,96,128]{2,1,0:T(8,128)(2,1)S(1)} collective-permute-done((bf16[8,96,128]{2,1,0:T(8,128)(2,1)S(1)}, bf16[8,96,128]{2,1,0:T(8,128)(2,1)S(1)}, u32[]{:S(2)}, u32[]{:S(2)}) %collective-permute-start.1) | collective-permute-done | bytes 196640 | tf_op jit(solution)/shard_map/ppermute | solution.py:374
  30.4 2.1 %shard_map.116 = (bf16[128,1536]{1,0:T(8,128)(2,1)S(1)}, f32[8,1536]{1,0:T(8,128)S(1)}, f32[144,1536]{1,0:T(8,128)S(1)}) custom-call(s32[10]{0:T(128)S(1)} %stack.40.place.refs_0_, bf16[8,96,128]{2,1,0:T(8,128)(2,1)S(1)} %get-tuple-element.25.refs_1_, bf16[8,96,128]{2,1,0:T(8,128)(2,1)S(1)} %collective-permute-done.1.refs_2_, ...), custom_call_target="tpu_custom_call" | custom-call | flops 301989888 | bytes 3000000 | tf_op jit(solution)/shard_map/pallas_call | solution.py:230
  32.5 3.0 %collective-permute-done.2.refs_2_ = bf16[1536,128]{1,0:T(8,128)(2,1)S(1)} collective-permute-done((bf16[1536,128]{1,0:T(8,128)(2,1)S(1)}, bf16[1536,128]{1,0:T(8,128)(2,1)S(1)}, u32[]{:S(2)}, u32[]{:S(2)}) %collective-permute-start.2) | collective-permute-done | bytes 393248 | tf_op jit(solution)/shard_map/ppermute | solution.py:381
  35.5 0.0 collective-permute-start.3
  35.5 0.0 collective-permute-done.6.refs_3_
  35.5 2.7 %collective-permute-start.7 = (bf16[1536,128]{1,0:T(8,128)(2,1)S(1)}, bf16[1536,128]{1,0:T(8,128)(2,1)S(1)}, u32[]{:S(2)}, u32[]{:S(2)}) collective-permute-start(bf16[1536,128]{1,0:T(8,128)(2,1)S(1)} %collective-permute-done.6.refs_3_), channel_id=1, source_target_pairs={{0,7},{1,0},{2,1},{3,2},{4,3},{5,4},{6,5},{7,6},{8,15},{9,8},{10,9... | collective-permute-start | bytes 1179656 | tf_op jit(solution)/shard_map/ppermute | solution.py:382
  38.2 0.0 collective-permute-done.10.refs_6_.other_flow
  38.2 3.0 %shard_map.117 = (f32[8,1536]{1,0:T(8,128)S(1)}, f32[144,1536]{1,0:T(8,128)S(1)}) custom-call(s32[10]{0:T(128)S(1)} %stack.40.place.refs_0_, bf16[128,1536]{1,0:T(8,128)(2,1)S(1)} %get-tuple-element.27.refs_1_, bf16[1536,128]{1,0:T(8,128)(2,1)S(1)} %collective-permute-done.2.refs_2_, bf16[1536,128]{1,0:T(8,128)(2,1)S(1)} %collective-permute-done.6.refs_3_, ...), custom_call_target="tpu_custom_call" | custom-call | flops 4831838208 | bytes 3000000 | tf_op jit(solution)/shard_map/pallas_call | solution.py:230
  41.2 4.0 %collective-permute-done.3.refs_2_ = bf16[1536,128]{1,0:T(8,128)(2,1)S(1)} collective-permute-done((bf16[1536,128]{1,0:T(8,128)(2,1)S(1)}, bf16[1536,128]{1,0:T(8,128)(2,1)S(1)}, u32[]{:S(2)}, u32[]{:S(2)}) %collective-permute-start.3) | collective-permute-done | bytes 393248 | tf_op jit(solution)/shard_map/ppermute | solution.py:381
  45.2 0.0 collective-permute-start.4
  45.2 0.0 collective-permute-done.7.refs_3_
  45.2 2.7 %collective-permute-start.8 = (bf16[1536,128]{1,0:T(8,128)(2,1)S(1)}, bf16[1536,128]{1,0:T(8,128)(2,1)S(1)}, u32[]{:S(2)}, u32[]{:S(2)}) collective-permute-start(bf16[1536,128]{1,0:T(8,128)(2,1)S(1)} %collective-permute-done.7.refs_3_), channel_id=1, source_target_pairs={{0,7},{1,0},{2,1},{3,2},{4,3},{5,4},{6,5},{7,6},{8,15},{9,8},{10,9... | collective-permute-start | bytes 1179656 | tf_op jit(solution)/shard_map/ppermute | solution.py:382
  47.9 3.1 %shard_map.118 = (f32[8,1536]{1,0:T(8,128)S(1)}, f32[144,1536]{1,0:T(8,128)S(1)}) custom-call(s32[10]{0:T(128)S(1)} %stack.40.place.refs_0_, bf16[128,1536]{1,0:T(8,128)(2,1)S(1)} %get-tuple-element.27.refs_1_, bf16[1536,128]{1,0:T(8,128)(2,1)S(1)} %collective-permute-done.3.refs_2_, bf16[1536,128]{1,0:T(8,128)(2,1)S(1)} %collective-permute-done.7.refs_3_, ...), custom_call_target="tpu_custom_call" | custom-call | flops 4831838208 | bytes 3000000 | tf_op jit(solution)/shard_map/pallas_call | solution.py:230
  51.0 3.1 %collective-permute-done.4.refs_2_ = bf16[1536,128]{1,0:T(8,128)(2,1)S(1)} collective-permute-done((bf16[1536,128]{1,0:T(8,128)(2,1)S(1)}, bf16[1536,128]{1,0:T(8,128)(2,1)S(1)}, u32[]{:S(2)}, u32[]{:S(2)}) %collective-permute-start.4) | collective-permute-done | bytes 393248 | tf_op jit(solution)/shard_map/ppermute | solution.py:381
  54.0 0.1 collective-permute-start.5
  54.1 0.0 collective-permute-done.8.refs_3_
  54.2 2.7 %collective-permute-start.9 = (bf16[768,128]{1,0:T(8,128)(2,1)S(1)}, bf16[768,128]{1,0:T(8,128)(2,1)S(1)}, u32[]{:S(2)}, u32[]{:S(2)}) collective-permute-start(bf16[768,128]{1,0:T(8,128)(2,1)S(1)} %slice.21), channel_id=1, source_target_pairs={{0,7},{1,0},{2,1},{3,2},{4,3},{5,4},{6,5},{7,6},{8,15},{9,8},{10,9... | collective-permute-start | bytes 589832 | tf_op jit(solution)/shard_map/ppermute | solution.py:394
  56.9 3.1 %shard_map.119 = (f32[8,1536]{1,0:T(8,128)S(1)}, f32[144,1536]{1,0:T(8,128)S(1)}) custom-call(s32[10]{0:T(128)S(1)} %stack.40.place.refs_0_, bf16[128,1536]{1,0:T(8,128)(2,1)S(1)} %get-tuple-element.27.refs_1_, bf16[1536,128]{1,0:T(8,128)(2,1)S(1)} %collective-permute-done.4.refs_2_, bf16[1536,128]{1,0:T(8,128)(2,1)S(1)} %collective-permute-done.8.refs_3_, ...), custom_call_target="tpu_custom_call" | custom-call | flops 4831838208 | bytes 3000000 | tf_op jit(solution)/shard_map/pallas_call | solution.py:230
  60.0 0.0 collective-permute-done.5.refs_2_
  60.0 0.0 collective-permute-done.9.refs_3_
  60.0 0.0 copy-start
  60.0 0.0 copy-start.1
  60.0 0.0 copy-start.2
  60.0 0.0 copy-start.3
  60.0 0.0 copy-start.4
  60.0 2.3 %shard_map.120 = (bf16[8,96,256]{2,1,0:T(8,128)(2,1)S(1)}, bf16[8,96,256]{2,1,0:T(8,128)(2,1)S(1)}) custom-call(s32[10]{0:T(128)S(1)} %stack.40.place.refs_0_, bf16[128,1536]{1,0:T(8,128)(2,1)S(1)} %get-tuple-element.27.refs_1_, bf16[768,128]{1,0:T(8,128)(2,1)S(1)} %collective-permute-done.5.refs_2_, bf16[768,128]{1,0:T(8,128)(2,1)S(1)} %collective-permute-done.9.refs_3_, ...), custom_call_target="tpu_custom_call" | custom-call | flops 2415919104 | bytes 3000000 | tf_op jit(solution)/shard_map/pallas_call | solution.py:230
  62.4 5.0 %collective-permute-start.11 = (bf16[8,96,256]{2,1,0:T(8,128)(2,1)S(1)}, bf16[8,96,256]{2,1,0:T(8,128)(2,1)S(1)}, u32[]{:S(2)}, u32[]{:S(2)}) collective-permute-start(bf16[8,96,256]{2,1,0:T(8,128)(2,1)S(1)} %get-tuple-element.37), channel_id=1, source_target_pairs={{0,64},{64,0},{1,65},{65,1},{2,66},{66,2},{3,67},{67,3},{4,68},{68... | collective-permute-start | bytes 1179656 | tf_op jit(solution)/shard_map/ppermute | solution.py:397
  67.4 1.3 %collective-permute-done.11.theirs = bf16[8,96,256]{2,1,0:T(8,128)(2,1)S(1)} collective-permute-done((bf16[8,96,256]{2,1,0:T(8,128)(2,1)S(1)}, bf16[8,96,256]{2,1,0:T(8,128)(2,1)S(1)}, u32[]{:S(2)}, u32[]{:S(2)}) %collective-permute-start.11) | collective-permute-done | bytes 393248 | tf_op jit(solution)/shard_map/ppermute | solution.py:397
  68.7 0.3 shard_map.121
  69.1 10.3 %all_to_all.11.attended = bf16[8,96,128]{2,1,0:T(8,128)(2,1)S(1)} all-to-all(bf16[8,96,128]{2,1,0:T(8,128)(2,1)S(1)} %shard_map.121), channel_id=1, replica_groups=mesh['xh'=2,'core'=2,'xl'=2,'y'=4,'z'=8] {'xl','y'}, dimensions={0} | all-to-all | bytes 393216 | tf_op jit(solution)/shard_map/all_to_all | solution.py:405
  79.4 0.0 copy-done
  79.4 0.0 copy-done.1
  79.4 0.0 copy-done.2
  79.4 0.0 copy-done.3
  79.4 0.0 copy-done.4
  79.4 3.8 %shard_map.122 = (bf16[80,96]{1,0:T(8,128)(2,1)S(1)}, bf16[80,96]{1,0:T(8,128)(2,1)S(1)}) custom-call(s32[10]{0:T(128)S(1)} %stack.40.place.refs_0_, bf16[8,96,128]{2,1,0:T(8,128)(2,1)S(1)} %all_to_all.11.attended, bf16[96,1024]{1,0:T(8,128)(2,1)S(1)} %get-tuple-element.21.own, bf16[192,1024]{1,0:T(8,128)(2,1)S(1)} %collective-permute-done.other, ...), custom_call_target="tpu_custom_call" | custom-call | tf_op jit(solution)/shard_map/pallas_call | solution.py:408
  83.2 1.8 %collective-permute-start.12 = (bf16[80,96]{1,0:T(8,128)(2,1)S(1)}, bf16[80,96]{1,0:T(8,128)(2,1)S(1)}, u32[]{:S(2)}, u32[]{:S(2)}) collective-permute-start(bf16[80,96]{1,0:T(8,128)(2,1)S(1)} %get-tuple-element.39), channel_id=1, source_target_pairs={{0,64},{64,0},{1,65},{65,1},{2,66},{66,2},{3,67},{67,3},{4,68},{68... | collective-permute-start | bytes 46088 | tf_op jit(solution)/shard_map/ppermute | solution.py:427
  85.0 0.8 collective-permute-done.12.theirs
  85.8 0.7 shard_map.123
  86.5 4.0 %collective-permute-start.13 = (bf16[80,192]{1,0:T(8,128)(2,1)S(1)}, bf16[80,192]{1,0:T(8,128)(2,1)S(1)}, u32[]{:S(2)}, u32[]{:S(2)}) collective-permute-start(bf16[80,192]{1,0:T(8,128)(2,1)S(1)} %shard_map.123), channel_id=1, source_target_pairs={{0,63},{1,62},{2,61},{3,60},{4,59},{5,58},{6,57},{7,56},{8,55},{9,... | collective-permute-start | bytes 92168 | tf_op jit(solution)/shard_map/ppermute | solution.py:437
  90.5 4.0 %collective-permute-done.13 = bf16[80,192]{1,0:T(8,128)(2,1)S(1)} collective-permute-done((bf16[80,192]{1,0:T(8,128)(2,1)S(1)}, bf16[80,192]{1,0:T(8,128)(2,1)S(1)}, u32[]{:S(2)}, u32[]{:S(2)}) %collective-permute-start.13) | collective-permute-done | bytes 30752 | tf_op jit(solution)/shard_map/ppermute | solution.py:437
  94.5 0.6 slice_add_fusion
  95.1 0.6 slice.22
  (3 shorter events, 0.0 us)
Async XLA Ops:
  0.6 6.0 %collective-permute-start = (bf16[192,1024]{1,0:T(8,128)(2,1)}, bf16[192,1024]{1,0:T(8,128)(2,1)S(1)}, u32[]{:S(2)}, u32[]{:S(2)}) collective-permute-start(bf16[192,1024]{1,0:T(8,128)(2,1)} %hidden.1), channel_id=1, source_target_pairs={{0,64},{64,0},{1,65},{65,1},{2,66},{66,2},{3,67},{67,3},{4,68},{68... | collective-permute-start | bytes 1179656 | tf_op jit(solution)/shard_map/ppermute | solution.py:342
  4.0 25.3 %copy-start.5 = (bf16[64,192]{1,0:T(8,128)(2,1)S(1)}, bf16[64,192]{1,0:T(8,128)(2,1)}, u32[]{:S(2)}) copy-start(bf16[64,192]{1,0:T(8,128)(2,1)} %flow.1) | copy-start | bytes 73732
  21.9 13.6 %collective-permute-start.2 = (bf16[1536,128]{1,0:T(8,128)(2,1)S(1)}, bf16[1536,128]{1,0:T(8,128)(2,1)S(1)}, u32[]{:S(2)}, u32[]{:S(2)}) collective-permute-start(bf16[1536,128]{1,0:T(8,128)(2,1)S(1)} %get-tuple-element.26.refs_3_), channel_id=1, source_target_pairs={{0,1},{1,2},{2,3},{3,4},{4,5},{5,6},{6,7},{7,0},{8,9},{9,10},{10,1... | collective-permute-start | bytes 1179656 | tf_op jit(solution)/shard_map/ppermute | solution.py:381
  23.6 11.9 %collective-permute-start.6 = (bf16[1536,128]{1,0:T(8,128)(2,1)S(1)}, bf16[1536,128]{1,0:T(8,128)(2,1)S(1)}, u32[]{:S(2)}, u32[]{:S(2)}) collective-permute-start(bf16[1536,128]{1,0:T(8,128)(2,1)S(1)} %get-tuple-element.26.refs_3_), channel_id=1, source_target_pairs={{0,7},{1,0},{2,1},{3,2},{4,3},{5,4},{6,5},{7,6},{8,15},{9,8},{10,9... | collective-permute-start | bytes 1179656 | tf_op jit(solution)/shard_map/ppermute | solution.py:382
  27.6 2.8 %collective-permute-start.1 = (bf16[8,96,128]{2,1,0:T(8,128)(2,1)S(1)}, bf16[8,96,128]{2,1,0:T(8,128)(2,1)S(1)}, u32[]{:S(2)}, u32[]{:S(2)}) collective-permute-start(bf16[8,96,128]{2,1,0:T(8,128)(2,1)S(1)} %get-tuple-element.25.refs_1_), channel_id=1, source_target_pairs={{0,64},{64,0},{1,65},{65,1},{2,66},{66,2},{3,67},{67,3},{4,68},{68... | collective-permute-start | bytes 589832 | tf_op jit(solution)/shard_map/ppermute | solution.py:374
  29.4 8.8 %collective-permute-start.10 = (bf16[64,192]{1,0:T(8,128)(2,1)S(1)}, bf16[64,192]{1,0:T(8,128)(2,1)S(1)}, u32[]{:S(2)}, u32[]{:S(2)}) collective-permute-start(bf16[64,192]{1,0:T(8,128)(2,1)S(1)} %copy-done.5), channel_id=1, source_target_pairs={{0,64},{64,0},{1,65},{65,1},{2,66},{66,2},{3,67},{67,3},{4,68},{68... | collective-permute-start | bytes 73736 | tf_op jit(solution)/shard_map/ppermute | solution.py:343
  35.5 9.7 %collective-permute-start.3 = (bf16[1536,128]{1,0:T(8,128)(2,1)S(1)}, bf16[1536,128]{1,0:T(8,128)(2,1)S(1)}, u32[]{:S(2)}, u32[]{:S(2)}) collective-permute-start(bf16[1536,128]{1,0:T(8,128)(2,1)S(1)} %collective-permute-done.2.refs_2_), channel_id=1, source_target_pairs={{0,1},{1,2},{2,3},{3,4},{4,5},{5,6},{6,7},{7,0},{8,9},{9,10},{10,1... | collective-permute-start | bytes 1179656 | tf_op jit(solution)/shard_map/ppermute | solution.py:381
  35.5 9.7 %collective-permute-start.7 = (bf16[1536,128]{1,0:T(8,128)(2,1)S(1)}, bf16[1536,128]{1,0:T(8,128)(2,1)S(1)}, u32[]{:S(2)}, u32[]{:S(2)}) collective-permute-start(bf16[1536,128]{1,0:T(8,128)(2,1)S(1)} %collective-permute-done.6.refs_3_), channel_id=1, source_target_pairs={{0,7},{1,0},{2,1},{3,2},{4,3},{5,4},{6,5},{7,6},{8,15},{9,8},{10,9... | collective-permute-start | bytes 1179656 | tf_op jit(solution)/shard_map/ppermute | solution.py:382
  45.2 8.8 %collective-permute-start.4 = (bf16[1536,128]{1,0:T(8,128)(2,1)S(1)}, bf16[1536,128]{1,0:T(8,128)(2,1)S(1)}, u32[]{:S(2)}, u32[]{:S(2)}) collective-permute-start(bf16[1536,128]{1,0:T(8,128)(2,1)S(1)} %collective-permute-done.3.refs_2_), channel_id=1, source_target_pairs={{0,1},{1,2},{2,3},{3,4},{4,5},{5,6},{6,7},{7,0},{8,9},{9,10},{10,1... | collective-permute-start | bytes 1179656 | tf_op jit(solution)/shard_map/ppermute | solution.py:381
  45.2 8.9 %collective-permute-start.8 = (bf16[1536,128]{1,0:T(8,128)(2,1)S(1)}, bf16[1536,128]{1,0:T(8,128)(2,1)S(1)}, u32[]{:S(2)}, u32[]{:S(2)}) collective-permute-start(bf16[1536,128]{1,0:T(8,128)(2,1)S(1)} %collective-permute-done.7.refs_3_), channel_id=1, source_target_pairs={{0,7},{1,0},{2,1},{3,2},{4,3},{5,4},{6,5},{7,6},{8,15},{9,8},{10,9... | collective-permute-start | bytes 1179656 | tf_op jit(solution)/shard_map/ppermute | solution.py:382
  54.0 5.9 %collective-permute-start.5 = (bf16[768,128]{1,0:T(8,128)(2,1)S(1)}, bf16[768,128]{1,0:T(8,128)(2,1)S(1)}, u32[]{:S(2)}, u32[]{:S(2)}) collective-permute-start(bf16[768,128]{1,0:T(8,128)(2,1)S(1)} %slice.20), channel_id=1, source_target_pairs={{0,1},{1,2},{2,3},{3,4},{4,5},{5,6},{6,7},{7,0},{8,9},{9,10},{10,1... | collective-permute-start | bytes 589832 | tf_op jit(solution)/shard_map/ppermute | solution.py:393
  54.2 5.8 %collective-permute-start.9 = (bf16[768,128]{1,0:T(8,128)(2,1)S(1)}, bf16[768,128]{1,0:T(8,128)(2,1)S(1)}, u32[]{:S(2)}, u32[]{:S(2)}) collective-permute-start(bf16[768,128]{1,0:T(8,128)(2,1)S(1)} %slice.21), channel_id=1, source_target_pairs={{0,7},{1,0},{2,1},{3,2},{4,3},{5,4},{6,5},{7,6},{8,15},{9,8},{10,9... | collective-permute-start | bytes 589832 | tf_op jit(solution)/shard_map/ppermute | solution.py:394
  60.0 19.4 %copy-start = (bf16[1024,2048]{1,0:T(8,128)(2,1)S(1)}, bf16[1024,2048]{1,0:T(8,128)(2,1)}, u32[]{:S(2)}) copy-start(bf16[1024,2048]{1,0:T(8,128)(2,1)} %w_up.1) | copy-start | bytes 12582916
  60.0 19.4 %copy-start.1 = (bf16[2048,1024]{1,0:T(8,128)(2,1)S(1)}, bf16[2048,1024]{1,0:T(8,128)(2,1)}, u32[]{:S(2)}) copy-start(bf16[2048,1024]{1,0:T(8,128)(2,1)} %w_down.1) | copy-start | bytes 12582916
  60.0 19.4 %copy-start.2 = (bf16[512,1024]{1,0:T(8,128)(2,1)S(1)}, bf16[512,1024]{1,0:T(8,128)(2,1)}, u32[]{:S(2)}) copy-start(bf16[512,1024]{1,0:T(8,128)(2,1)} %w_output.1) | copy-start | bytes 3145732
  60.0 19.4 %copy-start.3 = (bf16[64,1024]{1,0:T(8,128)(2,1)S(1)}, bf16[64,1024]{1,0:T(8,128)(2,1)}, u32[]{:S(2)}) copy-start(bf16[64,1024]{1,0:T(8,128)(2,1)} %w_shift.1) | copy-start | bytes 393220
  60.0 19.4 %copy-start.4 = (bf16[64,1024]{1,0:T(8,128)(2,1)S(1)}, bf16[64,1024]{1,0:T(8,128)(2,1)}, u32[]{:S(2)}) copy-start(bf16[64,1024]{1,0:T(8,128)(2,1)} %w_scale.1) | copy-start | bytes 393220
  62.4 6.4 %collective-permute-start.11 = (bf16[8,96,256]{2,1,0:T(8,128)(2,1)S(1)}, bf16[8,96,256]{2,1,0:T(8,128)(2,1)S(1)}, u32[]{:S(2)}, u32[]{:S(2)}) collective-permute-start(bf16[8,96,256]{2,1,0:T(8,128)(2,1)S(1)} %get-tuple-element.37), channel_id=1, source_target_pairs={{0,64},{64,0},{1,65},{65,1},{2,66},{66,2},{3,67},{67,3},{4,68},{68... | collective-permute-start | bytes 1179656 | tf_op jit(solution)/shard_map/ppermute | solution.py:397
  83.2 2.6 %collective-permute-start.12 = (bf16[80,96]{1,0:T(8,128)(2,1)S(1)}, bf16[80,96]{1,0:T(8,128)(2,1)S(1)}, u32[]{:S(2)}, u32[]{:S(2)}) collective-permute-start(bf16[80,96]{1,0:T(8,128)(2,1)S(1)} %get-tuple-element.39), channel_id=1, source_target_pairs={{0,64},{64,0},{1,65},{65,1},{2,66},{66,2},{3,67},{67,3},{4,68},{68... | collective-permute-start | bytes 46088 | tf_op jit(solution)/shard_map/ppermute | solution.py:427
  86.5 8.0 %collective-permute-start.13 = (bf16[80,192]{1,0:T(8,128)(2,1)S(1)}, bf16[80,192]{1,0:T(8,128)(2,1)S(1)}, u32[]{:S(2)}, u32[]{:S(2)}) collective-permute-start(bf16[80,192]{1,0:T(8,128)(2,1)S(1)} %shard_map.123), channel_id=1, source_target_pairs={{0,63},{1,62},{2,61},{3,60},{4,59},{5,58},{6,57},{7,56},{8,55},{9,... | collective-permute-start | bytes 92168 | tf_op jit(solution)/shard_map/ppermute | solution.py:437

commit v7 on v6

--- a/solution.py
+++ b/solution.py
@@ -30,6 +30,7 @@
 HALF = ROWS // 2
 BLOCKS = HALF // HEAD
 FIRST_COST, COST = 4, 32
+AFTER = 2
 TALL = HEAD + 16
 SENT = CHANNELS + 16
 
@@ -99,6 +100,19 @@
                 slots[sequence * HEADS + head, :, column * HEAD : (column + 1) * HEAD] = made[
                     part * PIECE : (part + 1) * PIECE, head * HEAD : (head + 1) * HEAD
                 ]
+
+
+def both_kernel(place, own, other, flow, other_flow, token, both):
+    del token
+    core = place[0]
+    rows = pl.ds(pl.multiple_of(core * PIECE, PIECE), PIECE)
+    both[:PIECE, :] = own[...]
+    both[PIECE:TOKENS, :] = other[rows, :]
+    both[TOKENS:, :] = jnp.zeros((CHANNELS, WIDTH), bf16)
+    flows = []
+    for source in (flow, other_flow):
+        flows.append(jnp.where(core == 0, source[:, :PIECE].astype(f32), source[:, PIECE:].astype(f32)))
+    both[TOKENS:, :TOKENS] = jnp.concatenate(flows, axis=1).astype(bf16)
 
 
 def pack_kernel(slots, chunk, queries):
@@ -255,7 +269,8 @@
     both = first * mine[:, :, :HEAD].reshape(ROWS, HEAD).astype(f32)
     both = both + second * theirs[:, :, :HEAD].reshape(ROWS, HEAD).astype(f32)
     both = (both / (first + second)).astype(bf16).reshape(PLANES, PIECE, HEAD)
-    out[...] = both
+    for plane in range(PLANES):
+        out[PLANES - 1 - plane] = both[plane]
 
 
 FF_PARTS = 2
@@ -265,10 +280,7 @@
 def dense_kernel(
     place,
     attended,
-    own,
-    other,
-    flow,
-    other_flow,
+    both,
     w_output,
     w_up,
     w_down,
@@ -278,8 +290,7 @@
     sent_other,
 ):
     core = place[0]
-    rows = pl.ds(pl.multiple_of(core * PIECE, PIECE), PIECE)
-    residual = jnp.concatenate([own[...], other[rows, :]], axis=0).astype(f32)
+    residual = both[:TOKENS, :].astype(f32)
     sides = []
     for sequence in (core, 1 - core):
         heads = [attended[sequence * HEADS + head] for head in range(HEADS)]
@@ -305,10 +316,8 @@
     low = (determinant - high.astype(f32)).astype(bf16)
     row = lax.broadcasted_iota(jnp.int32, (SENT - CHANNELS, TOKENS), 0)
     tail = jnp.where(row == 0, high.astype(f32), jnp.where(row == 1, low.astype(f32), 0.0))
-    flows = []
-    for source in (flow, other_flow):
-        flows.append(jnp.where(core == 0, source[:, :PIECE].astype(f32), source[:, PIECE:].astype(f32)))
-    moved = (jnp.concatenate(flows, axis=1) - shift) * jnp.exp(-log_scale)
+    flow = both[TOKENS:, :TOKENS].astype(f32)
+    moved = (flow - shift) * jnp.exp(-log_scale)
     sent = jnp.concatenate([moved, tail], axis=0).astype(bf16)
     sent_own[...] = sent[:, :PIECE]
     sent_other[...] = sent[:, PIECE:]
@@ -324,6 +333,12 @@
         term = jnp.dot(source[...], chosen, preferred_element_type=f32)
         total = term if total is None else total + term
     out[...] = total.astype(bf16)
+
+
+def final_kernel(block, latent, log_det):
+    latent[...] = block[:CHANNELS, :].astype(f32)
+    det = block[CHANNELS:, :].astype(f32)
+    log_det[...] = det[:1] + det[1:2]
 
 
 def shift_by(count, step):
@@ -376,7 +391,16 @@
     whole = (0, 1)
     up = down = chunk
     queries, *state = attend(place, (queries, other_queries), [chunk], [(whole, 0)], None, False)
-    early = {1: (other_flow,)}
+    both = pl.pallas_call(
+        both_kernel,
+        out_shape=jax.ShapeDtypeStruct((TOKENS + CHANNELS, WIDTH), bf16),
+        in_specs=[smem()] + [vmem()] * 5,
+        out_specs=vmem(),
+        compiler_params=params(8),
+    )(place, own, other, flow_input, other_flow, state[0])
+    opposite = [(plane, PLANES - 1 - plane) for plane in range(PLANES)]
+    both = lax.ppermute(both, ("xl", "y"), opposite)
+    early = {AFTER: (both,)}
     for step in range(1, 4):
         up = lax.ppermute(up, "z", shift_by(Z, 1))
         down = lax.ppermute(down, "z", shift_by(Z, -1))
@@ -408,16 +432,13 @@
     sent_own, sent_other = pl.pallas_call(
         dense_kernel,
         out_shape=[sent, sent],
-        in_specs=[smem()] + [vmem()] * 10,
+        in_specs=[smem()] + [vmem()] * 7,
         out_specs=[vmem()] * 2,
         compiler_params=params(16),
     )(
         place,
         attended,
-        own,
-        other,
-        flow_input,
-        other_flow,
+        both,
         w_output,
         w_up,
         w_down,
@@ -432,10 +453,18 @@
         out_specs=vmem(),
         compiler_params=params(8),
     )(place, sent_own, received)
-    count = XL * Y * Z
-    mirrored = [(index, count - 1 - index) for index in range(count)]
-    arrived = lax.ppermute(block, ("xl", "y", "z"), mirrored).astype(f32)
-    return (arrived[:CHANNELS], arrived[CHANNELS] + arrived[CHANNELS + 1])
+    block = lax.ppermute(block, "z", [(index, Z - 1 - index) for index in range(Z)])
+    latent, log_det = pl.pallas_call(
+        final_kernel,
+        out_shape=[
+            jax.ShapeDtypeStruct((CHANNELS, TOKENS), f32),
+            jax.ShapeDtypeStruct((1, TOKENS), f32),
+        ],
+        in_specs=[vmem()],
+        out_specs=[vmem()] * 2,
+        compiler_params=params(4),
+    )(block)
+    return (latent, log_det.reshape(TOKENS))
 
 
 def solution(mesh):

time: 95.9 us -> 91.9 us (0.958)
  waiting for transfers between devices: 17.2 us -> 13 us
  Pallas kernels: 22.6 us -> 23.9 us
    ppermute x3, waiting for transfers between devices: 10 us -> 7.62 us  [on_device(): up = lax.ppermute(up, 'z', shift_by(Z, 1))]
    ppermute x1 -> x2, waiting for transfers between devices: 3.96 us -> 2.05 us  [the longest x1 1.46 us: on_device(): lax.ppermute(block, 'z', [(index, Z - 1 - index) for index in range(Z)])]
    pallas_call x0 -> x2, Pallas kernels: none -> 1.33 us  [the longest x1 0.69 us: on_device(): pl.pallas_call(both_kernel, out_shape=jax.ShapeDtypeStruct((TOKENS + CHAN...]
    ppermute x1 -> x2, starting transfers between devices: 4.03 us -> 4.23 us  [the longest x1 3.13 us: on_device(): lax.ppermute(block, 'z', [(index, Z - 1 - index) for index in range(Z)])]
  transfers between devices with their start and end apart: 14 -> 15, of which waited for: 7 -> 8; matrix products, arithmetic and copies ran while one was open for 0% -> 0% of each run, Pallas kernels for 14% -> 16%
where the time goes in v7:
time: 91.9 us; the launch traced here: 91.7 us
  starting transfers between devices  30 us (33%)
  Pallas kernels  23.9 us (26%)
  blocking collectives  23.9 us (26%)
  waiting for transfers between devices  13 us (14%)
    all_to_all x1, blocking collectives, on_device(): slots = lax.all_to_all(slots, ('xl', 'y'), 0, 0, tiled=True)  13.6 us
    pallas_call x5, Pallas kernels, attend(): pl.pallas_call(functools.partial(attend_kernel, chunks, first, last, len(...  13.6 us
    all_to_all x1, blocking collectives, on_device(): attended = lax.all_to_all(attended, ('xl', 'y'), 0, 0, tiled=True)  10.3 us
    ppermute x3, starting transfers between devices, on_device(): down = lax.ppermute(down, 'z', shift_by(Z, -1))  9.37 us
    ppermute x3, waiting for transfers between devices, on_device(): up = lax.ppermute(up, 'z', shift_by(Z, 1))  7.62 us
    ppermute x1, starting transfers between devices, on_device(): theirs = lax.ppermute(others, 'core', other_core)  5.03 us
    pallas_call x1, Pallas kernels, on_device(): pl.pallas_call(dense_kernel, out_shape=[sent, sent], in_specs=[smem()] +...  3.77 us
    ppermute x1, starting transfers between devices, on_device(): other = lax.ppermute(hidden, 'core', other_core)  3.33 us
  transfers between devices with their start and end apart: 15, of which 8 were waited for; matrix products, arithmetic and copies ran while one was open for 0% of the time, Pallas kernels for 16%

profile of v7, /device:TPU:1, one launch (start us, length us, event | category | flops | bytes accessed | tf_op | source)
XLA Modules:
  0.0 91.7 jit_solution(17976812940570126710)
XLA Ops:
  0.6 3.3 %collective-permute-start = (bf16[192,1024]{1,0:T(8,128)(2,1)}, bf16[192,1024]{1,0:T(8,128)(2,1)S(1)}, u32[]{:S(2)}, u32[]{:S(2)}) collective-permute-start(bf16[192,1024]{1,0:T(8,128)(2,1)} %hidden.1), channel_id=1, source_target_pairs={{0,64},{64,0},{1,65},{65,1},{2,66},{66,2},{3,67},{67,3},{4,68},{68... | collective-permute-start | bytes 1179656 | tf_op jit(solution)/shard_map/ppermute | solution.py:357
  4.0 0.1 stack.40.place.refs_0_
  4.0 0.0 copy-start.5
  4.0 2.5 %shard_map.113 = (bf16[96,1024]{1,0:T(8,128)(2,1)S(1)}, bf16[1024,512]{1,0:T(8,128)(2,1)S(1)}, bf16[1024,512]{1,0:T(8,128)(2,1)S(1)}, bf16[1024,512]{1,0:T(8,128)(2,1)S(1)}) custom-call(s32[10]{0:T(128)S(1)} %stack.40.place.refs_0_, bf16[192,1024]{1,0:T(8,128)(2,1)} %hidden.1, bf16[1024,512]{1,0:T(8,128)(2,1)} %w_query.1, bf16[1024,512]{1,0:T(8,128)(2,1)} %w_key.1, ...), custom_call_target="tpu_custom_call" | custom-call | bytes 6600000 | tf_op jit(solution)/shard_map/pallas_call | solution.py:361
  6.6 0.0 collective-permute-done.other
  6.6 1.6 %shard_map.114 = bf16[8,96,384]{2,1,0:T(8,128)(2,1)S(1)} custom-call(s32[10]{0:T(128)S(1)} %stack.40.place.refs_0_, bf16[96,1024]{1,0:T(8,128)(2,1)S(1)} %get-tuple-element.23.own, bf16[192,1024]{1,0:T(8,128)(2,1)S(1)} %collective-permute-done.other, bf16[1024,512]{1,0:T(8,128)(2,1)S(1)} %get-tuple-element.24.w_query, ...), custom_call_target="tpu_custom_call" | custom-call | tf_op jit(solution)/shard_map/pallas_call | solution.py:370
  8.2 13.6 %all_to_all.10.slots = bf16[8,96,384]{2,1,0:T(8,128)(2,1)S(1)} all-to-all(bf16[8,96,384]{2,1,0:T(8,128)(2,1)S(1)} %shard_map.114), channel_id=1, replica_groups=mesh['xh'=2,'core'=2,'xl'=2,'y'=4,'z'=8] {'xl','y'}, dimensions={0} | all-to-all | bytes 1179648 | tf_op jit(solution)/shard_map/all_to_all | solution.py:378
  21.7 0.1 shard_map.115
  21.9 1.7 %collective-permute-start.2 = (bf16[1536,128]{1,0:T(8,128)(2,1)S(1)}, bf16[1536,128]{1,0:T(8,128)(2,1)S(1)}, u32[]{:S(2)}, u32[]{:S(2)}) collective-permute-start(bf16[1536,128]{1,0:T(8,128)(2,1)S(1)} %get-tuple-element.28.refs_3_), channel_id=1, source_target_pairs={{0,1},{1,2},{2,3},{3,4},{4,5},{5,6},{6,7},{7,0},{8,9},{9,10},{10,1... | collective-permute-start | bytes 1179656 | tf_op jit(solution)/shard_map/ppermute | solution.py:405
  23.6 4.0 %collective-permute-start.6 = (bf16[1536,128]{1,0:T(8,128)(2,1)S(1)}, bf16[1536,128]{1,0:T(8,128)(2,1)S(1)}, u32[]{:S(2)}, u32[]{:S(2)}) collective-permute-start(bf16[1536,128]{1,0:T(8,128)(2,1)S(1)} %get-tuple-element.28.refs_3_), channel_id=1, source_target_pairs={{0,7},{1,0},{2,1},{3,2},{4,3},{5,4},{6,5},{7,6},{8,15},{9,8},{10,9... | collective-permute-start | bytes 1179656 | tf_op jit(solution)/shard_map/ppermute | solution.py:406
  27.6 1.7 %collective-permute-start.1 = (bf16[8,96,128]{2,1,0:T(8,128)(2,1)S(1)}, bf16[8,96,128]{2,1,0:T(8,128)(2,1)S(1)}, u32[]{:S(2)}, u32[]{:S(2)}) collective-permute-start(bf16[8,96,128]{2,1,0:T(8,128)(2,1)S(1)} %get-tuple-element.27.refs_1_), channel_id=1, source_target_pairs={{0,64},{64,0},{1,65},{65,1},{2,66},{66,2},{3,67},{67,3},{4,68},{68... | collective-permute-start | bytes 589832 | tf_op jit(solution)/shard_map/ppermute | solution.py:389
  29.4 0.0 copy-done.5
  29.4 0.0 collective-permute-start.10
  29.4 1.1 %collective-permute-done.1.refs_2_ = bf16[8,96,128]{2,1,0:T(8,128)(2,1)S(1)} collective-permute-done((bf16[8,96,128]{2,1,0:T(8,128)(2,1)S(1)}, bf16[8,96,128]{2,1,0:T(8,128)(2,1)S(1)}, u32[]{:S(2)}, u32[]{:S(2)}) %collective-permute-start.1) | collective-permute-done | bytes 196640 | tf_op jit(solution)/shard_map/ppermute | solution.py:389
  30.4 2.1 %shard_map.116 = (bf16[128,1536]{1,0:T(8,128)(2,1)S(1)}, f32[8,1536]{1,0:T(8,128)S(1)}, f32[144,1536]{1,0:T(8,128)S(1)}) custom-call(s32[10]{0:T(128)S(1)} %stack.40.place.refs_0_, bf16[8,96,128]{2,1,0:T(8,128)(2,1)S(1)} %get-tuple-element.27.refs_1_, bf16[8,96,128]{2,1,0:T(8,128)(2,1)S(1)} %collective-permute-done.1.refs_2_, ...), custom_call_target="tpu_custom_call" | custom-call | flops 301989888 | bytes 3000000 | tf_op jit(solution)/shard_map/pallas_call | solution.py:244
  32.5 0.0 collective-permute-done.10.other_flow
  32.5 0.7 shard_map.118
  33.2 1.1 %collective-permute-start.11 = (bf16[256,1024]{1,0:T(8,128)(2,1)S(1)}, bf16[256,1024]{1,0:T(8,128)(2,1)S(1)}, u32[]{:S(2)}, u32[]{:S(2)}) collective-permute-start(bf16[256,1024]{1,0:T(8,128)(2,1)S(1)} %shard_map.118), channel_id=1, source_target_pairs={{0,56},{8,48},{16,40},{24,32},{32,24},{40,16},{48,8},{56,0},{1,57}... | collective-permute-start | bytes 1572872 | tf_op jit(solution)/shard_map/ppermute | solution.py:402
  34.3 1.2 %collective-permute-done.2.refs_2_ = bf16[1536,128]{1,0:T(8,128)(2,1)S(1)} collective-permute-done((bf16[1536,128]{1,0:T(8,128)(2,1)S(1)}, bf16[1536,128]{1,0:T(8,128)(2,1)S(1)}, u32[]{:S(2)}, u32[]{:S(2)}) %collective-permute-start.2) | collective-permute-done | bytes 393248 | tf_op jit(solution)/shard_map/ppermute | solution.py:405
  35.5 0.0 collective-permute-start.3
  35.5 0.0 collective-permute-done.6.refs_3_
  35.5 2.7 %collective-permute-start.7 = (bf16[1536,128]{1,0:T(8,128)(2,1)S(1)}, bf16[1536,128]{1,0:T(8,128)(2,1)S(1)}, u32[]{:S(2)}, u32[]{:S(2)}) collective-permute-start(bf16[1536,128]{1,0:T(8,128)(2,1)S(1)} %collective-permute-done.6.refs_3_), channel_id=1, source_target_pairs={{0,7},{1,0},{2,1},{3,2},{4,3},{5,4},{6,5},{7,6},{8,15},{9,8},{10,9... | collective-permute-start | bytes 1179656 | tf_op jit(solution)/shard_map/ppermute | solution.py:406
  38.2 3.1 %shard_map.117 = (f32[8,1536]{1,0:T(8,128)S(1)}, f32[144,1536]{1,0:T(8,128)S(1)}) custom-call(s32[10]{0:T(128)S(1)} %stack.40.place.refs_0_, bf16[128,1536]{1,0:T(8,128)(2,1)S(1)} %get-tuple-element.29.refs_1_, bf16[1536,128]{1,0:T(8,128)(2,1)S(1)} %collective-permute-done.2.refs_2_, bf16[1536,128]{1,0:T(8,128)(2,1)S(1)} %collective-permute-done.6.refs_3_, ...), custom_call_target="tpu_custom_call" | custom-call | flops 4831838208 | bytes 3000000 | tf_op jit(solution)/shard_map/pallas_call | solution.py:244
  41.3 4.0 %collective-permute-done.3.refs_2_ = bf16[1536,128]{1,0:T(8,128)(2,1)S(1)} collective-permute-done((bf16[1536,128]{1,0:T(8,128)(2,1)S(1)}, bf16[1536,128]{1,0:T(8,128)(2,1)S(1)}, u32[]{:S(2)}, u32[]{:S(2)}) %collective-permute-start.3) | collective-permute-done | bytes 393248 | tf_op jit(solution)/shard_map/ppermute | solution.py:405
  45.2 0.0 collective-permute-start.4
  45.2 0.0 collective-permute-done.7.refs_3_
  45.2 2.7 %collective-permute-start.8 = (bf16[1536,128]{1,0:T(8,128)(2,1)S(1)}, bf16[1536,128]{1,0:T(8,128)(2,1)S(1)}, u32[]{:S(2)}, u32[]{:S(2)}) collective-permute-start(bf16[1536,128]{1,0:T(8,128)(2,1)S(1)} %collective-permute-done.7.refs_3_), channel_id=1, source_target_pairs={{0,7},{1,0},{2,1},{3,2},{4,3},{5,4},{6,5},{7,6},{8,15},{9,8},{10,9... | collective-permute-start | bytes 1179656 | tf_op jit(solution)/shard_map/ppermute | solution.py:406
  47.9 0.6 collective-permute-done.11.refs_6_.both
  48.5 3.1 %shard_map.119 = (f32[8,1536]{1,0:T(8,128)S(1)}, f32[144,1536]{1,0:T(8,128)S(1)}) custom-call(s32[10]{0:T(128)S(1)} %stack.40.place.refs_0_, bf16[128,1536]{1,0:T(8,128)(2,1)S(1)} %get-tuple-element.29.refs_1_, bf16[1536,128]{1,0:T(8,128)(2,1)S(1)} %collective-permute-done.3.refs_2_, bf16[1536,128]{1,0:T(8,128)(2,1)S(1)} %collective-permute-done.7.refs_3_, ...), custom_call_target="tpu_custom_call" | custom-call | flops 4831838208 | bytes 3000000 | tf_op jit(solution)/shard_map/pallas_call | solution.py:244
  51.6 2.5 %collective-permute-done.4.refs_2_ = bf16[1536,128]{1,0:T(8,128)(2,1)S(1)} collective-permute-done((bf16[1536,128]{1,0:T(8,128)(2,1)S(1)}, bf16[1536,128]{1,0:T(8,128)(2,1)S(1)}, u32[]{:S(2)}, u32[]{:S(2)}) %collective-permute-start.4) | collective-permute-done | bytes 393248 | tf_op jit(solution)/shard_map/ppermute | solution.py:405
  54.0 0.1 collective-permute-start.5
  54.1 0.0 collective-permute-done.8.refs_3_
  54.2 2.7 %collective-permute-start.9 = (bf16[768,128]{1,0:T(8,128)(2,1)S(1)}, bf16[768,128]{1,0:T(8,128)(2,1)S(1)}, u32[]{:S(2)}, u32[]{:S(2)}) collective-permute-start(bf16[768,128]{1,0:T(8,128)(2,1)S(1)} %slice.9), channel_id=1, source_target_pairs={{0,7},{1,0},{2,1},{3,2},{4,3},{5,4},{6,5},{7,6},{8,15},{9,8},{10,9... | collective-permute-start | bytes 589832 | tf_op jit(solution)/shard_map/ppermute | solution.py:418
  56.9 3.1 %shard_map.120 = (f32[8,1536]{1,0:T(8,128)S(1)}, f32[144,1536]{1,0:T(8,128)S(1)}) custom-call(s32[10]{0:T(128)S(1)} %stack.40.place.refs_0_, bf16[128,1536]{1,0:T(8,128)(2,1)S(1)} %get-tuple-element.29.refs_1_, bf16[1536,128]{1,0:T(8,128)(2,1)S(1)} %collective-permute-done.4.refs_2_, bf16[1536,128]{1,0:T(8,128)(2,1)S(1)} %collective-permute-done.8.refs_3_, ...), custom_call_target="tpu_custom_call" | custom-call | flops 4831838208 | bytes 3000000 | tf_op jit(solution)/shard_map/pallas_call | solution.py:244
  60.0 0.0 collective-permute-done.5.refs_2_
  60.0 0.0 collective-permute-done.9.refs_3_
  60.0 0.0 copy-start
  60.0 0.0 copy-start.1
  60.0 0.0 copy-start.2
  60.0 0.0 copy-start.3
  60.0 0.0 copy-start.4
  60.0 2.3 %shard_map.121 = (bf16[8,96,256]{2,1,0:T(8,128)(2,1)S(1)}, bf16[8,96,256]{2,1,0:T(8,128)(2,1)S(1)}) custom-call(s32[10]{0:T(128)S(1)} %stack.40.place.refs_0_, bf16[128,1536]{1,0:T(8,128)(2,1)S(1)} %get-tuple-element.29.refs_1_, bf16[768,128]{1,0:T(8,128)(2,1)S(1)} %collective-permute-done.5.refs_2_, bf16[768,128]{1,0:T(8,128)(2,1)S(1)} %collective-permute-done.9.refs_3_, ...), custom_call_target="tpu_custom_call" | custom-call | flops 2415919104 | bytes 3000000 | tf_op jit(solution)/shard_map/pallas_call | solution.py:244
  62.4 5.0 %collective-permute-start.12 = (bf16[8,96,256]{2,1,0:T(8,128)(2,1)S(1)}, bf16[8,96,256]{2,1,0:T(8,128)(2,1)S(1)}, u32[]{:S(2)}, u32[]{:S(2)}) collective-permute-start(bf16[8,96,256]{2,1,0:T(8,128)(2,1)S(1)} %get-tuple-element.39), channel_id=1, source_target_pairs={{0,64},{64,0},{1,65},{65,1},{2,66},{66,2},{3,67},{67,3},{4,68},{68... | collective-permute-start | bytes 1179656 | tf_op jit(solution)/shard_map/ppermute | solution.py:421
  67.4 1.3 %collective-permute-done.12.theirs = bf16[8,96,256]{2,1,0:T(8,128)(2,1)S(1)} collective-permute-done((bf16[8,96,256]{2,1,0:T(8,128)(2,1)S(1)}, bf16[8,96,256]{2,1,0:T(8,128)(2,1)S(1)}, u32[]{:S(2)}, u32[]{:S(2)}) %collective-permute-start.12) | collective-permute-done | bytes 393248 | tf_op jit(solution)/shard_map/ppermute | solution.py:421
  68.7 0.3 shard_map.122
  69.1 10.3 %all_to_all.11.attended = bf16[8,96,128]{2,1,0:T(8,128)(2,1)S(1)} all-to-all(bf16[8,96,128]{2,1,0:T(8,128)(2,1)S(1)} %shard_map.122), channel_id=1, replica_groups=mesh['xh'=2,'core'=2,'xl'=2,'y'=4,'z'=8] {'xl','y'}, dimensions={0} | all-to-all | bytes 393216 | tf_op jit(solution)/shard_map/all_to_all | solution.py:429
  79.4 0.0 copy-done
  79.4 0.0 copy-done.1
  79.4 0.0 copy-done.2
  79.4 0.0 copy-done.3
  79.4 0.0 copy-done.4
  79.4 3.8 %shard_map.123 = (bf16[80,96]{1,0:T(8,128)(2,1)S(1)}, bf16[80,96]{1,0:T(8,128)(2,1)S(1)}) custom-call(s32[10]{0:T(128)S(1)} %stack.40.place.refs_0_, bf16[8,96,128]{2,1,0:T(8,128)(2,1)S(1)} %all_to_all.11.attended, bf16[256,1024]{1,0:T(8,128)(2,1)S(1)} %collective-permute-done.11.refs_6_.both, bf16[512,1024]{1,0:T(8,128)(2,1)S(1)} %copy-done.2, ...), custom_call_target="tpu_custom_call" | custom-call | tf_op jit(solution)/shard_map/pallas_call | solution.py:432
  83.2 1.8 %collective-permute-start.13 = (bf16[80,96]{1,0:T(8,128)(2,1)S(1)}, bf16[80,96]{1,0:T(8,128)(2,1)S(1)}, u32[]{:S(2)}, u32[]{:S(2)}) collective-permute-start(bf16[80,96]{1,0:T(8,128)(2,1)S(1)} %get-tuple-element.41), channel_id=1, source_target_pairs={{0,64},{64,0},{1,65},{65,1},{2,66},{66,2},{3,67},{67,3},{4,68},{68... | collective-permute-start | bytes 46088 | tf_op jit(solution)/shard_map/ppermute | solution.py:448
  84.9 0.8 collective-permute-done.13.theirs
  85.8 0.7 shard_map.124
  86.5 3.1 %collective-permute-start.14 = (bf16[80,192]{1,0:T(8,128)(2,1)S(1)}, bf16[80,192]{1,0:T(8,128)(2,1)S(1)}, u32[]{:S(2)}, u32[]{:S(2)}) collective-permute-start(bf16[80,192]{1,0:T(8,128)(2,1)S(1)} %shard_map.124), channel_id=1, source_target_pairs={{0,7},{1,6},{2,5},{3,4},{4,3},{5,2},{6,1},{7,0},{8,15},{9,14},{10,... | collective-permute-start | bytes 92168 | tf_op jit(solution)/shard_map/ppermute | solution.py:456
  89.6 1.5 %collective-permute-done.14.block = bf16[80,192]{1,0:T(8,128)(2,1)S(1)} collective-permute-done((bf16[80,192]{1,0:T(8,128)(2,1)S(1)}, bf16[80,192]{1,0:T(8,128)(2,1)S(1)}, u32[]{:S(2)}, u32[]{:S(2)}) %collective-permute-start.14) | collective-permute-done | bytes 30752 | tf_op jit(solution)/shard_map/ppermute | solution.py:456
  91.1 0.6 shard_map.125
  (2 shorter events, 0.0 us)
Async XLA Ops:
  0.6 6.0 %collective-permute-start = (bf16[192,1024]{1,0:T(8,128)(2,1)}, bf16[192,1024]{1,0:T(8,128)(2,1)S(1)}, u32[]{:S(2)}, u32[]{:S(2)}) collective-permute-start(bf16[192,1024]{1,0:T(8,128)(2,1)} %hidden.1), channel_id=1, source_target_pairs={{0,64},{64,0},{1,65},{65,1},{2,66},{66,2},{3,67},{67,3},{4,68},{68... | collective-permute-start | bytes 1179656 | tf_op jit(solution)/shard_map/ppermute | solution.py:357
  4.0 25.3 %copy-start.5 = (bf16[64,192]{1,0:T(8,128)(2,1)S(1)}, bf16[64,192]{1,0:T(8,128)(2,1)}, u32[]{:S(2)}) copy-start(bf16[64,192]{1,0:T(8,128)(2,1)} %flow.1) | copy-start | bytes 73732
  21.9 13.6 %collective-permute-start.2 = (bf16[1536,128]{1,0:T(8,128)(2,1)S(1)}, bf16[1536,128]{1,0:T(8,128)(2,1)S(1)}, u32[]{:S(2)}, u32[]{:S(2)}) collective-permute-start(bf16[1536,128]{1,0:T(8,128)(2,1)S(1)} %get-tuple-element.28.refs_3_), channel_id=1, source_target_pairs={{0,1},{1,2},{2,3},{3,4},{4,5},{5,6},{6,7},{7,0},{8,9},{9,10},{10,1... | collective-permute-start | bytes 1179656 | tf_op jit(solution)/shard_map/ppermute | solution.py:405
  23.6 11.9 %collective-permute-start.6 = (bf16[1536,128]{1,0:T(8,128)(2,1)S(1)}, bf16[1536,128]{1,0:T(8,128)(2,1)S(1)}, u32[]{:S(2)}, u32[]{:S(2)}) collective-permute-start(bf16[1536,128]{1,0:T(8,128)(2,1)S(1)} %get-tuple-element.28.refs_3_), channel_id=1, source_target_pairs={{0,7},{1,0},{2,1},{3,2},{4,3},{5,4},{6,5},{7,6},{8,15},{9,8},{10,9... | collective-permute-start | bytes 1179656 | tf_op jit(solution)/shard_map/ppermute | solution.py:406
  27.6 2.8 %collective-permute-start.1 = (bf16[8,96,128]{2,1,0:T(8,128)(2,1)S(1)}, bf16[8,96,128]{2,1,0:T(8,128)(2,1)S(1)}, u32[]{:S(2)}, u32[]{:S(2)}) collective-permute-start(bf16[8,96,128]{2,1,0:T(8,128)(2,1)S(1)} %get-tuple-element.27.refs_1_), channel_id=1, source_target_pairs={{0,64},{64,0},{1,65},{65,1},{2,66},{66,2},{3,67},{67,3},{4,68},{68... | collective-permute-start | bytes 589832 | tf_op jit(solution)/shard_map/ppermute | solution.py:389
  29.4 3.2 %collective-permute-start.10 = (bf16[64,192]{1,0:T(8,128)(2,1)S(1)}, bf16[64,192]{1,0:T(8,128)(2,1)S(1)}, u32[]{:S(2)}, u32[]{:S(2)}) collective-permute-start(bf16[64,192]{1,0:T(8,128)(2,1)S(1)} %copy-done.5), channel_id=1, source_target_pairs={{0,64},{64,0},{1,65},{65,1},{2,66},{66,2},{3,67},{67,3},{4,68},{68... | collective-permute-start | bytes 73736 | tf_op jit(solution)/shard_map/ppermute | solution.py:358
  33.2 15.3 %collective-permute-start.11 = (bf16[256,1024]{1,0:T(8,128)(2,1)S(1)}, bf16[256,1024]{1,0:T(8,128)(2,1)S(1)}, u32[]{:S(2)}, u32[]{:S(2)}) collective-permute-start(bf16[256,1024]{1,0:T(8,128)(2,1)S(1)} %shard_map.118), channel_id=1, source_target_pairs={{0,56},{8,48},{16,40},{24,32},{32,24},{40,16},{48,8},{56,0},{1,57}... | collective-permute-start | bytes 1572872 | tf_op jit(solution)/shard_map/ppermute | solution.py:402
  35.5 9.7 %collective-permute-start.3 = (bf16[1536,128]{1,0:T(8,128)(2,1)S(1)}, bf16[1536,128]{1,0:T(8,128)(2,1)S(1)}, u32[]{:S(2)}, u32[]{:S(2)}) collective-permute-start(bf16[1536,128]{1,0:T(8,128)(2,1)S(1)} %collective-permute-done.2.refs_2_), channel_id=1, source_target_pairs={{0,1},{1,2},{2,3},{3,4},{4,5},{5,6},{6,7},{7,0},{8,9},{9,10},{10,1... | collective-permute-start | bytes 1179656 | tf_op jit(solution)/shard_map/ppermute | solution.py:405
  35.5 9.7 %collective-permute-start.7 = (bf16[1536,128]{1,0:T(8,128)(2,1)S(1)}, bf16[1536,128]{1,0:T(8,128)(2,1)S(1)}, u32[]{:S(2)}, u32[]{:S(2)}) collective-permute-start(bf16[1536,128]{1,0:T(8,128)(2,1)S(1)} %collective-permute-done.6.refs_3_), channel_id=1, source_target_pairs={{0,7},{1,0},{2,1},{3,2},{4,3},{5,4},{6,5},{7,6},{8,15},{9,8},{10,9... | collective-permute-start | bytes 1179656 | tf_op jit(solution)/shard_map/ppermute | solution.py:406
  45.2 8.8 %collective-permute-start.4 = (bf16[1536,128]{1,0:T(8,128)(2,1)S(1)}, bf16[1536,128]{1,0:T(8,128)(2,1)S(1)}, u32[]{:S(2)}, u32[]{:S(2)}) collective-permute-start(bf16[1536,128]{1,0:T(8,128)(2,1)S(1)} %collective-permute-done.3.refs_2_), channel_id=1, source_target_pairs={{0,1},{1,2},{2,3},{3,4},{4,5},{5,6},{6,7},{7,0},{8,9},{9,10},{10,1... | collective-permute-start | bytes 1179656 | tf_op jit(solution)/shard_map/ppermute | solution.py:405
  45.2 8.9 %collective-permute-start.8 = (bf16[1536,128]{1,0:T(8,128)(2,1)S(1)}, bf16[1536,128]{1,0:T(8,128)(2,1)S(1)}, u32[]{:S(2)}, u32[]{:S(2)}) collective-permute-start(bf16[1536,128]{1,0:T(8,128)(2,1)S(1)} %collective-permute-done.7.refs_3_), channel_id=1, source_target_pairs={{0,7},{1,0},{2,1},{3,2},{4,3},{5,4},{6,5},{7,6},{8,15},{9,8},{10,9... | collective-permute-start | bytes 1179656 | tf_op jit(solution)/shard_map/ppermute | solution.py:406
  54.0 5.9 %collective-permute-start.5 = (bf16[768,128]{1,0:T(8,128)(2,1)S(1)}, bf16[768,128]{1,0:T(8,128)(2,1)S(1)}, u32[]{:S(2)}, u32[]{:S(2)}) collective-permute-start(bf16[768,128]{1,0:T(8,128)(2,1)S(1)} %slice.8), channel_id=1, source_target_pairs={{0,1},{1,2},{2,3},{3,4},{4,5},{5,6},{6,7},{7,0},{8,9},{9,10},{10,1... | collective-permute-start | bytes 589832 | tf_op jit(solution)/shard_map/ppermute | solution.py:417
  54.2 5.8 %collective-permute-start.9 = (bf16[768,128]{1,0:T(8,128)(2,1)S(1)}, bf16[768,128]{1,0:T(8,128)(2,1)S(1)}, u32[]{:S(2)}, u32[]{:S(2)}) collective-permute-start(bf16[768,128]{1,0:T(8,128)(2,1)S(1)} %slice.9), channel_id=1, source_target_pairs={{0,7},{1,0},{2,1},{3,2},{4,3},{5,4},{6,5},{7,6},{8,15},{9,8},{10,9... | collective-permute-start | bytes 589832 | tf_op jit(solution)/shard_map/ppermute | solution.py:418
  60.0 19.4 %copy-start = (bf16[1024,2048]{1,0:T(8,128)(2,1)S(1)}, bf16[1024,2048]{1,0:T(8,128)(2,1)}, u32[]{:S(2)}) copy-start(bf16[1024,2048]{1,0:T(8,128)(2,1)} %w_up.1) | copy-start | bytes 12582916
  60.0 19.4 %copy-start.1 = (bf16[2048,1024]{1,0:T(8,128)(2,1)S(1)}, bf16[2048,1024]{1,0:T(8,128)(2,1)}, u32[]{:S(2)}) copy-start(bf16[2048,1024]{1,0:T(8,128)(2,1)} %w_down.1) | copy-start | bytes 12582916
  60.0 19.4 %copy-start.2 = (bf16[512,1024]{1,0:T(8,128)(2,1)S(1)}, bf16[512,1024]{1,0:T(8,128)(2,1)}, u32[]{:S(2)}) copy-start(bf16[512,1024]{1,0:T(8,128)(2,1)} %w_output.1) | copy-start | bytes 3145732
  60.0 19.4 %copy-start.3 = (bf16[64,1024]{1,0:T(8,128)(2,1)S(1)}, bf16[64,1024]{1,0:T(8,128)(2,1)}, u32[]{:S(2)}) copy-start(bf16[64,1024]{1,0:T(8,128)(2,1)} %w_shift.1) | copy-start | bytes 393220
  60.0 19.4 %copy-start.4 = (bf16[64,1024]{1,0:T(8,128)(2,1)S(1)}, bf16[64,1024]{1,0:T(8,128)(2,1)}, u32[]{:S(2)}) copy-start(bf16[64,1024]{1,0:T(8,128)(2,1)} %w_scale.1) | copy-start | bytes 393220
  62.4 6.4 %collective-permute-start.12 = (bf16[8,96,256]{2,1,0:T(8,128)(2,1)S(1)}, bf16[8,96,256]{2,1,0:T(8,128)(2,1)S(1)}, u32[]{:S(2)}, u32[]{:S(2)}) collective-permute-start(bf16[8,96,256]{2,1,0:T(8,128)(2,1)S(1)} %get-tuple-element.39), channel_id=1, source_target_pairs={{0,64},{64,0},{1,65},{65,1},{2,66},{66,2},{3,67},{67,3},{4,68},{68... | collective-permute-start | bytes 1179656 | tf_op jit(solution)/shard_map/ppermute | solution.py:421
  83.2 2.6 %collective-permute-start.13 = (bf16[80,96]{1,0:T(8,128)(2,1)S(1)}, bf16[80,96]{1,0:T(8,128)(2,1)S(1)}, u32[]{:S(2)}, u32[]{:S(2)}) collective-permute-start(bf16[80,96]{1,0:T(8,128)(2,1)S(1)} %get-tuple-element.41), channel_id=1, source_target_pairs={{0,64},{64,0},{1,65},{65,1},{2,66},{66,2},{3,67},{67,3},{4,68},{68... | collective-permute-start | bytes 46088 | tf_op jit(solution)/shard_map/ppermute | solution.py:448
  86.5 4.6 %collective-permute-start.14 = (bf16[80,192]{1,0:T(8,128)(2,1)S(1)}, bf16[80,192]{1,0:T(8,128)(2,1)S(1)}, u32[]{:S(2)}, u32[]{:S(2)}) collective-permute-start(bf16[80,192]{1,0:T(8,128)(2,1)S(1)} %shard_map.124), channel_id=1, source_target_pairs={{0,7},{1,6},{2,5},{3,4},{4,3},{5,2},{6,1},{7,0},{8,15},{9,14},{10,... | collective-permute-start | bytes 92168 | tf_op jit(solution)/shard_map/ppermute | solution.py:456

commit v8 on v7

--- a/solution.py
+++ b/solution.py
@@ -93,7 +93,8 @@
     rows = pl.ds(pl.multiple_of(core * PIECE, PIECE), PIECE)
     normed[PIECE:, :] = layer_norm(other[rows, :].astype(f32)).astype(bf16)
     for column, weight in enumerate((w_query, w_key, w_value)):
-        made = jnp.dot(normed[...], weight[...], preferred_element_type=f32).astype(bf16)
+        made = jnp.dot(normed[...], weight[...], preferred_element_type=f32)
+        made = (made * POWER if column == 0 else made).astype(bf16)
         for part in range(2):
             sequence = core if part == 0 else 1 - core
             for head in range(HEADS):
@@ -196,9 +197,9 @@
         if first:
             sums = jnp.zeros((TALL, TILE), f32)
         else:
-            sums = numer_in[:, columns] * jnp.exp2((top - new_top) * POWER)
+            sums = numer_in[:, columns] * jnp.exp2(top - new_top)
         for value, product in found:
-            weights = jnp.exp2((product - new_top) * POWER).astype(bf16)
+            weights = jnp.exp2(product - new_top).astype(bf16)
             sums = sums + jnp.dot(value, weights, preferred_element_type=f32)
         if not last:
             top_out, numer_out = refs
@@ -209,7 +210,7 @@
         some = total > 0
         total = jnp.where(some, total, 1.0)
         mixed = (sums[:HEAD, :] / total).T
-        level = jnp.where(some, new_top * POWER + jnp.log2(total), lowest)
+        level = jnp.where(some, new_top + jnp.log2(total), lowest)
         level = jnp.broadcast_to(level, (HEAD, TILE)).T
         high = level.astype(bf16)
         rest = level - high.astype(f32)
@@ -223,11 +224,11 @@
                 refs[side][2 * tile + plane, :, :HEAD] = mixed[start : start + PIECE].astype(bf16)
                 refs[side][2 * tile + plane, :, HEAD:] = level[start : start + PIECE]
 
-    found = score(0)
+    ahead = [score(0), score(1)]
     for tile in range(TILES):
-        following = score(tile + 1) if tile + 1 < TILES else None
-        finish(tile, found)
-        found = following
+        if tile + 2 < TILES:
+            ahead.append(score(tile + 2))
+        finish(tile, ahead.pop(0))
 
 
 def attend(place, queries, segments, chunks, state, last, after=()):

time: 91.9 us -> 91.6 us (level)
  Pallas kernels: 23.9 us -> 22.9 us
    pallas_call x5, Pallas kernels: 13.6 us -> 12.5 us  [attend(): pl.pallas_call(functools.partial(attend_kernel, chunks, first, last, len(...]
  transfers between devices with their start and end apart: 15 -> 15, of which waited for: 8 -> 9; matrix products, arithmetic and copies ran while one was open for 0% -> 0% of each run, Pallas kernels for 16% -> 15%
where the time goes in v8:
time: 91.6 us; the launch traced here: 91.5 us
  starting transfers between devices  30.1 us (33%)
  blocking collectives  23.9 us (26%)
  Pallas kernels  22.9 us (25%)
  waiting for transfers between devices  13.6 us (15%)
    all_to_all x1, blocking collectives, on_device(): slots = lax.all_to_all(slots, ('xl', 'y'), 0, 0, tiled=True)  13.6 us
    pallas_call x5, Pallas kernels, attend(): pl.pallas_call(functools.partial(attend_kernel, chunks, first, last, len(...  12.5 us
    all_to_all x1, blocking collectives, on_device(): attended = lax.all_to_all(attended, ('xl', 'y'), 0, 0, tiled=True)  10.3 us
    ppermute x3, starting transfers between devices, on_device(): down = lax.ppermute(down, 'z', shift_by(Z, -1))  9.37 us
    ppermute x3, waiting for transfers between devices, on_device(): up = lax.ppermute(up, 'z', shift_by(Z, 1))  8.32 us
    ppermute x1, starting transfers between devices, on_device(): theirs = lax.ppermute(others, 'core', other_core)  5.18 us
    pallas_call x1, Pallas kernels, on_device(): pl.pallas_call(dense_kernel, out_shape=[sent, sent], in_specs=[smem()] +...  3.77 us
    ppermute x1, starting transfers between devices, on_device(): other = lax.ppermute(hidden, 'core', other_core)  3.33 us
  transfers between devices with their start and end apart: 15, of which 9 were waited for; matrix products, arithmetic and copies ran while one was open for 0% of the time, Pallas kernels for 15%

profile of v8, /device:TPU:1, one launch (start us, length us, event | category | flops | bytes accessed | tf_op | source)
XLA Modules:
  0.0 91.5 jit_solution(7656787155727008006)
XLA Ops:
  0.6 3.3 %collective-permute-start = (bf16[192,1024]{1,0:T(8,128)(2,1)}, bf16[192,1024]{1,0:T(8,128)(2,1)S(1)}, u32[]{:S(2)}, u32[]{:S(2)}) collective-permute-start(bf16[192,1024]{1,0:T(8,128)(2,1)} %hidden.1), channel_id=1, source_target_pairs={{0,64},{64,0},{1,65},{65,1},{2,66},{66,2},{3,67},{67,3},{4,68},{68... | collective-permute-start | bytes 1179656 | tf_op jit(solution)/shard_map/ppermute | solution.py:358
  4.0 0.1 stack.40.place.refs_0_
  4.0 0.0 copy-start.5
  4.0 2.5 %shard_map.113 = (bf16[96,1024]{1,0:T(8,128)(2,1)S(1)}, bf16[1024,512]{1,0:T(8,128)(2,1)S(1)}, bf16[1024,512]{1,0:T(8,128)(2,1)S(1)}, bf16[1024,512]{1,0:T(8,128)(2,1)S(1)}) custom-call(s32[10]{0:T(128)S(1)} %stack.40.place.refs_0_, bf16[192,1024]{1,0:T(8,128)(2,1)} %hidden.1, bf16[1024,512]{1,0:T(8,128)(2,1)} %w_query.1, bf16[1024,512]{1,0:T(8,128)(2,1)} %w_key.1, ...), custom_call_target="tpu_custom_call" | custom-call | bytes 6600000 | tf_op jit(solution)/shard_map/pallas_call | solution.py:362
  6.6 0.0 collective-permute-done.other
  6.6 1.6 %shard_map.114 = bf16[8,96,384]{2,1,0:T(8,128)(2,1)S(1)} custom-call(s32[10]{0:T(128)S(1)} %stack.40.place.refs_0_, bf16[96,1024]{1,0:T(8,128)(2,1)S(1)} %get-tuple-element.23.own, bf16[192,1024]{1,0:T(8,128)(2,1)S(1)} %collective-permute-done.other, bf16[1024,512]{1,0:T(8,128)(2,1)S(1)} %get-tuple-element.24.w_query, ...), custom_call_target="tpu_custom_call" | custom-call | tf_op jit(solution)/shard_map/pallas_call | solution.py:371
  8.2 13.6 %all_to_all.10.slots = bf16[8,96,384]{2,1,0:T(8,128)(2,1)S(1)} all-to-all(bf16[8,96,384]{2,1,0:T(8,128)(2,1)S(1)} %shard_map.114), channel_id=1, replica_groups=mesh['xh'=2,'core'=2,'xl'=2,'y'=4,'z'=8] {'xl','y'}, dimensions={0} | all-to-all | bytes 1179648 | tf_op jit(solution)/shard_map/all_to_all | solution.py:379
  21.8 0.1 shard_map.115
  21.9 1.7 %collective-permute-start.2 = (bf16[1536,128]{1,0:T(8,128)(2,1)S(1)}, bf16[1536,128]{1,0:T(8,128)(2,1)S(1)}, u32[]{:S(2)}, u32[]{:S(2)}) collective-permute-start(bf16[1536,128]{1,0:T(8,128)(2,1)S(1)} %get-tuple-element.28.refs_3_), channel_id=1, source_target_pairs={{0,1},{1,2},{2,3},{3,4},{4,5},{5,6},{6,7},{7,0},{8,9},{9,10},{10,1... | collective-permute-start | bytes 1179656 | tf_op jit(solution)/shard_map/ppermute | solution.py:406
  23.6 4.0 %collective-permute-start.6 = (bf16[1536,128]{1,0:T(8,128)(2,1)S(1)}, bf16[1536,128]{1,0:T(8,128)(2,1)S(1)}, u32[]{:S(2)}, u32[]{:S(2)}) collective-permute-start(bf16[1536,128]{1,0:T(8,128)(2,1)S(1)} %get-tuple-element.28.refs_3_), channel_id=1, source_target_pairs={{0,7},{1,0},{2,1},{3,2},{4,3},{5,4},{6,5},{7,6},{8,15},{9,8},{10,9... | collective-permute-start | bytes 1179656 | tf_op jit(solution)/shard_map/ppermute | solution.py:407
  27.6 1.7 %collective-permute-start.1 = (bf16[8,96,128]{2,1,0:T(8,128)(2,1)S(1)}, bf16[8,96,128]{2,1,0:T(8,128)(2,1)S(1)}, u32[]{:S(2)}, u32[]{:S(2)}) collective-permute-start(bf16[8,96,128]{2,1,0:T(8,128)(2,1)S(1)} %get-tuple-element.27.refs_1_), channel_id=1, source_target_pairs={{0,64},{64,0},{1,65},{65,1},{2,66},{66,2},{3,67},{67,3},{4,68},{68... | collective-permute-start | bytes 589832 | tf_op jit(solution)/shard_map/ppermute | solution.py:390
  29.4 0.0 copy-done.5
  29.4 0.0 collective-permute-start.10
  29.4 1.1 %collective-permute-done.1.refs_2_ = bf16[8,96,128]{2,1,0:T(8,128)(2,1)S(1)} collective-permute-done((bf16[8,96,128]{2,1,0:T(8,128)(2,1)S(1)}, bf16[8,96,128]{2,1,0:T(8,128)(2,1)S(1)}, u32[]{:S(2)}, u32[]{:S(2)}) %collective-permute-start.1) | collective-permute-done | bytes 196640 | tf_op jit(solution)/shard_map/ppermute | solution.py:390
  30.4 1.9 %shard_map.116 = (bf16[128,1536]{1,0:T(8,128)(2,1)S(1)}, f32[8,1536]{1,0:T(8,128)S(1)}, f32[144,1536]{1,0:T(8,128)S(1)}) custom-call(s32[10]{0:T(128)S(1)} %stack.40.place.refs_0_, bf16[8,96,128]{2,1,0:T(8,128)(2,1)S(1)} %get-tuple-element.27.refs_1_, bf16[8,96,128]{2,1,0:T(8,128)(2,1)S(1)} %collective-permute-done.1.refs_2_, ...), custom_call_target="tpu_custom_call" | custom-call | flops 301989888 | bytes 3000000 | tf_op jit(solution)/shard_map/pallas_call | solution.py:245
  32.4 0.0 collective-permute-done.10.other_flow
  32.4 0.7 shard_map.118
  33.1 1.1 %collective-permute-start.11 = (bf16[256,1024]{1,0:T(8,128)(2,1)S(1)}, bf16[256,1024]{1,0:T(8,128)(2,1)S(1)}, u32[]{:S(2)}, u32[]{:S(2)}) collective-permute-start(bf16[256,1024]{1,0:T(8,128)(2,1)S(1)} %shard_map.118), channel_id=1, source_target_pairs={{0,56},{8,48},{16,40},{24,32},{32,24},{40,16},{48,8},{56,0},{1,57}... | collective-permute-start | bytes 1572872 | tf_op jit(solution)/shard_map/ppermute | solution.py:403
  34.2 1.3 %collective-permute-done.2.refs_2_ = bf16[1536,128]{1,0:T(8,128)(2,1)S(1)} collective-permute-done((bf16[1536,128]{1,0:T(8,128)(2,1)S(1)}, bf16[1536,128]{1,0:T(8,128)(2,1)S(1)}, u32[]{:S(2)}, u32[]{:S(2)}) %collective-permute-start.2) | collective-permute-done | bytes 393248 | tf_op jit(solution)/shard_map/ppermute | solution.py:406
  35.5 0.0 collective-permute-start.3
  35.5 0.0 collective-permute-done.6.refs_3_
  35.5 2.7 %collective-permute-start.7 = (bf16[1536,128]{1,0:T(8,128)(2,1)S(1)}, bf16[1536,128]{1,0:T(8,128)(2,1)S(1)}, u32[]{:S(2)}, u32[]{:S(2)}) collective-permute-start(bf16[1536,128]{1,0:T(8,128)(2,1)S(1)} %collective-permute-done.6.refs_3_), channel_id=1, source_target_pairs={{0,7},{1,0},{2,1},{3,2},{4,3},{5,4},{6,5},{7,6},{8,15},{9,8},{10,9... | collective-permute-start | bytes 1179656 | tf_op jit(solution)/shard_map/ppermute | solution.py:407
  38.2 2.8 %shard_map.117 = (f32[8,1536]{1,0:T(8,128)S(1)}, f32[144,1536]{1,0:T(8,128)S(1)}) custom-call(s32[10]{0:T(128)S(1)} %stack.40.place.refs_0_, bf16[128,1536]{1,0:T(8,128)(2,1)S(1)} %get-tuple-element.29.refs_1_, bf16[1536,128]{1,0:T(8,128)(2,1)S(1)} %collective-permute-done.2.refs_2_, bf16[1536,128]{1,0:T(8,128)(2,1)S(1)} %collective-permute-done.6.refs_3_, ...), custom_call_target="tpu_custom_call" | custom-call | flops 4831838208 | bytes 3000000 | tf_op jit(solution)/shard_map/pallas_call | solution.py:245
  41.0 4.2 %collective-permute-done.3.refs_2_ = bf16[1536,128]{1,0:T(8,128)(2,1)S(1)} collective-permute-done((bf16[1536,128]{1,0:T(8,128)(2,1)S(1)}, bf16[1536,128]{1,0:T(8,128)(2,1)S(1)}, u32[]{:S(2)}, u32[]{:S(2)}) %collective-permute-start.3) | collective-permute-done | bytes 393248 | tf_op jit(solution)/shard_map/ppermute | solution.py:406
  45.2 0.0 collective-permute-start.4
  45.2 0.0 collective-permute-done.7.refs_3_
  45.2 2.7 %collective-permute-start.8 = (bf16[1536,128]{1,0:T(8,128)(2,1)S(1)}, bf16[1536,128]{1,0:T(8,128)(2,1)S(1)}, u32[]{:S(2)}, u32[]{:S(2)}) collective-permute-start(bf16[1536,128]{1,0:T(8,128)(2,1)S(1)} %collective-permute-done.7.refs_3_), channel_id=1, source_target_pairs={{0,7},{1,0},{2,1},{3,2},{4,3},{5,4},{6,5},{7,6},{8,15},{9,8},{10,9... | collective-permute-start | bytes 1179656 | tf_op jit(solution)/shard_map/ppermute | solution.py:407
  47.9 0.5 collective-permute-done.11.refs_6_.both
  48.4 2.8 %shard_map.119 = (f32[8,1536]{1,0:T(8,128)S(1)}, f32[144,1536]{1,0:T(8,128)S(1)}) custom-call(s32[10]{0:T(128)S(1)} %stack.40.place.refs_0_, bf16[128,1536]{1,0:T(8,128)(2,1)S(1)} %get-tuple-element.29.refs_1_, bf16[1536,128]{1,0:T(8,128)(2,1)S(1)} %collective-permute-done.3.refs_2_, bf16[1536,128]{1,0:T(8,128)(2,1)S(1)} %collective-permute-done.7.refs_3_, ...), custom_call_target="tpu_custom_call" | custom-call | flops 4831838208 | bytes 3000000 | tf_op jit(solution)/shard_map/pallas_call | solution.py:245
  51.2 2.8 %collective-permute-done.4.refs_2_ = bf16[1536,128]{1,0:T(8,128)(2,1)S(1)} collective-permute-done((bf16[1536,128]{1,0:T(8,128)(2,1)S(1)}, bf16[1536,128]{1,0:T(8,128)(2,1)S(1)}, u32[]{:S(2)}, u32[]{:S(2)}) %collective-permute-start.4) | collective-permute-done | bytes 393248 | tf_op jit(solution)/shard_map/ppermute | solution.py:406
  54.0 0.1 collective-permute-start.5
  54.1 0.0 collective-permute-done.8.refs_3_
  54.2 2.7 %collective-permute-start.9 = (bf16[768,128]{1,0:T(8,128)(2,1)S(1)}, bf16[768,128]{1,0:T(8,128)(2,1)S(1)}, u32[]{:S(2)}, u32[]{:S(2)}) collective-permute-start(bf16[768,128]{1,0:T(8,128)(2,1)S(1)} %slice.9), channel_id=1, source_target_pairs={{0,7},{1,0},{2,1},{3,2},{4,3},{5,4},{6,5},{7,6},{8,15},{9,8},{10,9... | collective-permute-start | bytes 589832 | tf_op jit(solution)/shard_map/ppermute | solution.py:419
  56.9 2.8 %shard_map.120 = (f32[8,1536]{1,0:T(8,128)S(1)}, f32[144,1536]{1,0:T(8,128)S(1)}) custom-call(s32[10]{0:T(128)S(1)} %stack.40.place.refs_0_, bf16[128,1536]{1,0:T(8,128)(2,1)S(1)} %get-tuple-element.29.refs_1_, bf16[1536,128]{1,0:T(8,128)(2,1)S(1)} %collective-permute-done.4.refs_2_, bf16[1536,128]{1,0:T(8,128)(2,1)S(1)} %collective-permute-done.8.refs_3_, ...), custom_call_target="tpu_custom_call" | custom-call | flops 4831838208 | bytes 3000000 | tf_op jit(solution)/shard_map/pallas_call | solution.py:245
  59.7 0.1 collective-permute-done.5.refs_2_
  59.9 0.0 collective-permute-done.9.refs_3_
  59.9 0.0 copy-start
  59.9 0.0 copy-start.1
  59.9 0.0 copy-start.2
  59.9 0.0 copy-start.3
  59.9 0.0 copy-start.4
  59.9 2.0 %shard_map.121 = (bf16[8,96,256]{2,1,0:T(8,128)(2,1)S(1)}, bf16[8,96,256]{2,1,0:T(8,128)(2,1)S(1)}) custom-call(s32[10]{0:T(128)S(1)} %stack.40.place.refs_0_, bf16[128,1536]{1,0:T(8,128)(2,1)S(1)} %get-tuple-element.29.refs_1_, bf16[768,128]{1,0:T(8,128)(2,1)S(1)} %collective-permute-done.5.refs_2_, bf16[768,128]{1,0:T(8,128)(2,1)S(1)} %collective-permute-done.9.refs_3_, ...), custom_call_target="tpu_custom_call" | custom-call | flops 2415919104 | bytes 3000000 | tf_op jit(solution)/shard_map/pallas_call | solution.py:245
  61.9 5.2 %collective-permute-start.12 = (bf16[8,96,256]{2,1,0:T(8,128)(2,1)S(1)}, bf16[8,96,256]{2,1,0:T(8,128)(2,1)S(1)}, u32[]{:S(2)}, u32[]{:S(2)}) collective-permute-start(bf16[8,96,256]{2,1,0:T(8,128)(2,1)S(1)} %get-tuple-element.39), channel_id=1, source_target_pairs={{0,64},{64,0},{1,65},{65,1},{2,66},{66,2},{3,67},{67,3},{4,68},{68... | collective-permute-start | bytes 1179656 | tf_op jit(solution)/shard_map/ppermute | solution.py:422
  67.1 1.3 %collective-permute-done.12.theirs = bf16[8,96,256]{2,1,0:T(8,128)(2,1)S(1)} collective-permute-done((bf16[8,96,256]{2,1,0:T(8,128)(2,1)S(1)}, bf16[8,96,256]{2,1,0:T(8,128)(2,1)S(1)}, u32[]{:S(2)}, u32[]{:S(2)}) %collective-permute-start.12) | collective-permute-done | bytes 393248 | tf_op jit(solution)/shard_map/ppermute | solution.py:422
  68.5 0.3 shard_map.122
  68.8 10.3 %all_to_all.11.attended = bf16[8,96,128]{2,1,0:T(8,128)(2,1)S(1)} all-to-all(bf16[8,96,128]{2,1,0:T(8,128)(2,1)S(1)} %shard_map.122), channel_id=1, replica_groups=mesh['xh'=2,'core'=2,'xl'=2,'y'=4,'z'=8] {'xl','y'}, dimensions={0} | all-to-all | bytes 393216 | tf_op jit(solution)/shard_map/all_to_all | solution.py:430
  79.1 0.0 copy-done
  79.1 0.0 copy-done.1
  79.1 0.0 copy-done.2
  79.1 0.0 copy-done.3
  79.1 0.0 copy-done.4
  79.1 3.8 %shard_map.123 = (bf16[80,96]{1,0:T(8,128)(2,1)S(1)}, bf16[80,96]{1,0:T(8,128)(2,1)S(1)}) custom-call(s32[10]{0:T(128)S(1)} %stack.40.place.refs_0_, bf16[8,96,128]{2,1,0:T(8,128)(2,1)S(1)} %all_to_all.11.attended, bf16[256,1024]{1,0:T(8,128)(2,1)S(1)} %collective-permute-done.11.refs_6_.both, bf16[512,1024]{1,0:T(8,128)(2,1)S(1)} %copy-done.2, ...), custom_call_target="tpu_custom_call" | custom-call | tf_op jit(solution)/shard_map/pallas_call | solution.py:433
  82.9 1.8 %collective-permute-start.13 = (bf16[80,96]{1,0:T(8,128)(2,1)S(1)}, bf16[80,96]{1,0:T(8,128)(2,1)S(1)}, u32[]{:S(2)}, u32[]{:S(2)}) collective-permute-start(bf16[80,96]{1,0:T(8,128)(2,1)S(1)} %get-tuple-element.41), channel_id=1, source_target_pairs={{0,64},{64,0},{1,65},{65,1},{2,66},{66,2},{3,67},{67,3},{4,68},{68... | collective-permute-start | bytes 46088 | tf_op jit(solution)/shard_map/ppermute | solution.py:449
  84.7 0.8 collective-permute-done.13.theirs
  85.5 0.7 shard_map.124
  86.2 3.1 %collective-permute-start.14 = (bf16[80,192]{1,0:T(8,128)(2,1)S(1)}, bf16[80,192]{1,0:T(8,128)(2,1)S(1)}, u32[]{:S(2)}, u32[]{:S(2)}) collective-permute-start(bf16[80,192]{1,0:T(8,128)(2,1)S(1)} %shard_map.124), channel_id=1, source_target_pairs={{0,7},{1,6},{2,5},{3,4},{4,3},{5,2},{6,1},{7,0},{8,15},{9,14},{10,... | collective-permute-start | bytes 92168 | tf_op jit(solution)/shard_map/ppermute | solution.py:457
  89.3 1.5 %collective-permute-done.14.block = bf16[80,192]{1,0:T(8,128)(2,1)S(1)} collective-permute-done((bf16[80,192]{1,0:T(8,128)(2,1)S(1)}, bf16[80,192]{1,0:T(8,128)(2,1)S(1)}, u32[]{:S(2)}, u32[]{:S(2)}) %collective-permute-start.14) | collective-permute-done | bytes 30752 | tf_op jit(solution)/shard_map/ppermute | solution.py:457
  90.8 0.6 shard_map.125
  (2 shorter events, 0.0 us)
Async XLA Ops:
  0.6 6.0 %collective-permute-start = (bf16[192,1024]{1,0:T(8,128)(2,1)}, bf16[192,1024]{1,0:T(8,128)(2,1)S(1)}, u32[]{:S(2)}, u32[]{:S(2)}) collective-permute-start(bf16[192,1024]{1,0:T(8,128)(2,1)} %hidden.1), channel_id=1, source_target_pairs={{0,64},{64,0},{1,65},{65,1},{2,66},{66,2},{3,67},{67,3},{4,68},{68... | collective-permute-start | bytes 1179656 | tf_op jit(solution)/shard_map/ppermute | solution.py:358
  4.0 25.3 %copy-start.5 = (bf16[64,192]{1,0:T(8,128)(2,1)S(1)}, bf16[64,192]{1,0:T(8,128)(2,1)}, u32[]{:S(2)}) copy-start(bf16[64,192]{1,0:T(8,128)(2,1)} %flow.1) | copy-start | bytes 73732
  21.9 13.6 %collective-permute-start.2 = (bf16[1536,128]{1,0:T(8,128)(2,1)S(1)}, bf16[1536,128]{1,0:T(8,128)(2,1)S(1)}, u32[]{:S(2)}, u32[]{:S(2)}) collective-permute-start(bf16[1536,128]{1,0:T(8,128)(2,1)S(1)} %get-tuple-element.28.refs_3_), channel_id=1, source_target_pairs={{0,1},{1,2},{2,3},{3,4},{4,5},{5,6},{6,7},{7,0},{8,9},{9,10},{10,1... | collective-permute-start | bytes 1179656 | tf_op jit(solution)/shard_map/ppermute | solution.py:406
  23.6 11.9 %collective-permute-start.6 = (bf16[1536,128]{1,0:T(8,128)(2,1)S(1)}, bf16[1536,128]{1,0:T(8,128)(2,1)S(1)}, u32[]{:S(2)}, u32[]{:S(2)}) collective-permute-start(bf16[1536,128]{1,0:T(8,128)(2,1)S(1)} %get-tuple-element.28.refs_3_), channel_id=1, source_target_pairs={{0,7},{1,0},{2,1},{3,2},{4,3},{5,4},{6,5},{7,6},{8,15},{9,8},{10,9... | collective-permute-start | bytes 1179656 | tf_op jit(solution)/shard_map/ppermute | solution.py:407
  27.6 2.8 %collective-permute-start.1 = (bf16[8,96,128]{2,1,0:T(8,128)(2,1)S(1)}, bf16[8,96,128]{2,1,0:T(8,128)(2,1)S(1)}, u32[]{:S(2)}, u32[]{:S(2)}) collective-permute-start(bf16[8,96,128]{2,1,0:T(8,128)(2,1)S(1)} %get-tuple-element.27.refs_1_), channel_id=1, source_target_pairs={{0,64},{64,0},{1,65},{65,1},{2,66},{66,2},{3,67},{67,3},{4,68},{68... | collective-permute-start | bytes 589832 | tf_op jit(solution)/shard_map/ppermute | solution.py:390
  29.4 3.0 %collective-permute-start.10 = (bf16[64,192]{1,0:T(8,128)(2,1)S(1)}, bf16[64,192]{1,0:T(8,128)(2,1)S(1)}, u32[]{:S(2)}, u32[]{:S(2)}) collective-permute-start(bf16[64,192]{1,0:T(8,128)(2,1)S(1)} %copy-done.5), channel_id=1, source_target_pairs={{0,64},{64,0},{1,65},{65,1},{2,66},{66,2},{3,67},{67,3},{4,68},{68... | collective-permute-start | bytes 73736 | tf_op jit(solution)/shard_map/ppermute | solution.py:359
  33.1 15.3 %collective-permute-start.11 = (bf16[256,1024]{1,0:T(8,128)(2,1)S(1)}, bf16[256,1024]{1,0:T(8,128)(2,1)S(1)}, u32[]{:S(2)}, u32[]{:S(2)}) collective-permute-start(bf16[256,1024]{1,0:T(8,128)(2,1)S(1)} %shard_map.118), channel_id=1, source_target_pairs={{0,56},{8,48},{16,40},{24,32},{32,24},{40,16},{48,8},{56,0},{1,57}... | collective-permute-start | bytes 1572872 | tf_op jit(solution)/shard_map/ppermute | solution.py:403
  35.5 9.7 %collective-permute-start.3 = (bf16[1536,128]{1,0:T(8,128)(2,1)S(1)}, bf16[1536,128]{1,0:T(8,128)(2,1)S(1)}, u32[]{:S(2)}, u32[]{:S(2)}) collective-permute-start(bf16[1536,128]{1,0:T(8,128)(2,1)S(1)} %collective-permute-done.2.refs_2_), channel_id=1, source_target_pairs={{0,1},{1,2},{2,3},{3,4},{4,5},{5,6},{6,7},{7,0},{8,9},{9,10},{10,1... | collective-permute-start | bytes 1179656 | tf_op jit(solution)/shard_map/ppermute | solution.py:406
  35.5 9.7 %collective-permute-start.7 = (bf16[1536,128]{1,0:T(8,128)(2,1)S(1)}, bf16[1536,128]{1,0:T(8,128)(2,1)S(1)}, u32[]{:S(2)}, u32[]{:S(2)}) collective-permute-start(bf16[1536,128]{1,0:T(8,128)(2,1)S(1)} %collective-permute-done.6.refs_3_), channel_id=1, source_target_pairs={{0,7},{1,0},{2,1},{3,2},{4,3},{5,4},{6,5},{7,6},{8,15},{9,8},{10,9... | collective-permute-start | bytes 1179656 | tf_op jit(solution)/shard_map/ppermute | solution.py:407
  45.2 8.8 %collective-permute-start.4 = (bf16[1536,128]{1,0:T(8,128)(2,1)S(1)}, bf16[1536,128]{1,0:T(8,128)(2,1)S(1)}, u32[]{:S(2)}, u32[]{:S(2)}) collective-permute-start(bf16[1536,128]{1,0:T(8,128)(2,1)S(1)} %collective-permute-done.3.refs_2_), channel_id=1, source_target_pairs={{0,1},{1,2},{2,3},{3,4},{4,5},{5,6},{6,7},{7,0},{8,9},{9,10},{10,1... | collective-permute-start | bytes 1179656 | tf_op jit(solution)/shard_map/ppermute | solution.py:406
  45.2 8.9 %collective-permute-start.8 = (bf16[1536,128]{1,0:T(8,128)(2,1)S(1)}, bf16[1536,128]{1,0:T(8,128)(2,1)S(1)}, u32[]{:S(2)}, u32[]{:S(2)}) collective-permute-start(bf16[1536,128]{1,0:T(8,128)(2,1)S(1)} %collective-permute-done.7.refs_3_), channel_id=1, source_target_pairs={{0,7},{1,0},{2,1},{3,2},{4,3},{5,4},{6,5},{7,6},{8,15},{9,8},{10,9... | collective-permute-start | bytes 1179656 | tf_op jit(solution)/shard_map/ppermute | solution.py:407
  54.0 5.8 %collective-permute-start.5 = (bf16[768,128]{1,0:T(8,128)(2,1)S(1)}, bf16[768,128]{1,0:T(8,128)(2,1)S(1)}, u32[]{:S(2)}, u32[]{:S(2)}) collective-permute-start(bf16[768,128]{1,0:T(8,128)(2,1)S(1)} %slice.8), channel_id=1, source_target_pairs={{0,1},{1,2},{2,3},{3,4},{4,5},{5,6},{6,7},{7,0},{8,9},{9,10},{10,1... | collective-permute-start | bytes 589832 | tf_op jit(solution)/shard_map/ppermute | solution.py:418
  54.2 5.7 %collective-permute-start.9 = (bf16[768,128]{1,0:T(8,128)(2,1)S(1)}, bf16[768,128]{1,0:T(8,128)(2,1)S(1)}, u32[]{:S(2)}, u32[]{:S(2)}) collective-permute-start(bf16[768,128]{1,0:T(8,128)(2,1)S(1)} %slice.9), channel_id=1, source_target_pairs={{0,7},{1,0},{2,1},{3,2},{4,3},{5,4},{6,5},{7,6},{8,15},{9,8},{10,9... | collective-permute-start | bytes 589832 | tf_op jit(solution)/shard_map/ppermute | solution.py:419
  59.9 19.3 %copy-start = (bf16[1024,2048]{1,0:T(8,128)(2,1)S(1)}, bf16[1024,2048]{1,0:T(8,128)(2,1)}, u32[]{:S(2)}) copy-start(bf16[1024,2048]{1,0:T(8,128)(2,1)} %w_up.1) | copy-start | bytes 12582916
  59.9 19.3 %copy-start.1 = (bf16[2048,1024]{1,0:T(8,128)(2,1)S(1)}, bf16[2048,1024]{1,0:T(8,128)(2,1)}, u32[]{:S(2)}) copy-start(bf16[2048,1024]{1,0:T(8,128)(2,1)} %w_down.1) | copy-start | bytes 12582916
  59.9 19.3 %copy-start.2 = (bf16[512,1024]{1,0:T(8,128)(2,1)S(1)}, bf16[512,1024]{1,0:T(8,128)(2,1)}, u32[]{:S(2)}) copy-start(bf16[512,1024]{1,0:T(8,128)(2,1)} %w_output.1) | copy-start | bytes 3145732
  59.9 19.3 %copy-start.3 = (bf16[64,1024]{1,0:T(8,128)(2,1)S(1)}, bf16[64,1024]{1,0:T(8,128)(2,1)}, u32[]{:S(2)}) copy-start(bf16[64,1024]{1,0:T(8,128)(2,1)} %w_shift.1) | copy-start | bytes 393220
  59.9 19.3 %copy-start.4 = (bf16[64,1024]{1,0:T(8,128)(2,1)S(1)}, bf16[64,1024]{1,0:T(8,128)(2,1)}, u32[]{:S(2)}) copy-start(bf16[64,1024]{1,0:T(8,128)(2,1)} %w_scale.1) | copy-start | bytes 393220
  61.9 6.5 %collective-permute-start.12 = (bf16[8,96,256]{2,1,0:T(8,128)(2,1)S(1)}, bf16[8,96,256]{2,1,0:T(8,128)(2,1)S(1)}, u32[]{:S(2)}, u32[]{:S(2)}) collective-permute-start(bf16[8,96,256]{2,1,0:T(8,128)(2,1)S(1)} %get-tuple-element.39), channel_id=1, source_target_pairs={{0,64},{64,0},{1,65},{65,1},{2,66},{66,2},{3,67},{67,3},{4,68},{68... | collective-permute-start | bytes 1179656 | tf_op jit(solution)/shard_map/ppermute | solution.py:422
  82.9 2.6 %collective-permute-start.13 = (bf16[80,96]{1,0:T(8,128)(2,1)S(1)}, bf16[80,96]{1,0:T(8,128)(2,1)S(1)}, u32[]{:S(2)}, u32[]{:S(2)}) collective-permute-start(bf16[80,96]{1,0:T(8,128)(2,1)S(1)} %get-tuple-element.41), channel_id=1, source_target_pairs={{0,64},{64,0},{1,65},{65,1},{2,66},{66,2},{3,67},{67,3},{4,68},{68... | collective-permute-start | bytes 46088 | tf_op jit(solution)/shard_map/ppermute | solution.py:449
  86.2 4.6 %collective-permute-start.14 = (bf16[80,192]{1,0:T(8,128)(2,1)S(1)}, bf16[80,192]{1,0:T(8,128)(2,1)S(1)}, u32[]{:S(2)}, u32[]{:S(2)}) collective-permute-start(bf16[80,192]{1,0:T(8,128)(2,1)S(1)} %shard_map.124), channel_id=1, source_target_pairs={{0,7},{1,6},{2,5},{3,4},{4,3},{5,2},{6,1},{7,0},{8,15},{9,14},{10,... | collective-permute-start | bytes 92168 | tf_op jit(solution)/shard_map/ppermute | solution.py:457

commit v9 on v8

--- a/solution.py
+++ b/solution.py
@@ -77,19 +77,22 @@
     return copies
 
 
-def load_kernel(place, hidden, w_query, w_key, w_value, own, query, key, value, sems, own_sem):
+def load_kernel(
+    place, hidden, w_query, w_key, w_value, own, own_normed, query, key, value, sems, own_sem
+):
     rows = pl.ds(pl.multiple_of(place[0] * PIECE, PIECE), PIECE)
     copy = pltpu.make_async_copy(hidden.at[rows], own, own_sem)
     copy.start()
     copies = start_loads((w_key, w_value, w_query), (key, value, query), sems)
     copy.wait()
+    own_normed[...] = layer_norm(own[...].astype(f32)).astype(bf16)
     for copy in copies:
         copy.wait()
 
 
-def qkv_kernel(place, own, other, w_query, w_key, w_value, slots, normed):
+def qkv_kernel(place, own_normed, other, w_query, w_key, w_value, slots, normed):
     core = place[0]
-    normed[:PIECE, :] = layer_norm(own[...].astype(f32)).astype(bf16)
+    normed[:PIECE, :] = own_normed[...]
     rows = pl.ds(pl.multiple_of(core * PIECE, PIECE), PIECE)
     normed[PIECE:, :] = layer_norm(other[rows, :].astype(f32)).astype(bf16)
     for column, weight in enumerate((w_query, w_key, w_value)):
@@ -359,11 +362,11 @@
     other_flow = lax.ppermute(flow_input, "core", other_core)
 
     square = pltpu.VMEM((WIDTH, INNER), bf16)
-    own, *weights = pl.pallas_call(
+    own, own_normed, *weights = pl.pallas_call(
         load_kernel,
-        out_shape=[pltpu.VMEM((PIECE, WIDTH), bf16), square, square, square],
+        out_shape=[pltpu.VMEM((PIECE, WIDTH), bf16)] * 2 + [square] * 3,
         in_specs=[smem()] + [hbm()] * 4,
-        out_specs=[vmem()] * 4,
+        out_specs=[vmem()] * 5,
         scratch_shapes=[pltpu.SemaphoreType.DMA((12,)), pltpu.SemaphoreType.DMA],
         compiler_params=params(8),
         cost_estimate=pl.CostEstimate(flops=0, bytes_accessed=6_600_000, transcendentals=0),
@@ -375,7 +378,7 @@
         out_specs=vmem(),
         scratch_shapes=[pltpu.VMEM((TOKENS, WIDTH), bf16)],
         compiler_params=params(8),
-    )(place, own, other, *weights)
+    )(place, own_normed, other, *weights)
     slots = lax.all_to_all(slots, ("xl", "y"), 0, 0, tiled=True)
     chunk, queries = pl.pallas_call(
         pack_kernel,

time: 91.6 us -> 92 us (level)
  no operation moved by 1% of the time
where the time goes in v9:
time: 92 us; the launch traced here: 91.9 us
  starting transfers between devices  30.2 us (33%)
  blocking collectives  24.2 us (26%)
  Pallas kernels  23.1 us (25%)
  waiting for transfers between devices  13.4 us (15%)
    all_to_all x1, blocking collectives, on_device(): slots = lax.all_to_all(slots, ('xl', 'y'), 0, 0, tiled=True)  13.6 us
    pallas_call x5, Pallas kernels, attend(): pl.pallas_call(functools.partial(attend_kernel, chunks, first, last, len(...  12.5 us
    all_to_all x1, blocking collectives, on_device(): attended = lax.all_to_all(attended, ('xl', 'y'), 0, 0, tiled=True)  10.6 us
    ppermute x3, starting transfers between devices, on_device(): down = lax.ppermute(down, 'z', shift_by(Z, -1))  9.38 us
    ppermute x3, waiting for transfers between devices, on_device(): up = lax.ppermute(up, 'z', shift_by(Z, 1))  8.14 us
    ppermute x1, starting transfers between devices, on_device(): theirs = lax.ppermute(others, 'core', other_core)  5.21 us
    pallas_call x1, Pallas kernels, on_device(): pl.pallas_call(dense_kernel, out_shape=[sent, sent], in_specs=[smem()] +...  3.77 us
    ppermute x1, starting transfers between devices, on_device(): other = lax.ppermute(hidden, 'core', other_core)  3.33 us
  transfers between devices with their start and end apart: 15, of which 9 were waited for; matrix products, arithmetic and copies ran while one was open for 0% of the time, Pallas kernels for 15%

profile of v9, /device:TPU:1, one launch (start us, length us, event | category | flops | bytes accessed | tf_op | source)
XLA Modules:
  0.0 91.9 jit_solution(932732911553113634)
XLA Ops:
  0.6 3.3 %collective-permute-start = (bf16[192,1024]{1,0:T(8,128)(2,1)}, bf16[192,1024]{1,0:T(8,128)(2,1)S(1)}, u32[]{:S(2)}, u32[]{:S(2)}) collective-permute-start(bf16[192,1024]{1,0:T(8,128)(2,1)} %hidden.1), channel_id=1, source_target_pairs={{0,64},{64,0},{1,65},{65,1},{2,66},{66,2},{3,67},{67,3},{4,68},{68... | collective-permute-start | bytes 1179656 | tf_op jit(solution)/shard_map/ppermute | solution.py:361
  4.0 0.1 stack.40.place.refs_0_
  4.0 0.0 copy-start.5
  4.0 2.8 %shard_map.113 = (bf16[96,1024]{1,0:T(8,128)(2,1)S(1)}, bf16[96,1024]{1,0:T(8,128)(2,1)S(1)}, bf16[1024,512]{1,0:T(8,128)(2,1)S(1)}, bf16[1024,512]{1,0:T(8,128)(2,1)S(1)}, bf16[1024,512]{1,0:T(8,128)(2,1)S(1)}) custom-call(s32[10]{0:T(128)S(1)} %stack.40.place.refs_0_, bf16[192,1024]{1,0:T(8,128)(2,1)} %hidden.1, bf16[1024,512]{1,0:T(8,128)(2,1)} %w_query.1, ...), custom_call_target="tpu_custom_call" | custom-call | bytes 6600000 | tf_op jit(solution)/shard_map/pallas_call | solution.py:365
  6.8 0.0 collective-permute-done.other
  6.8 1.5 %shard_map.114 = bf16[8,96,384]{2,1,0:T(8,128)(2,1)S(1)} custom-call(s32[10]{0:T(128)S(1)} %stack.40.place.refs_0_, bf16[96,1024]{1,0:T(8,128)(2,1)S(1)} %get-tuple-element.24.own_normed, bf16[192,1024]{1,0:T(8,128)(2,1)S(1)} %collective-permute-done.other, bf16[1024,512]{1,0:T(8,128)(2,1)S(1)} %get-tuple-element.25.w_query, ...), custom_call_target="tpu_custom_call" | custom-call | tf_op jit(solution)/shard_map/pallas_call | solution.py:374
  8.4 13.6 %all_to_all.10.slots = bf16[8,96,384]{2,1,0:T(8,128)(2,1)S(1)} all-to-all(bf16[8,96,384]{2,1,0:T(8,128)(2,1)S(1)} %shard_map.114), channel_id=1, replica_groups=mesh['xh'=2,'core'=2,'xl'=2,'y'=4,'z'=8] {'xl','y'}, dimensions={0} | all-to-all | bytes 1179648 | tf_op jit(solution)/shard_map/all_to_all | solution.py:382
  21.9 0.1 shard_map.115
  22.1 1.7 %collective-permute-start.2 = (bf16[1536,128]{1,0:T(8,128)(2,1)S(1)}, bf16[1536,128]{1,0:T(8,128)(2,1)S(1)}, u32[]{:S(2)}, u32[]{:S(2)}) collective-permute-start(bf16[1536,128]{1,0:T(8,128)(2,1)S(1)} %get-tuple-element.29.refs_3_), channel_id=1, source_target_pairs={{0,1},{1,2},{2,3},{3,4},{4,5},{5,6},{6,7},{7,0},{8,9},{9,10},{10,1... | collective-permute-start | bytes 1179656 | tf_op jit(solution)/shard_map/ppermute | solution.py:409
  23.8 4.0 %collective-permute-start.6 = (bf16[1536,128]{1,0:T(8,128)(2,1)S(1)}, bf16[1536,128]{1,0:T(8,128)(2,1)S(1)}, u32[]{:S(2)}, u32[]{:S(2)}) collective-permute-start(bf16[1536,128]{1,0:T(8,128)(2,1)S(1)} %get-tuple-element.29.refs_3_), channel_id=1, source_target_pairs={{0,7},{1,0},{2,1},{3,2},{4,3},{5,4},{6,5},{7,6},{8,15},{9,8},{10,9... | collective-permute-start | bytes 1179656 | tf_op jit(solution)/shard_map/ppermute | solution.py:410
  27.8 1.8 %collective-permute-start.1 = (bf16[8,96,128]{2,1,0:T(8,128)(2,1)S(1)}, bf16[8,96,128]{2,1,0:T(8,128)(2,1)S(1)}, u32[]{:S(2)}, u32[]{:S(2)}) collective-permute-start(bf16[8,96,128]{2,1,0:T(8,128)(2,1)S(1)} %get-tuple-element.28.refs_1_), channel_id=1, source_target_pairs={{0,64},{64,0},{1,65},{65,1},{2,66},{66,2},{3,67},{67,3},{4,68},{68... | collective-permute-start | bytes 589832 | tf_op jit(solution)/shard_map/ppermute | solution.py:393
  29.6 0.0 copy-done.5
  29.6 0.0 collective-permute-start.10
  29.6 1.1 %collective-permute-done.1.refs_2_ = bf16[8,96,128]{2,1,0:T(8,128)(2,1)S(1)} collective-permute-done((bf16[8,96,128]{2,1,0:T(8,128)(2,1)S(1)}, bf16[8,96,128]{2,1,0:T(8,128)(2,1)S(1)}, u32[]{:S(2)}, u32[]{:S(2)}) %collective-permute-start.1) | collective-permute-done | bytes 196640 | tf_op jit(solution)/shard_map/ppermute | solution.py:393
  30.7 1.9 %shard_map.116 = (bf16[128,1536]{1,0:T(8,128)(2,1)S(1)}, f32[8,1536]{1,0:T(8,128)S(1)}, f32[144,1536]{1,0:T(8,128)S(1)}) custom-call(s32[10]{0:T(128)S(1)} %stack.40.place.refs_0_, bf16[8,96,128]{2,1,0:T(8,128)(2,1)S(1)} %get-tuple-element.28.refs_1_, bf16[8,96,128]{2,1,0:T(8,128)(2,1)S(1)} %collective-permute-done.1.refs_2_, ...), custom_call_target="tpu_custom_call" | custom-call | flops 301989888 | bytes 3000000 | tf_op jit(solution)/shard_map/pallas_call | solution.py:248
  32.6 0.0 collective-permute-done.10.other_flow
  32.6 0.7 shard_map.118
  33.3 1.1 %collective-permute-start.11 = (bf16[256,1024]{1,0:T(8,128)(2,1)S(1)}, bf16[256,1024]{1,0:T(8,128)(2,1)S(1)}, u32[]{:S(2)}, u32[]{:S(2)}) collective-permute-start(bf16[256,1024]{1,0:T(8,128)(2,1)S(1)} %shard_map.118), channel_id=1, source_target_pairs={{0,56},{8,48},{16,40},{24,32},{32,24},{40,16},{48,8},{56,0},{1,57}... | collective-permute-start | bytes 1572872 | tf_op jit(solution)/shard_map/ppermute | solution.py:406
  34.4 1.3 %collective-permute-done.2.refs_2_ = bf16[1536,128]{1,0:T(8,128)(2,1)S(1)} collective-permute-done((bf16[1536,128]{1,0:T(8,128)(2,1)S(1)}, bf16[1536,128]{1,0:T(8,128)(2,1)S(1)}, u32[]{:S(2)}, u32[]{:S(2)}) %collective-permute-start.2) | collective-permute-done | bytes 393248 | tf_op jit(solution)/shard_map/ppermute | solution.py:409
  35.7 0.0 collective-permute-start.3
  35.7 0.0 collective-permute-done.6.refs_3_
  35.7 2.7 %collective-permute-start.7 = (bf16[1536,128]{1,0:T(8,128)(2,1)S(1)}, bf16[1536,128]{1,0:T(8,128)(2,1)S(1)}, u32[]{:S(2)}, u32[]{:S(2)}) collective-permute-start(bf16[1536,128]{1,0:T(8,128)(2,1)S(1)} %collective-permute-done.6.refs_3_), channel_id=1, source_target_pairs={{0,7},{1,0},{2,1},{3,2},{4,3},{5,4},{6,5},{7,6},{8,15},{9,8},{10,9... | collective-permute-start | bytes 1179656 | tf_op jit(solution)/shard_map/ppermute | solution.py:410
  38.4 2.8 %shard_map.117 = (f32[8,1536]{1,0:T(8,128)S(1)}, f32[144,1536]{1,0:T(8,128)S(1)}) custom-call(s32[10]{0:T(128)S(1)} %stack.40.place.refs_0_, bf16[128,1536]{1,0:T(8,128)(2,1)S(1)} %get-tuple-element.30.refs_1_, bf16[1536,128]{1,0:T(8,128)(2,1)S(1)} %collective-permute-done.2.refs_2_, bf16[1536,128]{1,0:T(8,128)(2,1)S(1)} %collective-permute-done.6.refs_3_, ...), custom_call_target="tpu_custom_call" | custom-call | flops 4831838208 | bytes 3000000 | tf_op jit(solution)/shard_map/pallas_call | solution.py:248
  41.2 4.2 %collective-permute-done.3.refs_2_ = bf16[1536,128]{1,0:T(8,128)(2,1)S(1)} collective-permute-done((bf16[1536,128]{1,0:T(8,128)(2,1)S(1)}, bf16[1536,128]{1,0:T(8,128)(2,1)S(1)}, u32[]{:S(2)}, u32[]{:S(2)}) %collective-permute-start.3) | collective-permute-done | bytes 393248 | tf_op jit(solution)/shard_map/ppermute | solution.py:409
  45.4 0.0 collective-permute-start.4
  45.4 0.0 collective-permute-done.7.refs_3_
  45.4 2.7 %collective-permute-start.8 = (bf16[1536,128]{1,0:T(8,128)(2,1)S(1)}, bf16[1536,128]{1,0:T(8,128)(2,1)S(1)}, u32[]{:S(2)}, u32[]{:S(2)}) collective-permute-start(bf16[1536,128]{1,0:T(8,128)(2,1)S(1)} %collective-permute-done.7.refs_3_), channel_id=1, source_target_pairs={{0,7},{1,0},{2,1},{3,2},{4,3},{5,4},{6,5},{7,6},{8,15},{9,8},{10,9... | collective-permute-start | bytes 1179656 | tf_op jit(solution)/shard_map/ppermute | solution.py:410
  48.1 0.5 collective-permute-done.11.refs_6_.both
  48.6 2.8 %shard_map.119 = (f32[8,1536]{1,0:T(8,128)S(1)}, f32[144,1536]{1,0:T(8,128)S(1)}) custom-call(s32[10]{0:T(128)S(1)} %stack.40.place.refs_0_, bf16[128,1536]{1,0:T(8,128)(2,1)S(1)} %get-tuple-element.30.refs_1_, bf16[1536,128]{1,0:T(8,128)(2,1)S(1)} %collective-permute-done.3.refs_2_, bf16[1536,128]{1,0:T(8,128)(2,1)S(1)} %collective-permute-done.7.refs_3_, ...), custom_call_target="tpu_custom_call" | custom-call | flops 4831838208 | bytes 3000000 | tf_op jit(solution)/shard_map/pallas_call | solution.py:248
  51.4 2.7 %collective-permute-done.4.refs_2_ = bf16[1536,128]{1,0:T(8,128)(2,1)S(1)} collective-permute-done((bf16[1536,128]{1,0:T(8,128)(2,1)S(1)}, bf16[1536,128]{1,0:T(8,128)(2,1)S(1)}, u32[]{:S(2)}, u32[]{:S(2)}) %collective-permute-start.4) | collective-permute-done | bytes 393248 | tf_op jit(solution)/shard_map/ppermute | solution.py:409
  54.2 0.1 collective-permute-start.5
  54.3 0.0 collective-permute-done.8.refs_3_
  54.3 2.7 %collective-permute-start.9 = (bf16[768,128]{1,0:T(8,128)(2,1)S(1)}, bf16[768,128]{1,0:T(8,128)(2,1)S(1)}, u32[]{:S(2)}, u32[]{:S(2)}) collective-permute-start(bf16[768,128]{1,0:T(8,128)(2,1)S(1)} %slice.9), channel_id=1, source_target_pairs={{0,7},{1,0},{2,1},{3,2},{4,3},{5,4},{6,5},{7,6},{8,15},{9,8},{10,9... | collective-permute-start | bytes 589832 | tf_op jit(solution)/shard_map/ppermute | solution.py:422
  57.0 2.8 %shard_map.120 = (f32[8,1536]{1,0:T(8,128)S(1)}, f32[144,1536]{1,0:T(8,128)S(1)}) custom-call(s32[10]{0:T(128)S(1)} %stack.40.place.refs_0_, bf16[128,1536]{1,0:T(8,128)(2,1)S(1)} %get-tuple-element.30.refs_1_, bf16[1536,128]{1,0:T(8,128)(2,1)S(1)} %collective-permute-done.4.refs_2_, bf16[1536,128]{1,0:T(8,128)(2,1)S(1)} %collective-permute-done.8.refs_3_, ...), custom_call_target="tpu_custom_call" | custom-call | flops 4831838208 | bytes 3000000 | tf_op jit(solution)/shard_map/pallas_call | solution.py:248
  59.9 0.1 collective-permute-done.5.refs_2_
  60.0 0.0 collective-permute-done.9.refs_3_
  60.0 0.0 copy-start
  60.0 0.0 copy-start.1
  60.0 0.0 copy-start.2
  60.0 0.0 copy-start.3
  60.0 0.0 copy-start.4
  60.0 2.0 %shard_map.121 = (bf16[8,96,256]{2,1,0:T(8,128)(2,1)S(1)}, bf16[8,96,256]{2,1,0:T(8,128)(2,1)S(1)}) custom-call(s32[10]{0:T(128)S(1)} %stack.40.place.refs_0_, bf16[128,1536]{1,0:T(8,128)(2,1)S(1)} %get-tuple-element.30.refs_1_, bf16[768,128]{1,0:T(8,128)(2,1)S(1)} %collective-permute-done.5.refs_2_, bf16[768,128]{1,0:T(8,128)(2,1)S(1)} %collective-permute-done.9.refs_3_, ...), custom_call_target="tpu_custom_call" | custom-call | flops 2415919104 | bytes 3000000 | tf_op jit(solution)/shard_map/pallas_call | solution.py:248
  62.1 5.2 %collective-permute-start.12 = (bf16[8,96,256]{2,1,0:T(8,128)(2,1)S(1)}, bf16[8,96,256]{2,1,0:T(8,128)(2,1)S(1)}, u32[]{:S(2)}, u32[]{:S(2)}) collective-permute-start(bf16[8,96,256]{2,1,0:T(8,128)(2,1)S(1)} %get-tuple-element.41), channel_id=1, source_target_pairs={{0,64},{64,0},{1,65},{65,1},{2,66},{66,2},{3,67},{67,3},{4,68},{68... | collective-permute-start | bytes 1179656 | tf_op jit(solution)/shard_map/ppermute | solution.py:425
  67.3 1.3 %collective-permute-done.12.theirs = bf16[8,96,256]{2,1,0:T(8,128)(2,1)S(1)} collective-permute-done((bf16[8,96,256]{2,1,0:T(8,128)(2,1)S(1)}, bf16[8,96,256]{2,1,0:T(8,128)(2,1)S(1)}, u32[]{:S(2)}, u32[]{:S(2)}) %collective-permute-start.12) | collective-permute-done | bytes 393248 | tf_op jit(solution)/shard_map/ppermute | solution.py:425
  68.6 0.3 shard_map.122
  68.9 10.6 %all_to_all.11.attended = bf16[8,96,128]{2,1,0:T(8,128)(2,1)S(1)} all-to-all(bf16[8,96,128]{2,1,0:T(8,128)(2,1)S(1)} %shard_map.122), channel_id=1, replica_groups=mesh['xh'=2,'core'=2,'xl'=2,'y'=4,'z'=8] {'xl','y'}, dimensions={0} | all-to-all | bytes 393216 | tf_op jit(solution)/shard_map/all_to_all | solution.py:433
  79.6 0.0 copy-done
  79.6 0.0 copy-done.1
  79.6 0.0 copy-done.2
  79.6 0.0 copy-done.3
  79.6 0.0 copy-done.4
  79.6 3.8 %shard_map.123 = (bf16[80,96]{1,0:T(8,128)(2,1)S(1)}, bf16[80,96]{1,0:T(8,128)(2,1)S(1)}) custom-call(s32[10]{0:T(128)S(1)} %stack.40.place.refs_0_, bf16[8,96,128]{2,1,0:T(8,128)(2,1)S(1)} %all_to_all.11.attended, bf16[256,1024]{1,0:T(8,128)(2,1)S(1)} %collective-permute-done.11.refs_6_.both, bf16[512,1024]{1,0:T(8,128)(2,1)S(1)} %copy-done.2, ...), custom_call_target="tpu_custom_call" | custom-call | tf_op jit(solution)/shard_map/pallas_call | solution.py:436
  83.4 1.8 %collective-permute-start.13 = (bf16[80,96]{1,0:T(8,128)(2,1)S(1)}, bf16[80,96]{1,0:T(8,128)(2,1)S(1)}, u32[]{:S(2)}, u32[]{:S(2)}) collective-permute-start(bf16[80,96]{1,0:T(8,128)(2,1)S(1)} %get-tuple-element.43), channel_id=1, source_target_pairs={{0,64},{64,0},{1,65},{65,1},{2,66},{66,2},{3,67},{67,3},{4,68},{68... | collective-permute-start | bytes 46088 | tf_op jit(solution)/shard_map/ppermute | solution.py:452
  85.2 0.8 collective-permute-done.13.theirs
  86.0 0.7 shard_map.124
  86.7 3.1 %collective-permute-start.14 = (bf16[80,192]{1,0:T(8,128)(2,1)S(1)}, bf16[80,192]{1,0:T(8,128)(2,1)S(1)}, u32[]{:S(2)}, u32[]{:S(2)}) collective-permute-start(bf16[80,192]{1,0:T(8,128)(2,1)S(1)} %shard_map.124), channel_id=1, source_target_pairs={{0,7},{1,6},{2,5},{3,4},{4,3},{5,2},{6,1},{7,0},{8,15},{9,14},{10,... | collective-permute-start | bytes 92168 | tf_op jit(solution)/shard_map/ppermute | solution.py:460
  89.8 1.4 %collective-permute-done.14.block = bf16[80,192]{1,0:T(8,128)(2,1)S(1)} collective-permute-done((bf16[80,192]{1,0:T(8,128)(2,1)S(1)}, bf16[80,192]{1,0:T(8,128)(2,1)S(1)}, u32[]{:S(2)}, u32[]{:S(2)}) %collective-permute-start.14) | collective-permute-done | bytes 30752 | tf_op jit(solution)/shard_map/ppermute | solution.py:460
  91.2 0.6 shard_map.125
  (2 shorter events, 0.0 us)
Async XLA Ops:
  0.6 6.2 %collective-permute-start = (bf16[192,1024]{1,0:T(8,128)(2,1)}, bf16[192,1024]{1,0:T(8,128)(2,1)S(1)}, u32[]{:S(2)}, u32[]{:S(2)}) collective-permute-start(bf16[192,1024]{1,0:T(8,128)(2,1)} %hidden.1), channel_id=1, source_target_pairs={{0,64},{64,0},{1,65},{65,1},{2,66},{66,2},{3,67},{67,3},{4,68},{68... | collective-permute-start | bytes 1179656 | tf_op jit(solution)/shard_map/ppermute | solution.py:361
  4.0 25.6 %copy-start.5 = (bf16[64,192]{1,0:T(8,128)(2,1)S(1)}, bf16[64,192]{1,0:T(8,128)(2,1)}, u32[]{:S(2)}) copy-start(bf16[64,192]{1,0:T(8,128)(2,1)} %flow.1) | copy-start | bytes 73732
  22.1 13.6 %collective-permute-start.2 = (bf16[1536,128]{1,0:T(8,128)(2,1)S(1)}, bf16[1536,128]{1,0:T(8,128)(2,1)S(1)}, u32[]{:S(2)}, u32[]{:S(2)}) collective-permute-start(bf16[1536,128]{1,0:T(8,128)(2,1)S(1)} %get-tuple-element.29.refs_3_), channel_id=1, source_target_pairs={{0,1},{1,2},{2,3},{3,4},{4,5},{5,6},{6,7},{7,0},{8,9},{9,10},{10,1... | collective-permute-start | bytes 1179656 | tf_op jit(solution)/shard_map/ppermute | solution.py:409
  23.8 11.9 %collective-permute-start.6 = (bf16[1536,128]{1,0:T(8,128)(2,1)S(1)}, bf16[1536,128]{1,0:T(8,128)(2,1)S(1)}, u32[]{:S(2)}, u32[]{:S(2)}) collective-permute-start(bf16[1536,128]{1,0:T(8,128)(2,1)S(1)} %get-tuple-element.29.refs_3_), channel_id=1, source_target_pairs={{0,7},{1,0},{2,1},{3,2},{4,3},{5,4},{6,5},{7,6},{8,15},{9,8},{10,9... | collective-permute-start | bytes 1179656 | tf_op jit(solution)/shard_map/ppermute | solution.py:410
  27.8 2.8 %collective-permute-start.1 = (bf16[8,96,128]{2,1,0:T(8,128)(2,1)S(1)}, bf16[8,96,128]{2,1,0:T(8,128)(2,1)S(1)}, u32[]{:S(2)}, u32[]{:S(2)}) collective-permute-start(bf16[8,96,128]{2,1,0:T(8,128)(2,1)S(1)} %get-tuple-element.28.refs_1_), channel_id=1, source_target_pairs={{0,64},{64,0},{1,65},{65,1},{2,66},{66,2},{3,67},{67,3},{4,68},{68... | collective-permute-start | bytes 589832 | tf_op jit(solution)/shard_map/ppermute | solution.py:393
  29.6 3.0 %collective-permute-start.10 = (bf16[64,192]{1,0:T(8,128)(2,1)S(1)}, bf16[64,192]{1,0:T(8,128)(2,1)S(1)}, u32[]{:S(2)}, u32[]{:S(2)}) collective-permute-start(bf16[64,192]{1,0:T(8,128)(2,1)S(1)} %copy-done.5), channel_id=1, source_target_pairs={{0,64},{64,0},{1,65},{65,1},{2,66},{66,2},{3,67},{67,3},{4,68},{68... | collective-permute-start | bytes 73736 | tf_op jit(solution)/shard_map/ppermute | solution.py:362
  33.3 15.3 %collective-permute-start.11 = (bf16[256,1024]{1,0:T(8,128)(2,1)S(1)}, bf16[256,1024]{1,0:T(8,128)(2,1)S(1)}, u32[]{:S(2)}, u32[]{:S(2)}) collective-permute-start(bf16[256,1024]{1,0:T(8,128)(2,1)S(1)} %shard_map.118), channel_id=1, source_target_pairs={{0,56},{8,48},{16,40},{24,32},{32,24},{40,16},{48,8},{56,0},{1,57}... | collective-permute-start | bytes 1572872 | tf_op jit(solution)/shard_map/ppermute | solution.py:406
  35.7 9.7 %collective-permute-start.3 = (bf16[1536,128]{1,0:T(8,128)(2,1)S(1)}, bf16[1536,128]{1,0:T(8,128)(2,1)S(1)}, u32[]{:S(2)}, u32[]{:S(2)}) collective-permute-start(bf16[1536,128]{1,0:T(8,128)(2,1)S(1)} %collective-permute-done.2.refs_2_), channel_id=1, source_target_pairs={{0,1},{1,2},{2,3},{3,4},{4,5},{5,6},{6,7},{7,0},{8,9},{9,10},{10,1... | collective-permute-start | bytes 1179656 | tf_op jit(solution)/shard_map/ppermute | solution.py:409
  35.7 9.7 %collective-permute-start.7 = (bf16[1536,128]{1,0:T(8,128)(2,1)S(1)}, bf16[1536,128]{1,0:T(8,128)(2,1)S(1)}, u32[]{:S(2)}, u32[]{:S(2)}) collective-permute-start(bf16[1536,128]{1,0:T(8,128)(2,1)S(1)} %collective-permute-done.6.refs_3_), channel_id=1, source_target_pairs={{0,7},{1,0},{2,1},{3,2},{4,3},{5,4},{6,5},{7,6},{8,15},{9,8},{10,9... | collective-permute-start | bytes 1179656 | tf_op jit(solution)/shard_map/ppermute | solution.py:410
  45.4 8.8 %collective-permute-start.4 = (bf16[1536,128]{1,0:T(8,128)(2,1)S(1)}, bf16[1536,128]{1,0:T(8,128)(2,1)S(1)}, u32[]{:S(2)}, u32[]{:S(2)}) collective-permute-start(bf16[1536,128]{1,0:T(8,128)(2,1)S(1)} %collective-permute-done.3.refs_2_), channel_id=1, source_target_pairs={{0,1},{1,2},{2,3},{3,4},{4,5},{5,6},{6,7},{7,0},{8,9},{9,10},{10,1... | collective-permute-start | bytes 1179656 | tf_op jit(solution)/shard_map/ppermute | solution.py:409
  45.4 8.9 %collective-permute-start.8 = (bf16[1536,128]{1,0:T(8,128)(2,1)S(1)}, bf16[1536,128]{1,0:T(8,128)(2,1)S(1)}, u32[]{:S(2)}, u32[]{:S(2)}) collective-permute-start(bf16[1536,128]{1,0:T(8,128)(2,1)S(1)} %collective-permute-done.7.refs_3_), channel_id=1, source_target_pairs={{0,7},{1,0},{2,1},{3,2},{4,3},{5,4},{6,5},{7,6},{8,15},{9,8},{10,9... | collective-permute-start | bytes 1179656 | tf_op jit(solution)/shard_map/ppermute | solution.py:410
  54.2 5.8 %collective-permute-start.5 = (bf16[768,128]{1,0:T(8,128)(2,1)S(1)}, bf16[768,128]{1,0:T(8,128)(2,1)S(1)}, u32[]{:S(2)}, u32[]{:S(2)}) collective-permute-start(bf16[768,128]{1,0:T(8,128)(2,1)S(1)} %slice.8), channel_id=1, source_target_pairs={{0,1},{1,2},{2,3},{3,4},{4,5},{5,6},{6,7},{7,0},{8,9},{9,10},{10,1... | collective-permute-start | bytes 589832 | tf_op jit(solution)/shard_map/ppermute | solution.py:421
  54.3 5.7 %collective-permute-start.9 = (bf16[768,128]{1,0:T(8,128)(2,1)S(1)}, bf16[768,128]{1,0:T(8,128)(2,1)S(1)}, u32[]{:S(2)}, u32[]{:S(2)}) collective-permute-start(bf16[768,128]{1,0:T(8,128)(2,1)S(1)} %slice.9), channel_id=1, source_target_pairs={{0,7},{1,0},{2,1},{3,2},{4,3},{5,4},{6,5},{7,6},{8,15},{9,8},{10,9... | collective-permute-start | bytes 589832 | tf_op jit(solution)/shard_map/ppermute | solution.py:422
  60.0 19.6 %copy-start = (bf16[1024,2048]{1,0:T(8,128)(2,1)S(1)}, bf16[1024,2048]{1,0:T(8,128)(2,1)}, u32[]{:S(2)}) copy-start(bf16[1024,2048]{1,0:T(8,128)(2,1)} %w_up.1) | copy-start | bytes 12582916
  60.0 19.6 %copy-start.1 = (bf16[2048,1024]{1,0:T(8,128)(2,1)S(1)}, bf16[2048,1024]{1,0:T(8,128)(2,1)}, u32[]{:S(2)}) copy-start(bf16[2048,1024]{1,0:T(8,128)(2,1)} %w_down.1) | copy-start | bytes 12582916
  60.0 19.6 %copy-start.2 = (bf16[512,1024]{1,0:T(8,128)(2,1)S(1)}, bf16[512,1024]{1,0:T(8,128)(2,1)}, u32[]{:S(2)}) copy-start(bf16[512,1024]{1,0:T(8,128)(2,1)} %w_output.1) | copy-start | bytes 3145732
  60.0 19.6 %copy-start.3 = (bf16[64,1024]{1,0:T(8,128)(2,1)S(1)}, bf16[64,1024]{1,0:T(8,128)(2,1)}, u32[]{:S(2)}) copy-start(bf16[64,1024]{1,0:T(8,128)(2,1)} %w_shift.1) | copy-start | bytes 393220
  60.0 19.6 %copy-start.4 = (bf16[64,1024]{1,0:T(8,128)(2,1)S(1)}, bf16[64,1024]{1,0:T(8,128)(2,1)}, u32[]{:S(2)}) copy-start(bf16[64,1024]{1,0:T(8,128)(2,1)} %w_scale.1) | copy-start | bytes 393220
  62.1 6.6 %collective-permute-start.12 = (bf16[8,96,256]{2,1,0:T(8,128)(2,1)S(1)}, bf16[8,96,256]{2,1,0:T(8,128)(2,1)S(1)}, u32[]{:S(2)}, u32[]{:S(2)}) collective-permute-start(bf16[8,96,256]{2,1,0:T(8,128)(2,1)S(1)} %get-tuple-element.41), channel_id=1, source_target_pairs={{0,64},{64,0},{1,65},{65,1},{2,66},{66,2},{3,67},{67,3},{4,68},{68... | collective-permute-start | bytes 1179656 | tf_op jit(solution)/shard_map/ppermute | solution.py:425
  83.4 2.6 %collective-permute-start.13 = (bf16[80,96]{1,0:T(8,128)(2,1)S(1)}, bf16[80,96]{1,0:T(8,128)(2,1)S(1)}, u32[]{:S(2)}, u32[]{:S(2)}) collective-permute-start(bf16[80,96]{1,0:T(8,128)(2,1)S(1)} %get-tuple-element.43), channel_id=1, source_target_pairs={{0,64},{64,0},{1,65},{65,1},{2,66},{66,2},{3,67},{67,3},{4,68},{68... | collective-permute-start | bytes 46088 | tf_op jit(solution)/shard_map/ppermute | solution.py:452
  86.7 4.5 %collective-permute-start.14 = (bf16[80,192]{1,0:T(8,128)(2,1)S(1)}, bf16[80,192]{1,0:T(8,128)(2,1)S(1)}, u32[]{:S(2)}, u32[]{:S(2)}) collective-permute-start(bf16[80,192]{1,0:T(8,128)(2,1)S(1)} %shard_map.124), channel_id=1, source_target_pairs={{0,7},{1,6},{2,5},{3,4},{4,3},{5,2},{6,1},{7,0},{8,15},{9,14},{10,... | collective-permute-start | bytes 92168 | tf_op jit(solution)/shard_map/ppermute | solution.py:460
